TPU v7x, 256 devices: a whole 4x4x8 slice. The times are simulated.
256 devices in a mesh: dp: 8 (over z), expert: 32 (over x, y, core).
Axes of the slice: x: 4, y: 4, z: 8, core: 2. Of those that a mesh axis runs over, the one named last changes fastest.
Arguments:
- tokens: bfloat16 [32768, 2048], P(('dp', 'expert')), parts along dimension 0, may hold values from -6 to 6
- expert_ids: int32 [32768, 8], P(('dp', 'expert')), parts along dimension 0, may hold values from 0 to 31, all different within a row; in each aligned block of 128 rows (0 to 127, 128 to 255, ...) at most 40 rows name the same one
- gate_weights: float32 [32768, 8], P(('dp', 'expert')), parts along dimension 0, may hold values from 0.1 to 1
- w_gate: bfloat16 [32, 2048, 768], P('expert'), may hold values from -0.125 to 0.125
- w_up: bfloat16 [32, 2048, 768], P('expert'), may hold values from -0.125 to 0.125
- w_down: bfloat16 [32, 768, 2048], P('expert'), may hold values from -0.21875 to 0.21875
Outputs:
- mixed: bfloat16 [32768, 2048], P(('dp', 'expert')), parts along dimension 0
There are 8 independent parts, one for each index of `dp`. A program takes and returns all parts, laid end to end along the dimension named above; an argument that names none is the same for every part. Nothing has to cross between parts.
Inputs may be any that keep to these rules, and one draw needn't show every extreme that they name: `expert_ids`: each row names 8 different experts. In each aligned block of 128 rows (the rows of one device) no expert is named by more than 40 rows, a bound that some block reaches.
All inputs are finite; a program needn't handle non-finite values.
Results may differ from a plain program's by a relative error of at most 0.0058.
Values may be sent and summed in bfloat16 or wider, within the bound.
No kernel may reach another device: no remote copies, remote signals or barrier semaphores. Data moves between devices by JAX's collectives and lax.ppermute only.
A program may use at most 64 MiB of HBM per device.

v0:
```python
import jax
import jax.numpy as jnp
from jax import lax
from jax.sharding import PartitionSpec as P


def per_device(tokens, expert_ids, gate_weights, w_gate, w_up, w_down):
    devices_count = lax.axis_size("expert")
    tok_count, top_count = expert_ids.shape
    width = tokens.shape[1]
    capacity = tok_count * top_count * 5 // (4 * devices_count)
    gate_mat = w_gate[0]
    up_mat = w_up[0]
    down_mat = w_down[0]
    flat_ids = expert_ids.reshape(-1)
    choose = (flat_ids[:, None] == jnp.arange(devices_count, dtype=jnp.int32)[None, :]).astype(
        jnp.int32
    )
    ranks = jnp.cumsum(choose, axis=0) - choose
    slot_ids = jnp.sum(ranks * choose, axis=1)
    token_rows = jnp.repeat(tokens, top_count, axis=0)
    outgoing = jnp.zeros((devices_count, capacity, width), jnp.bfloat16)
    outgoing = outgoing.at[flat_ids, slot_ids].set(token_rows)
    held = lax.all_to_all(outgoing, "expert", split_axis=0, concat_axis=0, tiled=True)
    lines = held.reshape(-1, width)
    gate_part = jnp.dot(lines, gate_mat, preferred_element_type=jnp.float32)
    up_part = jnp.dot(lines, up_mat, preferred_element_type=jnp.float32)
    hidden = (jax.nn.silu(gate_part) * up_part).astype(jnp.bfloat16)
    answer = jnp.dot(hidden, down_mat, preferred_element_type=jnp.float32).astype(jnp.bfloat16)
    answers = answer.reshape(held.shape)
    returned = lax.all_to_all(answers, "expert", split_axis=0, concat_axis=0, tiled=True)
    picked = returned[flat_ids, slot_ids]
    weighted = picked.astype(jnp.float32) * gate_weights.reshape(-1)[:, None]
    mixed = jnp.sum(weighted.reshape(tok_count, top_count, width), axis=1)
    return mixed.astype(jnp.bfloat16)


def solution(mesh):
    return jax.shard_map(
        per_device,
        mesh=mesh,
        in_specs=(
            P(("dp", "expert"), None),
            P(("dp", "expert"), None),
            P(("dp", "expert"), None),
            P("expert", None, None),
            P("expert", None, None),
            P("expert", None, None),
        ),
        out_specs=P(("dp", "expert"), None),
        check_vma=False,
    )
```

profile of v0, /device:TPU:104, one launch (start us, length us, event | category | flops | bytes accessed | tf_op | source)
XLA Modules:
  0.0 215.9 jit_solution(1870821361402229542)
XLA Ops:
  0.0 0.0 copy-start
  0.0 0.9 copy.8
  0.9 0.1 eq.29
  1.0 0.1 eq.25
  1.1 0.1 reshape.80
  1.2 9.0 %reduce-window.6 = s32[32,8,128]{2,1,0:T(8,128)S(1)} reduce-window(s32[32,8,128]{2,1,0:T(8,128)S(1)} %fusion.13, s32[]{:T(128)} %constant.4.clone.1), window={size=1x1x128 pad=0_0x0_0x127_0}, to_apply=%region_0.0 | reduce-window | flops 4161536 | bytes 262148 | tf_op jit(solution)/shard_map/reduce-window
  10.3 0.1 slice.10
  10.4 0.1 copy.11
  10.5 0.1 copy.12
  10.6 0.1 broadcast_add_fusion
  10.8 0.7 multiply_reduce_fusion
  11.5 0.8 and_reduce_fusion
  12.3 10.1 %scatter_custom_fusion = bf16[1280,2048]{1,0:T(8,128)(2,1)} fusion(s32[1024]{0:T(1024)S(1)} %broadcast_select_fusion, bf16[]{:T(256)} %constant.6.clone.1, bf16[128,2048]{1,0:T(8,128)(2,1)} %param.6), kind=kCustom, calls=%fused_computation.5 | custom fusion | bytes 5767170
  22.4 0.0 copy-start.2
  22.4 68.3 %all_to_all.10 = bf16[32,40,2048]{2,1,0:T(8,128)(2,1)S(1)} all-to-all(bf16[32,40,2048]{2,1,0:T(8,128)(2,1)} %bitcast.42), channel_id=1, replica_groups=mesh['dp'=8,'expert'=32] {'expert'}, dimensions={0} | all-to-all | bytes 10485760 | tf_op jit(solution)/shard_map/all_to_all | solution.py:24
  90.7 0.0 copy-done.2
  90.7 0.0 copy-start.3
  90.7 4.3 %fusion.6 = f32[1280,768]{1,0:T(8,128)S(1)} fusion(bf16[1280,2048]{1,0:T(8,128)(2,1)S(1)} %bitcast.44, bf16[1,2048,768]{2,1,0:T(8,128)(2,1)S(1)} %copy-done.2), kind=kOutput, calls=%fused_computation.11 | convolution fusion | flops 4026531840 | bytes 12320768 | tf_op jit(solution)/shard_map/dot_general | solution.py:26
  95.0 0.0 copy-done.3
  95.0 4.8 %fusion.3 = bf16[1280,768]{1,0:T(8,128)(2,1)S(1)} fusion(bf16[1280,2048]{1,0:T(8,128)(2,1)S(1)} %bitcast.45, f32[1280,768]{1,0:T(8,128)S(1)} %fusion.6, bf16[1,2048,768]{2,1,0:T(8,128)(2,1)S(1)} %copy-done.3), kind=kOutput, calls=%fused_computation.8 | convolution fusion | flops 4032430080 | bytes 14286848 | tf_op jit(solution)/shard_map/dot_general | solution.py:27
  99.8 0.0 copy-done
  99.8 6.1 %convolution_convert_fusion = bf16[1280,2048]{1,0:T(8,128)(2,1)} fusion(bf16[1280,768]{1,0:T(8,128)(2,1)S(1)} %fusion.3, bf16[1,768,2048]{2,1,0:T(8,128)(2,1)S(1)} %copy-done), kind=kOutput, calls=%fused_computation.4 | convolution fusion | flops 4029153280 | bytes 10354688 | tf_op jit(solution)/shard_map/dot_general | solution.py:29
  105.9 0.0 copy-start.1
  105.9 6.1 %all-to-all-start.1 = ((bf16[32,40,2048]{2,1,0:T(8,128)(2,1)}), bf16[32,40,2048]{2,1,0:T(8,128)(2,1)}, u32[]{:S(2)}, u32[]{:S(2)}) async-start(bf16[32,40,2048]{2,1,0:T(8,128)(2,1)} %bitcast.43), calls=%async_computation.1 | async-start | bytes 10485760 | tf_op jit(solution)/shard_map/all_to_all | solution.py:31
  112.0 0.0 copy-done.1
  112.0 0.1 copy.13
  112.1 70.9 %all-to-all-done.1 = bf16[32,40,2048]{2,1,0:T(8,128)(2,1)} async-done(((bf16[32,40,2048]{2,1,0:T(8,128)(2,1)}), bf16[32,40,2048]{2,1,0:T(8,128)(2,1)}, u32[]{:S(2)}, u32[]{:S(2)}) %all-to-all-start.1) | async-done | bytes 5242912 | tf_op jit(solution)/shard_map/all_to_all | solution.py:31
  183.0 25.6 %gather_fusion = bf16[1024,2048]{1,0:T(8,128)(2,1)} fusion(bf16[32,40,2048]{2,1,0:T(8,128)(2,1)} %all-to-all-done.1, s32[1024]{0:T(1024)S(1)} %bitcast.41), kind=kCustom, calls=%fused_computation | custom fusion | bytes 8396800 | tf_op jit(solution)/shard_map/gather | solution.py:32
  208.5 7.3 %fusion = bf16[128,2048]{1,0:T(8,128)(2,1)} fusion(bf16[1024,2048]{1,0:T(8,128)(2,1)} %gather_fusion, f32[128,8]{1,0:T(8,128)S(1)} %copy.13), kind=kLoop, calls=%fused_computation.3 | loop fusion | flops 6029312 | bytes 4722688 | tf_op jit(solution)/shard_map/reduce_sum | solution.py:34
  (6 shorter events, 0.1 us)
Async XLA Ops:
  0.0 99.8 %copy-start = (bf16[1,768,2048]{2,1,0:T(8,128)(2,1)S(1)}, bf16[1,768,2048]{2,1,0:T(8,128)(2,1)}, u32[]{:S(2)}) copy-start(bf16[1,768,2048]{2,1,0:T(8,128)(2,1)} %param.11) | copy-start | bytes 9437188
  22.4 68.3 %copy-start.2 = (bf16[1,2048,768]{2,1,0:T(8,128)(2,1)S(1)}, bf16[1,2048,768]{2,1,0:T(8,128)(2,1)}, u32[]{:S(2)}) copy-start(bf16[1,2048,768]{2,1,0:T(8,128)(2,1)} %param.9) | copy-start | bytes 9437188
  90.7 4.3 %copy-start.3 = (bf16[1,2048,768]{2,1,0:T(8,128)(2,1)S(1)}, bf16[1,2048,768]{2,1,0:T(8,128)(2,1)}, u32[]{:S(2)}) copy-start(bf16[1,2048,768]{2,1,0:T(8,128)(2,1)} %param.10) | copy-start | bytes 9437188
  105.9 6.1 %copy-start.1 = (f32[128,8]{0,1:T(8,128)S(1)}, f32[128,8]{0,1:T(8,128)}, u32[]{:S(2)}) copy-start(f32[128,8]{0,1:T(8,128)} %param.8) | copy-start | bytes 12292
  105.9 77.1 %all-to-all-start.1 = ((bf16[32,40,2048]{2,1,0:T(8,128)(2,1)}), bf16[32,40,2048]{2,1,0:T(8,128)(2,1)}, u32[]{:S(2)}, u32[]{:S(2)}) async-start(bf16[32,40,2048]{2,1,0:T(8,128)(2,1)} %bitcast.43), calls=%async_computation.1 | async-start | bytes 10485760 | tf_op jit(solution)/shard_map/all_to_all | solution.py:31
where the time goes:
time: 217 us; the launch traced here: 216 us
  waiting for transfers between devices  70.9 us (33%)
  blocking collectives  68.3 us (31%)
  local copies, waits for them, and re-layouts  37.3 us (17%)
  other arithmetic  18 us (8%)
  matrix products  15.2 us (7%)
  starting transfers between devices  6.09 us (3%)
    all_to_all x1, waiting for transfers between devices, per_device(): lax.all_to_all(answers, 'expert', split_axis=0, concat_axis=0, tiled=True)  70.9 us
    all_to_all x1, blocking collectives, per_device(): lax.all_to_all(outgoing, 'expert', split_axis=0, concat_axis=0, tiled=True)  68.3 us
    gather x1, local copies, waits for them, and re-layouts, per_device(): picked = returned[flat_ids, slot_ids]  25.6 us
    unnamed x11, local copies, waits for them, and re-layouts  11.1 us
    another operation x3, other arithmetic  9.15 us
    reduce_sum x1, other arithmetic, per_device(): mixed = jnp.sum(weighted.reshape(tok_count, top_count, width), axis=1)  7.33 us
    all_to_all x1, starting transfers between devices, per_device(): lax.all_to_all(answers, 'expert', split_axis=0, concat_axis=0, tiled=True)  6.09 us
    dot_general x1, matrix products, per_device(): jnp.dot(hidden, down_mat, preferred_element_type=jnp.float32)  6.05 us
  transfers between devices with their start and end apart: 1, of which 1 were waited for; matrix products, arithmetic and copies ran while one was open for 0% of the time, Pallas kernels for 0%

commit v1 on v0

v1 whole, which is shorter than its diff:
```python
import functools

import jax
import jax.numpy as jnp
from jax import lax
from jax.experimental import pallas as pl
from jax.experimental.pallas import tpu as pltpu
from jax.sharding import PartitionSpec as P

NX, NY, NC = 4, 4, 2
EXPERTS = NX * NY * NC
CAP = 40
META = 16
KF = 8


def index_of(x, y, c):
    return ((x % NX) * NY + (y % NY)) * NC + c


def spread_pairs(j):
    pairs = []
    for x in range(NX):
        for y in range(NY):
            pairs.append((index_of(x, y, 0), index_of(x + j, y, 0)))
            pairs.append((index_of(x, y, 1), index_of(x, y + j, 1)))
    return pairs


def deliver_pairs(k, f):
    pairs = []
    for x in range(NX):
        for y in range(NY):
            pairs.append((index_of(x, y, 0), index_of(x, y + k, f)))
            pairs.append((index_of(x, y, 1), index_of(x + k, y, 1 - f)))
    return pairs


def back(pairs):
    return [(b, a) for a, b in pairs]


def prep_kernel(tok_ref, ids_ref, gw_ref, out_ref):
    tok, top = ids_ref.shape
    lanes = 128
    ids = ids_ref[...]
    gw = gw_ref[...]
    lane = lax.broadcasted_iota(jnp.int32, (tok, lanes), 1)
    chosen = jnp.zeros((tok, lanes), jnp.float32)
    weight = jnp.zeros((tok, lanes), jnp.float32)
    for k in range(top):
        hit = ids[:, k : k + 1] == lane
        chosen = jnp.where(hit, 1.0, chosen)
        weight = jnp.where(hit, gw[:, k : k + 1], weight)
    row = lax.broadcasted_iota(jnp.int32, (tok, tok), 0)
    col = lax.broadcasted_iota(jnp.int32, (tok, tok), 1)
    earlier = jnp.where(col < row, 1.0, 0.0).astype(jnp.bfloat16)
    count = jnp.dot(earlier, chosen.astype(jnp.bfloat16), preferred_element_type=jnp.float32)
    slot = jnp.where(chosen > 0.5, count, -1.0)
    slot_t = slot.T
    weight_t = weight.T
    half = EXPERTS // 2
    meta = jnp.concatenate(
        [slot_t[:half], slot_t[half:EXPERTS], weight_t[:half], weight_t[half:EXPERTS]], axis=1
    ).astype(jnp.bfloat16)
    out_ref[:tok, :] = tok_ref[...]
    out_ref[tok:, : 4 * tok] = meta
    out_ref[tok:, 4 * tok :] = jnp.zeros((META, out_ref.shape[1] - 4 * tok), jnp.bfloat16)


def prep(tokens, ids, gw):
    tok, width = tokens.shape
    return pl.pallas_call(
        prep_kernel,
        out_shape=jax.ShapeDtypeStruct((tok + META, width), jnp.bfloat16),
        cost_estimate=pl.CostEstimate(flops=2 * tok**3, bytes_accessed=4 * tok * width, transcendentals=0),
        name="prep",
    )(tokens, ids, gw)


def select(q, meta, at, tok):
    half = EXPERTS // 2
    return jnp.dot(
        q[:, :half], meta[:, at : at + tok], preferred_element_type=jnp.float32
    ) + jnp.dot(q[:, half:], meta[:, at + tok : at + 2 * tok], preferred_element_type=jnp.float32)


def pack_kernel(q_ref, m0, m1, m2, m3, b0, b1, b2, b3, *outs):
    tok = b0.shape[0]
    q = q_ref[...]
    r = lax.broadcasted_iota(jnp.int32, (2 * CAP, 2 * tok), 0)
    t = lax.broadcasted_iota(jnp.int32, (2 * CAP, 2 * tok), 1)
    second = r >= CAP
    target = jnp.where(second, r - CAP, r)
    target = jnp.where(second == (t >= tok), target, -5).astype(jnp.float32)
    for p, (ma, mb, ba, bb) in enumerate(((m0, m1, b0, b1), (m2, m3, b2, b3))):
        slots = jnp.concatenate([select(q, m[...], 0, tok) for m in (ma, mb)], axis=1)
        rows = [
            jnp.where(slots[n : n + 1, :] == target, 1.0, 0.0).astype(jnp.bfloat16) for n in range(KF)
        ]
        pick = jnp.concatenate(rows, axis=0)
        block = jnp.concatenate([ba[...], bb[...]], axis=0)
        got = jnp.dot(pick, block, preferred_element_type=jnp.float32).astype(jnp.bfloat16)
        for n in range(KF):
            outs[n][2 * CAP * p : 2 * CAP * (p + 1), :] = got[2 * CAP * n : 2 * CAP * (n + 1), :]


def pack(q, blocks):
    rows, width = blocks[0].shape
    tok = rows - META
    cols = 512
    metas = pl.BlockSpec((META, 4 * tok), lambda i: (tok // META, 0))
    body = pl.BlockSpec((tok, cols), lambda i: (0, i))
    return pl.pallas_call(
        pack_kernel,
        grid=(width // cols,),
        in_specs=[pl.BlockSpec(q.shape, lambda i: (0, 0))] + [metas] * 4 + [body] * 4,
        out_specs=[pl.BlockSpec((4 * CAP, cols), lambda i: (0, i))] * KF,
        out_shape=[jax.ShapeDtypeStruct((4 * CAP, width), jnp.bfloat16)] * KF,
        cost_estimate=pl.CostEstimate(
            flops=2 * 2 * 640 * 256 * width, bytes_accessed=1800 * width * 2, transcendentals=0
        ),
        name="pack",
    )(q, *blocks, *blocks)


def combine_kernel(q_ref, m0, m1, m2, m3, *refs):
    backs, (own, o1, o2, o3) = refs[:KF], refs[KF:]
    tok = own.shape[0]
    q = q_ref[...]
    span = 2 * CAP * KF
    lane = lax.broadcasted_iota(jnp.int32, (2 * tok, span), 1)
    part = jnp.zeros((2 * tok, span), jnp.int32)
    for n in range(1, KF):
        part = jnp.where(lane >= 2 * CAP * n, 2 * CAP * n, part)
    r = lane - part
    t = lax.broadcasted_iota(jnp.int32, (2 * tok, span), 0)
    second = r >= CAP
    target = jnp.where(second, r - CAP, r)
    target = jnp.where(second == (t >= tok), target, -5).astype(jnp.float32)
    er = lax.broadcasted_iota(jnp.int32, (16, span), 0)
    el = lax.broadcasted_iota(jnp.int32, (16, span), 1)
    ep = jnp.zeros((16, span), jnp.int32)
    for n in range(1, KF):
        ep = jnp.where(el >= 2 * CAP * n, n, ep)
    expand = jnp.where(er == ep, 1.0, 0.0).astype(jnp.bfloat16)

    def widen(v):
        return lax.dot_general(
            v.astype(jnp.bfloat16), expand, (((0,), (0,)), ((), ())), preferred_element_type=jnp.float32
        )

    for p, (ma, mb, oa, ob) in enumerate(((m0, m1, own, o1), (m2, m3, o2, o3))):
        slots = jnp.concatenate([select(q, m[...], 0, tok) for m in (ma, mb)], axis=1)
        weights = jnp.concatenate([select(q, m[...], 2 * tok, tok) for m in (ma, mb)], axis=1)
        mix = jnp.where(widen(slots) == target, widen(weights), 0.0).astype(jnp.bfloat16)
        rows = jnp.concatenate([b[2 * CAP * p : 2 * CAP * (p + 1), :] for b in backs], axis=0)
        got = jnp.dot(mix, rows, preferred_element_type=jnp.float32)
        oa[...] = got[:tok].astype(oa.dtype)
        ob[...] = got[tok:].astype(ob.dtype)


def combine(q, blocks, backs):
    rows, width = blocks[0].shape
    tok = rows - META
    cols = 512
    metas = pl.BlockSpec((META, 4 * tok), lambda i: (tok // META, 0))
    out = pl.BlockSpec((tok, cols), lambda i: (0, i))
    return pl.pallas_call(
        combine_kernel,
        grid=(width // cols,),
        in_specs=[pl.BlockSpec(q.shape, lambda i: (0, 0))]
        + [metas] * 4
        + [pl.BlockSpec((4 * CAP, cols), lambda i: (0, i))] * KF,
        out_specs=[out] * 4,
        out_shape=[jax.ShapeDtypeStruct((tok, width), jnp.float32)]
        + [jax.ShapeDtypeStruct((tok, width), jnp.bfloat16)] * 3,
        cost_estimate=pl.CostEstimate(
            flops=2 * 2 * 640 * 256 * width, bytes_accessed=1800 * width * 2, transcendentals=0
        ),
        name="combine",
    )(q, *blocks, *backs)


def expert_kernel(count, *refs):
    slabs, (wg, wu, wd), outs, total = refs[:count], refs[count : count + 3], refs[count + 3 : -1], refs[-1]
    step = pl.program_id(0)
    lines = jnp.concatenate([s[...] for s in slabs], axis=0)
    gate = jnp.dot(lines, wg[...], preferred_element_type=jnp.float32)
    up = jnp.dot(lines, wu[...], preferred_element_type=jnp.float32)
    hidden = (gate / (1.0 + jnp.exp(-gate)) * up).astype(jnp.bfloat16)
    add = jnp.dot(hidden, wd[...], preferred_element_type=jnp.float32)

    @pl.when(step == 0)
    def _():
        total[...] = add

    @pl.when(step > 0)
    def _():
        total[...] += add

    @pl.when(step == pl.num_programs(0) - 1)
    def _():
        rows = slabs[0].shape[0]
        for n, o in enumerate(outs):
            o[...] = total[n * rows : (n + 1) * rows, :].astype(jnp.bfloat16)


def expert(slabs, w_gate, w_up, w_down):
    count = len(slabs)
    rows, width = slabs[0].shape
    ff = w_gate.shape[-1]
    tile = 256
    whole = pl.BlockSpec((rows, width), lambda i: (0, 0))
    into = pl.BlockSpec((None, width, tile), lambda i: (0, 0, i))
    down = pl.BlockSpec((None, tile, width), lambda i: (0, i, 0))
    return pl.pallas_call(
        functools.partial(expert_kernel, count),
        grid=(ff // tile,),
        in_specs=[whole] * count + [into, into, down],
        out_specs=[whole] * count,
        out_shape=[jax.ShapeDtypeStruct((rows, width), jnp.bfloat16)] * count,
        scratch_shapes=[pltpu.VMEM((count * rows, width), jnp.float32)],
        compiler_params=pltpu.CompilerParams(vmem_limit_bytes=48 * 1024 * 1024),
        cost_estimate=pl.CostEstimate(
            flops=6 * count * rows * width * ff,
            bytes_accessed=6 * width * ff + 4 * count * rows * width,
            transcendentals=count * rows * ff,
        ),
        name="expert",
    )(*slabs, w_gate, w_up, w_down)


def per_device(tokens, expert_ids, gate_weights, w_gate, w_up, w_down):
    me = lax.axis_index("expert")
    x, y, c = me // (NY * NC), (me // NC) % NY, me % NC
    n = jnp.arange(16, dtype=jnp.int32)
    k, f = n // NC, n % NC
    along_y = x * (NY * NC) + ((y + k) % NY) * NC + (c ^ f)
    along_x = ((x + k) % NX) * (NY * NC) + y * NC + (c ^ f)
    mine = jnp.where(n < KF, jnp.where(c == 0, along_y, along_x), -1)
    q = (mine[:, None] == jnp.arange(EXPERTS, dtype=jnp.int32)[None, :]).astype(jnp.bfloat16)

    send = lambda v, pairs: lax.ppermute(v, "expert", pairs)
    home = prep(tokens, expert_ids, gate_weights)
    blocks = [home] + [send(home, spread_pairs(j)) for j in (1, 2, 3)]
    packed = pack(q, blocks)
    arrived = {}
    for k in (1, 3, 2, 0):
        for f in (0, 1):
            slab = packed[NC * k + f]
            arrived[k, f] = slab if (k, f) == (0, 0) else send(slab, deliver_pairs(k, f))
    answers = {}
    for group in (((0, 0), (0, 1)), ((1, 0), (1, 1), (3, 0), (3, 1)), ((2, 0), (2, 1))):
        done = expert([arrived[g] for g in group], w_gate, w_up, w_down)
        answers.update(zip(group, done))
    backs = []
    for k in range(4):
        for f in (0, 1):
            slab = answers[k, f]
            backs.append(slab if (k, f) == (0, 0) else send(slab, back(deliver_pairs(k, f))))
    parts = combine(q, blocks, backs)
    mixed = parts[0]
    for j in (1, 2, 3):
        mixed = mixed + send(parts[j], back(spread_pairs(j))).astype(jnp.float32)
    return mixed.astype(jnp.bfloat16)


def solution(mesh):
    return jax.shard_map(
        per_device,
        mesh=mesh,
        in_specs=(
            P(("dp", "expert"), None),
            P(("dp", "expert"), None),
            P(("dp", "expert"), None),
            P("expert", None, None),
            P("expert", None, None),
            P("expert", None, None),
        ),
        out_specs=P(("dp", "expert"), None),
        check_vma=False,
    )
```

time: 217 us -> 142 us (0.65)
  the two profiles are of different devices: /device:TPU:104 before, /device:TPU:96 now
where the time goes in v1:
time: 142 us
  waiting for transfers between devices  69.4 us (49%)
  Pallas kernels  39.5 us (28%)
  starting transfers between devices  24.2 us (17%)
  local copies, waits for them, and re-layouts  5.63 us (4%)
  other arithmetic  2.98 us (2%)
    ppermute x20, waiting for transfers between devices, per_device(): send = lambda v, pairs: lax.ppermute(v, 'expert', pairs)  69.4 us
    ppermute x20, starting transfers between devices, per_device(): send = lambda v, pairs: lax.ppermute(v, 'expert', pairs)  24.2 us
    pallas_call x3, Pallas kernels, expert(): pl.pallas_call(functools.partial(expert_kernel, count), grid=(ff // tile,...  23.1 us
    pallas_call x1, Pallas kernels, combine(): pl.pallas_call(combine_kernel, grid=(width // cols,), in_specs=[pl.BlockS...  7.9 us
    pallas_call x1, Pallas kernels, pack(): pl.pallas_call(pack_kernel, grid=(width // cols,), in_specs=[pl.BlockSpec...  5.98 us
    unnamed x26, local copies, waits for them, and re-layouts  5.63 us
  transfers between devices with their start and end apart: 20, of which 8 were waited for; matrix products, arithmetic and copies ran while one was open for 0% of the time, Pallas kernels for 16%

profile of v1, /device:TPU:96, one launch (start us, length us, event | category | flops | bytes accessed | tf_op | source)
XLA Modules:
  0.0 141.9 jit_solution(12030076481585157668)
XLA Ops:
  0.0 1.4 copy.7.ids_ref
  1.4 1.4 copy.8.gw_ref
  2.8 2.5 %prep.1.m0.b0 = bf16[144,2048]{1,0:T(8,128)(2,1)} custom-call(bf16[128,2048]{1,0:T(8,128)(2,1)} %tok_ref.1, s32[128,8]{1,0:T(8,128)} %copy.7.ids_ref, f32[128,8]{1,0:T(8,128)} %copy.8.gw_ref), custom_call_target="tpu_custom_call" | custom-call | flops 4194304 | bytes 1048576 | tf_op jit(solution)/shard_map/prep/pallas_call | solution.py:73
  5.3 2.8 %collective-permute-start.2 = (bf16[144,2048]{1,0:T(8,128)(2,1)}, bf16[144,2048]{1,0:T(8,128)(2,1)}, u32[]{:S(2)}, u32[]{:S(2)}) collective-permute-start(bf16[144,2048]{1,0:T(8,128)(2,1)} %prep.1.m0.b0), channel_id=1, source_target_pairs={{0,24},{1,7},{2,26},{3,1},{4,28},{5,3},{6,30},{7,5},{8,0},{9,15},{... | collective-permute-start | bytes 1769480 | tf_op jit(solution)/shard_map/ppermute | solution.py:244
  8.1 0.8 collective-permute-start.1
  8.9 0.9 collective-permute-start
  9.8 0.7 fusion.q_ref
  10.5 11.7 %collective-permute-done.2.m3.b3 = bf16[144,2048]{1,0:T(8,128)(2,1)} collective-permute-done((bf16[144,2048]{1,0:T(8,128)(2,1)}, bf16[144,2048]{1,0:T(8,128)(2,1)}, u32[]{:S(2)}, u32[]{:S(2)}) %collective-permute-start.2) | collective-permute-done | bytes 589856 | tf_op jit(solution)/shard_map/ppermute | solution.py:244
  22.2 0.0 collective-permute-done.1.m2.b2
  22.2 3.9 %collective-permute-done.m1.b1 = bf16[144,2048]{1,0:T(8,128)(2,1)} collective-permute-done((bf16[144,2048]{1,0:T(8,128)(2,1)}, bf16[144,2048]{1,0:T(8,128)(2,1)}, u32[]{:S(2)}, u32[]{:S(2)}) %collective-permute-start) | collective-permute-done | bytes 589856 | tf_op jit(solution)/shard_map/ppermute | solution.py:244
  26.1 6.0 %pack.1 = (bf16[160,2048]{1,0:T(8,128)(2,1)}, bf16[160,2048]{1,0:T(8,128)(2,1)}, bf16[160,2048]{1,0:T(8,128)(2,1)}, bf16[160,2048]{1,0:T(8,128)(2,1)}, bf16[160,...) custom-call(bf16[16,32]{1,0:T(8,128)(2,1)} %fusion.q_ref, ...), custom_call_target="tpu_custom_call" | custom-call | flops 1342177280 | bytes 7372800 | tf_op jit(solution)/shard_map/pack/pallas_call | solution.py:114
  32.1 0.1 collective-permute-start.3
  32.2 1.7 %collective-permute-start.5 = (bf16[160,2048]{1,0:T(8,128)(2,1)}, bf16[160,2048]{1,0:T(8,128)(2,1)S(1)}, u32[]{:S(2)}, u32[]{:S(2)}) collective-permute-start(bf16[160,2048]{1,0:T(8,128)(2,1)} %get-tuple-element.29), channel_id=1, source_target_pairs={{0,2},{1,9},{2,4},{3,11},{4,6},{5,13},{6,0},{7,15},{8,10},{9,17},{... | collective-permute-start | bytes 1966088 | tf_op jit(solution)/shard_map/ppermute | solution.py:244
  33.9 0.0 collective-permute-start.6
  33.9 1.7 %collective-permute-start.7 = (bf16[160,2048]{1,0:T(8,128)(2,1)}, bf16[160,2048]{1,0:T(8,128)(2,1)S(1)}, u32[]{:S(2)}, u32[]{:S(2)}) collective-permute-start(bf16[160,2048]{1,0:T(8,128)(2,1)} %get-tuple-element.31), channel_id=1, source_target_pairs={{0,6},{1,25},{2,0},{3,27},{4,2},{5,29},{6,4},{7,31},{8,14},{9,1},{... | collective-permute-start | bytes 1966088 | tf_op jit(solution)/shard_map/ppermute | solution.py:244
  35.6 2.6 %collective-permute-start.8 = (bf16[160,2048]{1,0:T(8,128)(2,1)}, bf16[160,2048]{1,0:T(8,128)(2,1)S(1)}, u32[]{:S(2)}, u32[]{:S(2)}) collective-permute-start(bf16[160,2048]{1,0:T(8,128)(2,1)} %get-tuple-element.32), channel_id=1, source_target_pairs={{0,7},{1,24},{2,1},{3,26},{4,3},{5,28},{6,5},{7,30},{8,15},{9,0},{... | collective-permute-start | bytes 1966088 | tf_op jit(solution)/shard_map/ppermute | solution.py:244
  38.2 2.0 %collective-permute-start.11 = (bf16[160,2048]{1,0:T(8,128)(2,1)}, bf16[160,2048]{1,0:T(8,128)(2,1)S(1)}, u32[]{:S(2)}, u32[]{:S(2)}) collective-permute-start(bf16[160,2048]{1,0:T(8,128)(2,1)} %get-tuple-element.35), channel_id=1, source_target_pairs={{0,4},{1,17},{2,6},{3,19},{4,0},{5,21},{6,2},{7,23},{8,12},{9,25},... | collective-permute-start | bytes 1966088 | tf_op jit(solution)/shard_map/ppermute | solution.py:244
  40.2 1.1 copy-done.3
  41.3 6.4 %expert.3 = (bf16[160,2048]{1,0:T(8,128)(2,1)S(1)}, bf16[160,2048]{1,0:T(8,128)(2,1)S(1)}) custom-call(bf16[160,2048]{1,0:T(8,128)(2,1)S(1)} %copy-done.3, bf16[160,2048]{1,0:T(8,128)(2,1)S(1)} %collective-permute-done.3.refs_1_, bf16[1,2048,768]{2,1,0:T(8,128)(2,1)S(1)} %copy-done.1, bf16[1,2048,768]{2,1,0:T(8,128)(2,1)} %refs_3_.3, ...), custom_call_target="tpu_custom_call" | custom-call | flops 3019898880 | bytes 12058624 | tf_op jit(solution)/shard_map/expert/pallas_call | solution.py:217
  47.7 0.8 copy-done
  48.6 0.0 collective-permute-start.12
  48.6 16.2 %collective-permute-done.6.refs_1_ = bf16[160,2048]{1,0:T(8,128)(2,1)S(1)} collective-permute-done((bf16[160,2048]{1,0:T(8,128)(2,1)}, bf16[160,2048]{1,0:T(8,128)(2,1)S(1)}, u32[]{:S(2)}, u32[]{:S(2)}) %collective-permute-start.6) | collective-permute-done | bytes 655392 | tf_op jit(solution)/shard_map/ppermute | solution.py:244
  64.8 0.0 collective-permute-start.4
  64.8 0.0 collective-permute-done.8.refs_3_
  64.8 10.3 %expert.4 = (bf16[160,2048]{1,0:T(8,128)(2,1)S(1)}, bf16[160,2048]{1,0:T(8,128)(2,1)S(1)}, bf16[160,2048]{1,0:T(8,128)(2,1)S(1)}, bf16[160,2048]{1,0:T(8,128)(2,1)S(1)}) custom-call(bf16[160,2048]{1,0:T(8,128)(2,1)S(1)} %collective-permute-done.5.refs_0_, bf16[160,2048]{1,0:T(8,128)(2,1)S(1)} %collective-permute-done.6.refs_1_, ...), custom_call_target="tpu_custom_call" | custom-call | flops 6039797760 | bytes 14680064 | tf_op jit(solution)/shard_map/expert/pallas_call | solution.py:217
  75.2 3.1 %collective-permute-start.9 = (bf16[160,2048]{1,0:T(8,128)(2,1)S(1)}, bf16[160,2048]{1,0:T(8,128)(2,1)S(1)}, u32[]{:S(2)}, u32[]{:S(2)}) collective-permute-start(bf16[160,2048]{1,0:T(8,128)(2,1)S(1)} %get-tuple-element.33), channel_id=1, source_target_pairs={{2,0},{9,1},{4,2},{11,3},{6,4},{13,5},{0,6},{15,7},{10,8},{17,9},{... | collective-permute-start | bytes 1966088 | tf_op jit(solution)/shard_map/ppermute | solution.py:244
  78.3 0.0 collective-permute-start.10
  78.3 0.0 collective-permute-done.11.refs_0_
  78.3 0.0 collective-permute-start.15
  78.3 0.0 collective-permute-done.12.refs_1_
  78.3 0.1 collective-permute-start.16
  78.4 6.4 %expert.5 = (bf16[160,2048]{1,0:T(8,128)(2,1)S(1)}, bf16[160,2048]{1,0:T(8,128)(2,1)S(1)}) custom-call(bf16[160,2048]{1,0:T(8,128)(2,1)S(1)} %collective-permute-done.11.refs_0_, bf16[160,2048]{1,0:T(8,128)(2,1)S(1)} %collective-permute-done.12.refs_1_, bf16[1,2048,768]{2,1,0:T(8,128)(2,1)S(1)} %copy-done.2, bf16[1,2048,768]{2,1,0:T(8,128)(2,1)} %refs_3_.3, ...), custom_call_target="tpu_custom_call" | custom-call | flops 3019898880 | bytes 12058624 | tf_op jit(solution)/shard_map/expert/pallas_call | solution.py:217
  84.8 0.0 collective-permute-done.4.refs_1_
  84.8 4.5 %collective-permute-start.13 = (bf16[160,2048]{1,0:T(8,128)(2,1)S(1)}, bf16[160,2048]{1,0:T(8,128)(2,1)S(1)}, u32[]{:S(2)}, u32[]{:S(2)}) collective-permute-start(bf16[160,2048]{1,0:T(8,128)(2,1)S(1)} %get-tuple-element.37), channel_id=1, source_target_pairs={{4,0},{17,1},{6,2},{19,3},{0,4},{21,5},{2,6},{23,7},{12,8},{25,9},... | collective-permute-start | bytes 1966088 | tf_op jit(solution)/shard_map/ppermute | solution.py:244
  89.3 10.8 %collective-permute-done.9.refs_2_ = bf16[160,2048]{1,0:T(8,128)(2,1)S(1)} collective-permute-done((bf16[160,2048]{1,0:T(8,128)(2,1)S(1)}, bf16[160,2048]{1,0:T(8,128)(2,1)S(1)}, u32[]{:S(2)}, u32[]{:S(2)}) %collective-permute-start.9) | collective-permute-done | bytes 655392 | tf_op jit(solution)/shard_map/ppermute | solution.py:244
  100.1 0.0 collective-permute-start.14
  100.2 0.0 collective-permute-done.10.refs_3_
  100.2 0.0 collective-permute-done.15.refs_6_
  100.2 0.0 collective-permute-done.16.refs_7_
  100.2 5.8 %collective-permute-done.13.refs_4_ = bf16[160,2048]{1,0:T(8,128)(2,1)S(1)} collective-permute-done((bf16[160,2048]{1,0:T(8,128)(2,1)S(1)}, bf16[160,2048]{1,0:T(8,128)(2,1)S(1)}, u32[]{:S(2)}, u32[]{:S(2)}) %collective-permute-start.13) | collective-permute-done | bytes 655392 | tf_op jit(solution)/shard_map/ppermute | solution.py:244
  106.0 6.1 %collective-permute-done.14.refs_5_ = bf16[160,2048]{1,0:T(8,128)(2,1)S(1)} collective-permute-done((bf16[160,2048]{1,0:T(8,128)(2,1)S(1)}, bf16[160,2048]{1,0:T(8,128)(2,1)S(1)}, u32[]{:S(2)}, u32[]{:S(2)}) %collective-permute-start.14) | collective-permute-done | bytes 655392 | tf_op jit(solution)/shard_map/ppermute | solution.py:244
  112.1 0.8 copy-done.10
  113.0 7.9 %combine.1 = (f32[128,2048]{1,0:T(8,128)}, bf16[128,2048]{1,0:T(8,128)(2,1)}, bf16[128,2048]{1,0:T(8,128)(2,1)}, bf16[128,2048]{1,0:T(8,128)(2,1)}) custom-call(bf16[16,32]{1,0:T(8,128)(2,1)} %fusion.q_ref, bf16[144,2048]{1,0:T(8,128)(2,1)} %prep.1.m0.b0, bf16[144,2048]{1,0:T(8,128)(2,1)} %collective-permute-done.m1.b1, ...), custom_call_target="tpu_custom_call" | custom-call | flops 1342177280 | bytes 7372800 | tf_op jit(solution)/shard_map/combine/pallas_call | solution.py:169
  120.9 2.2 %collective-permute-start.17 = (bf16[128,2048]{1,0:T(8,128)(2,1)}, bf16[128,2048]{1,0:T(8,128)(2,1)S(1)}, u32[]{:S(2)}, u32[]{:S(2)}) collective-permute-start(bf16[128,2048]{1,0:T(8,128)(2,1)} %get-tuple-element.42), channel_id=1, source_target_pairs={{8,0},{3,1},{10,2},{5,3},{12,4},{7,5},{14,6},{1,7},{16,8},{11,9},{... | collective-permute-start | bytes 1572872 | tf_op jit(solution)/shard_map/ppermute | solution.py:244
  123.0 1.7 %collective-permute-start.18 = (bf16[128,2048]{1,0:T(8,128)(2,1)}, bf16[128,2048]{1,0:T(8,128)(2,1)S(1)}, u32[]{:S(2)}, u32[]{:S(2)}) collective-permute-start(bf16[128,2048]{1,0:T(8,128)(2,1)} %get-tuple-element.43), channel_id=1, source_target_pairs={{16,0},{5,1},{18,2},{7,3},{20,4},{1,5},{22,6},{3,7},{24,8},{13,9},... | collective-permute-start | bytes 1572872 | tf_op jit(solution)/shard_map/ppermute | solution.py:244
  124.7 11.0 %collective-permute-done.17 = bf16[128,2048]{1,0:T(8,128)(2,1)S(1)} collective-permute-done((bf16[128,2048]{1,0:T(8,128)(2,1)}, bf16[128,2048]{1,0:T(8,128)(2,1)S(1)}, u32[]{:S(2)}, u32[]{:S(2)}) %collective-permute-start.17) | collective-permute-done | bytes 524320 | tf_op jit(solution)/shard_map/ppermute | solution.py:244
  135.7 3.8 %collective-permute-done.19 = bf16[128,2048]{1,0:T(8,128)(2,1)S(1)} collective-permute-done((bf16[128,2048]{1,0:T(8,128)(2,1)}, bf16[128,2048]{1,0:T(8,128)(2,1)S(1)}, u32[]{:S(2)}, u32[]{:S(2)}) %collective-permute-start.19) | collective-permute-done | bytes 524320 | tf_op jit(solution)/shard_map/ppermute | solution.py:244
  139.6 2.3 %add_convert_fusion = bf16[128,2048]{1,0:T(8,128)(2,1)} fusion(bf16[128,2048]{1,0:T(8,128)(2,1)S(1)} %collective-permute-done.19, bf16[128,2048]{1,0:T(8,128)(2,1)S(1)} %collective-permute-done.18, f32[128,2048]{1,0:T(8,128)} %get-tuple-element.41, bf16[128,2048]{1,0:T(8,128)(2,1)S(1)} %collective-permute-done.17), kind=kLoop, calls=%fused_computation | loop fusion | flops 1835008 | bytes 3145728 | tf_op jit(solution)/shard_map/convert_element_type | solution.py:266
  (27 shorter events, 0.1 us)
Async XLA Ops:
  2.8 37.4 %copy-start.1 = (bf16[1,2048,768]{2,1,0:T(8,128)(2,1)S(1)}, bf16[1,2048,768]{2,1,0:T(8,128)(2,1)}, u32[]{:S(2)}) copy-start(bf16[1,2048,768]{2,1,0:T(8,128)(2,1)} %refs_2_.3) | copy-start | bytes 9437188
  5.3 16.8 %collective-permute-start.2 = (bf16[144,2048]{1,0:T(8,128)(2,1)}, bf16[144,2048]{1,0:T(8,128)(2,1)}, u32[]{:S(2)}, u32[]{:S(2)}) collective-permute-start(bf16[144,2048]{1,0:T(8,128)(2,1)} %prep.1.m0.b0), channel_id=1, source_target_pairs={{0,24},{1,7},{2,26},{3,1},{4,28},{5,3},{6,30},{7,5},{8,0},{9,15},{... | collective-permute-start | bytes 1769480 | tf_op jit(solution)/shard_map/ppermute | solution.py:244
  8.1 14.1 %collective-permute-start.1 = (bf16[144,2048]{1,0:T(8,128)(2,1)}, bf16[144,2048]{1,0:T(8,128)(2,1)}, u32[]{:S(2)}, u32[]{:S(2)}) collective-permute-start(bf16[144,2048]{1,0:T(8,128)(2,1)} %prep.1.m0.b0), channel_id=1, source_target_pairs={{0,16},{1,5},{2,18},{3,7},{4,20},{5,1},{6,22},{7,3},{8,24},{9,13},... | collective-permute-start | bytes 1769480 | tf_op jit(solution)/shard_map/ppermute | solution.py:244
  8.9 17.2 %collective-permute-start = (bf16[144,2048]{1,0:T(8,128)(2,1)}, bf16[144,2048]{1,0:T(8,128)(2,1)}, u32[]{:S(2)}, u32[]{:S(2)}) collective-permute-start(bf16[144,2048]{1,0:T(8,128)(2,1)} %prep.1.m0.b0), channel_id=1, source_target_pairs={{0,8},{1,3},{2,10},{3,5},{4,12},{5,7},{6,14},{7,1},{8,16},{9,11},{... | collective-permute-start | bytes 1769480 | tf_op jit(solution)/shard_map/ppermute | solution.py:244
  32.1 6.1 %collective-permute-start.3 = (bf16[160,2048]{1,0:T(8,128)(2,1)}, bf16[160,2048]{1,0:T(8,128)(2,1)S(1)}, u32[]{:S(2)}, u32[]{:S(2)}) collective-permute-start(bf16[160,2048]{1,0:T(8,128)(2,1)} %get-tuple-element.26), channel_id=1, source_target_pairs={{0,1},{1,0},{2,3},{3,2},{4,5},{5,4},{6,7},{7,6},{8,9},{9,8},{10,11... | collective-permute-start | bytes 1966088 | tf_op jit(solution)/shard_map/ppermute | solution.py:244
  32.2 16.3 %collective-permute-start.5 = (bf16[160,2048]{1,0:T(8,128)(2,1)}, bf16[160,2048]{1,0:T(8,128)(2,1)S(1)}, u32[]{:S(2)}, u32[]{:S(2)}) collective-permute-start(bf16[160,2048]{1,0:T(8,128)(2,1)} %get-tuple-element.29), channel_id=1, source_target_pairs={{0,2},{1,9},{2,4},{3,11},{4,6},{5,13},{6,0},{7,15},{8,10},{9,17},{... | collective-permute-start | bytes 1966088 | tf_op jit(solution)/shard_map/ppermute | solution.py:244
  33.9 30.9 %collective-permute-start.6 = (bf16[160,2048]{1,0:T(8,128)(2,1)}, bf16[160,2048]{1,0:T(8,128)(2,1)S(1)}, u32[]{:S(2)}, u32[]{:S(2)}) collective-permute-start(bf16[160,2048]{1,0:T(8,128)(2,1)} %get-tuple-element.30), channel_id=1, source_target_pairs={{0,3},{1,8},{2,5},{3,10},{4,7},{5,12},{6,1},{7,14},{8,11},{9,16},{... | collective-permute-start | bytes 1966088 | tf_op jit(solution)/shard_map/ppermute | solution.py:244
  33.9 30.9 %collective-permute-start.7 = (bf16[160,2048]{1,0:T(8,128)(2,1)}, bf16[160,2048]{1,0:T(8,128)(2,1)S(1)}, u32[]{:S(2)}, u32[]{:S(2)}) collective-permute-start(bf16[160,2048]{1,0:T(8,128)(2,1)} %get-tuple-element.31), channel_id=1, source_target_pairs={{0,6},{1,25},{2,0},{3,27},{4,2},{5,29},{6,4},{7,31},{8,14},{9,1},{... | collective-permute-start | bytes 1966088 | tf_op jit(solution)/shard_map/ppermute | solution.py:244
  35.6 29.3 %collective-permute-start.8 = (bf16[160,2048]{1,0:T(8,128)(2,1)}, bf16[160,2048]{1,0:T(8,128)(2,1)S(1)}, u32[]{:S(2)}, u32[]{:S(2)}) collective-permute-start(bf16[160,2048]{1,0:T(8,128)(2,1)} %get-tuple-element.32), channel_id=1, source_target_pairs={{0,7},{1,24},{2,1},{3,26},{4,3},{5,28},{6,5},{7,30},{8,15},{9,0},{... | collective-permute-start | bytes 1966088 | tf_op jit(solution)/shard_map/ppermute | solution.py:244
  38.2 40.1 %collective-permute-start.11 = (bf16[160,2048]{1,0:T(8,128)(2,1)}, bf16[160,2048]{1,0:T(8,128)(2,1)S(1)}, u32[]{:S(2)}, u32[]{:S(2)}) collective-permute-start(bf16[160,2048]{1,0:T(8,128)(2,1)} %get-tuple-element.35), channel_id=1, source_target_pairs={{0,4},{1,17},{2,6},{3,19},{4,0},{5,21},{6,2},{7,23},{8,12},{9,25},... | collective-permute-start | bytes 1966088 | tf_op jit(solution)/shard_map/ppermute | solution.py:244
  40.2 1.1 copy-start.3
  41.3 7.2 %copy-start.11 = (bf16[160,2048]{1,0:T(8,128)(2,1)S(1)}, bf16[160,2048]{1,0:T(8,128)(2,1)}, u32[]{:S(2)}) copy-start(bf16[160,2048]{1,0:T(8,128)(2,1)} %get-tuple-element.36) | copy-start | bytes 1966084
  47.7 0.8 copy-start
  48.6 29.8 %collective-permute-start.12 = (bf16[160,2048]{1,0:T(8,128)(2,1)S(1)}, bf16[160,2048]{1,0:T(8,128)(2,1)S(1)}, u32[]{:S(2)}, u32[]{:S(2)}) collective-permute-start(bf16[160,2048]{1,0:T(8,128)(2,1)S(1)} %copy-done.11), channel_id=1, source_target_pairs={{0,5},{1,16},{2,7},{3,18},{4,1},{5,20},{6,3},{7,22},{8,13},{9,24},... | collective-permute-start | bytes 1966088 | tf_op jit(solution)/shard_map/ppermute | solution.py:244
  64.8 13.6 %copy-start.2 = (bf16[1,2048,768]{2,1,0:T(8,128)(2,1)S(1)}, bf16[1,2048,768]{2,1,0:T(8,128)(2,1)}, u32[]{:S(2)}) copy-start(bf16[1,2048,768]{2,1,0:T(8,128)(2,1)} %refs_2_.3) | copy-start | bytes 9437188
  64.8 20.0 %collective-permute-start.4 = (bf16[160,2048]{1,0:T(8,128)(2,1)S(1)}, bf16[160,2048]{1,0:T(8,128)(2,1)S(1)}, u32[]{:S(2)}, u32[]{:S(2)}) collective-permute-start(bf16[160,2048]{1,0:T(8,128)(2,1)S(1)} %get-tuple-element.28), channel_id=1, source_target_pairs={{1,0},{0,1},{3,2},{2,3},{5,4},{4,5},{7,6},{6,7},{9,8},{8,9},{11,10... | collective-permute-start | bytes 1966088 | tf_op jit(solution)/shard_map/ppermute | solution.py:244
  75.2 25.0 %collective-permute-start.9 = (bf16[160,2048]{1,0:T(8,128)(2,1)S(1)}, bf16[160,2048]{1,0:T(8,128)(2,1)S(1)}, u32[]{:S(2)}, u32[]{:S(2)}) collective-permute-start(bf16[160,2048]{1,0:T(8,128)(2,1)S(1)} %get-tuple-element.33), channel_id=1, source_target_pairs={{2,0},{9,1},{4,2},{11,3},{6,4},{13,5},{0,6},{15,7},{10,8},{17,9},{... | collective-permute-start | bytes 1966088 | tf_op jit(solution)/shard_map/ppermute | solution.py:244
  78.3 21.8 %collective-permute-start.10 = (bf16[160,2048]{1,0:T(8,128)(2,1)S(1)}, bf16[160,2048]{1,0:T(8,128)(2,1)S(1)}, u32[]{:S(2)}, u32[]{:S(2)}) collective-permute-start(bf16[160,2048]{1,0:T(8,128)(2,1)S(1)} %get-tuple-element.34), channel_id=1, source_target_pairs={{3,0},{8,1},{5,2},{10,3},{7,4},{12,5},{1,6},{14,7},{11,8},{16,9},{... | collective-permute-start | bytes 1966088 | tf_op jit(solution)/shard_map/ppermute | solution.py:244
  78.3 21.8 %collective-permute-start.15 = (bf16[160,2048]{1,0:T(8,128)(2,1)S(1)}, bf16[160,2048]{1,0:T(8,128)(2,1)S(1)}, u32[]{:S(2)}, u32[]{:S(2)}) collective-permute-start(bf16[160,2048]{1,0:T(8,128)(2,1)S(1)} %get-tuple-element.39), channel_id=1, source_target_pairs={{6,0},{25,1},{0,2},{27,3},{2,4},{29,5},{4,6},{31,7},{14,8},{1,9},{... | collective-permute-start | bytes 1966088 | tf_op jit(solution)/shard_map/ppermute | solution.py:244
  78.3 21.8 %collective-permute-start.16 = (bf16[160,2048]{1,0:T(8,128)(2,1)S(1)}, bf16[160,2048]{1,0:T(8,128)(2,1)S(1)}, u32[]{:S(2)}, u32[]{:S(2)}) collective-permute-start(bf16[160,2048]{1,0:T(8,128)(2,1)S(1)} %get-tuple-element.40), channel_id=1, source_target_pairs={{7,0},{24,1},{1,2},{26,3},{3,4},{28,5},{5,6},{30,7},{15,8},{0,9},{... | collective-permute-start | bytes 1966088 | tf_op jit(solution)/shard_map/ppermute | solution.py:244
  84.8 27.3 %copy-start.4 = (bf16[160,2048]{1,0:T(8,128)(2,1)}, bf16[160,2048]{1,0:T(8,128)(2,1)S(1)}, u32[]{:S(2)}) copy-start(bf16[160,2048]{1,0:T(8,128)(2,1)S(1)} %collective-permute-done.4.refs_1_) | copy-start | bytes 1966084
  84.8 21.2 %collective-permute-start.13 = (bf16[160,2048]{1,0:T(8,128)(2,1)S(1)}, bf16[160,2048]{1,0:T(8,128)(2,1)S(1)}, u32[]{:S(2)}, u32[]{:S(2)}) collective-permute-start(bf16[160,2048]{1,0:T(8,128)(2,1)S(1)} %get-tuple-element.37), channel_id=1, source_target_pairs={{4,0},{17,1},{6,2},{19,3},{0,4},{21,5},{2,6},{23,7},{12,8},{25,9},... | collective-permute-start | bytes 1966088 | tf_op jit(solution)/shard_map/ppermute | solution.py:244
  100.1 11.9 %copy-start.5 = (bf16[160,2048]{1,0:T(8,128)(2,1)}, bf16[160,2048]{1,0:T(8,128)(2,1)S(1)}, u32[]{:S(2)}) copy-start(bf16[160,2048]{1,0:T(8,128)(2,1)S(1)} %collective-permute-done.9.refs_2_) | copy-start | bytes 1966084
  100.1 11.9 %collective-permute-start.14 = (bf16[160,2048]{1,0:T(8,128)(2,1)S(1)}, bf16[160,2048]{1,0:T(8,128)(2,1)S(1)}, u32[]{:S(2)}, u32[]{:S(2)}) collective-permute-start(bf16[160,2048]{1,0:T(8,128)(2,1)S(1)} %get-tuple-element.38), channel_id=1, source_target_pairs={{5,0},{16,1},{7,2},{18,3},{1,4},{20,5},{3,6},{22,7},{13,8},{24,9},... | collective-permute-start | bytes 1966088 | tf_op jit(solution)/shard_map/ppermute | solution.py:244
  100.2 11.9 %copy-start.6 = (bf16[160,2048]{1,0:T(8,128)(2,1)}, bf16[160,2048]{1,0:T(8,128)(2,1)S(1)}, u32[]{:S(2)}) copy-start(bf16[160,2048]{1,0:T(8,128)(2,1)S(1)} %collective-permute-done.10.refs_3_) | copy-start | bytes 1966084
  100.2 11.9 %copy-start.7 = (bf16[160,2048]{1,0:T(8,128)(2,1)}, bf16[160,2048]{1,0:T(8,128)(2,1)S(1)}, u32[]{:S(2)}) copy-start(bf16[160,2048]{1,0:T(8,128)(2,1)S(1)} %collective-permute-done.15.refs_6_) | copy-start | bytes 1966084
  100.2 11.9 %copy-start.8 = (bf16[160,2048]{1,0:T(8,128)(2,1)}, bf16[160,2048]{1,0:T(8,128)(2,1)S(1)}, u32[]{:S(2)}) copy-start(bf16[160,2048]{1,0:T(8,128)(2,1)S(1)} %collective-permute-done.16.refs_7_) | copy-start | bytes 1966084
  106.0 7.0 %copy-start.9 = (bf16[160,2048]{1,0:T(8,128)(2,1)}, bf16[160,2048]{1,0:T(8,128)(2,1)S(1)}, u32[]{:S(2)}) copy-start(bf16[160,2048]{1,0:T(8,128)(2,1)S(1)} %collective-permute-done.13.refs_4_) | copy-start | bytes 1966084
  112.1 0.8 copy-start.10
  120.9 14.8 %collective-permute-start.17 = (bf16[128,2048]{1,0:T(8,128)(2,1)}, bf16[128,2048]{1,0:T(8,128)(2,1)S(1)}, u32[]{:S(2)}, u32[]{:S(2)}) collective-permute-start(bf16[128,2048]{1,0:T(8,128)(2,1)} %get-tuple-element.42), channel_id=1, source_target_pairs={{8,0},{3,1},{10,2},{5,3},{12,4},{7,5},{14,6},{1,7},{16,8},{11,9},{... | collective-permute-start | bytes 1572872 | tf_op jit(solution)/shard_map/ppermute | solution.py:244
  123.0 12.7 %collective-permute-start.18 = (bf16[128,2048]{1,0:T(8,128)(2,1)}, bf16[128,2048]{1,0:T(8,128)(2,1)S(1)}, u32[]{:S(2)}, u32[]{:S(2)}) collective-permute-start(bf16[128,2048]{1,0:T(8,128)(2,1)} %get-tuple-element.43), channel_id=1, source_target_pairs={{16,0},{5,1},{18,2},{7,3},{20,4},{1,5},{22,6},{3,7},{24,8},{13,9},... | collective-permute-start | bytes 1572872 | tf_op jit(solution)/shard_map/ppermute | solution.py:244
  124.7 14.8 %collective-permute-start.19 = (bf16[128,2048]{1,0:T(8,128)(2,1)}, bf16[128,2048]{1,0:T(8,128)(2,1)S(1)}, u32[]{:S(2)}, u32[]{:S(2)}) collective-permute-start(bf16[128,2048]{1,0:T(8,128)(2,1)} %get-tuple-element.44), channel_id=1, source_target_pairs={{24,0},{7,1},{26,2},{1,3},{28,4},{3,5},{30,6},{5,7},{0,8},{15,9},{... | collective-permute-start | bytes 1572872 | tf_op jit(solution)/shard_map/ppermute | solution.py:244

commit v2 on v1

v2 whole, which is shorter than its diff:
```python
import functools

import jax
import jax.numpy as jnp
from jax import lax
from jax.experimental import pallas as pl
from jax.experimental.pallas import tpu as pltpu
from jax.sharding import PartitionSpec as P

NX, NY, NC = 4, 4, 2
EXPERTS = NX * NY * NC
CAP = 40
KF = 8


def index_of(x, y, c):
    return ((x % NX) * NY + (y % NY)) * NC + c


def spread_pairs(j):
    pairs = []
    for x in range(NX):
        for y in range(NY):
            pairs.append((index_of(x, y, 0), index_of(x + j, y, 0)))
            pairs.append((index_of(x, y, 1), index_of(x, y + j, 1)))
    return pairs


def deliver_pairs(k, f):
    pairs = []
    for x in range(NX):
        for y in range(NY):
            pairs.append((index_of(x, y, 0), index_of(x, y + k, f)))
            pairs.append((index_of(x, y, 1), index_of(x + k, y, 1 - f)))
    return pairs


def back(pairs):
    return [(b, a) for a, b in pairs]


def prep_kernel(ids_ref, gw_ref, out_ref):
    top, tok = ids_ref.shape
    ids = ids_ref[...]
    gw = gw_ref[...]
    name = lax.broadcasted_iota(jnp.int32, (EXPERTS, tok), 0)
    chosen = jnp.zeros((EXPERTS, tok), jnp.float32)
    weight = jnp.zeros((EXPERTS, tok), jnp.float32)
    for k in range(top):
        hit = ids[k : k + 1, :] == name
        chosen = jnp.where(hit, 1.0, chosen)
        weight = jnp.where(hit, gw[k : k + 1, :], weight)
    row = lax.broadcasted_iota(jnp.int32, (tok, tok), 0)
    col = lax.broadcasted_iota(jnp.int32, (tok, tok), 1)
    earlier = jnp.where(row < col, 1.0, 0.0).astype(jnp.bfloat16)
    count = jnp.dot(chosen.astype(jnp.bfloat16), earlier, preferred_element_type=jnp.float32)
    slot = jnp.where(chosen > 0.5, count, -1.0)
    half = EXPERTS // 2
    out_ref[...] = jnp.concatenate(
        [slot[:half], slot[half:], weight[:half], weight[half:]], axis=1
    ).astype(jnp.bfloat16)


def prep(ids, gw):
    tok = ids.shape[1]
    return pl.pallas_call(
        prep_kernel,
        out_shape=jax.ShapeDtypeStruct((EXPERTS // 2, 4 * tok), jnp.bfloat16),
        cost_estimate=pl.CostEstimate(flops=2 * EXPERTS * tok**2, bytes_accessed=32 * tok * 4, transcendentals=0),
        name="prep",
    )(ids, gw)


def select(q, meta, at, tok):
    half = EXPERTS // 2
    return jnp.dot(
        q[:, :half], meta[:, at : at + tok], preferred_element_type=jnp.float32
    ) + jnp.dot(q[:, half:], meta[:, at + tok : at + 2 * tok], preferred_element_type=jnp.float32)


def pack_kernel(which, q_ref, *refs):
    metas, blocks, outs = refs[:4], refs[4:8], refs[-len(which) :]
    tok, width = blocks[0].shape
    q = q_ref[...]
    r = lax.broadcasted_iota(jnp.int32, (2 * CAP, 2 * tok), 0)
    t = lax.broadcasted_iota(jnp.int32, (2 * CAP, 2 * tok), 1)
    second = r >= CAP
    target = jnp.where(second, r - CAP, r)
    target = jnp.where(second == (t >= tok), target, -5).astype(jnp.float32)
    cols = 512
    for p in range(2):
        slots = jnp.concatenate([select(q, m[...], 0, tok) for m in metas[2 * p : 2 * p + 2]], axis=1)
        pick = jnp.concatenate(
            [jnp.where(slots[n : n + 1, :] == target, 1.0, 0.0).astype(jnp.bfloat16) for n in which], axis=0
        )
        for at in range(0, width, cols):
            block = jnp.concatenate([b[:, at : at + cols] for b in blocks[2 * p : 2 * p + 2]], axis=0)
            got = jnp.dot(pick, block, preferred_element_type=jnp.float32).astype(jnp.bfloat16)
            for n, o in enumerate(outs):
                o[2 * CAP * p : 2 * CAP * (p + 1), at : at + cols] = got[2 * CAP * n : 2 * CAP * (n + 1), :]


def pack(which, q, metas, blocks, after=()):
    tok, width = blocks[0].shape
    count = len(which)
    vmem = pl.BlockSpec(memory_space=pltpu.VMEM)
    return pl.pallas_call(
        functools.partial(pack_kernel, which),
        in_specs=[vmem] * 9 + [pl.BlockSpec(memory_space=pl.ANY)] * len(after),
        out_specs=[vmem] * count,
        out_shape=[jax.ShapeDtypeStruct((4 * CAP, width), jnp.bfloat16)] * count,
        compiler_params=pltpu.CompilerParams(vmem_limit_bytes=24 * 1024 * 1024),
        cost_estimate=pl.CostEstimate(
            flops=2 * 4 * CAP * count * 2 * tok * width,
            bytes_accessed=2 * (4 * tok + 4 * CAP * count) * width,
            transcendentals=0,
        ),
        name="pack",
    )(q, *metas, *blocks, *after)


def combine_kernel(q_ref, *refs):
    metas, backs, outs = refs[:4], refs[4 : 4 + KF], refs[4 + KF :]
    tok, width = outs[0].shape
    q = q_ref[...]
    span = 2 * CAP * KF
    lane = lax.broadcasted_iota(jnp.int32, (2 * tok, span), 1)
    part = jnp.zeros((2 * tok, span), jnp.int32)
    er = lax.broadcasted_iota(jnp.int32, (16, span), 0)
    el = lax.broadcasted_iota(jnp.int32, (16, span), 1)
    ep = jnp.zeros((16, span), jnp.int32)
    for n in range(1, KF):
        part = jnp.where(lane >= 2 * CAP * n, 2 * CAP * n, part)
        ep = jnp.where(el >= 2 * CAP * n, n, ep)
    r = lane - part
    t = lax.broadcasted_iota(jnp.int32, (2 * tok, span), 0)
    second = r >= CAP
    target = jnp.where(second, r - CAP, r)
    target = jnp.where(second == (t >= tok), target, -5).astype(jnp.float32)
    expand = jnp.where(er == ep, 1.0, 0.0).astype(jnp.bfloat16)

    def widen(v):
        return lax.dot_general(
            v.astype(jnp.bfloat16), expand, (((0,), (0,)), ((), ())), preferred_element_type=jnp.float32
        )

    cols = 512
    for p in range(2):
        pair = metas[2 * p : 2 * p + 2]
        slots = jnp.concatenate([select(q, m[...], 0, tok) for m in pair], axis=1)
        weights = jnp.concatenate([select(q, m[...], 2 * tok, tok) for m in pair], axis=1)
        mix = jnp.where(widen(slots) == target, widen(weights), 0.0).astype(jnp.bfloat16)
        for at in range(0, width, cols):
            rows = jnp.concatenate(
                [b[2 * CAP * p : 2 * CAP * (p + 1), at : at + cols] for b in backs], axis=0
            )
            got = jnp.dot(mix, rows, preferred_element_type=jnp.float32)
            for n, o in enumerate(outs[2 * p : 2 * p + 2]):
                o[:, at : at + cols] = got[n * tok : (n + 1) * tok].astype(o.dtype)


def combine(q, metas, backs):
    tok = metas[0].shape[1] // 4
    width = backs[0].shape[1]
    vmem = pl.BlockSpec(memory_space=pltpu.VMEM)
    return pl.pallas_call(
        combine_kernel,
        in_specs=[vmem] * (5 + KF),
        out_specs=[vmem] * 4,
        out_shape=[jax.ShapeDtypeStruct((tok, width), jnp.float32)]
        + [jax.ShapeDtypeStruct((tok, width), jnp.bfloat16)] * 3,
        compiler_params=pltpu.CompilerParams(vmem_limit_bytes=24 * 1024 * 1024),
        cost_estimate=pl.CostEstimate(
            flops=2 * 2 * 2 * CAP * KF * 2 * tok * width,
            bytes_accessed=2 * (5 * tok + 4 * CAP * KF) * width,
            transcendentals=0,
        ),
        name="combine",
    )(q, *metas, *backs)


def expert_kernel(count, *refs):
    slabs, (wg, wu, wd), outs = refs[:count], refs[count : count + 3], refs[count + 3 :]
    rows, width = slabs[0].shape
    ff = wg.shape[-1]
    lines = jnp.concatenate([s[...] for s in slabs], axis=0)
    hidden = []
    for at in range(0, ff, 256):
        gate = jnp.dot(lines, wg[0, :, at : at + 256], preferred_element_type=jnp.float32)
        up = jnp.dot(lines, wu[0, :, at : at + 256], preferred_element_type=jnp.float32)
        hidden.append((gate / (1.0 + jnp.exp(-gate)) * up).astype(jnp.bfloat16))
    hidden = jnp.concatenate(hidden, axis=1)
    for at in range(0, width, 512):
        got = jnp.dot(hidden, wd[0, :, at : at + 512], preferred_element_type=jnp.float32)
        for n, o in enumerate(outs):
            o[:, at : at + 512] = got[n * rows : (n + 1) * rows].astype(jnp.bfloat16)


def expert(slabs, weights):
    count = len(slabs)
    rows, width = slabs[0].shape
    ff = weights[0].shape[-1]
    vmem = pl.BlockSpec(memory_space=pltpu.VMEM)
    return pl.pallas_call(
        functools.partial(expert_kernel, count),
        in_specs=[vmem] * (count + 3),
        out_specs=[vmem] * count,
        out_shape=[jax.ShapeDtypeStruct((rows, width), jnp.bfloat16)] * count,
        compiler_params=pltpu.CompilerParams(vmem_limit_bytes=24 * 1024 * 1024),
        cost_estimate=pl.CostEstimate(
            flops=6 * count * rows * width * ff,
            bytes_accessed=4 * count * rows * width,
            transcendentals=count * rows * ff,
        ),
        name="expert",
    )(*slabs, *[pltpu.with_memory_space_constraint(w, pltpu.VMEM) for w in weights])


def per_device(tokens, expert_ids, gate_weights, w_gate, w_up, w_down):
    me = lax.axis_index("expert")
    x, y, c = me // (NY * NC), (me // NC) % NY, me % NC
    n = jnp.arange(16, dtype=jnp.int32)
    k, f = n // NC, n % NC
    along_y = x * (NY * NC) + ((y + k) % NY) * NC + (c ^ f)
    along_x = ((x + k) % NX) * (NY * NC) + y * NC + (c ^ f)
    mine = jnp.where(n < KF, jnp.where(c == 0, along_y, along_x), -1)
    q = (mine[:, None] == jnp.arange(EXPERTS, dtype=jnp.int32)[None, :]).astype(jnp.bfloat16)

    send = lambda v, pairs: lax.ppermute(v, "expert", pairs)
    blocks = [tokens] + [send(tokens, spread_pairs(j)) for j in (1, 2, 3)]
    meta = prep(expert_ids.T, gate_weights.T)
    metas = [meta] + [send(meta, spread_pairs(j)) for j in (1, 2, 3)]
    weights = (w_gate, w_up, w_down)

    arrived = {}

    def deliver(keys, after=()):
        slabs = pack([NC * k + f for k, f in keys], q, metas, blocks, after)
        for (k, f), slab in zip(keys, slabs):
            arrived[k, f] = slab if (k, f) == (0, 0) else send(slab, deliver_pairs(k, f))

    backs = {}

    def work(keys):
        done = expert([arrived[g] for g in keys], weights)
        for (k, f), slab in zip(keys, done):
            backs[k, f] = slab if (k, f) == (0, 0) else send(slab, back(deliver_pairs(k, f)))
        return done[0]

    near = [(1, 0), (1, 1), (3, 0), (3, 1)]
    deliver(near + [(0, 0), (0, 1)])
    first = work([(0, 0), (0, 1)])
    deliver([(2, 0), (2, 1)], (first,))
    work(near[:2])
    work(near[2:])
    work([(2, 0), (2, 1)])
    parts = combine(q, metas, [backs[k, f] for k in range(4) for f in (0, 1)])
    mixed = parts[0]
    for j in (1, 2, 3):
        mixed = mixed + send(parts[j], back(spread_pairs(j))).astype(jnp.float32)
    return mixed.astype(jnp.bfloat16)


def solution(mesh):
    return jax.shard_map(
        per_device,
        mesh=mesh,
        in_specs=(
            P(("dp", "expert"), None),
            P(("dp", "expert"), None),
            P(("dp", "expert"), None),
            P("expert", None, None),
            P("expert", None, None),
            P("expert", None, None),
        ),
        out_specs=P(("dp", "expert"), None),
        check_vma=False,
    )
```

time: 142 us -> 120 us (0.85)
  Pallas kernels: 39.5 us -> 19.3 us
  starting transfers between devices: 24.2 us -> 38.3 us
  waiting for transfers between devices: 69.4 us -> 55.6 us
  other arithmetic: 2.98 us -> 1.16 us
    pallas_call x6 -> x8, Pallas kernels: 39.5 us -> 19.3 us  [the longest x4 13 us: expert(): pl.pallas_call(functools.partial(expert_kernel, count), in_specs=[vmem] *...]
    ppermute x20 -> x23, starting transfers between devices: 24.2 us -> 38.3 us  [per_device(): send = lambda v, pairs: lax.ppermute(v, 'expert', pairs)]
    ppermute x20 -> x23, waiting for transfers between devices: 69.4 us -> 55.6 us  [per_device(): send = lambda v, pairs: lax.ppermute(v, 'expert', pairs)]
    unnamed x26 -> x16, local copies, waits for them, and re-layouts: 5.63 us -> 5.55 us
  transfers between devices with their start and end apart: 20 -> 23, of which waited for: 8 -> 11; matrix products, arithmetic and copies ran while one was open for 0% -> 0% of each run, Pallas kernels for 16% -> 13%
where the time goes in v2:
time: 120 us
  waiting for transfers between devices  55.6 us (46%)
  starting transfers between devices  38.3 us (32%)
  Pallas kernels  19.3 us (16%)
  local copies, waits for them, and re-layouts  5.55 us (5%)
    ppermute x23, waiting for transfers between devices, per_device(): send = lambda v, pairs: lax.ppermute(v, 'expert', pairs)  55.6 us
    ppermute x23, starting transfers between devices, per_device(): send = lambda v, pairs: lax.ppermute(v, 'expert', pairs)  38.3 us
    pallas_call x4, Pallas kernels, expert(): pl.pallas_call(functools.partial(expert_kernel, count), in_specs=[vmem] *...  13 us
    unnamed x16, local copies, waits for them, and re-layouts  5.55 us
    pallas_call x1, Pallas kernels, combine(): pl.pallas_call(combine_kernel, in_specs=[vmem] * (5 + KF), out_specs=[vme...  2.61 us
  transfers between devices with their start and end apart: 23, of which 11 were waited for; matrix products, arithmetic and copies ran while one was open for 0% of the time, Pallas kernels for 13%

profile of v2, /device:TPU:96, one launch (start us, length us, event | category | flops | bytes accessed | tf_op | source)
XLA Modules:
  0.0 120.1 jit_solution(6618312544732862215)
XLA Ops:
  0.0 2.8 %collective-permute-start.5 = (bf16[128,2048]{1,0:T(8,128)(2,1)}, bf16[128,2048]{1,0:T(8,128)(2,1)S(1)}, u32[]{:S(2)}, u32[]{:S(2)}) collective-permute-start(bf16[128,2048]{1,0:T(8,128)(2,1)} %refs_4_.9), channel_id=1, source_target_pairs={{0,24},{1,7},{2,26},{3,1},{4,28},{5,3},{6,30},{7,5},{8,0},{9,15},{... | collective-permute-start | bytes 1572872 | tf_op jit(solution)/shard_map/ppermute | solution.py:229
  2.8 0.8 collective-permute-start.4
  3.6 0.9 collective-permute-start.3
  4.4 1.4 %prep.1.refs_0_ = bf16[16,512]{1,0:T(8,128)(2,1)} custom-call(s32[8,128]{1,0:T(8,128)} %bitcast.2, f32[8,128]{1,0:T(8,128)} %bitcast.3), custom_call_target="tpu_custom_call" | custom-call | flops 1048576 | bytes 16384 | tf_op jit(solution)/shard_map/prep/pallas_call | solution.py:66
  5.9 2.4 %collective-permute-start.2 = (bf16[16,512]{1,0:T(8,128)(2,1)}, bf16[16,512]{1,0:T(8,128)(2,1)S(1)}, u32[]{:S(2)}, u32[]{:S(2)}) collective-permute-start(bf16[16,512]{1,0:T(8,128)(2,1)} %prep.1.refs_0_), channel_id=1, source_target_pairs={{0,24},{1,7},{2,26},{3,1},{4,28},{5,3},{6,30},{7,5},{8,0},{9,15},{... | collective-permute-start | bytes 49160 | tf_op jit(solution)/shard_map/ppermute | solution.py:229
  8.2 1.5 %collective-permute-start.1 = (bf16[16,512]{1,0:T(8,128)(2,1)}, bf16[16,512]{1,0:T(8,128)(2,1)S(1)}, u32[]{:S(2)}, u32[]{:S(2)}) collective-permute-start(bf16[16,512]{1,0:T(8,128)(2,1)} %prep.1.refs_0_), channel_id=1, source_target_pairs={{0,16},{1,5},{2,18},{3,7},{4,20},{5,1},{6,22},{7,3},{8,24},{9,13},... | collective-permute-start | bytes 49160 | tf_op jit(solution)/shard_map/ppermute | solution.py:229
  9.8 5.9 %collective-permute-done.2.refs_3_ = bf16[16,512]{1,0:T(8,128)(2,1)S(1)} collective-permute-done((bf16[16,512]{1,0:T(8,128)(2,1)}, bf16[16,512]{1,0:T(8,128)(2,1)S(1)}, u32[]{:S(2)}, u32[]{:S(2)}) %collective-permute-start.2) | collective-permute-done | bytes 16416 | tf_op jit(solution)/shard_map/ppermute | solution.py:229
  15.7 0.0 collective-permute-start
  15.7 0.1 fusion.q_ref
  15.7 3.8 %collective-permute-done.1.refs_2_ = bf16[16,512]{1,0:T(8,128)(2,1)S(1)} collective-permute-done((bf16[16,512]{1,0:T(8,128)(2,1)}, bf16[16,512]{1,0:T(8,128)(2,1)S(1)}, u32[]{:S(2)}, u32[]{:S(2)}) %collective-permute-start.1) | collective-permute-done | bytes 16416 | tf_op jit(solution)/shard_map/ppermute | solution.py:229
  19.5 1.8 %collective-permute-done.refs_1_ = bf16[16,512]{1,0:T(8,128)(2,1)S(1)} collective-permute-done((bf16[16,512]{1,0:T(8,128)(2,1)}, bf16[16,512]{1,0:T(8,128)(2,1)S(1)}, u32[]{:S(2)}, u32[]{:S(2)}) %collective-permute-start) | collective-permute-done | bytes 16416 | tf_op jit(solution)/shard_map/ppermute | solution.py:229
  21.3 0.0 copy-start
  21.3 1.0 copy-done
  22.3 0.7 copy-done.2
  23.0 1.5 %pack.2 = (bf16[160,2048]{1,0:T(8,128)(2,1)S(1)}, bf16[160,2048]{1,0:T(8,128)(2,1)S(1)}, bf16[160,2048]{1,0:T(8,128)(2,1)S(1)}, bf16[160,2048]{1,0:T(8,128)(2,1)...) custom-call(bf16[16,32]{1,0:T(8,128)(2,1)S(1)} %fusion.q_ref, bf16[16,512]{1,0:T(8,128)(2,1)S(1)} %copy-done.2, ...), custom_call_target="tpu_custom_call" | custom-call | flops 1006632960 | bytes 6029312 | tf_op jit(solution)/shard_map/pack/pallas_call | solution.py:107
  24.5 0.1 collective-permute-start.6
  24.6 1.7 %collective-permute-start.8 = (bf16[160,2048]{1,0:T(8,128)(2,1)S(1)}, bf16[160,2048]{1,0:T(8,128)(2,1)S(1)}, u32[]{:S(2)}, u32[]{:S(2)}) collective-permute-start(bf16[160,2048]{1,0:T(8,128)(2,1)S(1)} %get-tuple-element.29), channel_id=1, source_target_pairs={{0,2},{1,9},{2,4},{3,11},{4,6},{5,13},{6,0},{7,15},{8,10},{9,17},{... | collective-permute-start | bytes 1966088 | tf_op jit(solution)/shard_map/ppermute | solution.py:229
  26.3 0.0 collective-permute-start.9
  26.3 1.7 %collective-permute-start.16 = (bf16[160,2048]{1,0:T(8,128)(2,1)S(1)}, bf16[160,2048]{1,0:T(8,128)(2,1)S(1)}, u32[]{:S(2)}, u32[]{:S(2)}) collective-permute-start(bf16[160,2048]{1,0:T(8,128)(2,1)S(1)} %get-tuple-element.37), channel_id=1, source_target_pairs={{0,6},{1,25},{2,0},{3,27},{4,2},{5,29},{6,4},{7,31},{8,14},{9,1},{... | collective-permute-start | bytes 1966088 | tf_op jit(solution)/shard_map/ppermute | solution.py:229
  28.0 2.6 %collective-permute-start.17 = (bf16[160,2048]{1,0:T(8,128)(2,1)S(1)}, bf16[160,2048]{1,0:T(8,128)(2,1)S(1)}, u32[]{:S(2)}, u32[]{:S(2)}) collective-permute-start(bf16[160,2048]{1,0:T(8,128)(2,1)S(1)} %get-tuple-element.38), channel_id=1, source_target_pairs={{0,7},{1,24},{2,1},{3,26},{4,3},{5,28},{6,5},{7,30},{8,15},{9,0},{... | collective-permute-start | bytes 1966088 | tf_op jit(solution)/shard_map/ppermute | solution.py:229
  30.6 1.9 %copy-done.5 = bf16[1,2048,768]{2,1,0:T(8,128)(2,1)S(1)} copy-done((bf16[1,2048,768]{2,1,0:T(8,128)(2,1)S(1)}, bf16[1,2048,768]{2,1,0:T(8,128)(2,1)}, u32[]{:S(2)}) %copy-start.5) | copy-done | bytes 3145752
  32.5 1.9 %copy-done.7 = bf16[1,768,2048]{2,1,0:T(8,128)(2,1)S(1)} copy-done((bf16[1,768,2048]{2,1,0:T(8,128)(2,1)S(1)}, bf16[1,768,2048]{2,1,0:T(8,128)(2,1)}, u32[]{:S(2)}) %copy-start.7) | copy-done | bytes 3145752
  34.4 3.2 %expert.4 = (bf16[160,2048]{1,0:T(8,128)(2,1)S(1)}, bf16[160,2048]{1,0:T(8,128)(2,1)S(1)}) custom-call(bf16[160,2048]{1,0:T(8,128)(2,1)S(1)} %get-tuple-element.25.refs_0_, bf16[160,2048]{1,0:T(8,128)(2,1)S(1)} %collective-permute-done.6.refs_1_, bf16[1,2048,768]{2,1,0:T(8,128)(2,1)S(1)} %copy-done.4, bf16[1,2048,768]{2,1,0:T(8,128)(2,1)S(1)} %copy-done.5, ...), custom_call_target="tpu_custom_call" | custom-call | flops 3019898880 | bytes 2621440 | tf_op jit(solution)/shard_map/expert/pallas_call | solution.py:204
  37.7 0.8 pack.3
  38.5 2.3 %collective-permute-start.12 = (bf16[160,2048]{1,0:T(8,128)(2,1)S(1)}, bf16[160,2048]{1,0:T(8,128)(2,1)S(1)}, u32[]{:S(2)}, u32[]{:S(2)}) collective-permute-start(bf16[160,2048]{1,0:T(8,128)(2,1)S(1)} %get-tuple-element.33), channel_id=1, source_target_pairs={{0,4},{1,17},{2,6},{3,19},{4,0},{5,21},{6,2},{7,23},{8,12},{9,25},... | collective-permute-start | bytes 1966088 | tf_op jit(solution)/shard_map/ppermute | solution.py:229
  40.8 0.1 collective-permute-start.13
  40.9 2.1 %collective-permute-done.9.refs_1_ = bf16[160,2048]{1,0:T(8,128)(2,1)S(1)} collective-permute-done((bf16[160,2048]{1,0:T(8,128)(2,1)S(1)}, bf16[160,2048]{1,0:T(8,128)(2,1)S(1)}, u32[]{:S(2)}, u32[]{:S(2)}) %collective-permute-start.9) | collective-permute-done | bytes 655392 | tf_op jit(solution)/shard_map/ppermute | solution.py:229
  43.0 0.4 collective-permute-start.7
  43.3 3.2 %expert.5 = (bf16[160,2048]{1,0:T(8,128)(2,1)S(1)}, bf16[160,2048]{1,0:T(8,128)(2,1)S(1)}) custom-call(bf16[160,2048]{1,0:T(8,128)(2,1)S(1)} %collective-permute-done.8.refs_0_, bf16[160,2048]{1,0:T(8,128)(2,1)S(1)} %collective-permute-done.9.refs_1_, bf16[1,2048,768]{2,1,0:T(8,128)(2,1)S(1)} %copy-done.4, bf16[1,2048,768]{2,1,0:T(8,128)(2,1)S(1)} %copy-done.6, ...), custom_call_target="tpu_custom_call" | custom-call | flops 3019898880 | bytes 2621440 | tf_op jit(solution)/shard_map/expert/pallas_call | solution.py:204
  46.6 2.7 %collective-permute-start.10 = (bf16[160,2048]{1,0:T(8,128)(2,1)S(1)}, bf16[160,2048]{1,0:T(8,128)(2,1)S(1)}, u32[]{:S(2)}, u32[]{:S(2)}) collective-permute-start(bf16[160,2048]{1,0:T(8,128)(2,1)S(1)} %get-tuple-element.31), channel_id=1, source_target_pairs={{2,0},{9,1},{4,2},{11,3},{6,4},{13,5},{0,6},{15,7},{10,8},{17,9},{... | collective-permute-start | bytes 1966088 | tf_op jit(solution)/shard_map/ppermute | solution.py:229
  49.3 3.2 %expert.7 = (bf16[160,2048]{1,0:T(8,128)(2,1)S(1)}, bf16[160,2048]{1,0:T(8,128)(2,1)S(1)}) custom-call(bf16[160,2048]{1,0:T(8,128)(2,1)S(1)} %collective-permute-done.16.refs_0_, bf16[160,2048]{1,0:T(8,128)(2,1)S(1)} %collective-permute-done.17.refs_1_, bf16[1,2048,768]{2,1,0:T(8,128)(2,1)S(1)} %copy-done.4, bf16[1,2048,768]{2,1,0:T(8,128)(2,1)S(1)} %copy-done.6, ...), custom_call_target="tpu_custom_call" | custom-call | flops 3019898880 | bytes 2621440 | tf_op jit(solution)/shard_map/expert/pallas_call | solution.py:204
  52.6 0.7 collective-permute-start.18
  53.3 4.0 %collective-permute-done.13.refs_1_ = bf16[160,2048]{1,0:T(8,128)(2,1)S(1)} collective-permute-done((bf16[160,2048]{1,0:T(8,128)(2,1)S(1)}, bf16[160,2048]{1,0:T(8,128)(2,1)S(1)}, u32[]{:S(2)}, u32[]{:S(2)}) %collective-permute-start.13) | collective-permute-done | bytes 655392 | tf_op jit(solution)/shard_map/ppermute | solution.py:229
  57.3 10.2 %collective-permute-start.19 = (bf16[160,2048]{1,0:T(8,128)(2,1)S(1)}, bf16[160,2048]{1,0:T(8,128)(2,1)S(1)}, u32[]{:S(2)}, u32[]{:S(2)}) collective-permute-start(bf16[160,2048]{1,0:T(8,128)(2,1)S(1)} %get-tuple-element.40), channel_id=1, source_target_pairs={{7,0},{24,1},{1,2},{26,3},{3,4},{28,5},{5,6},{30,7},{15,8},{0,9},{... | collective-permute-start | bytes 1966088 | tf_op jit(solution)/shard_map/ppermute | solution.py:229
  67.5 3.2 %expert.6 = (bf16[160,2048]{1,0:T(8,128)(2,1)S(1)}, bf16[160,2048]{1,0:T(8,128)(2,1)S(1)}) custom-call(bf16[160,2048]{1,0:T(8,128)(2,1)S(1)} %collective-permute-done.12.refs_0_, bf16[160,2048]{1,0:T(8,128)(2,1)S(1)} %collective-permute-done.13.refs_1_, bf16[1,2048,768]{2,1,0:T(8,128)(2,1)S(1)} %copy-done.4, bf16[1,2048,768]{2,1,0:T(8,128)(2,1)S(1)} %copy-done.6, ...), custom_call_target="tpu_custom_call" | custom-call | flops 3019898880 | bytes 2621440 | tf_op jit(solution)/shard_map/expert/pallas_call | solution.py:204
  70.8 0.8 collective-permute-start.14
  71.5 2.8 %collective-permute-start.15 = (bf16[160,2048]{1,0:T(8,128)(2,1)S(1)}, bf16[160,2048]{1,0:T(8,128)(2,1)S(1)}, u32[]{:S(2)}, u32[]{:S(2)}) collective-permute-start(bf16[160,2048]{1,0:T(8,128)(2,1)S(1)} %get-tuple-element.36), channel_id=1, source_target_pairs={{5,0},{16,1},{7,2},{18,3},{1,4},{20,5},{3,6},{22,7},{13,8},{24,9},... | collective-permute-start | bytes 1966088 | tf_op jit(solution)/shard_map/ppermute | solution.py:229
  74.4 4.6 %collective-permute-done.18.refs_10_ = bf16[160,2048]{1,0:T(8,128)(2,1)S(1)} collective-permute-done((bf16[160,2048]{1,0:T(8,128)(2,1)S(1)}, bf16[160,2048]{1,0:T(8,128)(2,1)S(1)}, u32[]{:S(2)}, u32[]{:S(2)}) %collective-permute-start.18) | collective-permute-done | bytes 655392 | tf_op jit(solution)/shard_map/ppermute | solution.py:229
  79.0 3.1 %collective-permute-done.19.refs_11_ = bf16[160,2048]{1,0:T(8,128)(2,1)S(1)} collective-permute-done((bf16[160,2048]{1,0:T(8,128)(2,1)S(1)}, bf16[160,2048]{1,0:T(8,128)(2,1)S(1)}, u32[]{:S(2)}, u32[]{:S(2)}) %collective-permute-start.19) | collective-permute-done | bytes 655392 | tf_op jit(solution)/shard_map/ppermute | solution.py:229
  82.1 11.6 %collective-permute-done.14.refs_8_ = bf16[160,2048]{1,0:T(8,128)(2,1)S(1)} collective-permute-done((bf16[160,2048]{1,0:T(8,128)(2,1)S(1)}, bf16[160,2048]{1,0:T(8,128)(2,1)S(1)}, u32[]{:S(2)}, u32[]{:S(2)}) %collective-permute-start.14) | collective-permute-done | bytes 655392 | tf_op jit(solution)/shard_map/ppermute | solution.py:229
  93.7 3.5 %collective-permute-done.15.refs_9_ = bf16[160,2048]{1,0:T(8,128)(2,1)S(1)} collective-permute-done((bf16[160,2048]{1,0:T(8,128)(2,1)S(1)}, bf16[160,2048]{1,0:T(8,128)(2,1)S(1)}, u32[]{:S(2)}, u32[]{:S(2)}) %collective-permute-start.15) | collective-permute-done | bytes 655392 | tf_op jit(solution)/shard_map/ppermute | solution.py:229
  97.2 2.6 %combine.1 = (f32[128,2048]{1,0:T(8,128)S(1)}, bf16[128,2048]{1,0:T(8,128)(2,1)S(1)}, bf16[128,2048]{1,0:T(8,128)(2,1)S(1)}, bf16[128,2048]{1,0:T(8,128)(2,1)S(1)}) custom-call(bf16[16,32]{1,0:T(8,128)(2,1)S(1)} %fusion.q_ref, bf16[16,512]{1,0:T(8,128)(2,1)S(1)} %copy-done.3, bf16[16,512]{1,0:T(8,128)(2,1)S(1)} %collective-permute-done.refs_1_, ...), custom_call_target="tpu_custom_call" | custom-call | flops 1342177280 | bytes 7864320 | tf_op jit(solution)/shard_map/combine/pallas_call | solution.py:166
  99.8 2.9 %collective-permute-start.20 = (bf16[128,2048]{1,0:T(8,128)(2,1)S(1)}, bf16[128,2048]{1,0:T(8,128)(2,1)S(1)}, u32[]{:S(2)}, u32[]{:S(2)}) collective-permute-start(bf16[128,2048]{1,0:T(8,128)(2,1)S(1)} %get-tuple-element.42), channel_id=1, source_target_pairs={{8,0},{3,1},{10,2},{5,3},{12,4},{7,5},{14,6},{1,7},{16,8},{11,9},{... | collective-permute-start | bytes 1572872 | tf_op jit(solution)/shard_map/ppermute | solution.py:229
  102.7 0.9 collective-permute-start.21
  103.6 0.0 collective-permute-start.22
  103.7 11.4 %collective-permute-done.20 = bf16[128,2048]{1,0:T(8,128)(2,1)S(1)} collective-permute-done((bf16[128,2048]{1,0:T(8,128)(2,1)S(1)}, bf16[128,2048]{1,0:T(8,128)(2,1)S(1)}, u32[]{:S(2)}, u32[]{:S(2)}) %collective-permute-start.20) | collective-permute-done | bytes 524320 | tf_op jit(solution)/shard_map/ppermute | solution.py:229
  115.1 4.0 %collective-permute-done.22 = bf16[128,2048]{1,0:T(8,128)(2,1)S(1)} collective-permute-done((bf16[128,2048]{1,0:T(8,128)(2,1)S(1)}, bf16[128,2048]{1,0:T(8,128)(2,1)S(1)}, u32[]{:S(2)}, u32[]{:S(2)}) %collective-permute-start.22) | collective-permute-done | bytes 524320 | tf_op jit(solution)/shard_map/ppermute | solution.py:229
  119.0 1.1 add_convert_fusion
  (25 shorter events, 0.1 us)
Async XLA Ops:
  0.0 21.3 %collective-permute-start.5 = (bf16[128,2048]{1,0:T(8,128)(2,1)}, bf16[128,2048]{1,0:T(8,128)(2,1)S(1)}, u32[]{:S(2)}, u32[]{:S(2)}) collective-permute-start(bf16[128,2048]{1,0:T(8,128)(2,1)} %refs_4_.9), channel_id=1, source_target_pairs={{0,24},{1,7},{2,26},{3,1},{4,28},{5,3},{6,30},{7,5},{8,0},{9,15},{... | collective-permute-start | bytes 1572872 | tf_op jit(solution)/shard_map/ppermute | solution.py:229
  2.8 18.5 %collective-permute-start.4 = (bf16[128,2048]{1,0:T(8,128)(2,1)}, bf16[128,2048]{1,0:T(8,128)(2,1)S(1)}, u32[]{:S(2)}, u32[]{:S(2)}) collective-permute-start(bf16[128,2048]{1,0:T(8,128)(2,1)} %refs_4_.9), channel_id=1, source_target_pairs={{0,16},{1,5},{2,18},{3,7},{4,20},{5,1},{6,22},{7,3},{8,24},{9,13},... | collective-permute-start | bytes 1572872 | tf_op jit(solution)/shard_map/ppermute | solution.py:229
  3.6 17.7 %collective-permute-start.3 = (bf16[128,2048]{1,0:T(8,128)(2,1)}, bf16[128,2048]{1,0:T(8,128)(2,1)S(1)}, u32[]{:S(2)}, u32[]{:S(2)}) collective-permute-start(bf16[128,2048]{1,0:T(8,128)(2,1)} %refs_4_.9), channel_id=1, source_target_pairs={{0,8},{1,3},{2,10},{3,5},{4,12},{5,7},{6,14},{7,1},{8,16},{9,11},{... | collective-permute-start | bytes 1572872 | tf_op jit(solution)/shard_map/ppermute | solution.py:229
  5.9 9.8 %collective-permute-start.2 = (bf16[16,512]{1,0:T(8,128)(2,1)}, bf16[16,512]{1,0:T(8,128)(2,1)S(1)}, u32[]{:S(2)}, u32[]{:S(2)}) collective-permute-start(bf16[16,512]{1,0:T(8,128)(2,1)} %prep.1.refs_0_), channel_id=1, source_target_pairs={{0,24},{1,7},{2,26},{3,1},{4,28},{5,3},{6,30},{7,5},{8,0},{9,15},{... | collective-permute-start | bytes 49160 | tf_op jit(solution)/shard_map/ppermute | solution.py:229
  8.2 11.2 %collective-permute-start.1 = (bf16[16,512]{1,0:T(8,128)(2,1)}, bf16[16,512]{1,0:T(8,128)(2,1)S(1)}, u32[]{:S(2)}, u32[]{:S(2)}) collective-permute-start(bf16[16,512]{1,0:T(8,128)(2,1)} %prep.1.refs_0_), channel_id=1, source_target_pairs={{0,16},{1,5},{2,18},{3,7},{4,20},{5,1},{6,22},{7,3},{8,24},{9,13},... | collective-permute-start | bytes 49160 | tf_op jit(solution)/shard_map/ppermute | solution.py:229
  15.7 5.6 %collective-permute-start = (bf16[16,512]{1,0:T(8,128)(2,1)}, bf16[16,512]{1,0:T(8,128)(2,1)S(1)}, u32[]{:S(2)}, u32[]{:S(2)}) collective-permute-start(bf16[16,512]{1,0:T(8,128)(2,1)} %prep.1.refs_0_), channel_id=1, source_target_pairs={{0,8},{1,3},{2,10},{3,5},{4,12},{5,7},{6,14},{7,1},{8,16},{9,11},{... | collective-permute-start | bytes 49160 | tf_op jit(solution)/shard_map/ppermute | solution.py:229
  21.3 1.0 copy-start
  22.3 0.7 copy-start.2
  23.0 7.6 %copy-start.4 = (bf16[1,2048,768]{2,1,0:T(8,128)(2,1)S(1)}, bf16[1,2048,768]{2,1,0:T(8,128)(2,1)}, u32[]{:S(2)}) copy-start(bf16[1,2048,768]{2,1,0:T(8,128)(2,1)} %refs_2_.7) | copy-start | bytes 9437188
  24.5 6.1 %collective-permute-start.6 = (bf16[160,2048]{1,0:T(8,128)(2,1)S(1)}, bf16[160,2048]{1,0:T(8,128)(2,1)S(1)}, u32[]{:S(2)}, u32[]{:S(2)}) collective-permute-start(bf16[160,2048]{1,0:T(8,128)(2,1)S(1)} %get-tuple-element.26), channel_id=1, source_target_pairs={{0,1},{1,0},{2,3},{3,2},{4,5},{5,4},{6,7},{7,6},{8,9},{9,8},{10,11... | collective-permute-start | bytes 1966088 | tf_op jit(solution)/shard_map/ppermute | solution.py:229
  24.6 16.1 %collective-permute-start.8 = (bf16[160,2048]{1,0:T(8,128)(2,1)S(1)}, bf16[160,2048]{1,0:T(8,128)(2,1)S(1)}, u32[]{:S(2)}, u32[]{:S(2)}) collective-permute-start(bf16[160,2048]{1,0:T(8,128)(2,1)S(1)} %get-tuple-element.29), channel_id=1, source_target_pairs={{0,2},{1,9},{2,4},{3,11},{4,6},{5,13},{6,0},{7,15},{8,10},{9,17},{... | collective-permute-start | bytes 1966088 | tf_op jit(solution)/shard_map/ppermute | solution.py:229
  26.3 16.7 %collective-permute-start.9 = (bf16[160,2048]{1,0:T(8,128)(2,1)S(1)}, bf16[160,2048]{1,0:T(8,128)(2,1)S(1)}, u32[]{:S(2)}, u32[]{:S(2)}) collective-permute-start(bf16[160,2048]{1,0:T(8,128)(2,1)S(1)} %get-tuple-element.30), channel_id=1, source_target_pairs={{0,3},{1,8},{2,5},{3,10},{4,7},{5,12},{6,1},{7,14},{8,11},{9,16},{... | collective-permute-start | bytes 1966088 | tf_op jit(solution)/shard_map/ppermute | solution.py:229
  26.3 20.3 %collective-permute-start.16 = (bf16[160,2048]{1,0:T(8,128)(2,1)S(1)}, bf16[160,2048]{1,0:T(8,128)(2,1)S(1)}, u32[]{:S(2)}, u32[]{:S(2)}) collective-permute-start(bf16[160,2048]{1,0:T(8,128)(2,1)S(1)} %get-tuple-element.37), channel_id=1, source_target_pairs={{0,6},{1,25},{2,0},{3,27},{4,2},{5,29},{6,4},{7,31},{8,14},{9,1},{... | collective-permute-start | bytes 1966088 | tf_op jit(solution)/shard_map/ppermute | solution.py:229
  28.0 21.4 %collective-permute-start.17 = (bf16[160,2048]{1,0:T(8,128)(2,1)S(1)}, bf16[160,2048]{1,0:T(8,128)(2,1)S(1)}, u32[]{:S(2)}, u32[]{:S(2)}) collective-permute-start(bf16[160,2048]{1,0:T(8,128)(2,1)S(1)} %get-tuple-element.38), channel_id=1, source_target_pairs={{0,7},{1,24},{2,1},{3,26},{4,3},{5,28},{6,5},{7,30},{8,15},{9,0},{... | collective-permute-start | bytes 1966088 | tf_op jit(solution)/shard_map/ppermute | solution.py:229
  30.6 1.9 %copy-start.5 = (bf16[1,2048,768]{2,1,0:T(8,128)(2,1)S(1)}, bf16[1,2048,768]{2,1,0:T(8,128)(2,1)}, u32[]{:S(2)}) copy-start(bf16[1,2048,768]{2,1,0:T(8,128)(2,1)} %refs_3_.7) | copy-start | bytes 9437188
  32.5 1.9 %copy-start.7 = (bf16[1,768,2048]{2,1,0:T(8,128)(2,1)S(1)}, bf16[1,768,2048]{2,1,0:T(8,128)(2,1)}, u32[]{:S(2)}) copy-start(bf16[1,768,2048]{2,1,0:T(8,128)(2,1)} %refs_4_.11) | copy-start | bytes 9437188
  34.4 3.3 %copy-start.1 = (bf16[128,2048]{1,0:T(8,128)(2,1)S(1)}, bf16[128,2048]{1,0:T(8,128)(2,1)}, u32[]{:S(2)}) copy-start(bf16[128,2048]{1,0:T(8,128)(2,1)} %refs_4_.9) | copy-start | bytes 1572868
  34.4 3.3 %copy-start.3 = (bf16[16,512]{1,0:T(8,128)(2,1)S(1)}, bf16[16,512]{1,0:T(8,128)(2,1)}, u32[]{:S(2)}) copy-start(bf16[16,512]{1,0:T(8,128)(2,1)} %prep.1.refs_0_) | copy-start | bytes 49156
  34.4 8.9 %copy-start.6 = (bf16[1,2048,768]{2,1,0:T(8,128)(2,1)S(1)}, bf16[1,2048,768]{2,1,0:T(8,128)(2,1)}, u32[]{:S(2)}) copy-start(bf16[1,2048,768]{2,1,0:T(8,128)(2,1)} %refs_3_.7) | copy-start | bytes 9437188
  38.5 14.1 %collective-permute-start.12 = (bf16[160,2048]{1,0:T(8,128)(2,1)S(1)}, bf16[160,2048]{1,0:T(8,128)(2,1)S(1)}, u32[]{:S(2)}, u32[]{:S(2)}) collective-permute-start(bf16[160,2048]{1,0:T(8,128)(2,1)S(1)} %get-tuple-element.33), channel_id=1, source_target_pairs={{0,4},{1,17},{2,6},{3,19},{4,0},{5,21},{6,2},{7,23},{8,12},{9,25},... | collective-permute-start | bytes 1966088 | tf_op jit(solution)/shard_map/ppermute | solution.py:229
  40.8 16.6 %collective-permute-start.13 = (bf16[160,2048]{1,0:T(8,128)(2,1)S(1)}, bf16[160,2048]{1,0:T(8,128)(2,1)S(1)}, u32[]{:S(2)}, u32[]{:S(2)}) collective-permute-start(bf16[160,2048]{1,0:T(8,128)(2,1)S(1)} %get-tuple-element.34), channel_id=1, source_target_pairs={{0,5},{1,16},{2,7},{3,18},{4,1},{5,20},{6,3},{7,22},{8,13},{9,24},... | collective-permute-start | bytes 1966088 | tf_op jit(solution)/shard_map/ppermute | solution.py:229
  43.0 27.8 %collective-permute-start.7 = (bf16[160,2048]{1,0:T(8,128)(2,1)S(1)}, bf16[160,2048]{1,0:T(8,128)(2,1)S(1)}, u32[]{:S(2)}, u32[]{:S(2)}) collective-permute-start(bf16[160,2048]{1,0:T(8,128)(2,1)S(1)} %get-tuple-element.28), channel_id=1, source_target_pairs={{1,0},{0,1},{3,2},{2,3},{5,4},{4,5},{7,6},{6,7},{9,8},{8,9},{11,10... | collective-permute-start | bytes 1966088 | tf_op jit(solution)/shard_map/ppermute | solution.py:229
  46.6 24.9 %collective-permute-start.10 = (bf16[160,2048]{1,0:T(8,128)(2,1)S(1)}, bf16[160,2048]{1,0:T(8,128)(2,1)S(1)}, u32[]{:S(2)}, u32[]{:S(2)}) collective-permute-start(bf16[160,2048]{1,0:T(8,128)(2,1)S(1)} %get-tuple-element.31), channel_id=1, source_target_pairs={{2,0},{9,1},{4,2},{11,3},{6,4},{13,5},{0,6},{15,7},{10,8},{17,9},{... | collective-permute-start | bytes 1966088 | tf_op jit(solution)/shard_map/ppermute | solution.py:229
  49.3 25.0 %collective-permute-start.11 = (bf16[160,2048]{1,0:T(8,128)(2,1)S(1)}, bf16[160,2048]{1,0:T(8,128)(2,1)S(1)}, u32[]{:S(2)}, u32[]{:S(2)}) collective-permute-start(bf16[160,2048]{1,0:T(8,128)(2,1)S(1)} %get-tuple-element.32), channel_id=1, source_target_pairs={{3,0},{8,1},{5,2},{10,3},{7,4},{12,5},{1,6},{14,7},{11,8},{16,9},{... | collective-permute-start | bytes 1966088 | tf_op jit(solution)/shard_map/ppermute | solution.py:229
  52.6 26.4 %collective-permute-start.18 = (bf16[160,2048]{1,0:T(8,128)(2,1)S(1)}, bf16[160,2048]{1,0:T(8,128)(2,1)S(1)}, u32[]{:S(2)}, u32[]{:S(2)}) collective-permute-start(bf16[160,2048]{1,0:T(8,128)(2,1)S(1)} %get-tuple-element.39), channel_id=1, source_target_pairs={{6,0},{25,1},{0,2},{27,3},{2,4},{29,5},{4,6},{31,7},{14,8},{1,9},{... | collective-permute-start | bytes 1966088 | tf_op jit(solution)/shard_map/ppermute | solution.py:229
  57.3 24.8 %collective-permute-start.19 = (bf16[160,2048]{1,0:T(8,128)(2,1)S(1)}, bf16[160,2048]{1,0:T(8,128)(2,1)S(1)}, u32[]{:S(2)}, u32[]{:S(2)}) collective-permute-start(bf16[160,2048]{1,0:T(8,128)(2,1)S(1)} %get-tuple-element.40), channel_id=1, source_target_pairs={{7,0},{24,1},{1,2},{26,3},{3,4},{28,5},{5,6},{30,7},{15,8},{0,9},{... | collective-permute-start | bytes 1966088 | tf_op jit(solution)/shard_map/ppermute | solution.py:229
  70.8 22.9 %collective-permute-start.14 = (bf16[160,2048]{1,0:T(8,128)(2,1)S(1)}, bf16[160,2048]{1,0:T(8,128)(2,1)S(1)}, u32[]{:S(2)}, u32[]{:S(2)}) collective-permute-start(bf16[160,2048]{1,0:T(8,128)(2,1)S(1)} %get-tuple-element.35), channel_id=1, source_target_pairs={{4,0},{17,1},{6,2},{19,3},{0,4},{21,5},{2,6},{23,7},{12,8},{25,9},... | collective-permute-start | bytes 1966088 | tf_op jit(solution)/shard_map/ppermute | solution.py:229
  71.5 25.6 %collective-permute-start.15 = (bf16[160,2048]{1,0:T(8,128)(2,1)S(1)}, bf16[160,2048]{1,0:T(8,128)(2,1)S(1)}, u32[]{:S(2)}, u32[]{:S(2)}) collective-permute-start(bf16[160,2048]{1,0:T(8,128)(2,1)S(1)} %get-tuple-element.36), channel_id=1, source_target_pairs={{5,0},{16,1},{7,2},{18,3},{1,4},{20,5},{3,6},{22,7},{13,8},{24,9},... | collective-permute-start | bytes 1966088 | tf_op jit(solution)/shard_map/ppermute | solution.py:229
  99.8 15.3 %collective-permute-start.20 = (bf16[128,2048]{1,0:T(8,128)(2,1)S(1)}, bf16[128,2048]{1,0:T(8,128)(2,1)S(1)}, u32[]{:S(2)}, u32[]{:S(2)}) collective-permute-start(bf16[128,2048]{1,0:T(8,128)(2,1)S(1)} %get-tuple-element.42), channel_id=1, source_target_pairs={{8,0},{3,1},{10,2},{5,3},{12,4},{7,5},{14,6},{1,7},{16,8},{11,9},{... | collective-permute-start | bytes 1572872 | tf_op jit(solution)/shard_map/ppermute | solution.py:229
  102.7 12.3 %collective-permute-start.21 = (bf16[128,2048]{1,0:T(8,128)(2,1)S(1)}, bf16[128,2048]{1,0:T(8,128)(2,1)S(1)}, u32[]{:S(2)}, u32[]{:S(2)}) collective-permute-start(bf16[128,2048]{1,0:T(8,128)(2,1)S(1)} %get-tuple-element.43), channel_id=1, source_target_pairs={{16,0},{5,1},{18,2},{7,3},{20,4},{1,5},{22,6},{3,7},{24,8},{13,9},... | collective-permute-start | bytes 1572872 | tf_op jit(solution)/shard_map/ppermute | solution.py:229
  103.6 15.4 %collective-permute-start.22 = (bf16[128,2048]{1,0:T(8,128)(2,1)S(1)}, bf16[128,2048]{1,0:T(8,128)(2,1)S(1)}, u32[]{:S(2)}, u32[]{:S(2)}) collective-permute-start(bf16[128,2048]{1,0:T(8,128)(2,1)S(1)} %get-tuple-element.44), channel_id=1, source_target_pairs={{24,0},{7,1},{26,2},{1,3},{28,4},{3,5},{30,6},{5,7},{0,8},{15,9},{... | collective-permute-start | bytes 1572872 | tf_op jit(solution)/shard_map/ppermute | solution.py:229

commit v3 on v2

v3 whole, which is shorter than its diff:
```python
import functools

import jax
import jax.numpy as jnp
from jax import lax
from jax.experimental import pallas as pl
from jax.experimental.pallas import tpu as pltpu
from jax.sharding import PartitionSpec as P

NX, NY, NC = 4, 4, 2
EXPERTS = NX * NY * NC
CAP = 40
KF = 8


def index_of(x, y, c):
    return ((x % NX) * NY + (y % NY)) * NC + c


def spread_pairs(j):
    pairs = []
    for x in range(NX):
        for y in range(NY):
            pairs.append((index_of(x, y, 0), index_of(x + j, y, 0)))
            pairs.append((index_of(x, y, 1), index_of(x, y + j, 1)))
    return pairs


def deliver_pairs(k):
    pairs = []
    for x in range(NX):
        for y in range(NY):
            pairs.append((index_of(x, y, 0), index_of(x, y + k, 0)))
            pairs.append((index_of(x, y, 1), index_of(x + k, y, 1)))
    return pairs


def spread_groups():
    return [[index_of(x, y, 0) for x in range(NX)] for y in range(NY)] + [
        [index_of(x, y, 1) for y in range(NY)] for x in range(NX)
    ]


def swap_pairs():
    return [(i, i ^ 1) for i in range(EXPERTS)]


def back(pairs):
    return [(b, a) for a, b in pairs]


def prep_kernel(ids_ref, gw_ref, tok_ref, out_ref, own_ref, sem):
    copy = pltpu.make_async_copy(tok_ref, own_ref, sem)
    copy.start()
    top, tok = ids_ref.shape
    ids = ids_ref[...]
    gw = gw_ref[...]
    name = lax.broadcasted_iota(jnp.int32, (EXPERTS, tok), 0)
    chosen = jnp.zeros((EXPERTS, tok), jnp.float32)
    weight = jnp.zeros((EXPERTS, tok), jnp.float32)
    for k in range(top):
        hit = ids[k : k + 1, :] == name
        chosen = jnp.where(hit, 1.0, chosen)
        weight = jnp.where(hit, gw[k : k + 1, :], weight)
    row = lax.broadcasted_iota(jnp.int32, (tok, tok), 0)
    col = lax.broadcasted_iota(jnp.int32, (tok, tok), 1)
    earlier = jnp.where(row < col, 1.0, 0.0).astype(jnp.bfloat16)
    count = jnp.dot(chosen.astype(jnp.bfloat16), earlier, preferred_element_type=jnp.float32)
    slot = jnp.where(chosen > 0.5, count, -1.0)
    half = EXPERTS // 2
    out_ref[...] = jnp.concatenate(
        [slot[:half], slot[half:], weight[:half], weight[half:]], axis=1
    ).astype(jnp.bfloat16)
    copy.wait()


def prep(ids, gw, tokens):
    tok = ids.shape[1]
    vmem = pl.BlockSpec(memory_space=pltpu.VMEM)
    return pl.pallas_call(
        prep_kernel,
        in_specs=[vmem, vmem, pl.BlockSpec(memory_space=pl.ANY)],
        out_specs=[vmem, vmem],
        out_shape=[
            jax.ShapeDtypeStruct((EXPERTS // 2, 4 * tok), jnp.bfloat16),
            pltpu.VMEM(tokens.shape, tokens.dtype),
        ],
        scratch_shapes=[pltpu.SemaphoreType.DMA],
        compiler_params=pltpu.CompilerParams(vmem_limit_bytes=4 * 1024 * 1024),
        cost_estimate=pl.CostEstimate(flops=2 * EXPERTS * tok**2, bytes_accessed=32 * tok * 4, transcendentals=0),
        name="prep",
    )(ids, gw, pltpu.with_memory_space_constraint(tokens, pltpu.HBM))


def select(q, meta, at, tok):
    half = EXPERTS // 2
    return jnp.dot(
        q[:, :half], meta[:, at : at + tok], preferred_element_type=jnp.float32
    ) + jnp.dot(q[:, half:], meta[:, at + tok : at + 2 * tok], preferred_element_type=jnp.float32)


def table(pos_ref, metas_ref, j):
    return metas_ref[lax.rem(pos_ref[0] + 4 - j, 4)]


def pack_kernel(which, pos_ref, q_ref, metas_ref, *refs):
    blocks, outs = refs[:4], refs[-len(which) :]
    tok, width = blocks[0].shape
    q = q_ref[...]
    span = 2 * CAP
    r = lax.broadcasted_iota(jnp.int32, (span, 2 * tok), 0)
    t = lax.broadcasted_iota(jnp.int32, (span, 2 * tok), 1)
    second = r >= CAP
    target = jnp.where(second, r - CAP, r)
    target = jnp.where(second == (t >= tok), target, -5).astype(jnp.float32)
    cols = 512
    for p in range(2):
        metas = [table(pos_ref, metas_ref, j) for j in (2 * p, 2 * p + 1)]
        slots = jnp.concatenate([select(q, m, 0, tok) for m in metas], axis=1)
        pick = jnp.concatenate(
            [
                jnp.where(slots[NC * k + f : NC * k + f + 1, :] == target, 1.0, 0.0).astype(jnp.bfloat16)
                for k in which
                for f in range(NC)
            ],
            axis=0,
        )
        for at in range(0, width, cols):
            block = jnp.concatenate([b[:, at : at + cols] for b in blocks[2 * p : 2 * p + 2]], axis=0)
            got = jnp.dot(pick, block, preferred_element_type=jnp.float32).astype(jnp.bfloat16)
            for n, o in enumerate(outs):
                for f in range(NC):
                    to, of = span * (2 * f + p), span * (NC * n + f)
                    o[to : to + span, at : at + cols] = got[of : of + span, :]


def pack(which, pos, q, metas, blocks, after=()):
    tok, width = blocks[0].shape
    count = len(which)
    rows = NC * 4 * CAP
    vmem = pl.BlockSpec(memory_space=pltpu.VMEM)
    return pl.pallas_call(
        functools.partial(pack_kernel, which),
        in_specs=[pl.BlockSpec(memory_space=pltpu.SMEM)] + [vmem] * 6 + [pl.BlockSpec(memory_space=pl.ANY)] * len(after),
        out_specs=[vmem] * count,
        out_shape=[jax.ShapeDtypeStruct((rows, width), jnp.bfloat16)] * count,
        compiler_params=pltpu.CompilerParams(vmem_limit_bytes=16 * 1024 * 1024),
        cost_estimate=pl.CostEstimate(
            flops=2 * rows * count * 2 * tok * width,
            bytes_accessed=2 * (4 * tok + rows * count) * width,
            transcendentals=0,
        ),
        name="pack",
    )(pos, q, metas, *blocks, *after)


def combine_kernel(pos_ref, q_ref, metas_ref, *refs):
    backs, outs = refs[:4], refs[4:]
    tok, width = outs[0].shape
    q = q_ref[...]
    half = 2 * CAP
    span = half * KF
    lane = lax.broadcasted_iota(jnp.int32, (2 * tok, span), 1)
    part = jnp.zeros((2 * tok, span), jnp.int32)
    er = lax.broadcasted_iota(jnp.int32, (16, span), 0)
    el = lax.broadcasted_iota(jnp.int32, (16, span), 1)
    ep = jnp.zeros((16, span), jnp.int32)
    for n in range(1, KF):
        part = jnp.where(lane >= half * n, half * n, part)
        ep = jnp.where(el >= half * n, n, ep)
    r = lane - part
    t = lax.broadcasted_iota(jnp.int32, (2 * tok, span), 0)
    second = r >= CAP
    target = jnp.where(second, r - CAP, r)
    target = jnp.where(second == (t >= tok), target, -5).astype(jnp.float32)
    expand = jnp.where(er == ep, 1.0, 0.0).astype(jnp.bfloat16)

    def widen(v):
        return lax.dot_general(
            v.astype(jnp.bfloat16), expand, (((0,), (0,)), ((), ())), preferred_element_type=jnp.float32
        )

    cols = 512
    for p in range(2):
        metas = [table(pos_ref, metas_ref, j) for j in (2 * p, 2 * p + 1)]
        slots = jnp.concatenate([select(q, m, 0, tok) for m in metas], axis=1)
        weights = jnp.concatenate([select(q, m, 2 * tok, tok) for m in metas], axis=1)
        mix = jnp.where(widen(slots) == target, widen(weights), 0.0).astype(jnp.bfloat16)
        for at in range(0, width, cols):
            rows = jnp.concatenate(
                [b[half * (2 * f + p) : half * (2 * f + p + 1), at : at + cols] for b in backs for f in range(NC)],
                axis=0,
            )
            got = jnp.dot(mix, rows, preferred_element_type=jnp.float32)
            for n, o in enumerate(outs[2 * p : 2 * p + 2]):
                o[:, at : at + cols] = got[n * tok : (n + 1) * tok].astype(o.dtype)


def combine(pos, q, metas, backs, tok):
    rows, width = backs[0].shape
    vmem = pl.BlockSpec(memory_space=pltpu.VMEM)
    return pl.pallas_call(
        combine_kernel,
        in_specs=[pl.BlockSpec(memory_space=pltpu.SMEM)] + [vmem] * 6,
        out_specs=[vmem] * 4,
        out_shape=[jax.ShapeDtypeStruct((tok, width), jnp.float32)]
        + [jax.ShapeDtypeStruct((tok, width), jnp.bfloat16)] * 3,
        compiler_params=pltpu.CompilerParams(vmem_limit_bytes=16 * 1024 * 1024),
        cost_estimate=pl.CostEstimate(
            flops=2 * 4 * rows * 2 * tok * width,
            bytes_accessed=2 * (5 * tok + 4 * rows) * width,
            transcendentals=0,
        ),
        name="combine",
    )(pos, q, metas, *backs)


def expert_kernel(count, *refs):
    slabs, weights, outs = refs[:count], refs[count : count + 6], refs[count + 6 :]
    width = slabs[0].shape[1]
    rows = slabs[0].shape[0] // NC
    for f in range(NC):
        wg, wu, wd = weights[3 * f : 3 * f + 3]
        ff = wg.shape[-1]
        lines = jnp.concatenate([s[f * rows : (f + 1) * rows, :] for s in slabs], axis=0)
        hidden = []
        for at in range(0, ff, 256):
            gate = jnp.dot(lines, wg[0, :, at : at + 256], preferred_element_type=jnp.float32)
            up = jnp.dot(lines, wu[0, :, at : at + 256], preferred_element_type=jnp.float32)
            hidden.append((gate / (1.0 + jnp.exp(-gate)) * up).astype(jnp.bfloat16))
        hidden = jnp.concatenate(hidden, axis=1)
        for at in range(0, width, 512):
            got = jnp.dot(hidden, wd[0, :, at : at + 512], preferred_element_type=jnp.float32)
            for n, o in enumerate(outs):
                o[f * rows : (f + 1) * rows, at : at + 512] = got[n * rows : (n + 1) * rows].astype(jnp.bfloat16)


def expert(slabs, weights):
    count = len(slabs)
    rows, width = slabs[0].shape
    ff = weights[0].shape[-1]
    vmem = pl.BlockSpec(memory_space=pltpu.VMEM)
    return pl.pallas_call(
        functools.partial(expert_kernel, count),
        in_specs=[vmem] * (count + 6),
        out_specs=[vmem] * count,
        out_shape=[jax.ShapeDtypeStruct((rows, width), jnp.bfloat16)] * count,
        compiler_params=pltpu.CompilerParams(vmem_limit_bytes=16 * 1024 * 1024),
        cost_estimate=pl.CostEstimate(
            flops=6 * count * rows * width * ff,
            bytes_accessed=4 * count * rows * width,
            transcendentals=count * rows * ff,
        ),
        name="expert",
    )(*slabs, *[pltpu.with_memory_space_constraint(w, pltpu.VMEM) for w in weights])


def hold_kernel(*refs):
    ins, outs, sems = refs[:3], refs[3:6], refs[6]
    copies = [pltpu.make_async_copy(a, b, sems.at[n]) for n, (a, b) in enumerate(zip(ins, outs))]
    for copy in copies:
        copy.start()
    for copy in copies:
        copy.wait()


def hold(*weights):
    return pl.pallas_call(
        hold_kernel,
        in_specs=[pl.BlockSpec(memory_space=pl.ANY)] * 3,
        out_specs=[pl.BlockSpec(memory_space=pltpu.VMEM)] * 3,
        out_shape=[pltpu.VMEM(w.shape, w.dtype) for w in weights],
        scratch_shapes=[pltpu.SemaphoreType.DMA((3,))],
        compiler_params=pltpu.CompilerParams(vmem_limit_bytes=4 * 1024 * 1024),
        cost_estimate=pl.CostEstimate(flops=0, bytes_accessed=4 * weights[0].size * 3, transcendentals=0),
        name="hold",
    )(*[pltpu.with_memory_space_constraint(w, pltpu.HBM) for w in weights])


def per_device(tokens, expert_ids, gate_weights, w_gate, w_up, w_down):
    me = lax.axis_index("expert")
    x, y, c = me // (NY * NC), (me // NC) % NY, me % NC
    n = jnp.arange(16, dtype=jnp.int32)
    k, f = n // NC, n % NC
    along_y = x * (NY * NC) + ((y + k) % NY) * NC + (c ^ f)
    along_x = ((x + k) % NX) * (NY * NC) + y * NC + (c ^ f)
    mine = jnp.where(n < KF, jnp.where(c == 0, along_y, along_x), -1)
    q = (mine[:, None] == jnp.arange(EXPERTS, dtype=jnp.int32)[None, :]).astype(jnp.bfloat16)
    pos = jnp.where(c == 0, x, y).reshape(1).astype(jnp.int32)

    send = lambda v, pairs: lax.ppermute(v, "expert", pairs)
    moved = [send(tokens, spread_pairs(j)) for j in (1, 2, 3)]
    meta, own = prep(expert_ids.T, gate_weights.T, tokens)
    blocks = [own] + moved
    metas = lax.all_gather(meta, "expert", axis=0, axis_index_groups=spread_groups())
    first = lax.optimization_barrier((w_gate, w_up, metas))[:2]
    weights = list(hold(w_gate, w_up, w_down)) + [send(w, swap_pairs()) for w in first]

    slabs = dict(zip((1, 3, 0), pack((1, 3, 0), pos, q, metas, blocks)))
    last = lax.optimization_barrier((w_down, slabs[0]))[0]
    weights.append(send(last, swap_pairs()))
    arrived = {k: send(slabs[k], deliver_pairs(k)) for k in (1, 3)}
    backs = {}
    (backs[0],) = expert([slabs[0]], weights)
    (far,) = pack((2,), pos, q, metas, blocks, (backs[0],))
    arrived[2] = send(far, deliver_pairs(2))
    for ks in ((1, 3), (2,)):
        for k, slab in zip(ks, expert([arrived[k] for k in ks], weights)):
            backs[k] = send(slab, back(deliver_pairs(k)))
    parts = combine(pos, q, metas, [backs[k] for k in range(4)], tokens.shape[0])
    mixed = parts[0]
    for j in (1, 2, 3):
        mixed = mixed + send(parts[j], back(spread_pairs(j))).astype(jnp.float32)
    return mixed.astype(jnp.bfloat16)


def solution(mesh):
    return jax.shard_map(
        per_device,
        mesh=mesh,
        in_specs=(
            P(("dp", "expert"), None),
            P(("dp", "expert"), None),
            P(("dp", "expert"), None),
            P("expert", None, None),
            P("expert", None, None),
            P("expert", None, None),
        ),
        out_specs=P(("dp", "expert"), None),
        check_vma=False,
    )
```

time: 120 us -> 116 us (0.967)
  starting transfers between devices: 38.3 us -> 21.8 us
  blocking collectives: 0 us -> 14.8 us
  waiting for transfers between devices: 55.6 us -> 43.3 us
  Pallas kernels: 19.3 us -> 31.1 us
  local copies, waits for them, and re-layouts: 5.55 us -> 3.2 us
    ppermute x23 -> x15, starting transfers between devices: 38.3 us -> 21.8 us  [per_device(): send = lambda v, pairs: lax.ppermute(v, 'expert', pairs)]
    all_gather x0 -> x1, blocking collectives: none -> 14.8 us  [per_device(): lax.all_gather(meta, 'expert', axis=0, axis_index_groups=spread_groups())]
    ppermute x23 -> x15, waiting for transfers between devices: 55.6 us -> 43.3 us  [per_device(): send = lambda v, pairs: lax.ppermute(v, 'expert', pairs)]
    pallas_call x4 -> x5, Pallas kernels: 6.36 us -> 12.6 us  [the longest x2 5.17 us: pack(): pl.pallas_call(functools.partial(pack_kernel, which), in_specs=[pl.BlockS...]
    pallas_call x4 -> x3, Pallas kernels: 13 us -> 18.5 us  [expert(): pl.pallas_call(functools.partial(expert_kernel, count), in_specs=[vmem] *...]
    unnamed x16 -> x10, local copies, waits for them, and re-layouts: 5.55 us -> 3.2 us
  transfers between devices with their start and end apart: 23 -> 15, of which waited for: 11 -> 6; matrix products, arithmetic and copies ran while one was open for 0% -> 0% of each run, Pallas kernels for 13% -> 25%
where the time goes in v3:
time: 116 us
  waiting for transfers between devices  43.3 us (37%)
  Pallas kernels  31.1 us (27%)
  starting transfers between devices  21.8 us (19%)
  blocking collectives  14.8 us (13%)
  local copies, waits for them, and re-layouts  3.2 us (3%)
  other arithmetic  1.23 us (1%)
    ppermute x15, waiting for transfers between devices, per_device(): send = lambda v, pairs: lax.ppermute(v, 'expert', pairs)  43.3 us
    ppermute x15, starting transfers between devices, per_device(): send = lambda v, pairs: lax.ppermute(v, 'expert', pairs)  21.8 us
    pallas_call x3, Pallas kernels, expert(): pl.pallas_call(functools.partial(expert_kernel, count), in_specs=[vmem] *...  18.5 us
    all_gather x1, blocking collectives, per_device(): lax.all_gather(meta, 'expert', axis=0, axis_index_groups=spread_groups())  14.8 us
    pallas_call x2, Pallas kernels, pack(): pl.pallas_call(functools.partial(pack_kernel, which), in_specs=[pl.BlockS...  5.17 us
    pallas_call x1, Pallas kernels, hold(): pl.pallas_call(hold_kernel, in_specs=[pl.BlockSpec(memory_space=pl.ANY)]...  3.78 us
    unnamed x10, local copies, waits for them, and re-layouts  3.2 us
    pallas_call x1, Pallas kernels, combine(): pl.pallas_call(combine_kernel, in_specs=[pl.BlockSpec(memory_space=pltpu....  2.63 us
  transfers between devices with their start and end apart: 15, of which 6 were waited for; matrix products, arithmetic and copies ran while one was open for 0% of the time, Pallas kernels for 25%

profile of v3, /device:TPU:96, one launch (start us, length us, event | category | flops | bytes accessed | tf_op | source)
XLA Modules:
  0.0 115.6 jit_solution(7433461643663103727)
XLA Ops:
  0.0 1.5 %collective-permute-start = (bf16[128,2048]{1,0:T(8,128)(2,1)}, bf16[128,2048]{1,0:T(8,128)(2,1)}, u32[]{:S(2)}, u32[]{:S(2)}) collective-permute-start(bf16[128,2048]{1,0:T(8,128)(2,1)} %tok_ref.1), channel_id=1, source_target_pairs={{0,8},{1,3},{2,10},{3,5},{4,12},{5,7},{6,14},{7,1},{8,16},{9,11},{... | collective-permute-start | bytes 1572872 | tf_op jit(solution)/shard_map/ppermute | solution.py:291
  1.5 1.7 %collective-permute-start.2 = (bf16[128,2048]{1,0:T(8,128)(2,1)}, bf16[128,2048]{1,0:T(8,128)(2,1)}, u32[]{:S(2)}, u32[]{:S(2)}) collective-permute-start(bf16[128,2048]{1,0:T(8,128)(2,1)} %tok_ref.1), channel_id=1, source_target_pairs={{0,24},{1,7},{2,26},{3,1},{4,28},{5,3},{6,30},{7,5},{8,0},{9,15},{... | collective-permute-start | bytes 1572872 | tf_op jit(solution)/shard_map/ppermute | solution.py:291
  3.2 1.8 %collective-permute-start.1 = (bf16[128,2048]{1,0:T(8,128)(2,1)}, bf16[128,2048]{1,0:T(8,128)(2,1)}, u32[]{:S(2)}, u32[]{:S(2)}) collective-permute-start(bf16[128,2048]{1,0:T(8,128)(2,1)} %tok_ref.1), channel_id=1, source_target_pairs={{0,16},{1,5},{2,18},{3,7},{4,20},{5,1},{6,22},{7,3},{8,24},{9,13},... | collective-permute-start | bytes 1572872 | tf_op jit(solution)/shard_map/ppermute | solution.py:291
  5.1 0.7 copy-done.2
  5.7 0.7 copy-done.3
  6.4 1.1 prep.1
  7.5 0.0 copy-start
  7.5 0.8 copy-done
  8.3 14.8 %all-gather = bf16[64,512]{1,0:T(8,128)(2,1)S(1)} all-gather(bf16[16,512]{1,0:T(8,128)(2,1)S(1)} %get-tuple-element.22), channel_id=2, replica_groups={{0,8,16,24},{2,10,18,26},{4,12,20,28},{6,14,22,30},{1,3,5,7},{9,11,13,1..., dimensions={0}, use_global_device_ids=true | all-gather | bytes 81920 | tf_op jit(solution)/shard_map/all_gather | solution.py:295
  23.0 0.0 collective-permute-start.3
  23.1 0.5 collective-permute-start.4
  23.6 0.1 fusion.q_ref
  23.7 0.0 collective-permute-done.refs_1_
  23.7 0.0 collective-permute-done.2.refs_3_
  23.7 0.0 collective-permute-done.1.refs_2_
  23.7 0.0 copy-start.1
  23.7 1.0 copy-done.1
  24.7 3.0 %pack.2 = (bf16[320,2048]{1,0:T(8,128)(2,1)S(1)}, bf16[320,2048]{1,0:T(8,128)(2,1)S(1)}, bf16[320,2048]{1,0:T(8,128)(2,1)S(1)}) custom-call(s32[1]{0:T(128)} %bitcast.pos_ref, bf16[16,32]{1,0:T(8,128)(2,1)S(1)} %fusion.q_ref, bf16[4,16,512]{2,1,0:T(8,128)(2,1)S(1)} %bitcast.4, bf16[128,2048]{1,0:T(8,128)(2,1)S(1)} %copy-done.1, ...), custom_call_target="tpu_custom_call" | custom-call | flops 1006632960 | bytes 6029312 | tf_op jit(solution)/shard_map/pack/pallas_call | solution.py:142
  27.7 0.0 copy-done.4
  27.7 0.2 collective-permute-start.5
  27.9 1.6 %collective-permute-start.6 = (bf16[320,2048]{1,0:T(8,128)(2,1)S(1)}, bf16[320,2048]{1,0:T(8,128)(2,1)S(1)}, u32[]{:S(2)}, u32[]{:S(2)}) collective-permute-start(bf16[320,2048]{1,0:T(8,128)(2,1)S(1)} %get-tuple-element.31), channel_id=1, source_target_pairs={{0,2},{1,9},{2,4},{3,11},{4,6},{5,13},{6,0},{7,15},{8,10},{9,17},{... | collective-permute-start | bytes 3932168 | tf_op jit(solution)/shard_map/ppermute | solution.py:291
  29.5 1.7 %collective-permute-start.7 = (bf16[320,2048]{1,0:T(8,128)(2,1)S(1)}, bf16[320,2048]{1,0:T(8,128)(2,1)S(1)}, u32[]{:S(2)}, u32[]{:S(2)}) collective-permute-start(bf16[320,2048]{1,0:T(8,128)(2,1)S(1)} %get-tuple-element.32), channel_id=1, source_target_pairs={{0,6},{1,25},{2,0},{3,27},{4,2},{5,29},{6,4},{7,31},{8,14},{9,1},{... | collective-permute-start | bytes 3932168 | tf_op jit(solution)/shard_map/ppermute | solution.py:291
  31.2 3.8 %hold.1 = (bf16[1,2048,768]{2,1,0:T(8,128)(2,1)S(1)}, bf16[1,2048,768]{2,1,0:T(8,128)(2,1)S(1)}, bf16[1,768,2048]{2,1,0:T(8,128)(2,1)S(1)}) custom-call(bf16[1,2048,768]{2,1,0:T(8,128)(2,1)} %refs_0_.1, bf16[1,2048,768]{2,1,0:T(8,128)(2,1)} %refs_1_.1, bf16[1,768,2048]{2,1,0:T(8,128)(2,1)} %refs_2_.1), custom_call_target="tpu_custom_call" | custom-call | bytes 18874368 | tf_op jit(solution)/shard_map/hold/pallas_call | solution.py:268
  35.0 0.0 collective-permute-done.3.refs_4_.refs_5_
  35.0 0.0 collective-permute-done.4.refs_5_.refs_6_
  35.0 2.7 %collective-permute-done.5.refs_6_.refs_7_ = bf16[1,768,2048]{2,1,0:T(8,128)(2,1)S(1)} collective-permute-done((bf16[1,768,2048]{2,1,0:T(8,128)(2,1)S(1)}, bf16[1,768,2048]{2,1,0:T(8,128)(2,1)S(1)}, u32[]{:S(2)}, u32[]{:S(2)}) %collective-permute-start.5) | collective-permute-done | bytes 3145760 | tf_op jit(solution)/shard_map/ppermute | solution.py:291
  37.7 5.1 %expert.3.refs_4_.refs_0_ = bf16[320,2048]{1,0:T(8,128)(2,1)S(1)} custom-call(bf16[320,2048]{1,0:T(8,128)(2,1)S(1)} %get-tuple-element.24.refs_0_, bf16[1,2048,768]{2,1,0:T(8,128)(2,1)S(1)} %get-tuple-element.25.refs_1_.refs_2_, bf16[1,2048,768]{2,1,0:T(8,128)(2,1)S(1)} %get-tuple-element.26.refs_2_.refs_3_, ...), custom_call_target="tpu_custom_call" | custom-call | flops 3019898880 | bytes 2621440 | tf_op jit(solution)/shard_map/expert/pallas_call | solution.py:243
  42.9 2.2 %pack.3 = bf16[320,2048]{1,0:T(8,128)(2,1)S(1)} custom-call(s32[1]{0:T(128)} %bitcast.pos_ref, bf16[16,32]{1,0:T(8,128)(2,1)S(1)} %fusion.q_ref, bf16[4,16,512]{2,1,0:T(8,128)(2,1)S(1)} %bitcast.5, bf16[128,2048]{1,0:T(8,128)(2,1)S(1)} %copy-done.1, bf16[128,2048]{1,0:T(8,128)(2,1)} %collective-permute-done.refs_1_, ...), custom_call_target="tpu_custom_call" | custom-call | flops 335544320 | bytes 3407872 | tf_op jit(solution)/shard_map/pack/pallas_call | solution.py:142
  45.0 3.5 %collective-permute-start.9 = (bf16[320,2048]{1,0:T(8,128)(2,1)S(1)}, bf16[320,2048]{1,0:T(8,128)(2,1)S(1)}, u32[]{:S(2)}, u32[]{:S(2)}) collective-permute-start(bf16[320,2048]{1,0:T(8,128)(2,1)S(1)} %pack.3), channel_id=1, source_target_pairs={{0,4},{1,17},{2,6},{3,19},{4,0},{5,21},{6,2},{7,23},{8,12},{9,25},... | collective-permute-start | bytes 3932168 | tf_op jit(solution)/shard_map/ppermute | solution.py:291
  48.5 0.0 collective-permute-done.6.refs_0_
  48.5 0.0 collective-permute-done.7.refs_1_
  48.5 8.2 %expert.4 = (bf16[320,2048]{1,0:T(8,128)(2,1)S(1)}, bf16[320,2048]{1,0:T(8,128)(2,1)S(1)}) custom-call(bf16[320,2048]{1,0:T(8,128)(2,1)S(1)} %collective-permute-done.6.refs_0_, bf16[320,2048]{1,0:T(8,128)(2,1)S(1)} %collective-permute-done.7.refs_1_, bf16[1,2048,768]{2,1,0:T(8,128)(2,1)S(1)} %get-tuple-element.25.refs_1_.refs_2_, ...), custom_call_target="tpu_custom_call" | custom-call | flops 6039797760 | bytes 5242880 | tf_op jit(solution)/shard_map/expert/pallas_call | solution.py:243
  56.7 1.5 %collective-permute-start.8 = (bf16[320,2048]{1,0:T(8,128)(2,1)S(1)}, bf16[320,2048]{1,0:T(8,128)(2,1)S(1)}, u32[]{:S(2)}, u32[]{:S(2)}) collective-permute-start(bf16[320,2048]{1,0:T(8,128)(2,1)S(1)} %get-tuple-element.33), channel_id=1, source_target_pairs={{2,0},{9,1},{4,2},{11,3},{6,4},{13,5},{0,6},{15,7},{10,8},{17,9},{... | collective-permute-start | bytes 3932168 | tf_op jit(solution)/shard_map/ppermute | solution.py:291
  58.3 0.6 collective-permute-start.11
  58.9 5.7 %collective-permute-done.9.refs_0_ = bf16[320,2048]{1,0:T(8,128)(2,1)S(1)} collective-permute-done((bf16[320,2048]{1,0:T(8,128)(2,1)S(1)}, bf16[320,2048]{1,0:T(8,128)(2,1)S(1)}, u32[]{:S(2)}, u32[]{:S(2)}) %collective-permute-start.9) | collective-permute-done | bytes 1310752 | tf_op jit(solution)/shard_map/ppermute | solution.py:291
  64.5 5.1 %expert.5 = bf16[320,2048]{1,0:T(8,128)(2,1)S(1)} custom-call(bf16[320,2048]{1,0:T(8,128)(2,1)S(1)} %collective-permute-done.9.refs_0_, bf16[1,2048,768]{2,1,0:T(8,128)(2,1)S(1)} %get-tuple-element.25.refs_1_.refs_2_, bf16[1,2048,768]{2,1,0:T(8,128)(2,1)S(1)} %get-tuple-element.26.refs_2_.refs_3_, ...), custom_call_target="tpu_custom_call" | custom-call | flops 3019898880 | bytes 2621440 | tf_op jit(solution)/shard_map/expert/pallas_call | solution.py:243
  69.7 3.3 %collective-permute-start.10 = (bf16[320,2048]{1,0:T(8,128)(2,1)S(1)}, bf16[320,2048]{1,0:T(8,128)(2,1)S(1)}, u32[]{:S(2)}, u32[]{:S(2)}) collective-permute-start(bf16[320,2048]{1,0:T(8,128)(2,1)S(1)} %expert.5), channel_id=1, source_target_pairs={{4,0},{17,1},{6,2},{19,3},{0,4},{21,5},{2,6},{23,7},{12,8},{25,9},... | collective-permute-start | bytes 3932168 | tf_op jit(solution)/shard_map/ppermute | solution.py:291
  73.0 5.9 %collective-permute-done.8.refs_1_ = bf16[320,2048]{1,0:T(8,128)(2,1)S(1)} collective-permute-done((bf16[320,2048]{1,0:T(8,128)(2,1)S(1)}, bf16[320,2048]{1,0:T(8,128)(2,1)S(1)}, u32[]{:S(2)}, u32[]{:S(2)}) %collective-permute-start.8) | collective-permute-done | bytes 1310752 | tf_op jit(solution)/shard_map/ppermute | solution.py:291
  78.9 0.0 collective-permute-done.11.refs_3_
  78.9 13.7 %collective-permute-done.10.refs_2_ = bf16[320,2048]{1,0:T(8,128)(2,1)S(1)} collective-permute-done((bf16[320,2048]{1,0:T(8,128)(2,1)S(1)}, bf16[320,2048]{1,0:T(8,128)(2,1)S(1)}, u32[]{:S(2)}, u32[]{:S(2)}) %collective-permute-start.10) | collective-permute-done | bytes 1310752 | tf_op jit(solution)/shard_map/ppermute | solution.py:291
  92.5 2.6 %combine.1 = (f32[128,2048]{1,0:T(8,128)S(1)}, bf16[128,2048]{1,0:T(8,128)(2,1)S(1)}, bf16[128,2048]{1,0:T(8,128)(2,1)S(1)}, bf16[128,2048]{1,0:T(8,128)(2,1)S(1)}) custom-call(s32[1]{0:T(128)} %bitcast.pos_ref, bf16[16,32]{1,0:T(8,128)(2,1)S(1)} %fusion.q_ref, bf16[4,16,512]{2,1,0:T(8,128)(2,1)S(1)} %bitcast.6, ...), custom_call_target="tpu_custom_call" | custom-call | flops 1342177280 | bytes 7864320 | tf_op jit(solution)/shard_map/combine/pallas_call | solution.py:202
  95.2 3.0 %collective-permute-start.12 = (bf16[128,2048]{1,0:T(8,128)(2,1)S(1)}, bf16[128,2048]{1,0:T(8,128)(2,1)S(1)}, u32[]{:S(2)}, u32[]{:S(2)}) collective-permute-start(bf16[128,2048]{1,0:T(8,128)(2,1)S(1)} %get-tuple-element.36), channel_id=1, source_target_pairs={{8,0},{3,1},{10,2},{5,3},{12,4},{7,5},{14,6},{1,7},{16,8},{11,9},{... | collective-permute-start | bytes 1572872 | tf_op jit(solution)/shard_map/ppermute | solution.py:291
  98.2 0.9 collective-permute-start.13
  99.0 0.1 collective-permute-start.14
  99.1 11.4 %collective-permute-done.12 = bf16[128,2048]{1,0:T(8,128)(2,1)S(1)} collective-permute-done((bf16[128,2048]{1,0:T(8,128)(2,1)S(1)}, bf16[128,2048]{1,0:T(8,128)(2,1)S(1)}, u32[]{:S(2)}, u32[]{:S(2)}) %collective-permute-start.12) | collective-permute-done | bytes 524320 | tf_op jit(solution)/shard_map/ppermute | solution.py:291
  110.5 0.0 collective-permute-done.13
  110.5 4.0 %collective-permute-done.14 = bf16[128,2048]{1,0:T(8,128)(2,1)S(1)} collective-permute-done((bf16[128,2048]{1,0:T(8,128)(2,1)S(1)}, bf16[128,2048]{1,0:T(8,128)(2,1)S(1)}, u32[]{:S(2)}, u32[]{:S(2)}) %collective-permute-start.14) | collective-permute-done | bytes 524320 | tf_op jit(solution)/shard_map/ppermute | solution.py:291
  114.5 1.1 add_convert_fusion
  (4 shorter events, 0.0 us)
Async XLA Ops:
  0.0 23.7 %collective-permute-start = (bf16[128,2048]{1,0:T(8,128)(2,1)}, bf16[128,2048]{1,0:T(8,128)(2,1)}, u32[]{:S(2)}, u32[]{:S(2)}) collective-permute-start(bf16[128,2048]{1,0:T(8,128)(2,1)} %tok_ref.1), channel_id=1, source_target_pairs={{0,8},{1,3},{2,10},{3,5},{4,12},{5,7},{6,14},{7,1},{8,16},{9,11},{... | collective-permute-start | bytes 1572872 | tf_op jit(solution)/shard_map/ppermute | solution.py:291
  1.5 22.2 %collective-permute-start.2 = (bf16[128,2048]{1,0:T(8,128)(2,1)}, bf16[128,2048]{1,0:T(8,128)(2,1)}, u32[]{:S(2)}, u32[]{:S(2)}) collective-permute-start(bf16[128,2048]{1,0:T(8,128)(2,1)} %tok_ref.1), channel_id=1, source_target_pairs={{0,24},{1,7},{2,26},{3,1},{4,28},{5,3},{6,30},{7,5},{8,0},{9,15},{... | collective-permute-start | bytes 1572872 | tf_op jit(solution)/shard_map/ppermute | solution.py:291
  3.2 20.4 %collective-permute-start.1 = (bf16[128,2048]{1,0:T(8,128)(2,1)}, bf16[128,2048]{1,0:T(8,128)(2,1)}, u32[]{:S(2)}, u32[]{:S(2)}) collective-permute-start(bf16[128,2048]{1,0:T(8,128)(2,1)} %tok_ref.1), channel_id=1, source_target_pairs={{0,16},{1,5},{2,18},{3,7},{4,20},{5,1},{6,22},{7,3},{8,24},{9,13},... | collective-permute-start | bytes 1572872 | tf_op jit(solution)/shard_map/ppermute | solution.py:291
  5.1 0.7 copy-start.2
  5.7 0.7 copy-start.3
  7.5 0.8 copy-start
  23.0 11.9 %collective-permute-start.3 = (bf16[1,2048,768]{2,1,0:T(8,128)(2,1)}, bf16[1,2048,768]{2,1,0:T(8,128)(2,1)S(1)}, u32[]{:S(2)}, u32[]{:S(2)}) collective-permute-start(bf16[1,2048,768]{2,1,0:T(8,128)(2,1)} %refs_0_.1), channel_id=1, source_target_pairs={{0,1},{1,0},{2,3},{3,2},{4,5},{5,4},{6,7},{7,6},{8,9},{9,8},{10,11... | collective-permute-start | bytes 9437192 | tf_op jit(solution)/shard_map/ppermute | solution.py:291
  23.1 11.9 %collective-permute-start.4 = (bf16[1,2048,768]{2,1,0:T(8,128)(2,1)}, bf16[1,2048,768]{2,1,0:T(8,128)(2,1)}, u32[]{:S(2)}, u32[]{:S(2)}) collective-permute-start(bf16[1,2048,768]{2,1,0:T(8,128)(2,1)} %refs_1_.1), channel_id=1, source_target_pairs={{0,1},{1,0},{2,3},{3,2},{4,5},{5,4},{6,7},{7,6},{8,9},{9,8},{10,11... | collective-permute-start | bytes 9437192 | tf_op jit(solution)/shard_map/ppermute | solution.py:291
  23.7 1.0 copy-start.1
  24.7 3.0 %copy-start.4 = (bf16[1,768,2048]{2,1,0:T(8,128)(2,1)S(1)}, bf16[1,768,2048]{2,1,0:T(8,128)(2,1)}, u32[]{:S(2)}) copy-start(bf16[1,768,2048]{2,1,0:T(8,128)(2,1)} %refs_2_.1) | copy-start | bytes 9437188
  27.7 10.0 %collective-permute-start.5 = (bf16[1,768,2048]{2,1,0:T(8,128)(2,1)S(1)}, bf16[1,768,2048]{2,1,0:T(8,128)(2,1)S(1)}, u32[]{:S(2)}, u32[]{:S(2)}) collective-permute-start(bf16[1,768,2048]{2,1,0:T(8,128)(2,1)S(1)} %copy-done.4), channel_id=1, source_target_pairs={{0,1},{1,0},{2,3},{3,2},{4,5},{5,4},{6,7},{7,6},{8,9},{9,8},{10,11... | collective-permute-start | bytes 9437192 | tf_op jit(solution)/shard_map/ppermute | solution.py:291
  27.9 20.6 %collective-permute-start.6 = (bf16[320,2048]{1,0:T(8,128)(2,1)S(1)}, bf16[320,2048]{1,0:T(8,128)(2,1)S(1)}, u32[]{:S(2)}, u32[]{:S(2)}) collective-permute-start(bf16[320,2048]{1,0:T(8,128)(2,1)S(1)} %get-tuple-element.31), channel_id=1, source_target_pairs={{0,2},{1,9},{2,4},{3,11},{4,6},{5,13},{6,0},{7,15},{8,10},{9,17},{... | collective-permute-start | bytes 3932168 | tf_op jit(solution)/shard_map/ppermute | solution.py:291
  29.5 19.0 %collective-permute-start.7 = (bf16[320,2048]{1,0:T(8,128)(2,1)S(1)}, bf16[320,2048]{1,0:T(8,128)(2,1)S(1)}, u32[]{:S(2)}, u32[]{:S(2)}) collective-permute-start(bf16[320,2048]{1,0:T(8,128)(2,1)S(1)} %get-tuple-element.32), channel_id=1, source_target_pairs={{0,6},{1,25},{2,0},{3,27},{4,2},{5,29},{6,4},{7,31},{8,14},{9,1},{... | collective-permute-start | bytes 3932168 | tf_op jit(solution)/shard_map/ppermute | solution.py:291
  45.0 19.5 %collective-permute-start.9 = (bf16[320,2048]{1,0:T(8,128)(2,1)S(1)}, bf16[320,2048]{1,0:T(8,128)(2,1)S(1)}, u32[]{:S(2)}, u32[]{:S(2)}) collective-permute-start(bf16[320,2048]{1,0:T(8,128)(2,1)S(1)} %pack.3), channel_id=1, source_target_pairs={{0,4},{1,17},{2,6},{3,19},{4,0},{5,21},{6,2},{7,23},{8,12},{9,25},... | collective-permute-start | bytes 3932168 | tf_op jit(solution)/shard_map/ppermute | solution.py:291
  56.7 22.1 %collective-permute-start.8 = (bf16[320,2048]{1,0:T(8,128)(2,1)S(1)}, bf16[320,2048]{1,0:T(8,128)(2,1)S(1)}, u32[]{:S(2)}, u32[]{:S(2)}) collective-permute-start(bf16[320,2048]{1,0:T(8,128)(2,1)S(1)} %get-tuple-element.33), channel_id=1, source_target_pairs={{2,0},{9,1},{4,2},{11,3},{6,4},{13,5},{0,6},{15,7},{10,8},{17,9},{... | collective-permute-start | bytes 3932168 | tf_op jit(solution)/shard_map/ppermute | solution.py:291
  58.3 20.6 %collective-permute-start.11 = (bf16[320,2048]{1,0:T(8,128)(2,1)S(1)}, bf16[320,2048]{1,0:T(8,128)(2,1)S(1)}, u32[]{:S(2)}, u32[]{:S(2)}) collective-permute-start(bf16[320,2048]{1,0:T(8,128)(2,1)S(1)} %get-tuple-element.34), channel_id=1, source_target_pairs={{6,0},{25,1},{0,2},{27,3},{2,4},{29,5},{4,6},{31,7},{14,8},{1,9},{... | collective-permute-start | bytes 3932168 | tf_op jit(solution)/shard_map/ppermute | solution.py:291
  69.7 22.8 %collective-permute-start.10 = (bf16[320,2048]{1,0:T(8,128)(2,1)S(1)}, bf16[320,2048]{1,0:T(8,128)(2,1)S(1)}, u32[]{:S(2)}, u32[]{:S(2)}) collective-permute-start(bf16[320,2048]{1,0:T(8,128)(2,1)S(1)} %expert.5), channel_id=1, source_target_pairs={{4,0},{17,1},{6,2},{19,3},{0,4},{21,5},{2,6},{23,7},{12,8},{25,9},... | collective-permute-start | bytes 3932168 | tf_op jit(solution)/shard_map/ppermute | solution.py:291
  95.2 15.3 %collective-permute-start.12 = (bf16[128,2048]{1,0:T(8,128)(2,1)S(1)}, bf16[128,2048]{1,0:T(8,128)(2,1)S(1)}, u32[]{:S(2)}, u32[]{:S(2)}) collective-permute-start(bf16[128,2048]{1,0:T(8,128)(2,1)S(1)} %get-tuple-element.36), channel_id=1, source_target_pairs={{8,0},{3,1},{10,2},{5,3},{12,4},{7,5},{14,6},{1,7},{16,8},{11,9},{... | collective-permute-start | bytes 1572872 | tf_op jit(solution)/shard_map/ppermute | solution.py:291
  98.2 12.3 %collective-permute-start.13 = (bf16[128,2048]{1,0:T(8,128)(2,1)S(1)}, bf16[128,2048]{1,0:T(8,128)(2,1)S(1)}, u32[]{:S(2)}, u32[]{:S(2)}) collective-permute-start(bf16[128,2048]{1,0:T(8,128)(2,1)S(1)} %get-tuple-element.37), channel_id=1, source_target_pairs={{16,0},{5,1},{18,2},{7,3},{20,4},{1,5},{22,6},{3,7},{24,8},{13,9},... | collective-permute-start | bytes 1572872 | tf_op jit(solution)/shard_map/ppermute | solution.py:291
  99.0 15.4 %collective-permute-start.14 = (bf16[128,2048]{1,0:T(8,128)(2,1)S(1)}, bf16[128,2048]{1,0:T(8,128)(2,1)S(1)}, u32[]{:S(2)}, u32[]{:S(2)}) collective-permute-start(bf16[128,2048]{1,0:T(8,128)(2,1)S(1)} %get-tuple-element.38), channel_id=1, source_target_pairs={{24,0},{7,1},{26,2},{1,3},{28,4},{3,5},{30,6},{5,7},{0,8},{15,9},{... | collective-permute-start | bytes 1572872 | tf_op jit(solution)/shard_map/ppermute | solution.py:291

commit v4 on v3

--- a/solution.py
+++ b/solution.py
@@ -10,6 +10,7 @@
 NX, NY, NC = 4, 4, 2
 EXPERTS = NX * NY * NC
 CAP = 40
+META = 16
 KF = 8
 
 
@@ -35,12 +36,6 @@
     return pairs
 
 
-def spread_groups():
-    return [[index_of(x, y, 0) for x in range(NX)] for y in range(NY)] + [
-        [index_of(x, y, 1) for y in range(NY)] for x in range(NX)
-    ]
-
-
 def swap_pairs():
     return [(i, i ^ 1) for i in range(EXPERTS)]
 
@@ -49,47 +44,61 @@
     return [(b, a) for a, b in pairs]
 
 
-def prep_kernel(ids_ref, gw_ref, tok_ref, out_ref, own_ref, sem):
-    copy = pltpu.make_async_copy(tok_ref, own_ref, sem)
-    copy.start()
+def prep_kernel(ids_hbm, gw_hbm, tok_hbm, out_ref, load_ref, ids_ref, gw_ref, sems):
     top, tok = ids_ref.shape
-    ids = ids_ref[...]
-    gw = gw_ref[...]
+    copies = [
+        pltpu.make_async_copy(ids_hbm, ids_ref, sems.at[0]),
+        pltpu.make_async_copy(gw_hbm, gw_ref, sems.at[1]),
+        pltpu.make_async_copy(tok_hbm, load_ref.at[pl.ds(0, tok)], sems.at[2]),
+    ]
+    for copy in copies:
+        copy.start()
+    row = lax.broadcasted_iota(jnp.int32, (tok, tok), 0)
+    col = lax.broadcasted_iota(jnp.int32, (tok, tok), 1)
+    earlier = jnp.where(row < col, 1.0, 0.0).astype(jnp.bfloat16)
     name = lax.broadcasted_iota(jnp.int32, (EXPERTS, tok), 0)
     chosen = jnp.zeros((EXPERTS, tok), jnp.float32)
     weight = jnp.zeros((EXPERTS, tok), jnp.float32)
+    copies[0].wait()
+    copies[1].wait()
+    ids = ids_ref[...]
+    gw = gw_ref[...]
     for k in range(top):
         hit = ids[k : k + 1, :] == name
         chosen = jnp.where(hit, 1.0, chosen)
         weight = jnp.where(hit, gw[k : k + 1, :], weight)
-    row = lax.broadcasted_iota(jnp.int32, (tok, tok), 0)
-    col = lax.broadcasted_iota(jnp.int32, (tok, tok), 1)
-    earlier = jnp.where(row < col, 1.0, 0.0).astype(jnp.bfloat16)
     count = jnp.dot(chosen.astype(jnp.bfloat16), earlier, preferred_element_type=jnp.float32)
     slot = jnp.where(chosen > 0.5, count, -1.0)
     half = EXPERTS // 2
-    out_ref[...] = jnp.concatenate(
-        [slot[:half], slot[half:], weight[:half], weight[half:]], axis=1
-    ).astype(jnp.bfloat16)
-    copy.wait()
+    meta = jnp.concatenate([slot[:half], slot[half:], weight[:half], weight[half:]], axis=1)
+    meta = meta.astype(jnp.bfloat16)
+    out_ref[...] = meta
+    load_ref[tok:, : 4 * tok] = meta
+    load_ref[tok:, 4 * tok :] = jnp.zeros((META, load_ref.shape[1] - 4 * tok), jnp.bfloat16)
+    copies[2].wait()
 
 
 def prep(ids, gw, tokens):
-    tok = ids.shape[1]
+    tok, width = tokens.shape
     vmem = pl.BlockSpec(memory_space=pltpu.VMEM)
+    hbm = pl.BlockSpec(memory_space=pl.ANY)
     return pl.pallas_call(
         prep_kernel,
-        in_specs=[vmem, vmem, pl.BlockSpec(memory_space=pl.ANY)],
+        in_specs=[hbm, hbm, hbm],
         out_specs=[vmem, vmem],
         out_shape=[
-            jax.ShapeDtypeStruct((EXPERTS // 2, 4 * tok), jnp.bfloat16),
-            pltpu.VMEM(tokens.shape, tokens.dtype),
+            pltpu.VMEM((META, 4 * tok), jnp.bfloat16),
+            pltpu.VMEM((tok + META, width), jnp.bfloat16),
         ],
-        scratch_shapes=[pltpu.SemaphoreType.DMA],
+        scratch_shapes=[
+            pltpu.VMEM(ids.shape, ids.dtype),
+            pltpu.VMEM(gw.shape, gw.dtype),
+            pltpu.SemaphoreType.DMA((3,)),
+        ],
         compiler_params=pltpu.CompilerParams(vmem_limit_bytes=4 * 1024 * 1024),
-        cost_estimate=pl.CostEstimate(flops=2 * EXPERTS * tok**2, bytes_accessed=32 * tok * 4, transcendentals=0),
+        cost_estimate=pl.CostEstimate(flops=2 * EXPERTS * tok**2, bytes_accessed=4 * tok * width, transcendentals=0),
         name="prep",
-    )(ids, gw, pltpu.with_memory_space_constraint(tokens, pltpu.HBM))
+    )(*[pltpu.with_memory_space_constraint(v, pltpu.HBM) for v in (ids, gw, tokens)])
 
 
 def select(q, meta, at, tok):
@@ -99,13 +108,16 @@
     ) + jnp.dot(q[:, half:], meta[:, at + tok : at + 2 * tok], preferred_element_type=jnp.float32)
 
 
-def table(pos_ref, metas_ref, j):
-    return metas_ref[lax.rem(pos_ref[0] + 4 - j, 4)]
-
-
-def pack_kernel(which, pos_ref, q_ref, metas_ref, *refs):
-    blocks, outs = refs[:4], refs[-len(which) :]
-    tok, width = blocks[0].shape
+def tables(metas, blocks):
+    m0, m1, m3 = metas
+    tok = blocks[0].shape[0] - META
+    return m0[...], m1[...], blocks[1][tok:, : 4 * tok], m3[...]
+
+
+def pack_kernel(which, q_ref, *refs):
+    metas, blocks, outs = refs[:3], refs[3:7], refs[-len(which) :]
+    tok, width = blocks[1].shape
+    metas = tables(metas, blocks[::2])
     q = q_ref[...]
     span = 2 * CAP
     r = lax.broadcasted_iota(jnp.int32, (span, 2 * tok), 0)
@@ -115,8 +127,8 @@
     target = jnp.where(second == (t >= tok), target, -5).astype(jnp.float32)
     cols = 512
     for p in range(2):
-        metas = [table(pos_ref, metas_ref, j) for j in (2 * p, 2 * p + 1)]
-        slots = jnp.concatenate([select(q, m, 0, tok) for m in metas], axis=1)
+        pair = metas[2 * p : 2 * p + 2]
+        slots = jnp.concatenate([select(q, m, 0, tok) for m in pair], axis=1)
         pick = jnp.concatenate(
             [
                 jnp.where(slots[NC * k + f : NC * k + f + 1, :] == target, 1.0, 0.0).astype(jnp.bfloat16)
@@ -126,7 +138,7 @@
             axis=0,
         )
         for at in range(0, width, cols):
-            block = jnp.concatenate([b[:, at : at + cols] for b in blocks[2 * p : 2 * p + 2]], axis=0)
+            block = jnp.concatenate([b[:tok, at : at + cols] for b in blocks[2 * p : 2 * p + 2]], axis=0)
             got = jnp.dot(pick, block, preferred_element_type=jnp.float32).astype(jnp.bfloat16)
             for n, o in enumerate(outs):
                 for f in range(NC):
@@ -134,14 +146,14 @@
                     o[to : to + span, at : at + cols] = got[of : of + span, :]
 
 
-def pack(which, pos, q, metas, blocks, after=()):
-    tok, width = blocks[0].shape
+def pack(which, q, metas, blocks, after=()):
+    tok, width = blocks[1].shape
     count = len(which)
     rows = NC * 4 * CAP
     vmem = pl.BlockSpec(memory_space=pltpu.VMEM)
     return pl.pallas_call(
         functools.partial(pack_kernel, which),
-        in_specs=[pl.BlockSpec(memory_space=pltpu.SMEM)] + [vmem] * 6 + [pl.BlockSpec(memory_space=pl.ANY)] * len(after),
+        in_specs=[vmem] * 8 + [pl.BlockSpec(memory_space=pl.ANY)] * len(after),
         out_specs=[vmem] * count,
         out_shape=[jax.ShapeDtypeStruct((rows, width), jnp.bfloat16)] * count,
         compiler_params=pltpu.CompilerParams(vmem_limit_bytes=16 * 1024 * 1024),
@@ -151,11 +163,12 @@
             transcendentals=0,
         ),
         name="pack",
-    )(pos, q, metas, *blocks, *after)
-
-
-def combine_kernel(pos_ref, q_ref, metas_ref, *refs):
-    backs, outs = refs[:4], refs[4:]
+    )(q, *metas, *blocks, *after)
+
+
+def combine_kernel(q_ref, *refs):
+    metas, blocks, backs, outs = refs[:3], refs[3:5], refs[5:9], refs[9:]
+    metas = tables(metas, blocks)
     tok, width = outs[0].shape
     q = q_ref[...]
     half = 2 * CAP
@@ -182,9 +195,9 @@
 
     cols = 512
     for p in range(2):
-        metas = [table(pos_ref, metas_ref, j) for j in (2 * p, 2 * p + 1)]
-        slots = jnp.concatenate([select(q, m, 0, tok) for m in metas], axis=1)
-        weights = jnp.concatenate([select(q, m, 2 * tok, tok) for m in metas], axis=1)
+        pair = metas[2 * p : 2 * p + 2]
+        slots = jnp.concatenate([select(q, m, 0, tok) for m in pair], axis=1)
+        weights = jnp.concatenate([select(q, m, 2 * tok, tok) for m in pair], axis=1)
         mix = jnp.where(widen(slots) == target, widen(weights), 0.0).astype(jnp.bfloat16)
         for at in range(0, width, cols):
             rows = jnp.concatenate(
@@ -196,12 +209,13 @@
                 o[:, at : at + cols] = got[n * tok : (n + 1) * tok].astype(o.dtype)
 
 
-def combine(pos, q, metas, backs, tok):
+def combine(q, metas, blocks, backs):
     rows, width = backs[0].shape
+    tok = blocks[1].shape[0]
     vmem = pl.BlockSpec(memory_space=pltpu.VMEM)
     return pl.pallas_call(
         combine_kernel,
-        in_specs=[pl.BlockSpec(memory_space=pltpu.SMEM)] + [vmem] * 6,
+        in_specs=[vmem] * 10,
         out_specs=[vmem] * 4,
         out_shape=[jax.ShapeDtypeStruct((tok, width), jnp.float32)]
         + [jax.ShapeDtypeStruct((tok, width), jnp.bfloat16)] * 3,
@@ -212,7 +226,7 @@
             transcendentals=0,
         ),
         name="combine",
-    )(pos, q, metas, *backs)
+    )(q, *metas, *blocks[::2], *backs)
 
 
 def expert_kernel(count, *refs):
@@ -286,28 +300,28 @@
     along_x = ((x + k) % NX) * (NY * NC) + y * NC + (c ^ f)
     mine = jnp.where(n < KF, jnp.where(c == 0, along_y, along_x), -1)
     q = (mine[:, None] == jnp.arange(EXPERTS, dtype=jnp.int32)[None, :]).astype(jnp.bfloat16)
-    pos = jnp.where(c == 0, x, y).reshape(1).astype(jnp.int32)
 
     send = lambda v, pairs: lax.ppermute(v, "expert", pairs)
-    moved = [send(tokens, spread_pairs(j)) for j in (1, 2, 3)]
-    meta, own = prep(expert_ids.T, gate_weights.T, tokens)
-    blocks = [own] + moved
-    metas = lax.all_gather(meta, "expert", axis=0, axis_index_groups=spread_groups())
-    first = lax.optimization_barrier((w_gate, w_up, metas))[:2]
+    moved = {j: send(tokens, spread_pairs(j)) for j in (1, 3)}
+    meta, load = prep(expert_ids.T, gate_weights.T, tokens)
+    moved[2] = send(load, spread_pairs(2))
+    blocks = [load, moved[1], moved[2], moved[3]]
+    metas = [meta] + [send(meta, spread_pairs(j)) for j in (1, 3)]
+    first = lax.optimization_barrier((w_gate, w_up, moved[1]))[:2]
     weights = list(hold(w_gate, w_up, w_down)) + [send(w, swap_pairs()) for w in first]
 
-    slabs = dict(zip((1, 3, 0), pack((1, 3, 0), pos, q, metas, blocks)))
+    slabs = dict(zip((1, 3, 0), pack((1, 3, 0), q, metas, blocks)))
     last = lax.optimization_barrier((w_down, slabs[0]))[0]
     weights.append(send(last, swap_pairs()))
     arrived = {k: send(slabs[k], deliver_pairs(k)) for k in (1, 3)}
     backs = {}
     (backs[0],) = expert([slabs[0]], weights)
-    (far,) = pack((2,), pos, q, metas, blocks, (backs[0],))
+    (far,) = pack((2,), q, metas, blocks, (backs[0],))
     arrived[2] = send(far, deliver_pairs(2))
     for ks in ((1, 3), (2,)):
         for k, slab in zip(ks, expert([arrived[k] for k in ks], weights)):
             backs[k] = send(slab, back(deliver_pairs(k)))
-    parts = combine(pos, q, metas, [backs[k] for k in range(4)], tokens.shape[0])
+    parts = combine(q, metas, blocks, [backs[k] for k in range(4)])
     mixed = parts[0]
     for j in (1, 2, 3):
         mixed = mixed + send(parts[j], back(spread_pairs(j))).astype(jnp.float32)

time: 116 us -> 107 us (0.922)
  blocking collectives: 14.8 us -> 0 us
  waiting for transfers between devices: 43.3 us -> 57.2 us
  Pallas kernels: 31.1 us -> 22.8 us
  local copies, waits for them, and re-layouts: 3.2 us -> 0.01 us
  starting transfers between devices: 21.8 us -> 24.9 us
    all_gather x1 -> x0, blocking collectives: 14.8 us -> none  [per_device(): lax.all_gather(meta, 'expert', axis=0, axis_index_groups=spread_groups())]
    ppermute x15 -> x17, waiting for transfers between devices: 43.3 us -> 57.2 us  [per_device(): send = lambda v, pairs: lax.ppermute(v, 'expert', pairs)]
    pallas_call x3, Pallas kernels: 18.5 us -> 13 us  [expert(): pl.pallas_call(functools.partial(expert_kernel, count), in_specs=[vmem] *...]
    unnamed x10 -> x2, local copies, waits for them, and re-layouts: 3.2 us -> 0.01 us
    ppermute x15 -> x17, starting transfers between devices: 21.8 us -> 24.9 us  [per_device(): send = lambda v, pairs: lax.ppermute(v, 'expert', pairs)]
    pallas_call x4, Pallas kernels: 8.85 us -> 6.04 us  [the longest x1 2.64 us: combine(): pl.pallas_call(combine_kernel, in_specs=[vmem] * 10, out_specs=[vmem] * 4...]
  transfers between devices with their start and end apart: 15 -> 17, of which waited for: 6 -> 9; matrix products, arithmetic and copies ran while one was open for 0% -> 0% of each run, Pallas kernels for 25% -> 18%
where the time goes in v4:
time: 107 us; the launch traced here: 106 us
  waiting for transfers between devices  57.2 us (53%)
  starting transfers between devices  24.9 us (23%)
  Pallas kernels  22.8 us (21%)
  other arithmetic  1.18 us (1%)
    ppermute x17, waiting for transfers between devices, per_device(): send = lambda v, pairs: lax.ppermute(v, 'expert', pairs)  57.2 us
    ppermute x17, starting transfers between devices, per_device(): send = lambda v, pairs: lax.ppermute(v, 'expert', pairs)  24.9 us
    pallas_call x3, Pallas kernels, expert(): pl.pallas_call(functools.partial(expert_kernel, count), in_specs=[vmem] *...  13 us
    pallas_call x1, Pallas kernels, hold(): pl.pallas_call(hold_kernel, in_specs=[pl.BlockSpec(memory_space=pl.ANY)]...  3.78 us
    pallas_call x1, Pallas kernels, combine(): pl.pallas_call(combine_kernel, in_specs=[vmem] * 10, out_specs=[vmem] * 4...  2.64 us
    pallas_call x2, Pallas kernels, pack(): pl.pallas_call(functools.partial(pack_kernel, which), in_specs=[vmem] * 8...  2.31 us
  transfers between devices with their start and end apart: 17, of which 9 were waited for; matrix products, arithmetic and copies ran while one was open for 0% of the time, Pallas kernels for 18%

profile of v4, /device:TPU:96, one launch (start us, length us, event | category | flops | bytes accessed | tf_op | source)
XLA Modules:
  0.0 106.1 jit_solution(3030924173342781231)
XLA Ops:
  0.0 1.1 %prep.1 = (bf16[16,512]{1,0:T(8,128)(2,1)S(1)}, bf16[144,2048]{1,0:T(8,128)(2,1)S(1)}) custom-call(s32[8,128]{1,0:T(8,128)} %bitcast.2, f32[8,128]{1,0:T(8,128)} %bitcast.3, bf16[128,2048]{1,0:T(8,128)(2,1)} %tok_hbm.1), custom_call_target="tpu_custom_call" | custom-call | flops 1048576 | bytes 1048576 | tf_op jit(solution)/shard_map/prep/pallas_call | solution.py:85
  1.1 3.1 %collective-permute-start.2 = (bf16[144,2048]{1,0:T(8,128)(2,1)S(1)}, bf16[144,2048]{1,0:T(8,128)(2,1)S(1)}, u32[]{:S(2)}, u32[]{:S(2)}) collective-permute-start(bf16[144,2048]{1,0:T(8,128)(2,1)S(1)} %get-tuple-element.23.refs_3_), channel_id=1, source_target_pairs={{0,16},{1,5},{2,18},{3,7},{4,20},{5,1},{6,22},{7,3},{8,24},{9,13},... | collective-permute-start | bytes 1769480 | tf_op jit(solution)/shard_map/ppermute | solution.py:304
  4.2 0.6 collective-permute-start.3
  4.8 2.6 %collective-permute-start.4 = (bf16[128,2048]{1,0:T(8,128)(2,1)}, bf16[128,2048]{1,0:T(8,128)(2,1)S(1)}, u32[]{:S(2)}, u32[]{:S(2)}) collective-permute-start(bf16[128,2048]{1,0:T(8,128)(2,1)} %tok_hbm.1), channel_id=1, source_target_pairs={{0,24},{1,7},{2,26},{3,1},{4,28},{5,3},{6,30},{7,5},{8,0},{9,15},{... | collective-permute-start | bytes 1572872 | tf_op jit(solution)/shard_map/ppermute | solution.py:304
  7.5 0.0 collective-permute-start.1
  7.5 2.0 %collective-permute-start = (bf16[16,512]{1,0:T(8,128)(2,1)S(1)}, bf16[16,512]{1,0:T(8,128)(2,1)S(1)}, u32[]{:S(2)}, u32[]{:S(2)}) collective-permute-start(bf16[16,512]{1,0:T(8,128)(2,1)S(1)} %get-tuple-element.22.refs_0_), channel_id=1, source_target_pairs={{0,8},{1,3},{2,10},{3,5},{4,12},{5,7},{6,14},{7,1},{8,16},{9,11},{... | collective-permute-start | bytes 49160 | tf_op jit(solution)/shard_map/ppermute | solution.py:304
  9.5 0.1 fusion.q_ref
  9.6 0.0 copy-start
  9.6 8.6 %collective-permute-done.3.refs_4_ = bf16[128,2048]{1,0:T(8,128)(2,1)S(1)} collective-permute-done((bf16[128,2048]{1,0:T(8,128)(2,1)}, bf16[128,2048]{1,0:T(8,128)(2,1)S(1)}, u32[]{:S(2)}, u32[]{:S(2)}) %collective-permute-start.3) | collective-permute-done | bytes 524320 | tf_op jit(solution)/shard_map/ppermute | solution.py:304
  18.2 0.0 collective-permute-start.5
  18.2 0.3 collective-permute-done.1.refs_2_
  18.5 0.2 collective-permute-start.6
  18.7 0.0 collective-permute-done.refs_1_
  18.7 0.0 collective-permute-done.4.refs_6_
  18.7 0.0 collective-permute-done.2.refs_5_.refs_4_
  18.7 1.5 %pack.2 = (bf16[320,2048]{1,0:T(8,128)(2,1)S(1)}, bf16[320,2048]{1,0:T(8,128)(2,1)S(1)}, bf16[320,2048]{1,0:T(8,128)(2,1)S(1)}) custom-call(bf16[16,32]{1,0:T(8,128)(2,1)S(1)} %fusion.q_ref, bf16[16,512]{1,0:T(8,128)(2,1)S(1)} %get-tuple-element.22.refs_0_, bf16[16,512]{1,0:T(8,128)(2,1)S(1)} %collective-permute-done.refs_1_, ...), custom_call_target="tpu_custom_call" | custom-call | flops 1006632960 | bytes 6029312 | tf_op jit(solution)/shard_map/pack/pallas_call | solution.py:154
  20.2 0.0 copy-done
  20.2 0.4 collective-permute-start.7
  20.6 1.6 %collective-permute-start.8 = (bf16[320,2048]{1,0:T(8,128)(2,1)S(1)}, bf16[320,2048]{1,0:T(8,128)(2,1)S(1)}, u32[]{:S(2)}, u32[]{:S(2)}) collective-permute-start(bf16[320,2048]{1,0:T(8,128)(2,1)S(1)} %get-tuple-element.31), channel_id=1, source_target_pairs={{0,2},{1,9},{2,4},{3,11},{4,6},{5,13},{6,0},{7,15},{8,10},{9,17},{... | collective-permute-start | bytes 3932168 | tf_op jit(solution)/shard_map/ppermute | solution.py:304
  22.2 1.7 %collective-permute-start.9 = (bf16[320,2048]{1,0:T(8,128)(2,1)S(1)}, bf16[320,2048]{1,0:T(8,128)(2,1)S(1)}, u32[]{:S(2)}, u32[]{:S(2)}) collective-permute-start(bf16[320,2048]{1,0:T(8,128)(2,1)S(1)} %get-tuple-element.32), channel_id=1, source_target_pairs={{0,6},{1,25},{2,0},{3,27},{4,2},{5,29},{6,4},{7,31},{8,14},{9,1},{... | collective-permute-start | bytes 3932168 | tf_op jit(solution)/shard_map/ppermute | solution.py:304
  23.9 3.8 %hold.1 = (bf16[1,2048,768]{2,1,0:T(8,128)(2,1)S(1)}, bf16[1,2048,768]{2,1,0:T(8,128)(2,1)S(1)}, bf16[1,768,2048]{2,1,0:T(8,128)(2,1)S(1)}) custom-call(bf16[1,2048,768]{2,1,0:T(8,128)(2,1)} %refs_0_.1, bf16[1,2048,768]{2,1,0:T(8,128)(2,1)} %refs_1_.1, bf16[1,768,2048]{2,1,0:T(8,128)(2,1)} %refs_2_.1), custom_call_target="tpu_custom_call" | custom-call | bytes 18874368 | tf_op jit(solution)/shard_map/hold/pallas_call | solution.py:282
  27.6 0.0 collective-permute-done.5.refs_4_.refs_5_
  27.7 5.4 %collective-permute-done.6.refs_5_.refs_6_ = bf16[1,2048,768]{2,1,0:T(8,128)(2,1)S(1)} collective-permute-done((bf16[1,2048,768]{2,1,0:T(8,128)(2,1)}, bf16[1,2048,768]{2,1,0:T(8,128)(2,1)S(1)}, u32[]{:S(2)}, u32[]{:S(2)}) %collective-permute-start.6) | collective-permute-done | bytes 3145760 | tf_op jit(solution)/shard_map/ppermute | solution.py:304
  33.1 0.0 collective-permute-done.7.refs_6_.refs_7_
  33.1 3.3 %expert.3.refs_7_.refs_5_ = bf16[320,2048]{1,0:T(8,128)(2,1)S(1)} custom-call(bf16[320,2048]{1,0:T(8,128)(2,1)S(1)} %get-tuple-element.24.refs_0_, bf16[1,2048,768]{2,1,0:T(8,128)(2,1)S(1)} %get-tuple-element.25.refs_1_.refs_2_, bf16[1,2048,768]{2,1,0:T(8,128)(2,1)S(1)} %get-tuple-element.26.refs_2_.refs_3_, ...), custom_call_target="tpu_custom_call" | custom-call | flops 3019898880 | bytes 2621440 | tf_op jit(solution)/shard_map/expert/pallas_call | solution.py:257
  36.4 0.8 pack.3
  37.2 3.5 %collective-permute-start.11 = (bf16[320,2048]{1,0:T(8,128)(2,1)S(1)}, bf16[320,2048]{1,0:T(8,128)(2,1)S(1)}, u32[]{:S(2)}, u32[]{:S(2)}) collective-permute-start(bf16[320,2048]{1,0:T(8,128)(2,1)S(1)} %pack.3), channel_id=1, source_target_pairs={{0,4},{1,17},{2,6},{3,19},{4,0},{5,21},{6,2},{7,23},{8,12},{9,25},... | collective-permute-start | bytes 3932168 | tf_op jit(solution)/shard_map/ppermute | solution.py:304
  40.7 0.0 collective-permute-done.8.refs_0_
  40.7 0.0 collective-permute-done.9.refs_1_
  40.7 6.3 %expert.4 = (bf16[320,2048]{1,0:T(8,128)(2,1)S(1)}, bf16[320,2048]{1,0:T(8,128)(2,1)S(1)}) custom-call(bf16[320,2048]{1,0:T(8,128)(2,1)S(1)} %collective-permute-done.8.refs_0_, bf16[320,2048]{1,0:T(8,128)(2,1)S(1)} %collective-permute-done.9.refs_1_, bf16[1,2048,768]{2,1,0:T(8,128)(2,1)S(1)} %get-tuple-element.25.refs_1_.refs_2_, ...), custom_call_target="tpu_custom_call" | custom-call | flops 6039797760 | bytes 5242880 | tf_op jit(solution)/shard_map/expert/pallas_call | solution.py:257
  47.0 2.1 %collective-permute-start.10 = (bf16[320,2048]{1,0:T(8,128)(2,1)S(1)}, bf16[320,2048]{1,0:T(8,128)(2,1)S(1)}, u32[]{:S(2)}, u32[]{:S(2)}) collective-permute-start(bf16[320,2048]{1,0:T(8,128)(2,1)S(1)} %get-tuple-element.33), channel_id=1, source_target_pairs={{2,0},{9,1},{4,2},{11,3},{6,4},{13,5},{0,6},{15,7},{10,8},{17,9},{... | collective-permute-start | bytes 3932168 | tf_op jit(solution)/shard_map/ppermute | solution.py:304
  49.1 0.0 collective-permute-start.13
  49.1 7.6 %collective-permute-done.11.refs_0_ = bf16[320,2048]{1,0:T(8,128)(2,1)S(1)} collective-permute-done((bf16[320,2048]{1,0:T(8,128)(2,1)S(1)}, bf16[320,2048]{1,0:T(8,128)(2,1)S(1)}, u32[]{:S(2)}, u32[]{:S(2)}) %collective-permute-start.11) | collective-permute-done | bytes 1310752 | tf_op jit(solution)/shard_map/ppermute | solution.py:304
  56.7 3.3 %expert.5 = bf16[320,2048]{1,0:T(8,128)(2,1)S(1)} custom-call(bf16[320,2048]{1,0:T(8,128)(2,1)S(1)} %collective-permute-done.11.refs_0_, bf16[1,2048,768]{2,1,0:T(8,128)(2,1)S(1)} %get-tuple-element.25.refs_1_.refs_2_, bf16[1,2048,768]{2,1,0:T(8,128)(2,1)S(1)} %get-tuple-element.26.refs_2_.refs_3_, ...), custom_call_target="tpu_custom_call" | custom-call | flops 3019898880 | bytes 2621440 | tf_op jit(solution)/shard_map/expert/pallas_call | solution.py:257
  60.0 3.3 %collective-permute-start.12 = (bf16[320,2048]{1,0:T(8,128)(2,1)S(1)}, bf16[320,2048]{1,0:T(8,128)(2,1)S(1)}, u32[]{:S(2)}, u32[]{:S(2)}) collective-permute-start(bf16[320,2048]{1,0:T(8,128)(2,1)S(1)} %expert.5), channel_id=1, source_target_pairs={{4,0},{17,1},{6,2},{19,3},{0,4},{21,5},{2,6},{23,7},{12,8},{25,9},... | collective-permute-start | bytes 3932168 | tf_op jit(solution)/shard_map/ppermute | solution.py:304
  63.3 7.7 %collective-permute-done.10.refs_6_ = bf16[320,2048]{1,0:T(8,128)(2,1)S(1)} collective-permute-done((bf16[320,2048]{1,0:T(8,128)(2,1)S(1)}, bf16[320,2048]{1,0:T(8,128)(2,1)S(1)}, u32[]{:S(2)}, u32[]{:S(2)}) %collective-permute-start.10) | collective-permute-done | bytes 1310752 | tf_op jit(solution)/shard_map/ppermute | solution.py:304
  71.0 0.0 collective-permute-done.13.refs_8_
  71.0 13.7 %collective-permute-done.12.refs_7_ = bf16[320,2048]{1,0:T(8,128)(2,1)S(1)} collective-permute-done((bf16[320,2048]{1,0:T(8,128)(2,1)S(1)}, bf16[320,2048]{1,0:T(8,128)(2,1)S(1)}, u32[]{:S(2)}, u32[]{:S(2)}) %collective-permute-start.12) | collective-permute-done | bytes 1310752 | tf_op jit(solution)/shard_map/ppermute | solution.py:304
  84.7 2.6 %combine.1 = (f32[128,2048]{1,0:T(8,128)S(1)}, bf16[128,2048]{1,0:T(8,128)(2,1)S(1)}, bf16[128,2048]{1,0:T(8,128)(2,1)S(1)}, bf16[128,2048]{1,0:T(8,128)(2,1)S(1)}) custom-call(bf16[16,32]{1,0:T(8,128)(2,1)S(1)} %fusion.q_ref, bf16[16,512]{1,0:T(8,128)(2,1)S(1)} %get-tuple-element.22.refs_0_, bf16[16,512]{1,0:T(8,128)(2,1)S(1)} %collective-permute-done.refs_1_, ...), custom_call_target="tpu_custom_call" | custom-call | flops 1342177280 | bytes 7864320 | tf_op jit(solution)/shard_map/combine/pallas_call | solution.py:216
  87.4 1.4 %collective-permute-start.14 = (bf16[128,2048]{1,0:T(8,128)(2,1)S(1)}, bf16[128,2048]{1,0:T(8,128)(2,1)S(1)}, u32[]{:S(2)}, u32[]{:S(2)}) collective-permute-start(bf16[128,2048]{1,0:T(8,128)(2,1)S(1)} %get-tuple-element.36), channel_id=1, source_target_pairs={{8,0},{3,1},{10,2},{5,3},{12,4},{7,5},{14,6},{1,7},{16,8},{11,9},{... | collective-permute-start | bytes 1572872 | tf_op jit(solution)/shard_map/ppermute | solution.py:304
  88.8 2.3 %collective-permute-start.15 = (bf16[128,2048]{1,0:T(8,128)(2,1)S(1)}, bf16[128,2048]{1,0:T(8,128)(2,1)S(1)}, u32[]{:S(2)}, u32[]{:S(2)}) collective-permute-start(bf16[128,2048]{1,0:T(8,128)(2,1)S(1)} %get-tuple-element.37), channel_id=1, source_target_pairs={{16,0},{5,1},{18,2},{7,3},{20,4},{1,5},{22,6},{3,7},{24,8},{13,9},... | collective-permute-start | bytes 1572872 | tf_op jit(solution)/shard_map/ppermute | solution.py:304
  91.1 0.2 collective-permute-start.16
  91.2 5.4 %collective-permute-done.14 = bf16[128,2048]{1,0:T(8,128)(2,1)S(1)} collective-permute-done((bf16[128,2048]{1,0:T(8,128)(2,1)S(1)}, bf16[128,2048]{1,0:T(8,128)(2,1)S(1)}, u32[]{:S(2)}, u32[]{:S(2)}) %collective-permute-start.14) | collective-permute-done | bytes 524320 | tf_op jit(solution)/shard_map/ppermute | solution.py:304
  96.6 2.9 %collective-permute-done.15 = bf16[128,2048]{1,0:T(8,128)(2,1)S(1)} collective-permute-done((bf16[128,2048]{1,0:T(8,128)(2,1)S(1)}, bf16[128,2048]{1,0:T(8,128)(2,1)S(1)}, u32[]{:S(2)}, u32[]{:S(2)}) %collective-permute-start.15) | collective-permute-done | bytes 524320 | tf_op jit(solution)/shard_map/ppermute | solution.py:304
  99.5 5.5 %collective-permute-done.16 = bf16[128,2048]{1,0:T(8,128)(2,1)S(1)} collective-permute-done((bf16[128,2048]{1,0:T(8,128)(2,1)S(1)}, bf16[128,2048]{1,0:T(8,128)(2,1)S(1)}, u32[]{:S(2)}, u32[]{:S(2)}) %collective-permute-start.16) | collective-permute-done | bytes 524320 | tf_op jit(solution)/shard_map/ppermute | solution.py:304
  105.1 1.1 %add_convert_fusion = bf16[128,2048]{1,0:T(8,128)(2,1)} fusion(bf16[128,2048]{1,0:T(8,128)(2,1)S(1)} %collective-permute-done.16, bf16[128,2048]{1,0:T(8,128)(2,1)S(1)} %collective-permute-done.15, f32[128,2048]{1,0:T(8,128)S(1)} %get-tuple-element.35, bf16[128,2048]{1,0:T(8,128)(2,1)S(1)} %collective-permute-done.14), kind=kLoop, calls=%fused_computation | loop fusion | flops 1835008 | bytes 3145728 | tf_op jit(solution)/shard_map/convert_element_type | solution.py:328
  (1 shorter events, 0.0 us)
Async XLA Ops:
  1.1 17.6 %collective-permute-start.2 = (bf16[144,2048]{1,0:T(8,128)(2,1)S(1)}, bf16[144,2048]{1,0:T(8,128)(2,1)S(1)}, u32[]{:S(2)}, u32[]{:S(2)}) collective-permute-start(bf16[144,2048]{1,0:T(8,128)(2,1)S(1)} %get-tuple-element.23.refs_3_), channel_id=1, source_target_pairs={{0,16},{1,5},{2,18},{3,7},{4,20},{5,1},{6,22},{7,3},{8,24},{9,13},... | collective-permute-start | bytes 1769480 | tf_op jit(solution)/shard_map/ppermute | solution.py:304
  4.2 14.0 %collective-permute-start.3 = (bf16[128,2048]{1,0:T(8,128)(2,1)}, bf16[128,2048]{1,0:T(8,128)(2,1)S(1)}, u32[]{:S(2)}, u32[]{:S(2)}) collective-permute-start(bf16[128,2048]{1,0:T(8,128)(2,1)} %tok_hbm.1), channel_id=1, source_target_pairs={{0,8},{1,3},{2,10},{3,5},{4,12},{5,7},{6,14},{7,1},{8,16},{9,11},{... | collective-permute-start | bytes 1572872 | tf_op jit(solution)/shard_map/ppermute | solution.py:304
  4.8 13.9 %collective-permute-start.4 = (bf16[128,2048]{1,0:T(8,128)(2,1)}, bf16[128,2048]{1,0:T(8,128)(2,1)S(1)}, u32[]{:S(2)}, u32[]{:S(2)}) collective-permute-start(bf16[128,2048]{1,0:T(8,128)(2,1)} %tok_hbm.1), channel_id=1, source_target_pairs={{0,24},{1,7},{2,26},{3,1},{4,28},{5,3},{6,30},{7,5},{8,0},{9,15},{... | collective-permute-start | bytes 1572872 | tf_op jit(solution)/shard_map/ppermute | solution.py:304
  7.5 11.0 %collective-permute-start.1 = (bf16[16,512]{1,0:T(8,128)(2,1)S(1)}, bf16[16,512]{1,0:T(8,128)(2,1)S(1)}, u32[]{:S(2)}, u32[]{:S(2)}) collective-permute-start(bf16[16,512]{1,0:T(8,128)(2,1)S(1)} %get-tuple-element.22.refs_0_), channel_id=1, source_target_pairs={{0,24},{1,7},{2,26},{3,1},{4,28},{5,3},{6,30},{7,5},{8,0},{9,15},{... | collective-permute-start | bytes 49160 | tf_op jit(solution)/shard_map/ppermute | solution.py:304
  7.5 11.2 %collective-permute-start = (bf16[16,512]{1,0:T(8,128)(2,1)S(1)}, bf16[16,512]{1,0:T(8,128)(2,1)S(1)}, u32[]{:S(2)}, u32[]{:S(2)}) collective-permute-start(bf16[16,512]{1,0:T(8,128)(2,1)S(1)} %get-tuple-element.22.refs_0_), channel_id=1, source_target_pairs={{0,8},{1,3},{2,10},{3,5},{4,12},{5,7},{6,14},{7,1},{8,16},{9,11},{... | collective-permute-start | bytes 49160 | tf_op jit(solution)/shard_map/ppermute | solution.py:304
  9.6 10.6 %copy-start = (bf16[1,768,2048]{2,1,0:T(8,128)(2,1)S(1)}, bf16[1,768,2048]{2,1,0:T(8,128)(2,1)}, u32[]{:S(2)}) copy-start(bf16[1,768,2048]{2,1,0:T(8,128)(2,1)} %refs_2_.1) | copy-start | bytes 9437188
  18.2 9.4 %collective-permute-start.5 = (bf16[1,2048,768]{2,1,0:T(8,128)(2,1)}, bf16[1,2048,768]{2,1,0:T(8,128)(2,1)S(1)}, u32[]{:S(2)}, u32[]{:S(2)}) collective-permute-start(bf16[1,2048,768]{2,1,0:T(8,128)(2,1)} %refs_0_.1), channel_id=1, source_target_pairs={{0,1},{1,0},{2,3},{3,2},{4,5},{5,4},{6,7},{7,6},{8,9},{9,8},{10,11... | collective-permute-start | bytes 9437192 | tf_op jit(solution)/shard_map/ppermute | solution.py:304
  18.5 14.6 %collective-permute-start.6 = (bf16[1,2048,768]{2,1,0:T(8,128)(2,1)}, bf16[1,2048,768]{2,1,0:T(8,128)(2,1)S(1)}, u32[]{:S(2)}, u32[]{:S(2)}) collective-permute-start(bf16[1,2048,768]{2,1,0:T(8,128)(2,1)} %refs_1_.1), channel_id=1, source_target_pairs={{0,1},{1,0},{2,3},{3,2},{4,5},{5,4},{6,7},{7,6},{8,9},{9,8},{10,11... | collective-permute-start | bytes 9437192 | tf_op jit(solution)/shard_map/ppermute | solution.py:304
  20.2 12.8 %collective-permute-start.7 = (bf16[1,768,2048]{2,1,0:T(8,128)(2,1)S(1)}, bf16[1,768,2048]{2,1,0:T(8,128)(2,1)S(1)}, u32[]{:S(2)}, u32[]{:S(2)}) collective-permute-start(bf16[1,768,2048]{2,1,0:T(8,128)(2,1)S(1)} %copy-done), channel_id=1, source_target_pairs={{0,1},{1,0},{2,3},{3,2},{4,5},{5,4},{6,7},{7,6},{8,9},{9,8},{10,11... | collective-permute-start | bytes 9437192 | tf_op jit(solution)/shard_map/ppermute | solution.py:304
  20.6 20.1 %collective-permute-start.8 = (bf16[320,2048]{1,0:T(8,128)(2,1)S(1)}, bf16[320,2048]{1,0:T(8,128)(2,1)S(1)}, u32[]{:S(2)}, u32[]{:S(2)}) collective-permute-start(bf16[320,2048]{1,0:T(8,128)(2,1)S(1)} %get-tuple-element.31), channel_id=1, source_target_pairs={{0,2},{1,9},{2,4},{3,11},{4,6},{5,13},{6,0},{7,15},{8,10},{9,17},{... | collective-permute-start | bytes 3932168 | tf_op jit(solution)/shard_map/ppermute | solution.py:304
  22.2 18.5 %collective-permute-start.9 = (bf16[320,2048]{1,0:T(8,128)(2,1)S(1)}, bf16[320,2048]{1,0:T(8,128)(2,1)S(1)}, u32[]{:S(2)}, u32[]{:S(2)}) collective-permute-start(bf16[320,2048]{1,0:T(8,128)(2,1)S(1)} %get-tuple-element.32), channel_id=1, source_target_pairs={{0,6},{1,25},{2,0},{3,27},{4,2},{5,29},{6,4},{7,31},{8,14},{9,1},{... | collective-permute-start | bytes 3932168 | tf_op jit(solution)/shard_map/ppermute | solution.py:304
  37.2 19.5 %collective-permute-start.11 = (bf16[320,2048]{1,0:T(8,128)(2,1)S(1)}, bf16[320,2048]{1,0:T(8,128)(2,1)S(1)}, u32[]{:S(2)}, u32[]{:S(2)}) collective-permute-start(bf16[320,2048]{1,0:T(8,128)(2,1)S(1)} %pack.3), channel_id=1, source_target_pairs={{0,4},{1,17},{2,6},{3,19},{4,0},{5,21},{6,2},{7,23},{8,12},{9,25},... | collective-permute-start | bytes 3932168 | tf_op jit(solution)/shard_map/ppermute | solution.py:304
  47.0 24.0 %collective-permute-start.10 = (bf16[320,2048]{1,0:T(8,128)(2,1)S(1)}, bf16[320,2048]{1,0:T(8,128)(2,1)S(1)}, u32[]{:S(2)}, u32[]{:S(2)}) collective-permute-start(bf16[320,2048]{1,0:T(8,128)(2,1)S(1)} %get-tuple-element.33), channel_id=1, source_target_pairs={{2,0},{9,1},{4,2},{11,3},{6,4},{13,5},{0,6},{15,7},{10,8},{17,9},{... | collective-permute-start | bytes 3932168 | tf_op jit(solution)/shard_map/ppermute | solution.py:304
  49.1 21.9 %collective-permute-start.13 = (bf16[320,2048]{1,0:T(8,128)(2,1)S(1)}, bf16[320,2048]{1,0:T(8,128)(2,1)S(1)}, u32[]{:S(2)}, u32[]{:S(2)}) collective-permute-start(bf16[320,2048]{1,0:T(8,128)(2,1)S(1)} %get-tuple-element.34), channel_id=1, source_target_pairs={{6,0},{25,1},{0,2},{27,3},{2,4},{29,5},{4,6},{31,7},{14,8},{1,9},{... | collective-permute-start | bytes 3932168 | tf_op jit(solution)/shard_map/ppermute | solution.py:304
  60.0 24.7 %collective-permute-start.12 = (bf16[320,2048]{1,0:T(8,128)(2,1)S(1)}, bf16[320,2048]{1,0:T(8,128)(2,1)S(1)}, u32[]{:S(2)}, u32[]{:S(2)}) collective-permute-start(bf16[320,2048]{1,0:T(8,128)(2,1)S(1)} %expert.5), channel_id=1, source_target_pairs={{4,0},{17,1},{6,2},{19,3},{0,4},{21,5},{2,6},{23,7},{12,8},{25,9},... | collective-permute-start | bytes 3932168 | tf_op jit(solution)/shard_map/ppermute | solution.py:304
  87.4 9.3 %collective-permute-start.14 = (bf16[128,2048]{1,0:T(8,128)(2,1)S(1)}, bf16[128,2048]{1,0:T(8,128)(2,1)S(1)}, u32[]{:S(2)}, u32[]{:S(2)}) collective-permute-start(bf16[128,2048]{1,0:T(8,128)(2,1)S(1)} %get-tuple-element.36), channel_id=1, source_target_pairs={{8,0},{3,1},{10,2},{5,3},{12,4},{7,5},{14,6},{1,7},{16,8},{11,9},{... | collective-permute-start | bytes 1572872 | tf_op jit(solution)/shard_map/ppermute | solution.py:304
  88.8 10.8 %collective-permute-start.15 = (bf16[128,2048]{1,0:T(8,128)(2,1)S(1)}, bf16[128,2048]{1,0:T(8,128)(2,1)S(1)}, u32[]{:S(2)}, u32[]{:S(2)}) collective-permute-start(bf16[128,2048]{1,0:T(8,128)(2,1)S(1)} %get-tuple-element.37), channel_id=1, source_target_pairs={{16,0},{5,1},{18,2},{7,3},{20,4},{1,5},{22,6},{3,7},{24,8},{13,9},... | collective-permute-start | bytes 1572872 | tf_op jit(solution)/shard_map/ppermute | solution.py:304
  91.1 14.0 %collective-permute-start.16 = (bf16[128,2048]{1,0:T(8,128)(2,1)S(1)}, bf16[128,2048]{1,0:T(8,128)(2,1)S(1)}, u32[]{:S(2)}, u32[]{:S(2)}) collective-permute-start(bf16[128,2048]{1,0:T(8,128)(2,1)S(1)} %get-tuple-element.38), channel_id=1, source_target_pairs={{24,0},{7,1},{26,2},{1,3},{28,4},{3,5},{30,6},{5,7},{0,8},{15,9},{... | collective-permute-start | bytes 1572872 | tf_op jit(solution)/shard_map/ppermute | solution.py:304

commit v5 on v4

v5 whole, which is shorter than its diff:
```python
import functools

import jax
import jax.numpy as jnp
from jax import lax
from jax.experimental import pallas as pl
from jax.experimental.pallas import tpu as pltpu
from jax.sharding import PartitionSpec as P

NX, NY, NC = 4, 4, 2
EXPERTS = NX * NY * NC
CAP = 40
EXTRA = 128
KF = 8


def index_of(x, y, c):
    return ((x % NX) * NY + (y % NY)) * NC + c


def spread_pairs(j):
    pairs = []
    for x in range(NX):
        for y in range(NY):
            pairs.append((index_of(x, y, 0), index_of(x + j, y, 0)))
            pairs.append((index_of(x, y, 1), index_of(x, y + j, 1)))
    return pairs


def deliver_pairs(k):
    pairs = []
    for x in range(NX):
        for y in range(NY):
            pairs.append((index_of(x, y, 0), index_of(x, y + k, 0)))
            pairs.append((index_of(x, y, 1), index_of(x + k, y, 1)))
    return pairs


def swap_pairs():
    return [(i, i ^ 1) for i in range(EXPERTS)]


def back(pairs):
    return [(b, a) for a, b in pairs]


def prep_kernel(ids_hbm, gw_hbm, tok_hbm, out_ref, ids_ref, gw_ref, sems):
    top, tok = ids_ref.shape
    width = tok_hbm.shape[1]
    copies = [
        pltpu.make_async_copy(ids_hbm, ids_ref, sems.at[0]),
        pltpu.make_async_copy(gw_hbm, gw_ref, sems.at[1]),
        pltpu.make_async_copy(tok_hbm, out_ref.at[:, pl.ds(0, width)], sems.at[2]),
    ]
    for copy in copies:
        copy.start()
    row = lax.broadcasted_iota(jnp.int32, (tok, tok), 0)
    col = lax.broadcasted_iota(jnp.int32, (tok, tok), 1)
    earlier = jnp.where(row < col, 1.0, 0.0).astype(jnp.bfloat16)
    name = lax.broadcasted_iota(jnp.int32, (EXPERTS, tok), 0)
    chosen = jnp.zeros((EXPERTS, tok), jnp.float32)
    weight = jnp.zeros((EXPERTS, tok), jnp.float32)
    copies[0].wait()
    copies[1].wait()
    ids = ids_ref[...]
    gw = gw_ref[...]
    for k in range(top):
        hit = ids[k : k + 1, :] == name
        chosen = jnp.where(hit, 1.0, chosen)
        weight = jnp.where(hit, gw[k : k + 1, :], weight)
    count = jnp.dot(chosen.astype(jnp.bfloat16), earlier, preferred_element_type=jnp.float32)
    slot = jnp.where(chosen > 0.5, count, -1.0)
    blank = jnp.zeros((EXTRA - 2 * EXPERTS, tok), jnp.float32)
    table = jnp.concatenate([slot, weight, blank], axis=0)
    out_ref[:, width:] = table.T.astype(jnp.bfloat16)
    copies[2].wait()


def prep(ids, gw, tokens):
    tok, width = tokens.shape
    hbm = pl.BlockSpec(memory_space=pl.ANY)
    return pl.pallas_call(
        prep_kernel,
        in_specs=[hbm, hbm, hbm],
        out_specs=pl.BlockSpec(memory_space=pltpu.VMEM),
        out_shape=pltpu.VMEM((tok, width + EXTRA), jnp.bfloat16),
        scratch_shapes=[
            pltpu.VMEM(ids.shape, ids.dtype),
            pltpu.VMEM(gw.shape, gw.dtype),
            pltpu.SemaphoreType.DMA((3,)),
        ],
        compiler_params=pltpu.CompilerParams(vmem_limit_bytes=4 * 1024 * 1024),
        cost_estimate=pl.CostEstimate(flops=2 * EXPERTS * tok**2, bytes_accessed=4 * tok * width, transcendentals=0),
        name="prep",
    )(*[pltpu.with_memory_space_constraint(v, pltpu.HBM) for v in (ids, gw, tokens)])


def select(q, blocks):
    width = blocks[0].shape[1] - EXTRA
    return jnp.concatenate(
        [
            lax.dot_general(q, b[:, width:], (((1,), (1,)), ((), ())), preferred_element_type=jnp.float32)
            for b in blocks
        ],
        axis=1,
    )


def pack_kernel(which, q_ref, *refs):
    blocks, outs = refs[:4], refs[4:]
    tok = blocks[0].shape[0]
    width = outs[0].shape[1]
    q = q_ref[0]
    half = 2 * CAP
    r = lax.broadcasted_iota(jnp.int32, (half, 2 * tok), 0)
    t = lax.broadcasted_iota(jnp.int32, (half, 2 * tok), 1)
    second = r >= CAP
    target = jnp.where(second, r - CAP, r)
    target = jnp.where(second == (t >= tok), target, -5).astype(jnp.float32)
    cols = 512
    for p in range(2):
        pair = blocks[2 * p : 2 * p + 2]
        slots = select(q, pair)
        pick = jnp.concatenate(
            [
                jnp.where(slots[NC * k + f : NC * k + f + 1, :] == target, 1.0, 0.0).astype(jnp.bfloat16)
                for k in which
                for f in range(NC)
            ],
            axis=0,
        )
        for at in range(0, width, cols):
            block = jnp.concatenate([b[:, at : at + cols] for b in pair], axis=0)
            got = jnp.dot(pick, block, preferred_element_type=jnp.float32).astype(jnp.bfloat16)
            for n, o in enumerate(outs):
                o[2 * half * p : 2 * half * (p + 1), at : at + cols] = got[2 * half * n : 2 * half * (n + 1), :]


def pack(which, q, blocks):
    tok = blocks[0].shape[0]
    width = blocks[0].shape[1] - EXTRA
    count = len(which)
    rows = NC * 4 * CAP
    vmem = pl.BlockSpec(memory_space=pltpu.VMEM)
    return pl.pallas_call(
        functools.partial(pack_kernel, which),
        in_specs=[vmem] * 5,
        out_specs=[vmem] * count,
        out_shape=[jax.ShapeDtypeStruct((rows, width), jnp.bfloat16)] * count,
        compiler_params=pltpu.CompilerParams(vmem_limit_bytes=16 * 1024 * 1024),
        cost_estimate=pl.CostEstimate(
            flops=2 * rows * count * 2 * tok * width,
            bytes_accessed=2 * (4 * tok + rows * count) * width,
            transcendentals=0,
        ),
        name="pack",
    )(q, *blocks)


def combine_kernel(spots, q_ref, *refs):
    pair, backs, outs = refs[:2], refs[2:6], refs[6:]
    tok, width = outs[0].shape
    half = 2 * CAP
    span = half * KF
    lane = lax.broadcasted_iota(jnp.int32, (2 * tok, span), 1)
    part = jnp.zeros((2 * tok, span), jnp.int32)
    er = lax.broadcasted_iota(jnp.int32, (16, span), 0)
    el = lax.broadcasted_iota(jnp.int32, (16, span), 1)
    ep = jnp.zeros((16, span), jnp.int32)
    for n in range(1, KF):
        part = jnp.where(lane >= half * n, half * n, part)
        ep = jnp.where(el >= half * n, n, ep)
    r = lane - part
    t = lax.broadcasted_iota(jnp.int32, (2 * tok, span), 0)
    second = r >= CAP
    target = jnp.where(second, r - CAP, r)
    target = jnp.where(second == (t >= tok), target, -5).astype(jnp.float32)
    expand = jnp.where(er == ep, 1.0, 0.0).astype(jnp.bfloat16)

    def widen(v):
        return lax.dot_general(
            v.astype(jnp.bfloat16), expand, (((0,), (0,)), ((), ())), preferred_element_type=jnp.float32
        )

    mix = jnp.where(widen(select(q_ref[0], pair)) == target, widen(select(q_ref[1], pair)), 0.0)
    mix = mix.astype(jnp.bfloat16)
    cols = 512
    for at in range(0, width, cols):
        rows = jnp.concatenate(
            [b[2 * half * p : 2 * half * (p + 1), at : at + cols] for b, p in zip(backs, spots)], axis=0
        )
        got = jnp.dot(mix, rows, preferred_element_type=jnp.float32)
        for n, o in enumerate(outs):
            o[:, at : at + cols] = got[n * tok : (n + 1) * tok].astype(o.dtype)


def combine(q, pair, backs, spots, dtypes):
    tok = pair[0].shape[0]
    width = backs[0].shape[1]
    rows = NC * 4 * CAP
    vmem = pl.BlockSpec(memory_space=pltpu.VMEM)
    return pl.pallas_call(
        functools.partial(combine_kernel, spots),
        in_specs=[vmem] * 7,
        out_specs=[vmem] * 2,
        out_shape=[jax.ShapeDtypeStruct((tok, width), d) for d in dtypes],
        compiler_params=pltpu.CompilerParams(vmem_limit_bytes=16 * 1024 * 1024),
        cost_estimate=pl.CostEstimate(
            flops=2 * 2 * rows * 2 * tok * width,
            bytes_accessed=2 * (3 * tok + 2 * rows) * width,
            transcendentals=0,
        ),
        name="combine",
    )(q, *pair, *backs)


def expert_kernel(count, *refs):
    slabs, weights, outs = refs[:count], refs[count : count + 6], refs[count + 6 :]
    width = slabs[0].shape[1]
    half = 2 * CAP
    for f in range(NC):
        wg, wu, wd = weights[3 * f : 3 * f + 3]
        ff = wg.shape[-1]
        spots = [half * (2 * p + f) for p in range(2)]
        lines = jnp.concatenate([s[at : at + half, :] for s in slabs for at in spots], axis=0)
        hidden = []
        for at in range(0, ff, 256):
            gate = jnp.dot(lines, wg[0, :, at : at + 256], preferred_element_type=jnp.float32)
            up = jnp.dot(lines, wu[0, :, at : at + 256], preferred_element_type=jnp.float32)
            hidden.append((gate / (1.0 + jnp.exp(-gate)) * up).astype(jnp.bfloat16))
        hidden = jnp.concatenate(hidden, axis=1)
        for at in range(0, width, 512):
            got = jnp.dot(hidden, wd[0, :, at : at + 512], preferred_element_type=jnp.float32)
            got = got.astype(jnp.bfloat16)
            if len(outs) == count:
                places = [(o, spot) for o in outs for spot in spots]
            else:
                places = [(o, half * f) for o in outs]
            for n, (o, spot) in enumerate(places):
                o[spot : spot + half, at : at + 512] = got[n * half : (n + 1) * half]


def expert(slabs, weights, split=False):
    count = len(slabs)
    rows, width = slabs[0].shape
    ff = weights[0].shape[-1]
    outs = 2 * count if split else count
    vmem = pl.BlockSpec(memory_space=pltpu.VMEM)
    return pl.pallas_call(
        functools.partial(expert_kernel, count),
        in_specs=[vmem] * (count + 6),
        out_specs=[vmem] * outs,
        out_shape=[jax.ShapeDtypeStruct((rows * count // outs, width), jnp.bfloat16)] * outs,
        compiler_params=pltpu.CompilerParams(vmem_limit_bytes=16 * 1024 * 1024),
        cost_estimate=pl.CostEstimate(
            flops=6 * count * rows * width * ff,
            bytes_accessed=4 * count * rows * width,
            transcendentals=count * rows * ff,
        ),
        name="expert",
    )(*slabs, *[pltpu.with_memory_space_constraint(w, pltpu.VMEM) for w in weights])


def hold_kernel(*refs):
    ins, outs, sems = refs[:3], refs[3:6], refs[6]
    copies = [pltpu.make_async_copy(a, b, sems.at[n]) for n, (a, b) in enumerate(zip(ins, outs))]
    for copy in copies:
        copy.start()
    for copy in copies:
        copy.wait()


def hold(*weights):
    return pl.pallas_call(
        hold_kernel,
        in_specs=[pl.BlockSpec(memory_space=pl.ANY)] * 3,
        out_specs=[pl.BlockSpec(memory_space=pltpu.VMEM)] * 3,
        out_shape=[pltpu.VMEM(w.shape, w.dtype) for w in weights],
        scratch_shapes=[pltpu.SemaphoreType.DMA((3,))],
        compiler_params=pltpu.CompilerParams(vmem_limit_bytes=4 * 1024 * 1024),
        cost_estimate=pl.CostEstimate(flops=0, bytes_accessed=4 * weights[0].size * 3, transcendentals=0),
        name="hold",
    )(*[pltpu.with_memory_space_constraint(w, pltpu.HBM) for w in weights])


def per_device(tokens, expert_ids, gate_weights, w_gate, w_up, w_down):
    me = lax.axis_index("expert")
    x, y, c = me // (NY * NC), (me // NC) % NY, me % NC
    n = jnp.arange(16, dtype=jnp.int32)
    k, f = n // NC, n % NC
    along_y = x * (NY * NC) + ((y + k) % NY) * NC + (c ^ f)
    along_x = ((x + k) % NX) * (NY * NC) + y * NC + (c ^ f)
    mine = jnp.where(n < KF, jnp.where(c == 0, along_y, along_x), -1)
    spot = jnp.arange(EXTRA, dtype=jnp.int32)[None, :]
    q = jnp.stack([mine[:, None] == spot, (mine[:, None] + EXPERTS == spot) & (n < KF)[:, None]])
    q = q.astype(jnp.bfloat16)

    send = lambda v, pairs: lax.ppermute(v, "expert", pairs)
    after = lambda v, other: lax.optimization_barrier((v, other))[0]
    home = prep(expert_ids.T, gate_weights.T, tokens)
    blocks = [home] + [send(home, spread_pairs(j)) for j in (1, 2, 3)]
    weights = list(hold(w_gate, w_up, w_down)) + [send(after(w, home), swap_pairs()) for w in (w_gate, w_up)]

    near = pack((1, 3), q, blocks)
    weights.append(send(after(w_down, near[0]), swap_pairs()))
    arrived = {k: send(slab, deliver_pairs(k)) for k, slab in zip((1, 3), near)}
    stay, far = pack((0, 2), q, blocks)
    backs = {}
    (backs[0],) = expert([stay], weights)
    arrived[2] = send(after(far, backs[0]), deliver_pairs(2))
    for k, slab in zip((1, 3), expert([arrived[1], arrived[3]], weights)):
        backs[k] = send(slab, back(deliver_pairs(k)))
    early, late = expert([arrived[2]], weights, split=True)[::-1]
    early = send(early, back(deliver_pairs(2)))
    late = send(after(late, (backs[1], backs[3])), back(deliver_pairs(2)))

    whole = [backs[k] for k in (0, 1)]
    part2, part3 = combine(
        q, blocks[2:], [*whole, early, backs[3]], (1, 1, 0, 1), (jnp.bfloat16, jnp.bfloat16)
    )
    part0, part1 = combine(q, blocks[:2], [*whole, late, backs[3]], (0, 0, 0, 0), (jnp.float32, jnp.bfloat16))
    mixed = part0
    for j, part in ((2, part2), (3, part3), (1, part1)):
        mixed = mixed + send(part, back(spread_pairs(j))).astype(jnp.float32)
    return mixed.astype(jnp.bfloat16)


def solution(mesh):
    return jax.shard_map(
        per_device,
        mesh=mesh,
        in_specs=(
            P(("dp", "expert"), None),
            P(("dp", "expert"), None),
            P(("dp", "expert"), None),
            P("expert", None, None),
            P("expert", None, None),
            P("expert", None, None),
        ),
        out_specs=P(("dp", "expert"), None),
        check_vma=False,
    )
```

time: 107 us -> 128 us (1.20)
  waiting for transfers between devices: 57.2 us -> 76 us
  Pallas kernels: 22.8 us -> 35 us
  starting transfers between devices: 24.9 us -> 15 us
    ppermute x17 -> x16, waiting for transfers between devices: 57.2 us -> 76 us  [per_device(): send = lambda v, pairs: lax.ppermute(v, 'expert', pairs)]
    ppermute x17 -> x16, starting transfers between devices: 24.9 us -> 15 us  [per_device(): send = lambda v, pairs: lax.ppermute(v, 'expert', pairs)]
    pallas_call x4 -> x5, Pallas kernels: 6.04 us -> 12.7 us  [the longest x2 5.49 us: combine(): pl.pallas_call(functools.partial(combine_kernel, spots), in_specs=[vmem]...]
    pallas_call x3, Pallas kernels: 13 us -> 18.5 us  [expert(): pl.pallas_call(functools.partial(expert_kernel, count), in_specs=[vmem] *...]
  transfers between devices with their start and end apart: 17 -> 16, of which waited for: 9 -> 8; matrix products, arithmetic and copies ran while one was open for 0% -> 0% of each run, Pallas kernels for 18% -> 26%
where the time goes in v5:
time: 128 us; the launch traced here: 127 us
  waiting for transfers between devices  76 us (59%)
  Pallas kernels  35 us (27%)
  starting transfers between devices  15 us (12%)
    ppermute x16, waiting for transfers between devices, per_device(): send = lambda v, pairs: lax.ppermute(v, 'expert', pairs)  76 us
    pallas_call x3, Pallas kernels, expert(): pl.pallas_call(functools.partial(expert_kernel, count), in_specs=[vmem] *...  18.5 us
    ppermute x16, starting transfers between devices, per_device(): send = lambda v, pairs: lax.ppermute(v, 'expert', pairs)  15 us
    pallas_call x2, Pallas kernels, combine(): pl.pallas_call(functools.partial(combine_kernel, spots), in_specs=[vmem]...  5.49 us
    pallas_call x2, Pallas kernels, pack(): pl.pallas_call(functools.partial(pack_kernel, which), in_specs=[vmem] * 5...  5.31 us
    pallas_call x1, Pallas kernels, hold(): pl.pallas_call(hold_kernel, in_specs=[pl.BlockSpec(memory_space=pl.ANY)]...  3.78 us
  transfers between devices with their start and end apart: 16, of which 8 were waited for; matrix products, arithmetic and copies ran while one was open for 0% of the time, Pallas kernels for 26%

profile of v5, /device:TPU:96, one launch (start us, length us, event | category | flops | bytes accessed | tf_op | source)
XLA Modules:
  0.0 127.3 jit_solution(8035615050490810119)
XLA Ops:
  0.0 1.9 %prep.1.refs_0_ = bf16[128,2176]{1,0:T(8,128)(2,1)} custom-call(s32[8,128]{1,0:T(8,128)} %bitcast.2, f32[8,128]{1,0:T(8,128)} %bitcast.3, bf16[128,2048]{1,0:T(8,128)(2,1)} %tok_hbm.1), custom_call_target="tpu_custom_call" | custom-call | flops 1048576 | bytes 1048576 | tf_op jit(solution)/shard_map/prep/pallas_call | solution.py:82
  1.9 2.8 %collective-permute-start.2 = (bf16[128,2176]{1,0:T(8,128)(2,1)}, bf16[128,2176]{1,0:T(8,128)(2,1)}, u32[]{:S(2)}, u32[]{:S(2)}) collective-permute-start(bf16[128,2176]{1,0:T(8,128)(2,1)} %prep.1.refs_0_), channel_id=1, source_target_pairs={{0,24},{1,7},{2,26},{3,1},{4,28},{5,3},{6,30},{7,5},{8,0},{9,15},{... | collective-permute-start | bytes 1671176 | tf_op jit(solution)/shard_map/ppermute | solution.py:298
  4.8 0.8 collective-permute-start.1
  5.6 0.9 collective-permute-start
  6.4 0.0 collective-permute-start.3
  6.4 0.5 collective-permute-start.4
  7.0 0.1 iota_compare_fusion.1
  7.1 11.1 %collective-permute-done.2.refs_3_.refs_1_ = bf16[128,2176]{1,0:T(8,128)(2,1)} collective-permute-done((bf16[128,2176]{1,0:T(8,128)(2,1)}, bf16[128,2176]{1,0:T(8,128)(2,1)}, u32[]{:S(2)}, u32[]{:S(2)}) %collective-permute-start.2) | collective-permute-done | bytes 557088 | tf_op jit(solution)/shard_map/ppermute | solution.py:298
  18.1 0.0 collective-permute-done.1.refs_2_.refs_0_
  18.1 3.9 %collective-permute-done.refs_1_ = bf16[128,2176]{1,0:T(8,128)(2,1)} collective-permute-done((bf16[128,2176]{1,0:T(8,128)(2,1)}, bf16[128,2176]{1,0:T(8,128)(2,1)}, u32[]{:S(2)}, u32[]{:S(2)}) %collective-permute-start) | collective-permute-done | bytes 557088 | tf_op jit(solution)/shard_map/ppermute | solution.py:298
  22.1 2.7 %pack.3 = (bf16[320,2048]{1,0:T(8,128)(2,1)S(1)}, bf16[320,2048]{1,0:T(8,128)(2,1)S(1)}) custom-call(bf16[2,16,128]{2,1,0:T(8,128)(2,1)S(1)} %add_convert_fusion.1.q_ref, bf16[128,2176]{1,0:T(8,128)(2,1)} %prep.1.refs_0_, bf16[128,2176]{1,0:T(8,128)(2,1)} %collective-permute-done.refs_1_, bf16[128,2176]{1,0:T(8,128)(2,1)} %collective-permute-done.1.refs_2_.refs_0_, ...), custom_call_target="tpu_custom_call" | custom-call | flops 671088640 | bytes 4718592 | tf_op jit(solution)/shard_map/pack/pallas_call | solution.py:145
  24.7 0.1 collective-permute-start.5
  24.8 3.1 %collective-permute-start.7 = (bf16[320,2048]{1,0:T(8,128)(2,1)S(1)}, bf16[320,2048]{1,0:T(8,128)(2,1)S(1)}, u32[]{:S(2)}, u32[]{:S(2)}) collective-permute-start(bf16[320,2048]{1,0:T(8,128)(2,1)S(1)} %get-tuple-element.33), channel_id=1, source_target_pairs={{0,6},{1,25},{2,0},{3,27},{4,2},{5,29},{6,4},{7,31},{8,14},{9,1},{... | collective-permute-start | bytes 3932168 | tf_op jit(solution)/shard_map/ppermute | solution.py:298
  27.9 0.0 collective-permute-start.6
  27.9 3.8 %hold.1 = (bf16[1,2048,768]{2,1,0:T(8,128)(2,1)S(1)}, bf16[1,2048,768]{2,1,0:T(8,128)(2,1)S(1)}, bf16[1,768,2048]{2,1,0:T(8,128)(2,1)S(1)}) custom-call(bf16[1,2048,768]{2,1,0:T(8,128)(2,1)} %refs_0_.1, bf16[1,2048,768]{2,1,0:T(8,128)(2,1)} %refs_1_.1, bf16[1,768,2048]{2,1,0:T(8,128)(2,1)} %refs_2_.1), custom_call_target="tpu_custom_call" | custom-call | bytes 18874368 | tf_op jit(solution)/shard_map/hold/pallas_call | solution.py:274
  31.7 2.7 %pack.2 = (bf16[320,2048]{1,0:T(8,128)(2,1)S(1)}, bf16[320,2048]{1,0:T(8,128)(2,1)S(1)}) custom-call(bf16[2,16,128]{2,1,0:T(8,128)(2,1)S(1)} %add_convert_fusion.1.q_ref, bf16[128,2176]{1,0:T(8,128)(2,1)} %prep.1.refs_0_, bf16[128,2176]{1,0:T(8,128)(2,1)} %collective-permute-done.refs_1_, bf16[128,2176]{1,0:T(8,128)(2,1)} %collective-permute-done.1.refs_2_.refs_0_, ...), custom_call_target="tpu_custom_call" | custom-call | flops 671088640 | bytes 4718592 | tf_op jit(solution)/shard_map/pack/pallas_call | solution.py:145
  34.4 0.0 collective-permute-done.3.refs_4_.refs_5_
  34.4 0.0 collective-permute-done.4.refs_5_.refs_6_
  34.4 0.0 collective-permute-done.5.refs_6_.refs_7_
  34.4 5.2 %expert.3.refs_2_ = bf16[320,2048]{1,0:T(8,128)(2,1)S(1)} custom-call(bf16[320,2048]{1,0:T(8,128)(2,1)S(1)} %get-tuple-element.25.refs_0_, bf16[1,2048,768]{2,1,0:T(8,128)(2,1)S(1)} %get-tuple-element.26.refs_1_.refs_2_, bf16[1,2048,768]{2,1,0:T(8,128)(2,1)S(1)} %get-tuple-element.27.refs_2_.refs_3_, ...), custom_call_target="tpu_custom_call" | custom-call | flops 3019898880 | bytes 2621440 | tf_op jit(solution)/shard_map/expert/pallas_call | solution.py:249
  39.6 2.5 %collective-permute-start.9 = (bf16[320,2048]{1,0:T(8,128)(2,1)S(1)}, bf16[320,2048]{1,0:T(8,128)(2,1)S(1)}, u32[]{:S(2)}, u32[]{:S(2)}) collective-permute-start(bf16[320,2048]{1,0:T(8,128)(2,1)S(1)} %get-tuple-element.36), channel_id=1, source_target_pairs={{0,4},{1,17},{2,6},{3,19},{4,0},{5,21},{6,2},{7,23},{8,12},{9,25},... | collective-permute-start | bytes 3932168 | tf_op jit(solution)/shard_map/ppermute | solution.py:298
  42.1 1.0 collective-permute-done.7.refs_1_
  43.1 17.7 %collective-permute-done.6.refs_0_ = bf16[320,2048]{1,0:T(8,128)(2,1)S(1)} collective-permute-done((bf16[320,2048]{1,0:T(8,128)(2,1)S(1)}, bf16[320,2048]{1,0:T(8,128)(2,1)S(1)}, u32[]{:S(2)}, u32[]{:S(2)}) %collective-permute-start.6) | collective-permute-done | bytes 1310752 | tf_op jit(solution)/shard_map/ppermute | solution.py:298
  60.8 8.2 %expert.4 = (bf16[320,2048]{1,0:T(8,128)(2,1)S(1)}, bf16[320,2048]{1,0:T(8,128)(2,1)S(1)}) custom-call(bf16[320,2048]{1,0:T(8,128)(2,1)S(1)} %collective-permute-done.6.refs_0_, bf16[320,2048]{1,0:T(8,128)(2,1)S(1)} %collective-permute-done.7.refs_1_, bf16[1,2048,768]{2,1,0:T(8,128)(2,1)S(1)} %get-tuple-element.26.refs_1_.refs_2_, ...), custom_call_target="tpu_custom_call" | custom-call | flops 6039797760 | bytes 5242880 | tf_op jit(solution)/shard_map/expert/pallas_call | solution.py:249
  69.0 0.1 collective-permute-start.8
  69.1 2.0 %collective-permute-start.10 = (bf16[320,2048]{1,0:T(8,128)(2,1)S(1)}, bf16[320,2048]{1,0:T(8,128)(2,1)S(1)}, u32[]{:S(2)}, u32[]{:S(2)}) collective-permute-start(bf16[320,2048]{1,0:T(8,128)(2,1)S(1)} %get-tuple-element.38), channel_id=1, source_target_pairs={{6,0},{25,1},{0,2},{27,3},{2,4},{29,5},{4,6},{31,7},{14,8},{1,9},{... | collective-permute-start | bytes 3932168 | tf_op jit(solution)/shard_map/ppermute | solution.py:298
  71.1 0.0 collective-permute-done.9.refs_0_
  71.1 5.1 %expert.5 = (bf16[160,2048]{1,0:T(8,128)(2,1)S(1)}, bf16[160,2048]{1,0:T(8,128)(2,1)S(1)}) custom-call(bf16[320,2048]{1,0:T(8,128)(2,1)S(1)} %collective-permute-done.9.refs_0_, bf16[1,2048,768]{2,1,0:T(8,128)(2,1)S(1)} %get-tuple-element.26.refs_1_.refs_2_, bf16[1,2048,768]{2,1,0:T(8,128)(2,1)S(1)} %get-tuple-element.27.refs_2_.refs_3_, ...), custom_call_target="tpu_custom_call" | custom-call | flops 3019898880 | bytes 2621440 | tf_op jit(solution)/shard_map/expert/pallas_call | solution.py:249
  76.3 0.1 collective-permute-start.12
  76.4 10.3 %collective-permute-done.8.refs_3_ = bf16[320,2048]{1,0:T(8,128)(2,1)S(1)} collective-permute-done((bf16[320,2048]{1,0:T(8,128)(2,1)S(1)}, bf16[320,2048]{1,0:T(8,128)(2,1)S(1)}, u32[]{:S(2)}, u32[]{:S(2)}) %collective-permute-start.8) | collective-permute-done | bytes 1310752 | tf_op jit(solution)/shard_map/ppermute | solution.py:298
  86.7 8.3 %collective-permute-done.10.refs_5_ = bf16[320,2048]{1,0:T(8,128)(2,1)S(1)} collective-permute-done((bf16[320,2048]{1,0:T(8,128)(2,1)S(1)}, bf16[320,2048]{1,0:T(8,128)(2,1)S(1)}, u32[]{:S(2)}, u32[]{:S(2)}) %collective-permute-start.10) | collective-permute-done | bytes 1310752 | tf_op jit(solution)/shard_map/ppermute | solution.py:298
  95.0 0.0 collective-permute-start.11
  95.0 0.0 collective-permute-done.12.refs_4_
  95.0 2.7 %combine.3 = (bf16[128,2048]{1,0:T(8,128)(2,1)S(1)}, bf16[128,2048]{1,0:T(8,128)(2,1)S(1)}) custom-call(bf16[2,16,128]{2,1,0:T(8,128)(2,1)S(1)} %add_convert_fusion.1.q_ref, bf16[128,2176]{1,0:T(8,128)(2,1)} %collective-permute-done.1.refs_2_.refs_0_, bf16[128,2176]{1,0:T(8,128)(2,1)} %collective-permute-done.2.refs_3_.refs_1_, ...), custom_call_target="tpu_custom_call" | custom-call | flops 671088640 | bytes 4194304 | tf_op jit(solution)/shard_map/combine/pallas_call | solution.py:202
  97.8 0.9 collective-permute-start.13
  98.7 0.7 collective-permute-start.14
  99.3 14.9 %collective-permute-done.11.refs_4_ = bf16[160,2048]{1,0:T(8,128)(2,1)S(1)} collective-permute-done((bf16[160,2048]{1,0:T(8,128)(2,1)S(1)}, bf16[160,2048]{1,0:T(8,128)(2,1)S(1)}, u32[]{:S(2)}, u32[]{:S(2)}) %collective-permute-start.11) | collective-permute-done | bytes 655392 | tf_op jit(solution)/shard_map/ppermute | solution.py:298
  114.2 2.7 %combine.2 = (f32[128,2048]{1,0:T(8,128)S(1)}, bf16[128,2048]{1,0:T(8,128)(2,1)S(1)}) custom-call(bf16[2,16,128]{2,1,0:T(8,128)(2,1)S(1)} %add_convert_fusion.1.q_ref, bf16[128,2176]{1,0:T(8,128)(2,1)} %prep.1.refs_0_, bf16[128,2176]{1,0:T(8,128)(2,1)} %collective-permute-done.refs_1_, bf16[320,2048]{1,0:T(8,128)(2,1)S(1)} %expert.3.refs_2_, ...), custom_call_target="tpu_custom_call" | custom-call | flops 671088640 | bytes 4194304 | tf_op jit(solution)/shard_map/combine/pallas_call | solution.py:202
  117.0 0.6 collective-permute-start.15
  117.6 0.0 collective-permute-done.13
  117.6 0.0 collective-permute-done.14
  117.6 8.7 %collective-permute-done.15 = bf16[128,2048]{1,0:T(8,128)(2,1)S(1)} collective-permute-done((bf16[128,2048]{1,0:T(8,128)(2,1)S(1)}, bf16[128,2048]{1,0:T(8,128)(2,1)S(1)}, u32[]{:S(2)}, u32[]{:S(2)}) %collective-permute-start.15) | collective-permute-done | bytes 524320 | tf_op jit(solution)/shard_map/ppermute | solution.py:298
  126.3 1.1 add_convert_fusion
  (3 shorter events, 0.0 us)
Async XLA Ops:
  1.9 16.2 %collective-permute-start.2 = (bf16[128,2176]{1,0:T(8,128)(2,1)}, bf16[128,2176]{1,0:T(8,128)(2,1)}, u32[]{:S(2)}, u32[]{:S(2)}) collective-permute-start(bf16[128,2176]{1,0:T(8,128)(2,1)} %prep.1.refs_0_), channel_id=1, source_target_pairs={{0,24},{1,7},{2,26},{3,1},{4,28},{5,3},{6,30},{7,5},{8,0},{9,15},{... | collective-permute-start | bytes 1671176 | tf_op jit(solution)/shard_map/ppermute | solution.py:298
  4.8 13.4 %collective-permute-start.1 = (bf16[128,2176]{1,0:T(8,128)(2,1)}, bf16[128,2176]{1,0:T(8,128)(2,1)}, u32[]{:S(2)}, u32[]{:S(2)}) collective-permute-start(bf16[128,2176]{1,0:T(8,128)(2,1)} %prep.1.refs_0_), channel_id=1, source_target_pairs={{0,16},{1,5},{2,18},{3,7},{4,20},{5,1},{6,22},{7,3},{8,24},{9,13},... | collective-permute-start | bytes 1671176 | tf_op jit(solution)/shard_map/ppermute | solution.py:298
  5.6 16.5 %collective-permute-start = (bf16[128,2176]{1,0:T(8,128)(2,1)}, bf16[128,2176]{1,0:T(8,128)(2,1)}, u32[]{:S(2)}, u32[]{:S(2)}) collective-permute-start(bf16[128,2176]{1,0:T(8,128)(2,1)} %prep.1.refs_0_), channel_id=1, source_target_pairs={{0,8},{1,3},{2,10},{3,5},{4,12},{5,7},{6,14},{7,1},{8,16},{9,11},{... | collective-permute-start | bytes 1671176 | tf_op jit(solution)/shard_map/ppermute | solution.py:298
  6.4 27.9 %collective-permute-start.3 = (bf16[1,2048,768]{2,1,0:T(8,128)(2,1)}, bf16[1,2048,768]{2,1,0:T(8,128)(2,1)S(1)}, u32[]{:S(2)}, u32[]{:S(2)}) collective-permute-start(bf16[1,2048,768]{2,1,0:T(8,128)(2,1)} %refs_0_.1), channel_id=1, source_target_pairs={{0,1},{1,0},{2,3},{3,2},{4,5},{5,4},{6,7},{7,6},{8,9},{9,8},{10,11... | collective-permute-start | bytes 9437192 | tf_op jit(solution)/shard_map/ppermute | solution.py:298
  6.4 28.0 %collective-permute-start.4 = (bf16[1,2048,768]{2,1,0:T(8,128)(2,1)}, bf16[1,2048,768]{2,1,0:T(8,128)(2,1)}, u32[]{:S(2)}, u32[]{:S(2)}) collective-permute-start(bf16[1,2048,768]{2,1,0:T(8,128)(2,1)} %refs_1_.1), channel_id=1, source_target_pairs={{0,1},{1,0},{2,3},{3,2},{4,5},{5,4},{6,7},{7,6},{8,9},{9,8},{10,11... | collective-permute-start | bytes 9437192 | tf_op jit(solution)/shard_map/ppermute | solution.py:298
  24.7 9.7 %collective-permute-start.5 = (bf16[1,768,2048]{2,1,0:T(8,128)(2,1)}, bf16[1,768,2048]{2,1,0:T(8,128)(2,1)S(1)}, u32[]{:S(2)}, u32[]{:S(2)}) collective-permute-start(bf16[1,768,2048]{2,1,0:T(8,128)(2,1)} %refs_2_.1), channel_id=1, source_target_pairs={{0,1},{1,0},{2,3},{3,2},{4,5},{5,4},{6,7},{7,6},{8,9},{9,8},{10,11... | collective-permute-start | bytes 9437192 | tf_op jit(solution)/shard_map/ppermute | solution.py:298
  24.8 18.2 %collective-permute-start.7 = (bf16[320,2048]{1,0:T(8,128)(2,1)S(1)}, bf16[320,2048]{1,0:T(8,128)(2,1)S(1)}, u32[]{:S(2)}, u32[]{:S(2)}) collective-permute-start(bf16[320,2048]{1,0:T(8,128)(2,1)S(1)} %get-tuple-element.33), channel_id=1, source_target_pairs={{0,6},{1,25},{2,0},{3,27},{4,2},{5,29},{6,4},{7,31},{8,14},{9,1},{... | collective-permute-start | bytes 3932168 | tf_op jit(solution)/shard_map/ppermute | solution.py:298
  27.9 32.9 %collective-permute-start.6 = (bf16[320,2048]{1,0:T(8,128)(2,1)S(1)}, bf16[320,2048]{1,0:T(8,128)(2,1)S(1)}, u32[]{:S(2)}, u32[]{:S(2)}) collective-permute-start(bf16[320,2048]{1,0:T(8,128)(2,1)S(1)} %get-tuple-element.31), channel_id=1, source_target_pairs={{0,2},{1,9},{2,4},{3,11},{4,6},{5,13},{6,0},{7,15},{8,10},{9,17},{... | collective-permute-start | bytes 3932168 | tf_op jit(solution)/shard_map/ppermute | solution.py:298
  39.6 31.5 %collective-permute-start.9 = (bf16[320,2048]{1,0:T(8,128)(2,1)S(1)}, bf16[320,2048]{1,0:T(8,128)(2,1)S(1)}, u32[]{:S(2)}, u32[]{:S(2)}) collective-permute-start(bf16[320,2048]{1,0:T(8,128)(2,1)S(1)} %get-tuple-element.36), channel_id=1, source_target_pairs={{0,4},{1,17},{2,6},{3,19},{4,0},{5,21},{6,2},{7,23},{8,12},{9,25},... | collective-permute-start | bytes 3932168 | tf_op jit(solution)/shard_map/ppermute | solution.py:298
  69.0 17.7 %collective-permute-start.8 = (bf16[320,2048]{1,0:T(8,128)(2,1)S(1)}, bf16[320,2048]{1,0:T(8,128)(2,1)S(1)}, u32[]{:S(2)}, u32[]{:S(2)}) collective-permute-start(bf16[320,2048]{1,0:T(8,128)(2,1)S(1)} %get-tuple-element.34), channel_id=1, source_target_pairs={{2,0},{9,1},{4,2},{11,3},{6,4},{13,5},{0,6},{15,7},{10,8},{17,9},{... | collective-permute-start | bytes 3932168 | tf_op jit(solution)/shard_map/ppermute | solution.py:298
  69.1 25.9 %collective-permute-start.10 = (bf16[320,2048]{1,0:T(8,128)(2,1)S(1)}, bf16[320,2048]{1,0:T(8,128)(2,1)S(1)}, u32[]{:S(2)}, u32[]{:S(2)}) collective-permute-start(bf16[320,2048]{1,0:T(8,128)(2,1)S(1)} %get-tuple-element.38), channel_id=1, source_target_pairs={{6,0},{25,1},{0,2},{27,3},{2,4},{29,5},{4,6},{31,7},{14,8},{1,9},{... | collective-permute-start | bytes 3932168 | tf_op jit(solution)/shard_map/ppermute | solution.py:298
  76.3 18.8 %collective-permute-start.12 = (bf16[160,2048]{1,0:T(8,128)(2,1)S(1)}, bf16[160,2048]{1,0:T(8,128)(2,1)S(1)}, u32[]{:S(2)}, u32[]{:S(2)}) collective-permute-start(bf16[160,2048]{1,0:T(8,128)(2,1)S(1)} %get-tuple-element.41), channel_id=1, source_target_pairs={{4,0},{17,1},{6,2},{19,3},{0,4},{21,5},{2,6},{23,7},{12,8},{25,9},... | collective-permute-start | bytes 1966088 | tf_op jit(solution)/shard_map/ppermute | solution.py:298
  95.0 19.2 %collective-permute-start.11 = (bf16[160,2048]{1,0:T(8,128)(2,1)S(1)}, bf16[160,2048]{1,0:T(8,128)(2,1)S(1)}, u32[]{:S(2)}, u32[]{:S(2)}) collective-permute-start(bf16[160,2048]{1,0:T(8,128)(2,1)S(1)} %get-tuple-element.39), channel_id=1, source_target_pairs={{4,0},{17,1},{6,2},{19,3},{0,4},{21,5},{2,6},{23,7},{12,8},{25,9},... | collective-permute-start | bytes 1966088 | tf_op jit(solution)/shard_map/ppermute | solution.py:298
  97.8 19.8 %collective-permute-start.13 = (bf16[128,2048]{1,0:T(8,128)(2,1)S(1)}, bf16[128,2048]{1,0:T(8,128)(2,1)S(1)}, u32[]{:S(2)}, u32[]{:S(2)}) collective-permute-start(bf16[128,2048]{1,0:T(8,128)(2,1)S(1)} %get-tuple-element.42), channel_id=1, source_target_pairs={{16,0},{5,1},{18,2},{7,3},{20,4},{1,5},{22,6},{3,7},{24,8},{13,9},... | collective-permute-start | bytes 1572872 | tf_op jit(solution)/shard_map/ppermute | solution.py:298
  98.7 18.9 %collective-permute-start.14 = (bf16[128,2048]{1,0:T(8,128)(2,1)S(1)}, bf16[128,2048]{1,0:T(8,128)(2,1)S(1)}, u32[]{:S(2)}, u32[]{:S(2)}) collective-permute-start(bf16[128,2048]{1,0:T(8,128)(2,1)S(1)} %get-tuple-element.43), channel_id=1, source_target_pairs={{24,0},{7,1},{26,2},{1,3},{28,4},{3,5},{30,6},{5,7},{0,8},{15,9},{... | collective-permute-start | bytes 1572872 | tf_op jit(solution)/shard_map/ppermute | solution.py:298
  117.0 9.3 %collective-permute-start.15 = (bf16[128,2048]{1,0:T(8,128)(2,1)S(1)}, bf16[128,2048]{1,0:T(8,128)(2,1)S(1)}, u32[]{:S(2)}, u32[]{:S(2)}) collective-permute-start(bf16[128,2048]{1,0:T(8,128)(2,1)S(1)} %get-tuple-element.44), channel_id=1, source_target_pairs={{8,0},{3,1},{10,2},{5,3},{12,4},{7,5},{14,6},{1,7},{16,8},{11,9},{... | collective-permute-start | bytes 1572872 | tf_op jit(solution)/shard_map/ppermute | solution.py:298

commit v6 on v5

--- a/solution.py
+++ b/solution.py
@@ -44,7 +44,7 @@
     return [(b, a) for a, b in pairs]
 
 
-def prep_kernel(ids_hbm, gw_hbm, tok_hbm, out_ref, ids_ref, gw_ref, sems):
+def prep_kernel(ids_hbm, gw_hbm, tok_hbm, out_ref, q_ref, ids_ref, gw_ref, sems):
     top, tok = ids_ref.shape
     width = tok_hbm.shape[1]
     copies = [
@@ -73,6 +73,16 @@
     blank = jnp.zeros((EXTRA - 2 * EXPERTS, tok), jnp.float32)
     table = jnp.concatenate([slot, weight, blank], axis=0)
     out_ref[:, width:] = table.T.astype(jnp.bfloat16)
+    me = lax.axis_index("expert")
+    x, y, c = me >> 3, (me >> 1) & 3, me & 1
+    n = lax.broadcasted_iota(jnp.int32, (16, EXTRA), 0)
+    spot = lax.broadcasted_iota(jnp.int32, (16, EXTRA), 1)
+    k, f = n >> 1, n & 1
+    along_y = x * (NY * NC) + ((y + k) & 3) * NC + ((c + f) & 1)
+    along_x = ((x + k) & 3) * (NY * NC) + y * NC + ((c + f) & 1)
+    mine = jnp.where(n < KF, jnp.where(c == 0, along_y, along_x), -EXTRA)
+    q_ref[0] = jnp.where(mine == spot, 1.0, 0.0).astype(jnp.bfloat16)
+    q_ref[1] = jnp.where(mine + EXPERTS == spot, 1.0, 0.0).astype(jnp.bfloat16)
     copies[2].wait()
 
 
@@ -82,8 +92,11 @@
     return pl.pallas_call(
         prep_kernel,
         in_specs=[hbm, hbm, hbm],
-        out_specs=pl.BlockSpec(memory_space=pltpu.VMEM),
-        out_shape=pltpu.VMEM((tok, width + EXTRA), jnp.bfloat16),
+        out_specs=[pl.BlockSpec(memory_space=pltpu.VMEM)] * 2,
+        out_shape=[
+            pltpu.VMEM((tok, width + EXTRA), jnp.bfloat16),
+            pltpu.VMEM((2, 16, EXTRA), jnp.bfloat16),
+        ],
         scratch_shapes=[
             pltpu.VMEM(ids.shape, ids.dtype),
             pltpu.VMEM(gw.shape, gw.dtype),
@@ -284,22 +297,11 @@
 
 
 def per_device(tokens, expert_ids, gate_weights, w_gate, w_up, w_down):
-    me = lax.axis_index("expert")
-    x, y, c = me // (NY * NC), (me // NC) % NY, me % NC
-    n = jnp.arange(16, dtype=jnp.int32)
-    k, f = n // NC, n % NC
-    along_y = x * (NY * NC) + ((y + k) % NY) * NC + (c ^ f)
-    along_x = ((x + k) % NX) * (NY * NC) + y * NC + (c ^ f)
-    mine = jnp.where(n < KF, jnp.where(c == 0, along_y, along_x), -1)
-    spot = jnp.arange(EXTRA, dtype=jnp.int32)[None, :]
-    q = jnp.stack([mine[:, None] == spot, (mine[:, None] + EXPERTS == spot) & (n < KF)[:, None]])
-    q = q.astype(jnp.bfloat16)
-
     send = lambda v, pairs: lax.ppermute(v, "expert", pairs)
     after = lambda v, other: lax.optimization_barrier((v, other))[0]
-    home = prep(expert_ids.T, gate_weights.T, tokens)
+    home, q = prep(expert_ids.T, gate_weights.T, tokens)
     blocks = [home] + [send(home, spread_pairs(j)) for j in (1, 2, 3)]
-    weights = list(hold(w_gate, w_up, w_down)) + [send(after(w, home), swap_pairs()) for w in (w_gate, w_up)]
+    weights = list(hold(w_gate, w_up, w_down)) + [send(w, swap_pairs()) for w in (w_gate, w_up)]
 
     near = pack((1, 3), q, blocks)
     weights.append(send(after(w_down, near[0]), swap_pairs()))
@@ -307,7 +309,7 @@
     stay, far = pack((0, 2), q, blocks)
     backs = {}
     (backs[0],) = expert([stay], weights)
-    arrived[2] = send(after(far, backs[0]), deliver_pairs(2))
+    arrived[2] = send(after(far, (arrived[1], arrived[3])), deliver_pairs(2))
     for k, slab in zip((1, 3), expert([arrived[1], arrived[3]], weights)):
         backs[k] = send(slab, back(deliver_pairs(k)))
     early, late = expert([arrived[2]], weights, split=True)[::-1]

time: 128 us -> 108 us (0.84)
  Pallas kernels: 35 us -> 22.9 us
  waiting for transfers between devices: 76 us -> 70.8 us
  starting transfers between devices: 15 us -> 13.2 us
    pallas_call x3, Pallas kernels: 18.5 us -> 12.8 us  [expert(): pl.pallas_call(functools.partial(expert_kernel, count), in_specs=[vmem] *...]
    ppermute x16, waiting for transfers between devices: 76 us -> 70.8 us  [per_device(): send = lambda v, pairs: lax.ppermute(v, 'expert', pairs)]
    pallas_call x2, Pallas kernels: 5.31 us -> 2.2 us  [pack(): pl.pallas_call(functools.partial(pack_kernel, which), in_specs=[vmem] * 5...]
    pallas_call x2, Pallas kernels: 5.49 us -> 3.04 us  [combine(): pl.pallas_call(functools.partial(combine_kernel, spots), in_specs=[vmem]...]
    ppermute x16, starting transfers between devices: 15 us -> 13.2 us  [per_device(): send = lambda v, pairs: lax.ppermute(v, 'expert', pairs)]
  transfers between devices with their start and end apart: 16 -> 16, of which waited for: 8 -> 11; matrix products, arithmetic and copies ran while one was open for 0% -> 0% of each run, Pallas kernels for 26% -> 20%
where the time goes in v6:
time: 108 us
  waiting for transfers between devices  70.8 us (66%)
  Pallas kernels  22.9 us (21%)
  starting transfers between devices  13.2 us (12%)
  other arithmetic  1.13 us (1%)
    ppermute x16, waiting for transfers between devices, per_device(): send = lambda v, pairs: lax.ppermute(v, 'expert', pairs)  70.8 us
    ppermute x16, starting transfers between devices, per_device(): send = lambda v, pairs: lax.ppermute(v, 'expert', pairs)  13.2 us
    pallas_call x3, Pallas kernels, expert(): pl.pallas_call(functools.partial(expert_kernel, count), in_specs=[vmem] *...  12.8 us
    pallas_call x1, Pallas kernels, hold(): pl.pallas_call(hold_kernel, in_specs=[pl.BlockSpec(memory_space=pl.ANY)]...  3.78 us
    pallas_call x2, Pallas kernels, combine(): pl.pallas_call(functools.partial(combine_kernel, spots), in_specs=[vmem]...  3.04 us
    pallas_call x2, Pallas kernels, pack(): pl.pallas_call(functools.partial(pack_kernel, which), in_specs=[vmem] * 5...  2.2 us
  transfers between devices with their start and end apart: 16, of which 11 were waited for; matrix products, arithmetic and copies ran while one was open for 0% of the time, Pallas kernels for 20%

profile of v6, /device:TPU:96, one launch (start us, length us, event | category | flops | bytes accessed | tf_op | source)
XLA Modules:
  0.0 108.2 jit_solution(11232568887859583859)
XLA Ops:
  0.0 1.1 %prep.1 = (bf16[128,2176]{1,0:T(8,128)(2,1)S(1)}, bf16[2,16,128]{2,1,0:T(8,128)(2,1)S(1)}) custom-call(s32[8,128]{1,0:T(8,128)} %bitcast.2, f32[8,128]{1,0:T(8,128)} %bitcast.3, bf16[128,2048]{1,0:T(8,128)(2,1)} %tok_hbm.1), custom_call_target="tpu_custom_call" | custom-call | flops 1048576 | bytes 1048576 | tf_op jit(solution)/shard_map/prep/pallas_call | solution.py:92
  1.1 2.8 %collective-permute-start.2 = (bf16[128,2176]{1,0:T(8,128)(2,1)S(1)}, bf16[128,2176]{1,0:T(8,128)(2,1)S(1)}, u32[]{:S(2)}, u32[]{:S(2)}) collective-permute-start(bf16[128,2176]{1,0:T(8,128)(2,1)S(1)} %get-tuple-element.26.refs_0_), channel_id=1, source_target_pairs={{0,24},{1,7},{2,26},{3,1},{4,28},{5,3},{6,30},{7,5},{8,0},{9,15},{... | collective-permute-start | bytes 1671176 | tf_op jit(solution)/shard_map/ppermute | solution.py:300
  3.9 0.8 collective-permute-start.1
  4.7 0.9 collective-permute-start
  5.6 0.0 collective-permute-start.3
  5.6 0.5 collective-permute-start.4
  6.1 10.9 %collective-permute-done.2.refs_3_.refs_1_ = bf16[128,2176]{1,0:T(8,128)(2,1)S(1)} collective-permute-done((bf16[128,2176]{1,0:T(8,128)(2,1)S(1)}, bf16[128,2176]{1,0:T(8,128)(2,1)S(1)}, u32[]{:S(2)}, u32[]{:S(2)}) %collective-permute-start.2) | collective-permute-done | bytes 557088 | tf_op jit(solution)/shard_map/ppermute | solution.py:300
  17.0 0.0 collective-permute-done.1.refs_2_.refs_0_
  17.0 3.9 %collective-permute-done.refs_1_ = bf16[128,2176]{1,0:T(8,128)(2,1)S(1)} collective-permute-done((bf16[128,2176]{1,0:T(8,128)(2,1)S(1)}, bf16[128,2176]{1,0:T(8,128)(2,1)S(1)}, u32[]{:S(2)}, u32[]{:S(2)}) %collective-permute-start) | collective-permute-done | bytes 557088 | tf_op jit(solution)/shard_map/ppermute | solution.py:300
  20.9 1.1 %pack.3 = (bf16[320,2048]{1,0:T(8,128)(2,1)S(1)}, bf16[320,2048]{1,0:T(8,128)(2,1)S(1)}) custom-call(bf16[2,16,128]{2,1,0:T(8,128)(2,1)S(1)} %get-tuple-element.25.q_ref, bf16[128,2176]{1,0:T(8,128)(2,1)S(1)} %get-tuple-element.26.refs_0_, bf16[128,2176]{1,0:T(8,128)(2,1)S(1)} %collective-permute-done.refs_1_, ...), custom_call_target="tpu_custom_call" | custom-call | flops 671088640 | bytes 4718592 | tf_op jit(solution)/shard_map/pack/pallas_call | solution.py:158
  22.1 0.1 collective-permute-start.5
  22.2 3.1 %collective-permute-start.7 = (bf16[320,2048]{1,0:T(8,128)(2,1)S(1)}, bf16[320,2048]{1,0:T(8,128)(2,1)S(1)}, u32[]{:S(2)}, u32[]{:S(2)}) collective-permute-start(bf16[320,2048]{1,0:T(8,128)(2,1)S(1)} %get-tuple-element.33), channel_id=1, source_target_pairs={{0,6},{1,25},{2,0},{3,27},{4,2},{5,29},{6,4},{7,31},{8,14},{9,1},{... | collective-permute-start | bytes 3932168 | tf_op jit(solution)/shard_map/ppermute | solution.py:300
  25.2 0.0 collective-permute-start.6
  25.2 3.8 %hold.1 = (bf16[1,2048,768]{2,1,0:T(8,128)(2,1)S(1)}, bf16[1,2048,768]{2,1,0:T(8,128)(2,1)S(1)}, bf16[1,768,2048]{2,1,0:T(8,128)(2,1)S(1)}) custom-call(bf16[1,2048,768]{2,1,0:T(8,128)(2,1)} %refs_0_.1, bf16[1,2048,768]{2,1,0:T(8,128)(2,1)} %refs_1_.1, bf16[1,768,2048]{2,1,0:T(8,128)(2,1)} %refs_2_.1), custom_call_target="tpu_custom_call" | custom-call | bytes 18874368 | tf_op jit(solution)/shard_map/hold/pallas_call | solution.py:287
  29.0 1.1 %pack.2 = (bf16[320,2048]{1,0:T(8,128)(2,1)S(1)}, bf16[320,2048]{1,0:T(8,128)(2,1)S(1)}) custom-call(bf16[2,16,128]{2,1,0:T(8,128)(2,1)S(1)} %get-tuple-element.25.q_ref, bf16[128,2176]{1,0:T(8,128)(2,1)S(1)} %get-tuple-element.26.refs_0_, bf16[128,2176]{1,0:T(8,128)(2,1)S(1)} %collective-permute-done.refs_1_, ...), custom_call_target="tpu_custom_call" | custom-call | flops 671088640 | bytes 4718592 | tf_op jit(solution)/shard_map/pack/pallas_call | solution.py:158
  30.1 10.2 %collective-permute-done.7.refs_1_ = bf16[320,2048]{1,0:T(8,128)(2,1)S(1)} collective-permute-done((bf16[320,2048]{1,0:T(8,128)(2,1)S(1)}, bf16[320,2048]{1,0:T(8,128)(2,1)S(1)}, u32[]{:S(2)}, u32[]{:S(2)}) %collective-permute-start.7) | collective-permute-done | bytes 1310752 | tf_op jit(solution)/shard_map/ppermute | solution.py:300
  40.4 3.7 %collective-permute-done.6.refs_0_ = bf16[320,2048]{1,0:T(8,128)(2,1)S(1)} collective-permute-done((bf16[320,2048]{1,0:T(8,128)(2,1)S(1)}, bf16[320,2048]{1,0:T(8,128)(2,1)S(1)}, u32[]{:S(2)}, u32[]{:S(2)}) %collective-permute-start.6) | collective-permute-done | bytes 1310752 | tf_op jit(solution)/shard_map/ppermute | solution.py:300
  44.1 0.0 collective-permute-start.9
  44.1 0.0 collective-permute-done.3.refs_4_.refs_5_
  44.1 0.0 collective-permute-done.4.refs_5_.refs_6_
  44.1 0.0 collective-permute-done.5.refs_6_.refs_7_
  44.1 6.3 %expert.4 = (bf16[320,2048]{1,0:T(8,128)(2,1)S(1)}, bf16[320,2048]{1,0:T(8,128)(2,1)S(1)}) custom-call(bf16[320,2048]{1,0:T(8,128)(2,1)S(1)} %collective-permute-done.6.refs_0_, bf16[320,2048]{1,0:T(8,128)(2,1)S(1)} %collective-permute-done.7.refs_1_, bf16[1,2048,768]{2,1,0:T(8,128)(2,1)S(1)} %get-tuple-element.28.refs_1_.refs_2_, ...), custom_call_target="tpu_custom_call" | custom-call | flops 6039797760 | bytes 5242880 | tf_op jit(solution)/shard_map/expert/pallas_call | solution.py:262
  50.4 1.7 %collective-permute-start.8 = (bf16[320,2048]{1,0:T(8,128)(2,1)S(1)}, bf16[320,2048]{1,0:T(8,128)(2,1)S(1)}, u32[]{:S(2)}, u32[]{:S(2)}) collective-permute-start(bf16[320,2048]{1,0:T(8,128)(2,1)S(1)} %get-tuple-element.34), channel_id=1, source_target_pairs={{2,0},{9,1},{4,2},{11,3},{6,4},{13,5},{0,6},{15,7},{10,8},{17,9},{... | collective-permute-start | bytes 3932168 | tf_op jit(solution)/shard_map/ppermute | solution.py:300
  52.1 0.6 collective-permute-start.10
  52.7 10.6 %collective-permute-done.9.refs_0_ = bf16[320,2048]{1,0:T(8,128)(2,1)S(1)} collective-permute-done((bf16[320,2048]{1,0:T(8,128)(2,1)S(1)}, bf16[320,2048]{1,0:T(8,128)(2,1)S(1)}, u32[]{:S(2)}, u32[]{:S(2)}) %collective-permute-start.9) | collective-permute-done | bytes 1310752 | tf_op jit(solution)/shard_map/ppermute | solution.py:300
  63.3 3.3 %expert.5 = (bf16[160,2048]{1,0:T(8,128)(2,1)S(1)}, bf16[160,2048]{1,0:T(8,128)(2,1)S(1)}) custom-call(bf16[320,2048]{1,0:T(8,128)(2,1)S(1)} %collective-permute-done.9.refs_0_, bf16[1,2048,768]{2,1,0:T(8,128)(2,1)S(1)} %get-tuple-element.28.refs_1_.refs_2_, bf16[1,2048,768]{2,1,0:T(8,128)(2,1)S(1)} %get-tuple-element.29.refs_2_.refs_3_, ...), custom_call_target="tpu_custom_call" | custom-call | flops 3019898880 | bytes 2621440 | tf_op jit(solution)/shard_map/expert/pallas_call | solution.py:262
  66.5 0.1 collective-permute-start.12
  66.6 8.0 %collective-permute-done.8.refs_3_ = bf16[320,2048]{1,0:T(8,128)(2,1)S(1)} collective-permute-done((bf16[320,2048]{1,0:T(8,128)(2,1)S(1)}, bf16[320,2048]{1,0:T(8,128)(2,1)S(1)}, u32[]{:S(2)}, u32[]{:S(2)}) %collective-permute-start.8) | collective-permute-done | bytes 1310752 | tf_op jit(solution)/shard_map/ppermute | solution.py:300
  74.6 2.6 %collective-permute-done.10.refs_5_ = bf16[320,2048]{1,0:T(8,128)(2,1)S(1)} collective-permute-done((bf16[320,2048]{1,0:T(8,128)(2,1)S(1)}, bf16[320,2048]{1,0:T(8,128)(2,1)S(1)}, u32[]{:S(2)}, u32[]{:S(2)}) %collective-permute-start.10) | collective-permute-done | bytes 1310752 | tf_op jit(solution)/shard_map/ppermute | solution.py:300
  77.2 0.0 collective-permute-start.11
  77.2 3.3 %expert.3.refs_2_ = bf16[320,2048]{1,0:T(8,128)(2,1)S(1)} custom-call(bf16[320,2048]{1,0:T(8,128)(2,1)S(1)} %get-tuple-element.27.refs_0_, bf16[1,2048,768]{2,1,0:T(8,128)(2,1)S(1)} %get-tuple-element.28.refs_1_.refs_2_, bf16[1,2048,768]{2,1,0:T(8,128)(2,1)S(1)} %get-tuple-element.29.refs_2_.refs_3_, ...), custom_call_target="tpu_custom_call" | custom-call | flops 3019898880 | bytes 2621440 | tf_op jit(solution)/shard_map/expert/pallas_call | solution.py:262
  80.5 3.8 %collective-permute-done.12.refs_4_ = bf16[160,2048]{1,0:T(8,128)(2,1)S(1)} collective-permute-done((bf16[160,2048]{1,0:T(8,128)(2,1)S(1)}, bf16[160,2048]{1,0:T(8,128)(2,1)S(1)}, u32[]{:S(2)}, u32[]{:S(2)}) %collective-permute-start.12) | collective-permute-done | bytes 655392 | tf_op jit(solution)/shard_map/ppermute | solution.py:300
  84.3 1.5 %combine.3 = (bf16[128,2048]{1,0:T(8,128)(2,1)S(1)}, bf16[128,2048]{1,0:T(8,128)(2,1)S(1)}) custom-call(bf16[2,16,128]{2,1,0:T(8,128)(2,1)S(1)} %get-tuple-element.25.q_ref, bf16[128,2176]{1,0:T(8,128)(2,1)S(1)} %collective-permute-done.1.refs_2_.refs_0_, bf16[128,2176]{1,0:T(8,128)(2,1)S(1)} %collective-permute-done.2.refs_3_.refs_1_, ...), custom_call_target="tpu_custom_call" | custom-call | flops 671088640 | bytes 4194304 | tf_op jit(solution)/shard_map/combine/pallas_call | solution.py:215
  85.8 0.9 collective-permute-start.13
  86.7 0.7 collective-permute-start.14
  87.4 8.9 %collective-permute-done.11.refs_4_ = bf16[160,2048]{1,0:T(8,128)(2,1)S(1)} collective-permute-done((bf16[160,2048]{1,0:T(8,128)(2,1)S(1)}, bf16[160,2048]{1,0:T(8,128)(2,1)S(1)}, u32[]{:S(2)}, u32[]{:S(2)}) %collective-permute-start.11) | collective-permute-done | bytes 655392 | tf_op jit(solution)/shard_map/ppermute | solution.py:300
  96.2 1.5 %combine.2 = (f32[128,2048]{1,0:T(8,128)S(1)}, bf16[128,2048]{1,0:T(8,128)(2,1)S(1)}) custom-call(bf16[2,16,128]{2,1,0:T(8,128)(2,1)S(1)} %get-tuple-element.25.q_ref, bf16[128,2176]{1,0:T(8,128)(2,1)S(1)} %get-tuple-element.26.refs_0_, bf16[128,2176]{1,0:T(8,128)(2,1)S(1)} %collective-permute-done.refs_1_, bf16[320,2048]{1,0:T(8,128)(2,1)S(1)} %expert.3.refs_2_, ...), custom_call_target="tpu_custom_call" | custom-call | flops 671088640 | bytes 4194304 | tf_op jit(solution)/shard_map/combine/pallas_call | solution.py:215
  97.8 1.0 collective-permute-start.15
  98.8 0.0 collective-permute-done.13
  98.8 3.4 %collective-permute-done.14 = bf16[128,2048]{1,0:T(8,128)(2,1)S(1)} collective-permute-done((bf16[128,2048]{1,0:T(8,128)(2,1)S(1)}, bf16[128,2048]{1,0:T(8,128)(2,1)S(1)}, u32[]{:S(2)}, u32[]{:S(2)}) %collective-permute-start.14) | collective-permute-done | bytes 524320 | tf_op jit(solution)/shard_map/ppermute | solution.py:300
  102.2 4.8 %collective-permute-done.15 = bf16[128,2048]{1,0:T(8,128)(2,1)S(1)} collective-permute-done((bf16[128,2048]{1,0:T(8,128)(2,1)S(1)}, bf16[128,2048]{1,0:T(8,128)(2,1)S(1)}, u32[]{:S(2)}, u32[]{:S(2)}) %collective-permute-start.15) | collective-permute-done | bytes 524320 | tf_op jit(solution)/shard_map/ppermute | solution.py:300
  107.0 1.1 %add_convert_fusion = bf16[128,2048]{1,0:T(8,128)(2,1)} fusion(bf16[128,2048]{1,0:T(8,128)(2,1)S(1)} %collective-permute-done.15, bf16[128,2048]{1,0:T(8,128)(2,1)S(1)} %collective-permute-done.14, f32[128,2048]{1,0:T(8,128)S(1)} %get-tuple-element.40, bf16[128,2048]{1,0:T(8,128)(2,1)S(1)} %collective-permute-done.13), kind=kLoop, calls=%fused_computation | loop fusion | flops 1835008 | bytes 3145728 | tf_op jit(solution)/shard_map/convert_element_type | solution.py:327
Async XLA Ops:
  1.1 15.9 %collective-permute-start.2 = (bf16[128,2176]{1,0:T(8,128)(2,1)S(1)}, bf16[128,2176]{1,0:T(8,128)(2,1)S(1)}, u32[]{:S(2)}, u32[]{:S(2)}) collective-permute-start(bf16[128,2176]{1,0:T(8,128)(2,1)S(1)} %get-tuple-element.26.refs_0_), channel_id=1, source_target_pairs={{0,24},{1,7},{2,26},{3,1},{4,28},{5,3},{6,30},{7,5},{8,0},{9,15},{... | collective-permute-start | bytes 1671176 | tf_op jit(solution)/shard_map/ppermute | solution.py:300
  3.9 13.1 %collective-permute-start.1 = (bf16[128,2176]{1,0:T(8,128)(2,1)S(1)}, bf16[128,2176]{1,0:T(8,128)(2,1)S(1)}, u32[]{:S(2)}, u32[]{:S(2)}) collective-permute-start(bf16[128,2176]{1,0:T(8,128)(2,1)S(1)} %get-tuple-element.26.refs_0_), channel_id=1, source_target_pairs={{0,16},{1,5},{2,18},{3,7},{4,20},{5,1},{6,22},{7,3},{8,24},{9,13},... | collective-permute-start | bytes 1671176 | tf_op jit(solution)/shard_map/ppermute | solution.py:300
  4.7 16.2 %collective-permute-start = (bf16[128,2176]{1,0:T(8,128)(2,1)S(1)}, bf16[128,2176]{1,0:T(8,128)(2,1)S(1)}, u32[]{:S(2)}, u32[]{:S(2)}) collective-permute-start(bf16[128,2176]{1,0:T(8,128)(2,1)S(1)} %get-tuple-element.26.refs_0_), channel_id=1, source_target_pairs={{0,8},{1,3},{2,10},{3,5},{4,12},{5,7},{6,14},{7,1},{8,16},{9,11},{... | collective-permute-start | bytes 1671176 | tf_op jit(solution)/shard_map/ppermute | solution.py:300
  5.6 38.4 %collective-permute-start.3 = (bf16[1,2048,768]{2,1,0:T(8,128)(2,1)}, bf16[1,2048,768]{2,1,0:T(8,128)(2,1)S(1)}, u32[]{:S(2)}, u32[]{:S(2)}) collective-permute-start(bf16[1,2048,768]{2,1,0:T(8,128)(2,1)} %refs_0_.1), channel_id=1, source_target_pairs={{0,1},{1,0},{2,3},{3,2},{4,5},{5,4},{6,7},{7,6},{8,9},{9,8},{10,11... | collective-permute-start | bytes 9437192 | tf_op jit(solution)/shard_map/ppermute | solution.py:300
  5.6 38.4 %collective-permute-start.4 = (bf16[1,2048,768]{2,1,0:T(8,128)(2,1)}, bf16[1,2048,768]{2,1,0:T(8,128)(2,1)S(1)}, u32[]{:S(2)}, u32[]{:S(2)}) collective-permute-start(bf16[1,2048,768]{2,1,0:T(8,128)(2,1)} %refs_1_.1), channel_id=1, source_target_pairs={{0,1},{1,0},{2,3},{3,2},{4,5},{5,4},{6,7},{7,6},{8,9},{9,8},{10,11... | collective-permute-start | bytes 9437192 | tf_op jit(solution)/shard_map/ppermute | solution.py:300
  22.1 22.0 %collective-permute-start.5 = (bf16[1,768,2048]{2,1,0:T(8,128)(2,1)}, bf16[1,768,2048]{2,1,0:T(8,128)(2,1)S(1)}, u32[]{:S(2)}, u32[]{:S(2)}) collective-permute-start(bf16[1,768,2048]{2,1,0:T(8,128)(2,1)} %refs_2_.1), channel_id=1, source_target_pairs={{0,1},{1,0},{2,3},{3,2},{4,5},{5,4},{6,7},{7,6},{8,9},{9,8},{10,11... | collective-permute-start | bytes 9437192 | tf_op jit(solution)/shard_map/ppermute | solution.py:300
  22.2 18.2 %collective-permute-start.7 = (bf16[320,2048]{1,0:T(8,128)(2,1)S(1)}, bf16[320,2048]{1,0:T(8,128)(2,1)S(1)}, u32[]{:S(2)}, u32[]{:S(2)}) collective-permute-start(bf16[320,2048]{1,0:T(8,128)(2,1)S(1)} %get-tuple-element.33), channel_id=1, source_target_pairs={{0,6},{1,25},{2,0},{3,27},{4,2},{5,29},{6,4},{7,31},{8,14},{9,1},{... | collective-permute-start | bytes 3932168 | tf_op jit(solution)/shard_map/ppermute | solution.py:300
  25.2 18.8 %collective-permute-start.6 = (bf16[320,2048]{1,0:T(8,128)(2,1)S(1)}, bf16[320,2048]{1,0:T(8,128)(2,1)S(1)}, u32[]{:S(2)}, u32[]{:S(2)}) collective-permute-start(bf16[320,2048]{1,0:T(8,128)(2,1)S(1)} %get-tuple-element.31), channel_id=1, source_target_pairs={{0,2},{1,9},{2,4},{3,11},{4,6},{5,13},{6,0},{7,15},{8,10},{9,17},{... | collective-permute-start | bytes 3932168 | tf_op jit(solution)/shard_map/ppermute | solution.py:300
  44.1 19.2 %collective-permute-start.9 = (bf16[320,2048]{1,0:T(8,128)(2,1)S(1)}, bf16[320,2048]{1,0:T(8,128)(2,1)S(1)}, u32[]{:S(2)}, u32[]{:S(2)}) collective-permute-start(bf16[320,2048]{1,0:T(8,128)(2,1)S(1)} %get-tuple-element.36), channel_id=1, source_target_pairs={{0,4},{1,17},{2,6},{3,19},{4,0},{5,21},{6,2},{7,23},{8,12},{9,25},... | collective-permute-start | bytes 3932168 | tf_op jit(solution)/shard_map/ppermute | solution.py:300
  50.4 24.2 %collective-permute-start.8 = (bf16[320,2048]{1,0:T(8,128)(2,1)S(1)}, bf16[320,2048]{1,0:T(8,128)(2,1)S(1)}, u32[]{:S(2)}, u32[]{:S(2)}) collective-permute-start(bf16[320,2048]{1,0:T(8,128)(2,1)S(1)} %get-tuple-element.34), channel_id=1, source_target_pairs={{2,0},{9,1},{4,2},{11,3},{6,4},{13,5},{0,6},{15,7},{10,8},{17,9},{... | collective-permute-start | bytes 3932168 | tf_op jit(solution)/shard_map/ppermute | solution.py:300
  52.1 25.1 %collective-permute-start.10 = (bf16[320,2048]{1,0:T(8,128)(2,1)S(1)}, bf16[320,2048]{1,0:T(8,128)(2,1)S(1)}, u32[]{:S(2)}, u32[]{:S(2)}) collective-permute-start(bf16[320,2048]{1,0:T(8,128)(2,1)S(1)} %get-tuple-element.38), channel_id=1, source_target_pairs={{6,0},{25,1},{0,2},{27,3},{2,4},{29,5},{4,6},{31,7},{14,8},{1,9},{... | collective-permute-start | bytes 3932168 | tf_op jit(solution)/shard_map/ppermute | solution.py:300
  66.5 17.7 %collective-permute-start.12 = (bf16[160,2048]{1,0:T(8,128)(2,1)S(1)}, bf16[160,2048]{1,0:T(8,128)(2,1)S(1)}, u32[]{:S(2)}, u32[]{:S(2)}) collective-permute-start(bf16[160,2048]{1,0:T(8,128)(2,1)S(1)} %get-tuple-element.41), channel_id=1, source_target_pairs={{4,0},{17,1},{6,2},{19,3},{0,4},{21,5},{2,6},{23,7},{12,8},{25,9},... | collective-permute-start | bytes 1966088 | tf_op jit(solution)/shard_map/ppermute | solution.py:300
  77.2 19.0 %collective-permute-start.11 = (bf16[160,2048]{1,0:T(8,128)(2,1)S(1)}, bf16[160,2048]{1,0:T(8,128)(2,1)S(1)}, u32[]{:S(2)}, u32[]{:S(2)}) collective-permute-start(bf16[160,2048]{1,0:T(8,128)(2,1)S(1)} %get-tuple-element.39), channel_id=1, source_target_pairs={{4,0},{17,1},{6,2},{19,3},{0,4},{21,5},{2,6},{23,7},{12,8},{25,9},... | collective-permute-start | bytes 1966088 | tf_op jit(solution)/shard_map/ppermute | solution.py:300
  85.8 13.0 %collective-permute-start.13 = (bf16[128,2048]{1,0:T(8,128)(2,1)S(1)}, bf16[128,2048]{1,0:T(8,128)(2,1)S(1)}, u32[]{:S(2)}, u32[]{:S(2)}) collective-permute-start(bf16[128,2048]{1,0:T(8,128)(2,1)S(1)} %get-tuple-element.42), channel_id=1, source_target_pairs={{16,0},{5,1},{18,2},{7,3},{20,4},{1,5},{22,6},{3,7},{24,8},{13,9},... | collective-permute-start | bytes 1572872 | tf_op jit(solution)/shard_map/ppermute | solution.py:300
  86.7 15.5 %collective-permute-start.14 = (bf16[128,2048]{1,0:T(8,128)(2,1)S(1)}, bf16[128,2048]{1,0:T(8,128)(2,1)S(1)}, u32[]{:S(2)}, u32[]{:S(2)}) collective-permute-start(bf16[128,2048]{1,0:T(8,128)(2,1)S(1)} %get-tuple-element.43), channel_id=1, source_target_pairs={{24,0},{7,1},{26,2},{1,3},{28,4},{3,5},{30,6},{5,7},{0,8},{15,9},{... | collective-permute-start | bytes 1572872 | tf_op jit(solution)/shard_map/ppermute | solution.py:300
  97.8 9.3 %collective-permute-start.15 = (bf16[128,2048]{1,0:T(8,128)(2,1)S(1)}, bf16[128,2048]{1,0:T(8,128)(2,1)S(1)}, u32[]{:S(2)}, u32[]{:S(2)}) collective-permute-start(bf16[128,2048]{1,0:T(8,128)(2,1)S(1)} %get-tuple-element.44), channel_id=1, source_target_pairs={{8,0},{3,1},{10,2},{5,3},{12,4},{7,5},{14,6},{1,7},{16,8},{11,9},{... | collective-permute-start | bytes 1572872 | tf_op jit(solution)/shard_map/ppermute | solution.py:300

commit v7 on v6

--- a/solution.py
+++ b/solution.py
@@ -120,7 +120,8 @@
 
 
 def pack_kernel(which, q_ref, *refs):
-    blocks, outs = refs[:4], refs[4:]
+    outs = refs[len(refs) - len(which) :]
+    blocks = refs[: len(refs) - len(which)]
     tok = blocks[0].shape[0]
     width = outs[0].shape[1]
     q = q_ref[0]
@@ -131,7 +132,7 @@
     target = jnp.where(second, r - CAP, r)
     target = jnp.where(second == (t >= tok), target, -5).astype(jnp.float32)
     cols = 512
-    for p in range(2):
+    for p in range(len(blocks) // 2):
         pair = blocks[2 * p : 2 * p + 2]
         slots = select(q, pair)
         pick = jnp.concatenate(
@@ -153,17 +154,17 @@
     tok = blocks[0].shape[0]
     width = blocks[0].shape[1] - EXTRA
     count = len(which)
-    rows = NC * 4 * CAP
+    rows = NC * len(blocks) * CAP
     vmem = pl.BlockSpec(memory_space=pltpu.VMEM)
     return pl.pallas_call(
         functools.partial(pack_kernel, which),
-        in_specs=[vmem] * 5,
+        in_specs=[vmem] * (1 + len(blocks)),
         out_specs=[vmem] * count,
         out_shape=[jax.ShapeDtypeStruct((rows, width), jnp.bfloat16)] * count,
         compiler_params=pltpu.CompilerParams(vmem_limit_bytes=16 * 1024 * 1024),
         cost_estimate=pl.CostEstimate(
             flops=2 * rows * count * 2 * tok * width,
-            bytes_accessed=2 * (4 * tok + rows * count) * width,
+            bytes_accessed=2 * (len(blocks) * tok + rows * count) * width,
             transcendentals=0,
         ),
         name="pack",
@@ -227,102 +228,120 @@
     )(q, *pair, *backs)
 
 
-def expert_kernel(count, *refs):
-    slabs, weights, outs = refs[:count], refs[count : count + 6], refs[count + 6 :]
+def halves(refs):
+    size = 2 * NC * CAP
+    return [(ref, at) for ref in refs for at in range(0, ref.shape[0], size)]
+
+
+def expert_kernel(count, ff, *refs):
+    slabs, bundles, outs = refs[:count], refs[count : count + 2], refs[count + 2 :]
     width = slabs[0].shape[1]
     half = 2 * CAP
-    for f in range(NC):
-        wg, wu, wd = weights[3 * f : 3 * f + 3]
-        ff = wg.shape[-1]
-        spots = [half * (2 * p + f) for p in range(2)]
-        lines = jnp.concatenate([s[at : at + half, :] for s in slabs for at in spots], axis=0)
+    for f, w in enumerate(bundles):
+        lines = jnp.concatenate([s[at + half * f : at + half * (f + 1), :] for s, at in halves(slabs)], axis=0)
         hidden = []
         for at in range(0, ff, 256):
-            gate = jnp.dot(lines, wg[0, :, at : at + 256], preferred_element_type=jnp.float32)
-            up = jnp.dot(lines, wu[0, :, at : at + 256], preferred_element_type=jnp.float32)
+            gate = jnp.dot(lines, w[:width, at : at + 256], preferred_element_type=jnp.float32)
+            up = jnp.dot(lines, w[:width, ff + at : ff + at + 256], preferred_element_type=jnp.float32)
             hidden.append((gate / (1.0 + jnp.exp(-gate)) * up).astype(jnp.bfloat16))
-        hidden = jnp.concatenate(hidden, axis=1)
+        whole = jnp.concatenate(hidden, axis=1)
         for at in range(0, width, 512):
-            got = jnp.dot(hidden, wd[0, :, at : at + 512], preferred_element_type=jnp.float32)
+            if at < 2 * ff:
+                down = w[width : width + ff, at : at + 512]
+            else:
+                down = jnp.concatenate([w[width + ff :, 512 * i : 512 * (i + 1)] for i in range(ff // 256)], axis=0)
+            got = jnp.dot(whole, down, preferred_element_type=jnp.float32)
             got = got.astype(jnp.bfloat16)
-            if len(outs) == count:
-                places = [(o, spot) for o in outs for spot in spots]
-            else:
-                places = [(o, half * f) for o in outs]
-            for n, (o, spot) in enumerate(places):
-                o[spot : spot + half, at : at + 512] = got[n * half : (n + 1) * half]
-
-
-def expert(slabs, weights, split=False):
+            for n, (o, to) in enumerate(halves(outs)):
+                o[to + half * f : to + half * (f + 1), at : at + 512] = got[n * half : (n + 1) * half]
+
+
+def expert(slabs, bundles, outs):
     count = len(slabs)
-    rows, width = slabs[0].shape
-    ff = weights[0].shape[-1]
-    outs = 2 * count if split else count
+    rows = sum(s.shape[0] for s in slabs)
+    width = slabs[0].shape[1]
+    ff = bundles[0].shape[1] // 2
     vmem = pl.BlockSpec(memory_space=pltpu.VMEM)
     return pl.pallas_call(
-        functools.partial(expert_kernel, count),
-        in_specs=[vmem] * (count + 6),
+        functools.partial(expert_kernel, count, ff),
+        in_specs=[vmem] * (count + 2),
         out_specs=[vmem] * outs,
-        out_shape=[jax.ShapeDtypeStruct((rows * count // outs, width), jnp.bfloat16)] * outs,
+        out_shape=[jax.ShapeDtypeStruct((rows // outs, width), jnp.bfloat16)] * outs,
         compiler_params=pltpu.CompilerParams(vmem_limit_bytes=16 * 1024 * 1024),
         cost_estimate=pl.CostEstimate(
-            flops=6 * count * rows * width * ff,
-            bytes_accessed=4 * count * rows * width,
-            transcendentals=count * rows * ff,
+            flops=6 * rows * width * ff,
+            bytes_accessed=4 * rows * width,
+            transcendentals=rows * ff,
         ),
         name="expert",
-    )(*slabs, *[pltpu.with_memory_space_constraint(w, pltpu.VMEM) for w in weights])
-
-
-def hold_kernel(*refs):
-    ins, outs, sems = refs[:3], refs[3:6], refs[6]
-    copies = [pltpu.make_async_copy(a, b, sems.at[n]) for n, (a, b) in enumerate(zip(ins, outs))]
+    )(*slabs, *[pltpu.with_memory_space_constraint(w, pltpu.VMEM) for w in bundles])
+
+
+def hold_kernel(wg, wu, wd, out_ref, mark_ref, sems):
+    width, ff = wg.shape[1:]
+    moves = [
+        (wg.at[0], out_ref.at[pl.ds(0, width), pl.ds(0, ff)]),
+        (wu.at[0], out_ref.at[pl.ds(0, width), pl.ds(ff, ff)]),
+        (wd.at[0, :, pl.ds(0, 2 * ff)], out_ref.at[pl.ds(width, ff)]),
+    ]
+    for i in range(ff // 256):
+        moves.append(
+            (
+                wd.at[0, pl.ds(256 * i, 256), pl.ds(2 * ff, 512)],
+                out_ref.at[pl.ds(width + ff, 256), pl.ds(512 * i, 512)],
+            )
+        )
+    copies = [pltpu.make_async_copy(a, b, sems.at[n]) for n, (a, b) in enumerate(moves)]
     for copy in copies:
         copy.start()
+    mark_ref[...] = jnp.zeros_like(mark_ref)
     for copy in copies:
         copy.wait()
 
 
 def hold(*weights):
+    width, ff = weights[0].shape[1:]
     return pl.pallas_call(
         hold_kernel,
         in_specs=[pl.BlockSpec(memory_space=pl.ANY)] * 3,
-        out_specs=[pl.BlockSpec(memory_space=pltpu.VMEM)] * 3,
-        out_shape=[pltpu.VMEM(w.shape, w.dtype) for w in weights],
-        scratch_shapes=[pltpu.SemaphoreType.DMA((3,))],
+        out_specs=[pl.BlockSpec(memory_space=pltpu.VMEM)] * 2,
+        out_shape=[
+            pltpu.VMEM((width + ff + 256, 2 * ff), weights[0].dtype),
+            pltpu.VMEM((8, 128), jnp.float32),
+        ],
+        scratch_shapes=[pltpu.SemaphoreType.DMA((6,))],
         compiler_params=pltpu.CompilerParams(vmem_limit_bytes=4 * 1024 * 1024),
         cost_estimate=pl.CostEstimate(flops=0, bytes_accessed=4 * weights[0].size * 3, transcendentals=0),
         name="hold",
-    )(*[pltpu.with_memory_space_constraint(w, pltpu.HBM) for w in weights])
+    )(*[pltpu.with_memory_space_constraint(w, pltpu.HBM) for w in weights])[0]
 
 
 def per_device(tokens, expert_ids, gate_weights, w_gate, w_up, w_down):
     send = lambda v, pairs: lax.ppermute(v, "expert", pairs)
     after = lambda v, other: lax.optimization_barrier((v, other))[0]
     home, q = prep(expert_ids.T, gate_weights.T, tokens)
-    blocks = [home] + [send(home, spread_pairs(j)) for j in (1, 2, 3)]
-    weights = list(hold(w_gate, w_up, w_down)) + [send(w, swap_pairs()) for w in (w_gate, w_up)]
-
-    near = pack((1, 3), q, blocks)
-    weights.append(send(after(w_down, near[0]), swap_pairs()))
-    arrived = {k: send(slab, deliver_pairs(k)) for k, slab in zip((1, 3), near)}
-    stay, far = pack((0, 2), q, blocks)
+    moved = {j: send(home, spread_pairs(j)) for j in (1, 3, 2)}
+    pairs = [[home, moved[2]], [moved[1], moved[3]]]
+    near = [pack((1, 3), q, pair) for pair in pairs]
+    bundle = hold(w_gate, w_up, w_down)
+    weights = [bundle, send(after(bundle, moved[2]), swap_pairs())]
+
+    arrived = {k: [send(slabs[n], deliver_pairs(k)) for slabs in near] for n, k in enumerate((1, 3))}
+    stay, far = pack((0, 2), q, pairs[0] + pairs[1])
     backs = {}
-    (backs[0],) = expert([stay], weights)
-    arrived[2] = send(after(far, (arrived[1], arrived[3])), deliver_pairs(2))
-    for k, slab in zip((1, 3), expert([arrived[1], arrived[3]], weights)):
+    (backs[0],) = expert([stay], weights, 1)
+    arrived[2] = [send(after(far, (arrived[1], arrived[3])), deliver_pairs(2))]
+    for k, slab in zip((1, 3), expert(arrived[1] + arrived[3], weights, 2)):
         backs[k] = send(slab, back(deliver_pairs(k)))
-    early, late = expert([arrived[2]], weights, split=True)[::-1]
+    early, late = expert(arrived[2], weights, 2)
     early = send(early, back(deliver_pairs(2)))
     late = send(after(late, (backs[1], backs[3])), back(deliver_pairs(2)))
 
     whole = [backs[k] for k in (0, 1)]
-    part2, part3 = combine(
-        q, blocks[2:], [*whole, early, backs[3]], (1, 1, 0, 1), (jnp.bfloat16, jnp.bfloat16)
-    )
-    part0, part1 = combine(q, blocks[:2], [*whole, late, backs[3]], (0, 0, 0, 0), (jnp.float32, jnp.bfloat16))
+    part0, part2 = combine(q, pairs[0], [*whole, early, backs[3]], (0, 0, 0, 0), (jnp.float32, jnp.bfloat16))
+    part1, part3 = combine(q, pairs[1], [*whole, late, backs[3]], (1, 1, 0, 1), (jnp.bfloat16, jnp.bfloat16))
     mixed = part0
-    for j, part in ((2, part2), (3, part3), (1, part1)):
+    for j, part in ((2, part2), (1, part1), (3, part3)):
         mixed = mixed + send(part, back(spread_pairs(j))).astype(jnp.float32)
     return mixed.astype(jnp.bfloat16)
 

time: 108 us -> 113 us (1.046)
  the two profiles are of different devices: /device:TPU:96 before, /device:TPU:104 now
where the time goes in v7:
time: 113 us
  waiting for transfers between devices  67.5 us (60%)
  Pallas kernels  23.6 us (21%)
  starting transfers between devices  20.4 us (18%)
    ppermute x16, waiting for transfers between devices, per_device(): send = lambda v, pairs: lax.ppermute(v, 'expert', pairs)  67.5 us
    ppermute x16, starting transfers between devices, per_device(): send = lambda v, pairs: lax.ppermute(v, 'expert', pairs)  20.4 us
    pallas_call x3, Pallas kernels, expert(): pl.pallas_call(functools.partial(expert_kernel, count, ff), in_specs=[vme...  12.8 us
    pallas_call x1, Pallas kernels, hold(): pl.pallas_call(hold_kernel, in_specs=[pl.BlockSpec(memory_space=pl.ANY)]...  4.33 us
    pallas_call x2, Pallas kernels, combine(): pl.pallas_call(functools.partial(combine_kernel, spots), in_specs=[vmem]...  3.04 us
    pallas_call x3, Pallas kernels, pack(): pl.pallas_call(functools.partial(pack_kernel, which), in_specs=[vmem] * (...  2.33 us
  transfers between devices with their start and end apart: 16, of which 11 were waited for; matrix products, arithmetic and copies ran while one was open for 0% of the time, Pallas kernels for 20%

profile of v7, /device:TPU:104, one launch (start us, length us, event | category | flops | bytes accessed | tf_op | source)
XLA Modules:
  0.0 112.8 jit_solution(15869746062256633735)
XLA Ops:
  0.0 1.1 prep.1
  1.1 3.1 %collective-permute-start = (bf16[128,2176]{1,0:T(8,128)(2,1)S(1)}, bf16[128,2176]{1,0:T(8,128)(2,1)S(1)}, u32[]{:S(2)}, u32[]{:S(2)}) collective-permute-start(bf16[128,2176]{1,0:T(8,128)(2,1)S(1)} %get-tuple-element.26.refs_0_), channel_id=1, source_target_pairs={{0,16},{1,5},{2,18},{3,7},{4,20},{5,1},{6,22},{7,3},{8,24},{9,13},... | collective-permute-start | bytes 1671176 | tf_op jit(solution)/shard_map/ppermute | solution.py:320
  4.2 4.3 %hold.1 = (bf16[3072,1536]{1,0:T(8,128)(2,1)S(1)}, f32[8,128]{1,0:T(8,128)}) custom-call(bf16[1,2048,768]{2,1,0:T(8,128)(2,1)} %wg.1, bf16[1,2048,768]{2,1,0:T(8,128)(2,1)} %wu.1, bf16[1,768,2048]{2,1,0:T(8,128)(2,1)} %wd.1), custom_call_target="tpu_custom_call" | custom-call | bytes 18874368 | tf_op jit(solution)/shard_map/hold/pallas_call | solution.py:304
  8.6 3.7 %collective-permute-done.refs_1_ = bf16[128,2176]{1,0:T(8,128)(2,1)S(1)} collective-permute-done((bf16[128,2176]{1,0:T(8,128)(2,1)S(1)}, bf16[128,2176]{1,0:T(8,128)(2,1)S(1)}, u32[]{:S(2)}, u32[]{:S(2)}) %collective-permute-start) | collective-permute-done | bytes 557088 | tf_op jit(solution)/shard_map/ppermute | solution.py:320
  12.2 0.0 collective-permute-start.3
  12.2 2.8 %collective-permute-start.2 = (bf16[128,2176]{1,0:T(8,128)(2,1)S(1)}, bf16[128,2176]{1,0:T(8,128)(2,1)S(1)}, u32[]{:S(2)}, u32[]{:S(2)}) collective-permute-start(bf16[128,2176]{1,0:T(8,128)(2,1)S(1)} %get-tuple-element.26.refs_0_), channel_id=1, source_target_pairs={{0,24},{1,7},{2,26},{3,1},{4,28},{5,3},{6,30},{7,5},{8,0},{9,15},{... | collective-permute-start | bytes 1671176 | tf_op jit(solution)/shard_map/ppermute | solution.py:320
  15.0 0.0 collective-permute-start.1
  15.0 0.6 pack.4
  15.6 1.7 %collective-permute-start.4 = (bf16[160,2048]{1,0:T(8,128)(2,1)S(1)}, bf16[160,2048]{1,0:T(8,128)(2,1)S(1)}, u32[]{:S(2)}, u32[]{:S(2)}) collective-permute-start(bf16[160,2048]{1,0:T(8,128)(2,1)S(1)} %get-tuple-element.30), channel_id=1, source_target_pairs={{0,2},{1,9},{2,4},{3,11},{4,6},{5,13},{6,0},{7,15},{8,10},{9,17},{... | collective-permute-start | bytes 1966088 | tf_op jit(solution)/shard_map/ppermute | solution.py:320
  17.3 0.5 collective-permute-start.6
  17.7 8.3 %collective-permute-done.2.refs_3_.refs_1_ = bf16[128,2176]{1,0:T(8,128)(2,1)S(1)} collective-permute-done((bf16[128,2176]{1,0:T(8,128)(2,1)S(1)}, bf16[128,2176]{1,0:T(8,128)(2,1)S(1)}, u32[]{:S(2)}, u32[]{:S(2)}) %collective-permute-start.2) | collective-permute-done | bytes 557088 | tf_op jit(solution)/shard_map/ppermute | solution.py:320
  26.0 5.7 %collective-permute-done.1.refs_2_.refs_0_ = bf16[128,2176]{1,0:T(8,128)(2,1)S(1)} collective-permute-done((bf16[128,2176]{1,0:T(8,128)(2,1)S(1)}, bf16[128,2176]{1,0:T(8,128)(2,1)S(1)}, u32[]{:S(2)}, u32[]{:S(2)}) %collective-permute-start.1) | collective-permute-done | bytes 557088 | tf_op jit(solution)/shard_map/ppermute | solution.py:320
  31.7 0.6 pack.5
  32.3 1.7 %collective-permute-start.5 = (bf16[160,2048]{1,0:T(8,128)(2,1)S(1)}, bf16[160,2048]{1,0:T(8,128)(2,1)S(1)}, u32[]{:S(2)}, u32[]{:S(2)}) collective-permute-start(bf16[160,2048]{1,0:T(8,128)(2,1)S(1)} %get-tuple-element.31), channel_id=1, source_target_pairs={{0,2},{1,9},{2,4},{3,11},{4,6},{5,13},{6,0},{7,15},{8,10},{9,17},{... | collective-permute-start | bytes 1966088 | tf_op jit(solution)/shard_map/ppermute | solution.py:320
  34.0 0.4 collective-permute-start.7
  34.4 1.1 pack.3
  35.5 0.0 collective-permute-done.4.refs_0_
  35.5 0.0 collective-permute-done.6.refs_2_
  35.6 7.4 %collective-permute-done.5.refs_1_ = bf16[160,2048]{1,0:T(8,128)(2,1)S(1)} collective-permute-done((bf16[160,2048]{1,0:T(8,128)(2,1)S(1)}, bf16[160,2048]{1,0:T(8,128)(2,1)S(1)}, u32[]{:S(2)}, u32[]{:S(2)}) %collective-permute-start.5) | collective-permute-done | bytes 655392 | tf_op jit(solution)/shard_map/ppermute | solution.py:320
  43.0 1.6 %collective-permute-done.7.refs_3_ = bf16[160,2048]{1,0:T(8,128)(2,1)S(1)} collective-permute-done((bf16[160,2048]{1,0:T(8,128)(2,1)S(1)}, bf16[160,2048]{1,0:T(8,128)(2,1)S(1)}, u32[]{:S(2)}, u32[]{:S(2)}) %collective-permute-start.7) | collective-permute-done | bytes 655392 | tf_op jit(solution)/shard_map/ppermute | solution.py:320
  44.6 1.9 %collective-permute-start.9 = (bf16[320,2048]{1,0:T(8,128)(2,1)S(1)}, bf16[320,2048]{1,0:T(8,128)(2,1)S(1)}, u32[]{:S(2)}, u32[]{:S(2)}) collective-permute-start(bf16[320,2048]{1,0:T(8,128)(2,1)S(1)} %get-tuple-element.36), channel_id=1, source_target_pairs={{0,4},{1,17},{2,6},{3,19},{4,0},{5,21},{6,2},{7,23},{8,12},{9,25},... | collective-permute-start | bytes 3932168 | tf_op jit(solution)/shard_map/ppermute | solution.py:320
  46.5 0.0 collective-permute-done.3.refs_2_.refs_5_
  46.5 6.3 %expert.4 = (bf16[320,2048]{1,0:T(8,128)(2,1)S(1)}, bf16[320,2048]{1,0:T(8,128)(2,1)S(1)}) custom-call(bf16[160,2048]{1,0:T(8,128)(2,1)S(1)} %collective-permute-done.4.refs_0_, bf16[160,2048]{1,0:T(8,128)(2,1)S(1)} %collective-permute-done.5.refs_1_, bf16[160,2048]{1,0:T(8,128)(2,1)S(1)} %collective-permute-done.6.refs_2_, ...), custom_call_target="tpu_custom_call" | custom-call | flops 6039797760 | bytes 5242880 | tf_op jit(solution)/shard_map/expert/pallas_call | solution.py:265
  52.8 1.5 %collective-permute-start.8 = (bf16[320,2048]{1,0:T(8,128)(2,1)S(1)}, bf16[320,2048]{1,0:T(8,128)(2,1)S(1)}, u32[]{:S(2)}, u32[]{:S(2)}) collective-permute-start(bf16[320,2048]{1,0:T(8,128)(2,1)S(1)} %get-tuple-element.34), channel_id=1, source_target_pairs={{2,0},{9,1},{4,2},{11,3},{6,4},{13,5},{0,6},{15,7},{10,8},{17,9},{... | collective-permute-start | bytes 3932168 | tf_op jit(solution)/shard_map/ppermute | solution.py:320
  54.3 0.8 collective-permute-start.11
  55.1 8.7 %collective-permute-done.9.refs_0_ = bf16[320,2048]{1,0:T(8,128)(2,1)S(1)} collective-permute-done((bf16[320,2048]{1,0:T(8,128)(2,1)S(1)}, bf16[320,2048]{1,0:T(8,128)(2,1)S(1)}, u32[]{:S(2)}, u32[]{:S(2)}) %collective-permute-start.9) | collective-permute-done | bytes 1310752 | tf_op jit(solution)/shard_map/ppermute | solution.py:320
  63.8 3.3 %expert.5 = (bf16[160,2048]{1,0:T(8,128)(2,1)S(1)}, bf16[160,2048]{1,0:T(8,128)(2,1)S(1)}) custom-call(bf16[320,2048]{1,0:T(8,128)(2,1)S(1)} %collective-permute-done.9.refs_0_, bf16[3072,1536]{1,0:T(8,128)(2,1)S(1)} %get-tuple-element.29.refs_1_.refs_4_, bf16[3072,1536]{1,0:T(8,128)(2,1)S(1)} %collective-permute-done.3.refs_2_.refs_5_), custom_call_target="tpu_custom_call" | custom-call | flops 3019898880 | bytes 2621440 | tf_op jit(solution)/shard_map/expert/pallas_call | solution.py:265
  67.1 2.0 %collective-permute-start.10 = (bf16[160,2048]{1,0:T(8,128)(2,1)S(1)}, bf16[160,2048]{1,0:T(8,128)(2,1)S(1)}, u32[]{:S(2)}, u32[]{:S(2)}) collective-permute-start(bf16[160,2048]{1,0:T(8,128)(2,1)S(1)} %get-tuple-element.37), channel_id=1, source_target_pairs={{4,0},{17,1},{6,2},{19,3},{0,4},{21,5},{2,6},{23,7},{12,8},{25,9},... | collective-permute-start | bytes 1966088 | tf_op jit(solution)/shard_map/ppermute | solution.py:320
  69.1 8.7 %collective-permute-done.8.refs_3_ = bf16[320,2048]{1,0:T(8,128)(2,1)S(1)} collective-permute-done((bf16[320,2048]{1,0:T(8,128)(2,1)S(1)}, bf16[320,2048]{1,0:T(8,128)(2,1)S(1)}, u32[]{:S(2)}, u32[]{:S(2)}) %collective-permute-start.8) | collective-permute-done | bytes 1310752 | tf_op jit(solution)/shard_map/ppermute | solution.py:320
  77.7 0.0 collective-permute-done.11.refs_5_
  77.7 1.9 %collective-permute-start.13 = (bf16[160,2048]{1,0:T(8,128)(2,1)S(1)}, bf16[160,2048]{1,0:T(8,128)(2,1)S(1)}, u32[]{:S(2)}, u32[]{:S(2)}) collective-permute-start(bf16[160,2048]{1,0:T(8,128)(2,1)S(1)} %get-tuple-element.42), channel_id=1, source_target_pairs={{4,0},{17,1},{6,2},{19,3},{0,4},{21,5},{2,6},{23,7},{12,8},{25,9},... | collective-permute-start | bytes 1966088 | tf_op jit(solution)/shard_map/ppermute | solution.py:320
  79.7 3.3 %expert.3.refs_2_ = bf16[320,2048]{1,0:T(8,128)(2,1)S(1)} custom-call(bf16[320,2048]{1,0:T(8,128)(2,1)S(1)} %get-tuple-element.27.refs_0_, bf16[3072,1536]{1,0:T(8,128)(2,1)S(1)} %get-tuple-element.29.refs_1_.refs_4_, bf16[3072,1536]{1,0:T(8,128)(2,1)S(1)} %collective-permute-done.3.refs_2_.refs_5_), custom_call_target="tpu_custom_call" | custom-call | flops 3019898880 | bytes 2621440 | tf_op jit(solution)/shard_map/expert/pallas_call | solution.py:265
  82.9 2.6 %collective-permute-done.10.refs_4_ = bf16[160,2048]{1,0:T(8,128)(2,1)S(1)} collective-permute-done((bf16[160,2048]{1,0:T(8,128)(2,1)S(1)}, bf16[160,2048]{1,0:T(8,128)(2,1)S(1)}, u32[]{:S(2)}, u32[]{:S(2)}) %collective-permute-start.10) | collective-permute-done | bytes 655392 | tf_op jit(solution)/shard_map/ppermute | solution.py:320
  85.5 1.5 %combine.2 = (f32[128,2048]{1,0:T(8,128)S(1)}, bf16[128,2048]{1,0:T(8,128)(2,1)S(1)}) custom-call(bf16[2,16,128]{2,1,0:T(8,128)(2,1)S(1)} %get-tuple-element.25.q_ref, bf16[128,2176]{1,0:T(8,128)(2,1)S(1)} %get-tuple-element.26.refs_0_, bf16[128,2176]{1,0:T(8,128)(2,1)S(1)} %collective-permute-done.refs_1_, bf16[320,2048]{1,0:T(8,128)(2,1)S(1)} %expert.3.refs_2_, ...), custom_call_target="tpu_custom_call" | custom-call | flops 671088640 | bytes 4194304 | tf_op jit(solution)/shard_map/combine/pallas_call | solution.py:216
  87.0 0.1 collective-permute-start.12
  87.1 12.5 %collective-permute-done.13.refs_4_ = bf16[160,2048]{1,0:T(8,128)(2,1)S(1)} collective-permute-done((bf16[160,2048]{1,0:T(8,128)(2,1)S(1)}, bf16[160,2048]{1,0:T(8,128)(2,1)S(1)}, u32[]{:S(2)}, u32[]{:S(2)}) %collective-permute-start.13) | collective-permute-done | bytes 655392 | tf_op jit(solution)/shard_map/ppermute | solution.py:320
  99.6 1.5 %combine.3 = (bf16[128,2048]{1,0:T(8,128)(2,1)S(1)}, bf16[128,2048]{1,0:T(8,128)(2,1)S(1)}) custom-call(bf16[2,16,128]{2,1,0:T(8,128)(2,1)S(1)} %get-tuple-element.25.q_ref, bf16[128,2176]{1,0:T(8,128)(2,1)S(1)} %collective-permute-done.1.refs_2_.refs_0_, bf16[128,2176]{1,0:T(8,128)(2,1)S(1)} %collective-permute-done.2.refs_3_.refs_1_, ...), custom_call_target="tpu_custom_call" | custom-call | flops 671088640 | bytes 4194304 | tf_op jit(solution)/shard_map/combine/pallas_call | solution.py:216
  101.1 0.1 collective-permute-start.14
  101.2 2.0 %collective-permute-start.15 = (bf16[128,2048]{1,0:T(8,128)(2,1)S(1)}, bf16[128,2048]{1,0:T(8,128)(2,1)S(1)}, u32[]{:S(2)}, u32[]{:S(2)}) collective-permute-start(bf16[128,2048]{1,0:T(8,128)(2,1)S(1)} %get-tuple-element.44), channel_id=1, source_target_pairs={{24,0},{7,1},{26,2},{1,3},{28,4},{3,5},{30,6},{5,7},{0,8},{15,9},{... | collective-permute-start | bytes 1572872 | tf_op jit(solution)/shard_map/ppermute | solution.py:320
  103.2 0.0 collective-permute-done.12
  103.2 7.2 %collective-permute-done.14 = bf16[128,2048]{1,0:T(8,128)(2,1)S(1)} collective-permute-done((bf16[128,2048]{1,0:T(8,128)(2,1)S(1)}, bf16[128,2048]{1,0:T(8,128)(2,1)S(1)}, u32[]{:S(2)}, u32[]{:S(2)}) %collective-permute-start.14) | collective-permute-done | bytes 524320 | tf_op jit(solution)/shard_map/ppermute | solution.py:320
  110.4 1.3 %collective-permute-done.15 = bf16[128,2048]{1,0:T(8,128)(2,1)S(1)} collective-permute-done((bf16[128,2048]{1,0:T(8,128)(2,1)S(1)}, bf16[128,2048]{1,0:T(8,128)(2,1)S(1)}, u32[]{:S(2)}, u32[]{:S(2)}) %collective-permute-start.15) | collective-permute-done | bytes 524320 | tf_op jit(solution)/shard_map/ppermute | solution.py:320
  111.7 1.1 add_convert_fusion
Async XLA Ops:
  1.1 11.1 %collective-permute-start = (bf16[128,2176]{1,0:T(8,128)(2,1)S(1)}, bf16[128,2176]{1,0:T(8,128)(2,1)S(1)}, u32[]{:S(2)}, u32[]{:S(2)}) collective-permute-start(bf16[128,2176]{1,0:T(8,128)(2,1)S(1)} %get-tuple-element.26.refs_0_), channel_id=1, source_target_pairs={{0,16},{1,5},{2,18},{3,7},{4,20},{5,1},{6,22},{7,3},{8,24},{9,13},... | collective-permute-start | bytes 1671176 | tf_op jit(solution)/shard_map/ppermute | solution.py:320
  12.2 34.3 %collective-permute-start.3 = (bf16[3072,1536]{1,0:T(8,128)(2,1)S(1)}, bf16[3072,1536]{1,0:T(8,128)(2,1)S(1)}, u32[]{:S(2)}, u32[]{:S(2)}) collective-permute-start(bf16[3072,1536]{1,0:T(8,128)(2,1)S(1)} %get-tuple-element.29.refs_1_.refs_4_), channel_id=1, source_target_pairs={{0,1},{1,0},{2,3},{3,2},{4,5},{5,4},{6,7},{7,6},{8,9},{9,8},{10,11... | collective-permute-start | bytes 28311560 | tf_op jit(solution)/shard_map/ppermute | solution.py:320
  12.2 13.8 %collective-permute-start.2 = (bf16[128,2176]{1,0:T(8,128)(2,1)S(1)}, bf16[128,2176]{1,0:T(8,128)(2,1)S(1)}, u32[]{:S(2)}, u32[]{:S(2)}) collective-permute-start(bf16[128,2176]{1,0:T(8,128)(2,1)S(1)} %get-tuple-element.26.refs_0_), channel_id=1, source_target_pairs={{0,24},{1,7},{2,26},{3,1},{4,28},{5,3},{6,30},{7,5},{8,0},{9,15},{... | collective-permute-start | bytes 1671176 | tf_op jit(solution)/shard_map/ppermute | solution.py:320
  15.0 16.7 %collective-permute-start.1 = (bf16[128,2176]{1,0:T(8,128)(2,1)S(1)}, bf16[128,2176]{1,0:T(8,128)(2,1)S(1)}, u32[]{:S(2)}, u32[]{:S(2)}) collective-permute-start(bf16[128,2176]{1,0:T(8,128)(2,1)S(1)} %get-tuple-element.26.refs_0_), channel_id=1, source_target_pairs={{0,8},{1,3},{2,10},{3,5},{4,12},{5,7},{6,14},{7,1},{8,16},{9,11},{... | collective-permute-start | bytes 1671176 | tf_op jit(solution)/shard_map/ppermute | solution.py:320
  15.6 19.9 %collective-permute-start.4 = (bf16[160,2048]{1,0:T(8,128)(2,1)S(1)}, bf16[160,2048]{1,0:T(8,128)(2,1)S(1)}, u32[]{:S(2)}, u32[]{:S(2)}) collective-permute-start(bf16[160,2048]{1,0:T(8,128)(2,1)S(1)} %get-tuple-element.30), channel_id=1, source_target_pairs={{0,2},{1,9},{2,4},{3,11},{4,6},{5,13},{6,0},{7,15},{8,10},{9,17},{... | collective-permute-start | bytes 1966088 | tf_op jit(solution)/shard_map/ppermute | solution.py:320
  17.3 18.3 %collective-permute-start.6 = (bf16[160,2048]{1,0:T(8,128)(2,1)S(1)}, bf16[160,2048]{1,0:T(8,128)(2,1)S(1)}, u32[]{:S(2)}, u32[]{:S(2)}) collective-permute-start(bf16[160,2048]{1,0:T(8,128)(2,1)S(1)} %get-tuple-element.32), channel_id=1, source_target_pairs={{0,6},{1,25},{2,0},{3,27},{4,2},{5,29},{6,4},{7,31},{8,14},{9,1},{... | collective-permute-start | bytes 1966088 | tf_op jit(solution)/shard_map/ppermute | solution.py:320
  32.3 10.7 %collective-permute-start.5 = (bf16[160,2048]{1,0:T(8,128)(2,1)S(1)}, bf16[160,2048]{1,0:T(8,128)(2,1)S(1)}, u32[]{:S(2)}, u32[]{:S(2)}) collective-permute-start(bf16[160,2048]{1,0:T(8,128)(2,1)S(1)} %get-tuple-element.31), channel_id=1, source_target_pairs={{0,2},{1,9},{2,4},{3,11},{4,6},{5,13},{6,0},{7,15},{8,10},{9,17},{... | collective-permute-start | bytes 1966088 | tf_op jit(solution)/shard_map/ppermute | solution.py:320
  34.0 10.6 %collective-permute-start.7 = (bf16[160,2048]{1,0:T(8,128)(2,1)S(1)}, bf16[160,2048]{1,0:T(8,128)(2,1)S(1)}, u32[]{:S(2)}, u32[]{:S(2)}) collective-permute-start(bf16[160,2048]{1,0:T(8,128)(2,1)S(1)} %get-tuple-element.33), channel_id=1, source_target_pairs={{0,6},{1,25},{2,0},{3,27},{4,2},{5,29},{6,4},{7,31},{8,14},{9,1},{... | collective-permute-start | bytes 1966088 | tf_op jit(solution)/shard_map/ppermute | solution.py:320
  44.6 19.2 %collective-permute-start.9 = (bf16[320,2048]{1,0:T(8,128)(2,1)S(1)}, bf16[320,2048]{1,0:T(8,128)(2,1)S(1)}, u32[]{:S(2)}, u32[]{:S(2)}) collective-permute-start(bf16[320,2048]{1,0:T(8,128)(2,1)S(1)} %get-tuple-element.36), channel_id=1, source_target_pairs={{0,4},{1,17},{2,6},{3,19},{4,0},{5,21},{6,2},{7,23},{8,12},{9,25},... | collective-permute-start | bytes 3932168 | tf_op jit(solution)/shard_map/ppermute | solution.py:320
  52.8 24.9 %collective-permute-start.8 = (bf16[320,2048]{1,0:T(8,128)(2,1)S(1)}, bf16[320,2048]{1,0:T(8,128)(2,1)S(1)}, u32[]{:S(2)}, u32[]{:S(2)}) collective-permute-start(bf16[320,2048]{1,0:T(8,128)(2,1)S(1)} %get-tuple-element.34), channel_id=1, source_target_pairs={{2,0},{9,1},{4,2},{11,3},{6,4},{13,5},{0,6},{15,7},{10,8},{17,9},{... | collective-permute-start | bytes 3932168 | tf_op jit(solution)/shard_map/ppermute | solution.py:320
  54.3 23.4 %collective-permute-start.11 = (bf16[320,2048]{1,0:T(8,128)(2,1)S(1)}, bf16[320,2048]{1,0:T(8,128)(2,1)S(1)}, u32[]{:S(2)}, u32[]{:S(2)}) collective-permute-start(bf16[320,2048]{1,0:T(8,128)(2,1)S(1)} %get-tuple-element.38), channel_id=1, source_target_pairs={{6,0},{25,1},{0,2},{27,3},{2,4},{29,5},{4,6},{31,7},{14,8},{1,9},{... | collective-permute-start | bytes 3932168 | tf_op jit(solution)/shard_map/ppermute | solution.py:320
  67.1 18.4 %collective-permute-start.10 = (bf16[160,2048]{1,0:T(8,128)(2,1)S(1)}, bf16[160,2048]{1,0:T(8,128)(2,1)S(1)}, u32[]{:S(2)}, u32[]{:S(2)}) collective-permute-start(bf16[160,2048]{1,0:T(8,128)(2,1)S(1)} %get-tuple-element.37), channel_id=1, source_target_pairs={{4,0},{17,1},{6,2},{19,3},{0,4},{21,5},{2,6},{23,7},{12,8},{25,9},... | collective-permute-start | bytes 1966088 | tf_op jit(solution)/shard_map/ppermute | solution.py:320
  77.7 21.9 %collective-permute-start.13 = (bf16[160,2048]{1,0:T(8,128)(2,1)S(1)}, bf16[160,2048]{1,0:T(8,128)(2,1)S(1)}, u32[]{:S(2)}, u32[]{:S(2)}) collective-permute-start(bf16[160,2048]{1,0:T(8,128)(2,1)S(1)} %get-tuple-element.42), channel_id=1, source_target_pairs={{4,0},{17,1},{6,2},{19,3},{0,4},{21,5},{2,6},{23,7},{12,8},{25,9},... | collective-permute-start | bytes 1966088 | tf_op jit(solution)/shard_map/ppermute | solution.py:320
  87.0 16.2 %collective-permute-start.12 = (bf16[128,2048]{1,0:T(8,128)(2,1)S(1)}, bf16[128,2048]{1,0:T(8,128)(2,1)S(1)}, u32[]{:S(2)}, u32[]{:S(2)}) collective-permute-start(bf16[128,2048]{1,0:T(8,128)(2,1)S(1)} %get-tuple-element.40), channel_id=1, source_target_pairs={{16,0},{5,1},{18,2},{7,3},{20,4},{1,5},{22,6},{3,7},{24,8},{13,9},... | collective-permute-start | bytes 1572872 | tf_op jit(solution)/shard_map/ppermute | solution.py:320
  101.1 9.3 %collective-permute-start.14 = (bf16[128,2048]{1,0:T(8,128)(2,1)S(1)}, bf16[128,2048]{1,0:T(8,128)(2,1)S(1)}, u32[]{:S(2)}, u32[]{:S(2)}) collective-permute-start(bf16[128,2048]{1,0:T(8,128)(2,1)S(1)} %get-tuple-element.43), channel_id=1, source_target_pairs={{8,0},{3,1},{10,2},{5,3},{12,4},{7,5},{14,6},{1,7},{16,8},{11,9},{... | collective-permute-start | bytes 1572872 | tf_op jit(solution)/shard_map/ppermute | solution.py:320
  101.2 10.5 %collective-permute-start.15 = (bf16[128,2048]{1,0:T(8,128)(2,1)S(1)}, bf16[128,2048]{1,0:T(8,128)(2,1)S(1)}, u32[]{:S(2)}, u32[]{:S(2)}) collective-permute-start(bf16[128,2048]{1,0:T(8,128)(2,1)S(1)} %get-tuple-element.44), channel_id=1, source_target_pairs={{24,0},{7,1},{26,2},{1,3},{28,4},{3,5},{30,6},{5,7},{0,8},{15,9},{... | collective-permute-start | bytes 1572872 | tf_op jit(solution)/shard_map/ppermute | solution.py:320

commit v8 on v7

--- a/solution.py
+++ b/solution.py
@@ -320,28 +320,28 @@
     send = lambda v, pairs: lax.ppermute(v, "expert", pairs)
     after = lambda v, other: lax.optimization_barrier((v, other))[0]
     home, q = prep(expert_ids.T, gate_weights.T, tokens)
-    moved = {j: send(home, spread_pairs(j)) for j in (1, 3, 2)}
+    moved = {j: send(home, spread_pairs(j)) for j in (1, 2, 3)}
     pairs = [[home, moved[2]], [moved[1], moved[3]]]
-    near = [pack((1, 3), q, pair) for pair in pairs]
     bundle = hold(w_gate, w_up, w_down)
-    weights = [bundle, send(after(bundle, moved[2]), swap_pairs())]
-
-    arrived = {k: [send(slabs[n], deliver_pairs(k)) for slabs in near] for n, k in enumerate((1, 3))}
+
+    near = pack((1, 3), q, pairs[0] + pairs[1])
+    weights = [bundle, send(after(bundle, near[0]), swap_pairs())]
+    arrived = {k: send(slab, deliver_pairs(k)) for k, slab in zip((1, 3), near)}
     stay, far = pack((0, 2), q, pairs[0] + pairs[1])
     backs = {}
     (backs[0],) = expert([stay], weights, 1)
-    arrived[2] = [send(after(far, (arrived[1], arrived[3])), deliver_pairs(2))]
-    for k, slab in zip((1, 3), expert(arrived[1] + arrived[3], weights, 2)):
+    arrived[2] = send(after(far, (arrived[1], arrived[3])), deliver_pairs(2))
+    for k, slab in zip((1, 3), expert([arrived[1], arrived[3]], weights, 2)):
         backs[k] = send(slab, back(deliver_pairs(k)))
-    early, late = expert(arrived[2], weights, 2)
+    late, early = expert([arrived[2]], weights, 2)
     early = send(early, back(deliver_pairs(2)))
     late = send(after(late, (backs[1], backs[3])), back(deliver_pairs(2)))
 
     whole = [backs[k] for k in (0, 1)]
-    part0, part2 = combine(q, pairs[0], [*whole, early, backs[3]], (0, 0, 0, 0), (jnp.float32, jnp.bfloat16))
-    part1, part3 = combine(q, pairs[1], [*whole, late, backs[3]], (1, 1, 0, 1), (jnp.bfloat16, jnp.bfloat16))
+    part1, part3 = combine(q, pairs[1], [*whole, early, backs[3]], (1, 1, 0, 1), (jnp.bfloat16, jnp.bfloat16))
+    part0, part2 = combine(q, pairs[0], [*whole, late, backs[3]], (0, 0, 0, 0), (jnp.float32, jnp.bfloat16))
     mixed = part0
-    for j, part in ((2, part2), (1, part1), (3, part3)):
+    for j, part in ((1, part1), (3, part3), (2, part2)):
         mixed = mixed + send(part, back(spread_pairs(j))).astype(jnp.float32)
     return mixed.astype(jnp.bfloat16)
 

time: 113 us -> 109 us (0.965)
  the two profiles are of different devices: /device:TPU:104 before, /device:TPU:96 now
where the time goes in v8:
time: 109 us
  waiting for transfers between devices  71.5 us (66%)
  Pallas kernels  23.4 us (21%)
  starting transfers between devices  12.7 us (12%)
  other arithmetic  1.1 us (1%)
    ppermute x14, waiting for transfers between devices, per_device(): send = lambda v, pairs: lax.ppermute(v, 'expert', pairs)  71.5 us
    pallas_call x3, Pallas kernels, expert(): pl.pallas_call(functools.partial(expert_kernel, count, ff), in_specs=[vme...  12.8 us
    ppermute x14, starting transfers between devices, per_device(): send = lambda v, pairs: lax.ppermute(v, 'expert', pairs)  12.7 us
    pallas_call x1, Pallas kernels, hold(): pl.pallas_call(hold_kernel, in_specs=[pl.BlockSpec(memory_space=pl.ANY)]...  4.33 us
    pallas_call x2, Pallas kernels, combine(): pl.pallas_call(functools.partial(combine_kernel, spots), in_specs=[vmem]...  3.04 us
    pallas_call x2, Pallas kernels, pack(): pl.pallas_call(functools.partial(pack_kernel, which), in_specs=[vmem] * (...  2.19 us
  transfers between devices with their start and end apart: 14, of which 10 were waited for; matrix products, arithmetic and copies ran while one was open for 0% of the time, Pallas kernels for 20%

profile of v8, /device:TPU:96, one launch (start us, length us, event | category | flops | bytes accessed | tf_op | source)
XLA Modules:
  0.0 108.9 jit_solution(6602704053970278206)
XLA Ops:
  0.0 1.1 %prep.1 = (bf16[128,2176]{1,0:T(8,128)(2,1)S(1)}, bf16[2,16,128]{2,1,0:T(8,128)(2,1)S(1)}) custom-call(s32[8,128]{1,0:T(8,128)} %bitcast.2, f32[8,128]{1,0:T(8,128)} %bitcast.3, bf16[128,2048]{1,0:T(8,128)(2,1)} %tok_hbm.1), custom_call_target="tpu_custom_call" | custom-call | flops 1048576 | bytes 1048576 | tf_op jit(solution)/shard_map/prep/pallas_call | solution.py:92
  1.1 2.8 %collective-permute-start.2 = (bf16[128,2176]{1,0:T(8,128)(2,1)S(1)}, bf16[128,2176]{1,0:T(8,128)(2,1)S(1)}, u32[]{:S(2)}, u32[]{:S(2)}) collective-permute-start(bf16[128,2176]{1,0:T(8,128)(2,1)S(1)} %get-tuple-element.24.refs_0_), channel_id=1, source_target_pairs={{0,24},{1,7},{2,26},{3,1},{4,28},{5,3},{6,30},{7,5},{8,0},{9,15},{... | collective-permute-start | bytes 1671176 | tf_op jit(solution)/shard_map/ppermute | solution.py:320
  3.9 0.0 collective-permute-start.1
  3.9 2.3 %collective-permute-start = (bf16[128,2176]{1,0:T(8,128)(2,1)S(1)}, bf16[128,2176]{1,0:T(8,128)(2,1)S(1)}, u32[]{:S(2)}, u32[]{:S(2)}) collective-permute-start(bf16[128,2176]{1,0:T(8,128)(2,1)S(1)} %get-tuple-element.24.refs_0_), channel_id=1, source_target_pairs={{0,16},{1,5},{2,18},{3,7},{4,20},{5,1},{6,22},{7,3},{8,24},{9,13},... | collective-permute-start | bytes 1671176 | tf_op jit(solution)/shard_map/ppermute | solution.py:320
  6.2 4.3 %hold.1 = (bf16[3072,1536]{1,0:T(8,128)(2,1)S(1)}, f32[8,128]{1,0:T(8,128)}) custom-call(bf16[1,2048,768]{2,1,0:T(8,128)(2,1)} %wg.1, bf16[1,2048,768]{2,1,0:T(8,128)(2,1)} %wu.1, bf16[1,768,2048]{2,1,0:T(8,128)(2,1)} %wd.1), custom_call_target="tpu_custom_call" | custom-call | bytes 18874368 | tf_op jit(solution)/shard_map/hold/pallas_call | solution.py:304
  10.6 6.4 %collective-permute-done.2.refs_3_.refs_1_ = bf16[128,2176]{1,0:T(8,128)(2,1)S(1)} collective-permute-done((bf16[128,2176]{1,0:T(8,128)(2,1)S(1)}, bf16[128,2176]{1,0:T(8,128)(2,1)S(1)}, u32[]{:S(2)}, u32[]{:S(2)}) %collective-permute-start.2) | collective-permute-done | bytes 557088 | tf_op jit(solution)/shard_map/ppermute | solution.py:320
  17.0 3.7 %collective-permute-done.1.refs_2_.refs_0_ = bf16[128,2176]{1,0:T(8,128)(2,1)S(1)} collective-permute-done((bf16[128,2176]{1,0:T(8,128)(2,1)S(1)}, bf16[128,2176]{1,0:T(8,128)(2,1)S(1)}, u32[]{:S(2)}, u32[]{:S(2)}) %collective-permute-start.1) | collective-permute-done | bytes 557088 | tf_op jit(solution)/shard_map/ppermute | solution.py:320
  20.7 0.0 collective-permute-done.refs_1_
  20.7 1.1 %pack.3 = (bf16[320,2048]{1,0:T(8,128)(2,1)S(1)}, bf16[320,2048]{1,0:T(8,128)(2,1)S(1)}) custom-call(bf16[2,16,128]{2,1,0:T(8,128)(2,1)S(1)} %get-tuple-element.23.q_ref, bf16[128,2176]{1,0:T(8,128)(2,1)S(1)} %get-tuple-element.24.refs_0_, bf16[128,2176]{1,0:T(8,128)(2,1)S(1)} %collective-permute-done.refs_1_, ...), custom_call_target="tpu_custom_call" | custom-call | flops 671088640 | bytes 4718592 | tf_op jit(solution)/shard_map/pack/pallas_call | solution.py:159
  21.8 0.1 collective-permute-start.3
  21.9 3.1 %collective-permute-start.5 = (bf16[320,2048]{1,0:T(8,128)(2,1)S(1)}, bf16[320,2048]{1,0:T(8,128)(2,1)S(1)}, u32[]{:S(2)}, u32[]{:S(2)}) collective-permute-start(bf16[320,2048]{1,0:T(8,128)(2,1)S(1)} %get-tuple-element.29), channel_id=1, source_target_pairs={{0,6},{1,25},{2,0},{3,27},{4,2},{5,29},{6,4},{7,31},{8,14},{9,1},{... | collective-permute-start | bytes 3932168 | tf_op jit(solution)/shard_map/ppermute | solution.py:320
  25.0 0.0 collective-permute-start.4
  25.0 1.1 %pack.2 = (bf16[320,2048]{1,0:T(8,128)(2,1)S(1)}, bf16[320,2048]{1,0:T(8,128)(2,1)S(1)}) custom-call(bf16[2,16,128]{2,1,0:T(8,128)(2,1)S(1)} %get-tuple-element.23.q_ref, bf16[128,2176]{1,0:T(8,128)(2,1)S(1)} %get-tuple-element.24.refs_0_, bf16[128,2176]{1,0:T(8,128)(2,1)S(1)} %collective-permute-done.refs_1_, ...), custom_call_target="tpu_custom_call" | custom-call | flops 671088640 | bytes 4718592 | tf_op jit(solution)/shard_map/pack/pallas_call | solution.py:159
  26.1 14.0 %collective-permute-done.5.refs_1_ = bf16[320,2048]{1,0:T(8,128)(2,1)S(1)} collective-permute-done((bf16[320,2048]{1,0:T(8,128)(2,1)S(1)}, bf16[320,2048]{1,0:T(8,128)(2,1)S(1)}, u32[]{:S(2)}, u32[]{:S(2)}) %collective-permute-start.5) | collective-permute-done | bytes 1310752 | tf_op jit(solution)/shard_map/ppermute | solution.py:320
  40.1 3.7 %collective-permute-done.4.refs_0_ = bf16[320,2048]{1,0:T(8,128)(2,1)S(1)} collective-permute-done((bf16[320,2048]{1,0:T(8,128)(2,1)S(1)}, bf16[320,2048]{1,0:T(8,128)(2,1)S(1)}, u32[]{:S(2)}, u32[]{:S(2)}) %collective-permute-start.4) | collective-permute-done | bytes 1310752 | tf_op jit(solution)/shard_map/ppermute | solution.py:320
  43.8 0.0 collective-permute-start.7
  43.8 0.0 collective-permute-done.3.refs_2_.refs_3_
  43.8 6.3 %expert.4 = (bf16[320,2048]{1,0:T(8,128)(2,1)S(1)}, bf16[320,2048]{1,0:T(8,128)(2,1)S(1)}) custom-call(bf16[320,2048]{1,0:T(8,128)(2,1)S(1)} %collective-permute-done.4.refs_0_, bf16[320,2048]{1,0:T(8,128)(2,1)S(1)} %collective-permute-done.5.refs_1_, bf16[3072,1536]{1,0:T(8,128)(2,1)S(1)} %get-tuple-element.28.refs_1_.refs_2_, ...), custom_call_target="tpu_custom_call" | custom-call | flops 6039797760 | bytes 5242880 | tf_op jit(solution)/shard_map/expert/pallas_call | solution.py:265
  50.1 1.5 %collective-permute-start.6 = (bf16[320,2048]{1,0:T(8,128)(2,1)S(1)}, bf16[320,2048]{1,0:T(8,128)(2,1)S(1)}, u32[]{:S(2)}, u32[]{:S(2)}) collective-permute-start(bf16[320,2048]{1,0:T(8,128)(2,1)S(1)} %get-tuple-element.30), channel_id=1, source_target_pairs={{2,0},{9,1},{4,2},{11,3},{6,4},{13,5},{0,6},{15,7},{10,8},{17,9},{... | collective-permute-start | bytes 3932168 | tf_op jit(solution)/shard_map/ppermute | solution.py:320
  51.6 0.6 collective-permute-start.8
  52.2 10.8 %collective-permute-done.7.refs_0_ = bf16[320,2048]{1,0:T(8,128)(2,1)S(1)} collective-permute-done((bf16[320,2048]{1,0:T(8,128)(2,1)S(1)}, bf16[320,2048]{1,0:T(8,128)(2,1)S(1)}, u32[]{:S(2)}, u32[]{:S(2)}) %collective-permute-start.7) | collective-permute-done | bytes 1310752 | tf_op jit(solution)/shard_map/ppermute | solution.py:320
  63.0 3.3 %expert.5 = (bf16[160,2048]{1,0:T(8,128)(2,1)S(1)}, bf16[160,2048]{1,0:T(8,128)(2,1)S(1)}) custom-call(bf16[320,2048]{1,0:T(8,128)(2,1)S(1)} %collective-permute-done.7.refs_0_, bf16[3072,1536]{1,0:T(8,128)(2,1)S(1)} %get-tuple-element.28.refs_1_.refs_2_, bf16[3072,1536]{1,0:T(8,128)(2,1)S(1)} %collective-permute-done.3.refs_2_.refs_3_), custom_call_target="tpu_custom_call" | custom-call | flops 3019898880 | bytes 2621440 | tf_op jit(solution)/shard_map/expert/pallas_call | solution.py:265
  66.3 0.1 collective-permute-start.10
  66.4 8.0 %collective-permute-done.6.refs_3_ = bf16[320,2048]{1,0:T(8,128)(2,1)S(1)} collective-permute-done((bf16[320,2048]{1,0:T(8,128)(2,1)S(1)}, bf16[320,2048]{1,0:T(8,128)(2,1)S(1)}, u32[]{:S(2)}, u32[]{:S(2)}) %collective-permute-start.6) | collective-permute-done | bytes 1310752 | tf_op jit(solution)/shard_map/ppermute | solution.py:320
  74.3 2.6 %collective-permute-done.8.refs_5_ = bf16[320,2048]{1,0:T(8,128)(2,1)S(1)} collective-permute-done((bf16[320,2048]{1,0:T(8,128)(2,1)S(1)}, bf16[320,2048]{1,0:T(8,128)(2,1)S(1)}, u32[]{:S(2)}, u32[]{:S(2)}) %collective-permute-start.8) | collective-permute-done | bytes 1310752 | tf_op jit(solution)/shard_map/ppermute | solution.py:320
  76.9 0.0 collective-permute-start.9
  76.9 3.3 %expert.3.refs_2_ = bf16[320,2048]{1,0:T(8,128)(2,1)S(1)} custom-call(bf16[320,2048]{1,0:T(8,128)(2,1)S(1)} %get-tuple-element.25.refs_0_, bf16[3072,1536]{1,0:T(8,128)(2,1)S(1)} %get-tuple-element.28.refs_1_.refs_2_, bf16[3072,1536]{1,0:T(8,128)(2,1)S(1)} %collective-permute-done.3.refs_2_.refs_3_), custom_call_target="tpu_custom_call" | custom-call | flops 3019898880 | bytes 2621440 | tf_op jit(solution)/shard_map/expert/pallas_call | solution.py:265
  80.2 3.8 %collective-permute-done.10.refs_4_ = bf16[160,2048]{1,0:T(8,128)(2,1)S(1)} collective-permute-done((bf16[160,2048]{1,0:T(8,128)(2,1)S(1)}, bf16[160,2048]{1,0:T(8,128)(2,1)S(1)}, u32[]{:S(2)}, u32[]{:S(2)}) %collective-permute-start.10) | collective-permute-done | bytes 655392 | tf_op jit(solution)/shard_map/ppermute | solution.py:320
  84.0 1.5 %combine.3 = (bf16[128,2048]{1,0:T(8,128)(2,1)S(1)}, bf16[128,2048]{1,0:T(8,128)(2,1)S(1)}) custom-call(bf16[2,16,128]{2,1,0:T(8,128)(2,1)S(1)} %get-tuple-element.23.q_ref, bf16[128,2176]{1,0:T(8,128)(2,1)S(1)} %collective-permute-done.1.refs_2_.refs_0_, bf16[128,2176]{1,0:T(8,128)(2,1)S(1)} %collective-permute-done.2.refs_3_.refs_1_, ...), custom_call_target="tpu_custom_call" | custom-call | flops 671088640 | bytes 4194304 | tf_op jit(solution)/shard_map/combine/pallas_call | solution.py:216
  85.5 0.1 collective-permute-start.11
  85.6 2.0 %collective-permute-start.12 = (bf16[128,2048]{1,0:T(8,128)(2,1)S(1)}, bf16[128,2048]{1,0:T(8,128)(2,1)S(1)}, u32[]{:S(2)}, u32[]{:S(2)}) collective-permute-start(bf16[128,2048]{1,0:T(8,128)(2,1)S(1)} %get-tuple-element.39), channel_id=1, source_target_pairs={{24,0},{7,1},{26,2},{1,3},{28,4},{3,5},{30,6},{5,7},{0,8},{15,9},{... | collective-permute-start | bytes 1572872 | tf_op jit(solution)/shard_map/ppermute | solution.py:320
  87.6 7.9 %collective-permute-done.9.refs_4_ = bf16[160,2048]{1,0:T(8,128)(2,1)S(1)} collective-permute-done((bf16[160,2048]{1,0:T(8,128)(2,1)S(1)}, bf16[160,2048]{1,0:T(8,128)(2,1)S(1)}, u32[]{:S(2)}, u32[]{:S(2)}) %collective-permute-start.9) | collective-permute-done | bytes 655392 | tf_op jit(solution)/shard_map/ppermute | solution.py:320
  95.5 1.5 %combine.2 = (f32[128,2048]{1,0:T(8,128)S(1)}, bf16[128,2048]{1,0:T(8,128)(2,1)S(1)}) custom-call(bf16[2,16,128]{2,1,0:T(8,128)(2,1)S(1)} %get-tuple-element.23.q_ref, bf16[128,2176]{1,0:T(8,128)(2,1)S(1)} %get-tuple-element.24.refs_0_, bf16[128,2176]{1,0:T(8,128)(2,1)S(1)} %collective-permute-done.refs_1_, bf16[320,2048]{1,0:T(8,128)(2,1)S(1)} %expert.3.refs_2_, ...), custom_call_target="tpu_custom_call" | custom-call | flops 671088640 | bytes 4194304 | tf_op jit(solution)/shard_map/combine/pallas_call | solution.py:216
  97.1 0.1 collective-permute-start.13
  97.2 0.0 collective-permute-done.11
  97.2 0.0 collective-permute-done.12
  97.2 10.7 %collective-permute-done.13 = bf16[128,2048]{1,0:T(8,128)(2,1)S(1)} collective-permute-done((bf16[128,2048]{1,0:T(8,128)(2,1)S(1)}, bf16[128,2048]{1,0:T(8,128)(2,1)S(1)}, u32[]{:S(2)}, u32[]{:S(2)}) %collective-permute-start.13) | collective-permute-done | bytes 524320 | tf_op jit(solution)/shard_map/ppermute | solution.py:320
  107.8 1.1 %add_convert_fusion = bf16[128,2048]{1,0:T(8,128)(2,1)} fusion(bf16[128,2048]{1,0:T(8,128)(2,1)S(1)} %collective-permute-done.13, bf16[128,2048]{1,0:T(8,128)(2,1)S(1)} %collective-permute-done.12, f32[128,2048]{1,0:T(8,128)S(1)} %get-tuple-element.36, bf16[128,2048]{1,0:T(8,128)(2,1)S(1)} %collective-permute-done.11), kind=kLoop, calls=%fused_computation | loop fusion | flops 1835008 | bytes 3145728 | tf_op jit(solution)/shard_map/convert_element_type | solution.py:346
Async XLA Ops:
  1.1 15.9 %collective-permute-start.2 = (bf16[128,2176]{1,0:T(8,128)(2,1)S(1)}, bf16[128,2176]{1,0:T(8,128)(2,1)S(1)}, u32[]{:S(2)}, u32[]{:S(2)}) collective-permute-start(bf16[128,2176]{1,0:T(8,128)(2,1)S(1)} %get-tuple-element.24.refs_0_), channel_id=1, source_target_pairs={{0,24},{1,7},{2,26},{3,1},{4,28},{5,3},{6,30},{7,5},{8,0},{9,15},{... | collective-permute-start | bytes 1671176 | tf_op jit(solution)/shard_map/ppermute | solution.py:320
  3.9 16.7 %collective-permute-start.1 = (bf16[128,2176]{1,0:T(8,128)(2,1)S(1)}, bf16[128,2176]{1,0:T(8,128)(2,1)S(1)}, u32[]{:S(2)}, u32[]{:S(2)}) collective-permute-start(bf16[128,2176]{1,0:T(8,128)(2,1)S(1)} %get-tuple-element.24.refs_0_), channel_id=1, source_target_pairs={{0,8},{1,3},{2,10},{3,5},{4,12},{5,7},{6,14},{7,1},{8,16},{9,11},{... | collective-permute-start | bytes 1671176 | tf_op jit(solution)/shard_map/ppermute | solution.py:320
  3.9 16.7 %collective-permute-start = (bf16[128,2176]{1,0:T(8,128)(2,1)S(1)}, bf16[128,2176]{1,0:T(8,128)(2,1)S(1)}, u32[]{:S(2)}, u32[]{:S(2)}) collective-permute-start(bf16[128,2176]{1,0:T(8,128)(2,1)S(1)} %get-tuple-element.24.refs_0_), channel_id=1, source_target_pairs={{0,16},{1,5},{2,18},{3,7},{4,20},{5,1},{6,22},{7,3},{8,24},{9,13},... | collective-permute-start | bytes 1671176 | tf_op jit(solution)/shard_map/ppermute | solution.py:320
  21.8 22.0 %collective-permute-start.3 = (bf16[3072,1536]{1,0:T(8,128)(2,1)S(1)}, bf16[3072,1536]{1,0:T(8,128)(2,1)S(1)}, u32[]{:S(2)}, u32[]{:S(2)}) collective-permute-start(bf16[3072,1536]{1,0:T(8,128)(2,1)S(1)} %get-tuple-element.28.refs_1_.refs_2_), channel_id=1, source_target_pairs={{0,1},{1,0},{2,3},{3,2},{4,5},{5,4},{6,7},{7,6},{8,9},{9,8},{10,11... | collective-permute-start | bytes 28311560 | tf_op jit(solution)/shard_map/ppermute | solution.py:320
  21.9 18.2 %collective-permute-start.5 = (bf16[320,2048]{1,0:T(8,128)(2,1)S(1)}, bf16[320,2048]{1,0:T(8,128)(2,1)S(1)}, u32[]{:S(2)}, u32[]{:S(2)}) collective-permute-start(bf16[320,2048]{1,0:T(8,128)(2,1)S(1)} %get-tuple-element.29), channel_id=1, source_target_pairs={{0,6},{1,25},{2,0},{3,27},{4,2},{5,29},{6,4},{7,31},{8,14},{9,1},{... | collective-permute-start | bytes 3932168 | tf_op jit(solution)/shard_map/ppermute | solution.py:320
  25.0 18.8 %collective-permute-start.4 = (bf16[320,2048]{1,0:T(8,128)(2,1)S(1)}, bf16[320,2048]{1,0:T(8,128)(2,1)S(1)}, u32[]{:S(2)}, u32[]{:S(2)}) collective-permute-start(bf16[320,2048]{1,0:T(8,128)(2,1)S(1)} %get-tuple-element.27), channel_id=1, source_target_pairs={{0,2},{1,9},{2,4},{3,11},{4,6},{5,13},{6,0},{7,15},{8,10},{9,17},{... | collective-permute-start | bytes 3932168 | tf_op jit(solution)/shard_map/ppermute | solution.py:320
  43.8 19.2 %collective-permute-start.7 = (bf16[320,2048]{1,0:T(8,128)(2,1)S(1)}, bf16[320,2048]{1,0:T(8,128)(2,1)S(1)}, u32[]{:S(2)}, u32[]{:S(2)}) collective-permute-start(bf16[320,2048]{1,0:T(8,128)(2,1)S(1)} %get-tuple-element.32), channel_id=1, source_target_pairs={{0,4},{1,17},{2,6},{3,19},{4,0},{5,21},{6,2},{7,23},{8,12},{9,25},... | collective-permute-start | bytes 3932168 | tf_op jit(solution)/shard_map/ppermute | solution.py:320
  50.1 24.2 %collective-permute-start.6 = (bf16[320,2048]{1,0:T(8,128)(2,1)S(1)}, bf16[320,2048]{1,0:T(8,128)(2,1)S(1)}, u32[]{:S(2)}, u32[]{:S(2)}) collective-permute-start(bf16[320,2048]{1,0:T(8,128)(2,1)S(1)} %get-tuple-element.30), channel_id=1, source_target_pairs={{2,0},{9,1},{4,2},{11,3},{6,4},{13,5},{0,6},{15,7},{10,8},{17,9},{... | collective-permute-start | bytes 3932168 | tf_op jit(solution)/shard_map/ppermute | solution.py:320
  51.6 25.3 %collective-permute-start.8 = (bf16[320,2048]{1,0:T(8,128)(2,1)S(1)}, bf16[320,2048]{1,0:T(8,128)(2,1)S(1)}, u32[]{:S(2)}, u32[]{:S(2)}) collective-permute-start(bf16[320,2048]{1,0:T(8,128)(2,1)S(1)} %get-tuple-element.34), channel_id=1, source_target_pairs={{6,0},{25,1},{0,2},{27,3},{2,4},{29,5},{4,6},{31,7},{14,8},{1,9},{... | collective-permute-start | bytes 3932168 | tf_op jit(solution)/shard_map/ppermute | solution.py:320
  66.3 17.7 %collective-permute-start.10 = (bf16[160,2048]{1,0:T(8,128)(2,1)S(1)}, bf16[160,2048]{1,0:T(8,128)(2,1)S(1)}, u32[]{:S(2)}, u32[]{:S(2)}) collective-permute-start(bf16[160,2048]{1,0:T(8,128)(2,1)S(1)} %get-tuple-element.37), channel_id=1, source_target_pairs={{4,0},{17,1},{6,2},{19,3},{0,4},{21,5},{2,6},{23,7},{12,8},{25,9},... | collective-permute-start | bytes 1966088 | tf_op jit(solution)/shard_map/ppermute | solution.py:320
  76.9 18.6 %collective-permute-start.9 = (bf16[160,2048]{1,0:T(8,128)(2,1)S(1)}, bf16[160,2048]{1,0:T(8,128)(2,1)S(1)}, u32[]{:S(2)}, u32[]{:S(2)}) collective-permute-start(bf16[160,2048]{1,0:T(8,128)(2,1)S(1)} %get-tuple-element.35), channel_id=1, source_target_pairs={{4,0},{17,1},{6,2},{19,3},{0,4},{21,5},{2,6},{23,7},{12,8},{25,9},... | collective-permute-start | bytes 1966088 | tf_op jit(solution)/shard_map/ppermute | solution.py:320
  85.5 11.6 %collective-permute-start.11 = (bf16[128,2048]{1,0:T(8,128)(2,1)S(1)}, bf16[128,2048]{1,0:T(8,128)(2,1)S(1)}, u32[]{:S(2)}, u32[]{:S(2)}) collective-permute-start(bf16[128,2048]{1,0:T(8,128)(2,1)S(1)} %get-tuple-element.38), channel_id=1, source_target_pairs={{8,0},{3,1},{10,2},{5,3},{12,4},{7,5},{14,6},{1,7},{16,8},{11,9},{... | collective-permute-start | bytes 1572872 | tf_op jit(solution)/shard_map/ppermute | solution.py:320
  85.6 11.5 %collective-permute-start.12 = (bf16[128,2048]{1,0:T(8,128)(2,1)S(1)}, bf16[128,2048]{1,0:T(8,128)(2,1)S(1)}, u32[]{:S(2)}, u32[]{:S(2)}) collective-permute-start(bf16[128,2048]{1,0:T(8,128)(2,1)S(1)} %get-tuple-element.39), channel_id=1, source_target_pairs={{24,0},{7,1},{26,2},{1,3},{28,4},{3,5},{30,6},{5,7},{0,8},{15,9},{... | collective-permute-start | bytes 1572872 | tf_op jit(solution)/shard_map/ppermute | solution.py:320
  97.1 10.8 %collective-permute-start.13 = (bf16[128,2048]{1,0:T(8,128)(2,1)S(1)}, bf16[128,2048]{1,0:T(8,128)(2,1)S(1)}, u32[]{:S(2)}, u32[]{:S(2)}) collective-permute-start(bf16[128,2048]{1,0:T(8,128)(2,1)S(1)} %get-tuple-element.40), channel_id=1, source_target_pairs={{16,0},{5,1},{18,2},{7,3},{20,4},{1,5},{22,6},{3,7},{24,8},{13,9},... | collective-permute-start | bytes 1572872 | tf_op jit(solution)/shard_map/ppermute | solution.py:320

commit v9 on v8

--- a/solution.py
+++ b/solution.py
@@ -121,7 +121,7 @@
 
 def pack_kernel(which, q_ref, *refs):
     outs = refs[len(refs) - len(which) :]
-    blocks = refs[: len(refs) - len(which)]
+    blocks = [refs[n] for n in (0, 3, 2, 1)]
     tok = blocks[0].shape[0]
     width = outs[0].shape[1]
     q = q_ref[0]
@@ -168,22 +168,25 @@
             transcendentals=0,
         ),
         name="pack",
-    )(q, *blocks)
-
-
-def combine_kernel(spots, q_ref, *refs):
-    pair, backs, outs = refs[:2], refs[2:6], refs[6:]
+    )(q, *[blocks[n] for n in (0, 3, 2, 1)])
+
+
+def combine_kernel(which, q_ref, *refs):
+    count = len(which)
+    blocks, backs, sums, outs = refs[:4], refs[4 : 4 + count], refs[4 + count : -4], refs[-4:]
+    blocks = [blocks[n] for n in (0, 3, 2, 1)]
     tok, width = outs[0].shape
     half = 2 * CAP
-    span = half * KF
+    places = [NC * k + f for k in which for f in range(NC)]
+    span = half * len(places)
     lane = lax.broadcasted_iota(jnp.int32, (2 * tok, span), 1)
     part = jnp.zeros((2 * tok, span), jnp.int32)
     er = lax.broadcasted_iota(jnp.int32, (16, span), 0)
     el = lax.broadcasted_iota(jnp.int32, (16, span), 1)
-    ep = jnp.zeros((16, span), jnp.int32)
-    for n in range(1, KF):
+    ep = jnp.full((16, span), places[0], jnp.int32)
+    for n in range(1, len(places)):
         part = jnp.where(lane >= half * n, half * n, part)
-        ep = jnp.where(el >= half * n, n, ep)
+        ep = jnp.where(el >= half * n, places[n], ep)
     r = lane - part
     t = lax.broadcasted_iota(jnp.int32, (2 * tok, span), 0)
     second = r >= CAP
@@ -196,36 +199,87 @@
             v.astype(jnp.bfloat16), expand, (((0,), (0,)), ((), ())), preferred_element_type=jnp.float32
         )
 
+    cols = 512
+    for p in range(2):
+        pair = blocks[2 * p : 2 * p + 2]
+        mix = jnp.where(widen(select(q_ref[0], pair)) == target, widen(select(q_ref[1], pair)), 0.0)
+        mix = mix.astype(jnp.bfloat16)
+        for at in range(0, width, cols):
+            rows = jnp.concatenate([b[2 * half * p : 2 * half * (p + 1), at : at + cols] for b in backs], axis=0)
+            got = jnp.dot(mix, rows, preferred_element_type=jnp.float32)
+            for n in range(2):
+                new = got[n * tok : (n + 1) * tok]
+                if sums:
+                    new = new + sums[2 * p + n][:, at : at + cols]
+                outs[2 * p + n][:, at : at + cols] = new.astype(outs[2 * p + n].dtype)
+
+
+def combine(which, q, blocks, backs, sums, dtypes):
+    tok = blocks[0].shape[0]
+    rows, width = backs[0].shape
+    vmem = pl.BlockSpec(memory_space=pltpu.VMEM)
+    return pl.pallas_call(
+        functools.partial(combine_kernel, which),
+        in_specs=[vmem] * (5 + len(backs) + len(sums)),
+        out_specs=[vmem] * 4,
+        out_shape=[jax.ShapeDtypeStruct((tok, width), d) for d in dtypes],
+        compiler_params=pltpu.CompilerParams(vmem_limit_bytes=16 * 1024 * 1024),
+        cost_estimate=pl.CostEstimate(
+            flops=2 * len(which) * rows * 2 * tok * width,
+            bytes_accessed=2 * (6 * tok + len(which) * rows) * width,
+            transcendentals=0,
+        ),
+        name="combine",
+    )(q, *[blocks[n] for n in (0, 3, 2, 1)], *backs, *sums)
+
+
+def finish_kernel(q_ref, *refs):
+    pair, back_ref, sums, outs = refs[:2], refs[2], refs[3:5], refs[5:]
+    tok, width = outs[0].shape
+    half = 2 * CAP
+    span = half * NC
+    lane = lax.broadcasted_iota(jnp.int32, (2 * tok, span), 1)
+    er = lax.broadcasted_iota(jnp.int32, (16, span), 0)
+    el = lax.broadcasted_iota(jnp.int32, (16, span), 1)
+    r = jnp.where(lane >= half, lane - half, lane)
+    t = lax.broadcasted_iota(jnp.int32, (2 * tok, span), 0)
+    second = r >= CAP
+    target = jnp.where(second, r - CAP, r)
+    target = jnp.where(second == (t >= tok), target, -5).astype(jnp.float32)
+    expand = jnp.where(er == jnp.where(el >= half, 2 * NC + 1, 2 * NC), 1.0, 0.0).astype(jnp.bfloat16)
+
+    def widen(v):
+        return lax.dot_general(
+            v.astype(jnp.bfloat16), expand, (((0,), (0,)), ((), ())), preferred_element_type=jnp.float32
+        )
+
     mix = jnp.where(widen(select(q_ref[0], pair)) == target, widen(select(q_ref[1], pair)), 0.0)
     mix = mix.astype(jnp.bfloat16)
     cols = 512
     for at in range(0, width, cols):
-        rows = jnp.concatenate(
-            [b[2 * half * p : 2 * half * (p + 1), at : at + cols] for b, p in zip(backs, spots)], axis=0
-        )
-        got = jnp.dot(mix, rows, preferred_element_type=jnp.float32)
-        for n, o in enumerate(outs):
-            o[:, at : at + cols] = got[n * tok : (n + 1) * tok].astype(o.dtype)
-
-
-def combine(q, pair, backs, spots, dtypes):
+        got = jnp.dot(mix, back_ref[:, at : at + cols], preferred_element_type=jnp.float32)
+        for n in range(2):
+            new = got[n * tok : (n + 1) * tok] + sums[n][:, at : at + cols]
+            outs[n][:, at : at + cols] = new.astype(outs[n].dtype)
+
+
+def finish(q, pair, slab, sums, dtypes):
     tok = pair[0].shape[0]
-    width = backs[0].shape[1]
-    rows = NC * 4 * CAP
+    rows, width = slab.shape
     vmem = pl.BlockSpec(memory_space=pltpu.VMEM)
     return pl.pallas_call(
-        functools.partial(combine_kernel, spots),
-        in_specs=[vmem] * 7,
+        finish_kernel,
+        in_specs=[vmem] * 6,
         out_specs=[vmem] * 2,
         out_shape=[jax.ShapeDtypeStruct((tok, width), d) for d in dtypes],
         compiler_params=pltpu.CompilerParams(vmem_limit_bytes=16 * 1024 * 1024),
         cost_estimate=pl.CostEstimate(
-            flops=2 * 2 * rows * 2 * tok * width,
-            bytes_accessed=2 * (3 * tok + 2 * rows) * width,
+            flops=2 * rows * 2 * tok * width,
+            bytes_accessed=2 * (6 * tok + rows) * width,
             transcendentals=0,
         ),
-        name="combine",
-    )(q, *pair, *backs)
+        name="finish",
+    )(q, *pair, slab, *sums)
 
 
 def halves(refs):
@@ -320,7 +374,7 @@
     send = lambda v, pairs: lax.ppermute(v, "expert", pairs)
     after = lambda v, other: lax.optimization_barrier((v, other))[0]
     home, q = prep(expert_ids.T, gate_weights.T, tokens)
-    moved = {j: send(home, spread_pairs(j)) for j in (1, 2, 3)}
+    moved = {j: send(home, spread_pairs(j)) for j in (1, 3, 2)}
     pairs = [[home, moved[2]], [moved[1], moved[3]]]
     bundle = hold(w_gate, w_up, w_down)
 
@@ -330,20 +384,26 @@
     stay, far = pack((0, 2), q, pairs[0] + pairs[1])
     backs = {}
     (backs[0],) = expert([stay], weights, 1)
-    arrived[2] = send(after(far, (arrived[1], arrived[3])), deliver_pairs(2))
+    arrived[2] = send(after(far, arrived[3]), deliver_pairs(2))
     for k, slab in zip((1, 3), expert([arrived[1], arrived[3]], weights, 2)):
         backs[k] = send(slab, back(deliver_pairs(k)))
-    late, early = expert([arrived[2]], weights, 2)
-    early = send(early, back(deliver_pairs(2)))
-    late = send(after(late, (backs[1], backs[3])), back(deliver_pairs(2)))
-
-    whole = [backs[k] for k in (0, 1)]
-    part1, part3 = combine(q, pairs[1], [*whole, early, backs[3]], (1, 1, 0, 1), (jnp.bfloat16, jnp.bfloat16))
-    part0, part2 = combine(q, pairs[0], [*whole, late, backs[3]], (0, 0, 0, 0), (jnp.float32, jnp.bfloat16))
-    mixed = part0
-    for j, part in ((1, part1), (3, part3), (2, part2)):
-        mixed = mixed + send(part, back(spread_pairs(j))).astype(jnp.float32)
-    return mixed.astype(jnp.bfloat16)
+    halves2 = expert([arrived[2]], weights, 2)
+    early = send(halves2[0], back(deliver_pairs(2)))
+    late = send(after(halves2[1], (backs[1], backs[3])), back(deliver_pairs(2)))
+
+    f32, bf16 = jnp.float32, jnp.bfloat16
+    sums = combine((0, 1, 3), q, pairs[0] + pairs[1], [backs[k] for k in (0, 1, 3)], [], [f32] * 4)
+    parts = {}
+    for p, slab in ((0, early), (1, late)):
+        kinds = (f32, bf16) if p == 0 else (bf16, bf16)
+        parts[p] = finish(q, pairs[p], slab, sums[2 * p : 2 * p + 2], kinds)
+    part0, part2 = parts[0]
+    part1, part3 = parts[1]
+    mixed = part0 + send(part2, back(spread_pairs(2))).astype(f32)
+    mixed = lax.optimization_barrier(mixed)
+    for j, part in ((1, part1), (3, part3)):
+        mixed = mixed + send(part, back(spread_pairs(j))).astype(f32)
+    return mixed.astype(bf16)
 
 
 def solution(mesh):

time: 109 us -> 104 us (0.954); the launches traced: 109 us -> 103 us
  waiting for transfers between devices: 71.5 us -> 56.2 us
  starting transfers between devices: 12.7 us -> 20.4 us
  Pallas kernels: 23.4 us -> 24.7 us
    ppermute x14, waiting for transfers between devices: 71.5 us -> 56.2 us  [per_device(): send = lambda v, pairs: lax.ppermute(v, 'expert', pairs)]
    ppermute x14, starting transfers between devices: 12.7 us -> 20.4 us  [per_device(): send = lambda v, pairs: lax.ppermute(v, 'expert', pairs)]
    pallas_call x2 -> x3, Pallas kernels: 3.04 us -> 4.33 us  [the longest x1 2.4 us: combine(): pl.pallas_call(functools.partial(combine_kernel, which), in_specs=[vmem]...]
  transfers between devices with their start and end apart: 14 -> 14, of which waited for: 10 -> 10; matrix products, arithmetic and copies ran while one was open for 0% -> 0% of each run, Pallas kernels for 20% -> 22%
where the time goes in v9:
time: 104 us; the launch traced here: 103 us
  waiting for transfers between devices  56.2 us (54%)
  Pallas kernels  24.7 us (24%)
  starting transfers between devices  20.4 us (20%)
  other arithmetic  1.09 us (1%)
    ppermute x14, waiting for transfers between devices, per_device(): send = lambda v, pairs: lax.ppermute(v, 'expert', pairs)  56.2 us
    ppermute x14, starting transfers between devices, per_device(): send = lambda v, pairs: lax.ppermute(v, 'expert', pairs)  20.4 us
    pallas_call x3, Pallas kernels, expert(): pl.pallas_call(functools.partial(expert_kernel, count, ff), in_specs=[vme...  12.8 us
    pallas_call x1, Pallas kernels, hold(): pl.pallas_call(hold_kernel, in_specs=[pl.BlockSpec(memory_space=pl.ANY)]...  4.33 us
    pallas_call x1, Pallas kernels, combine(): pl.pallas_call(functools.partial(combine_kernel, which), in_specs=[vmem]...  2.4 us
    pallas_call x2, Pallas kernels, pack(): pl.pallas_call(functools.partial(pack_kernel, which), in_specs=[vmem] * (...  2.19 us
  transfers between devices with their start and end apart: 14, of which 10 were waited for; matrix products, arithmetic and copies ran while one was open for 0% of the time, Pallas kernels for 22%

profile of v9, /device:TPU:96, one launch (start us, length us, event | category | flops | bytes accessed | tf_op | source)
XLA Modules:
  0.0 102.6 jit_solution(7826801816985170694)
XLA Ops:
  0.0 1.1 %prep.1 = (bf16[128,2176]{1,0:T(8,128)(2,1)S(1)}, bf16[2,16,128]{2,1,0:T(8,128)(2,1)S(1)}) custom-call(s32[8,128]{1,0:T(8,128)} %bitcast.2, f32[8,128]{1,0:T(8,128)} %bitcast.3, bf16[128,2048]{1,0:T(8,128)(2,1)} %tok_hbm.1), custom_call_target="tpu_custom_call" | custom-call | flops 1048576 | bytes 1048576 | tf_op jit(solution)/shard_map/prep/pallas_call | solution.py:92
  1.1 1.6 %collective-permute-start.2 = (bf16[128,2176]{1,0:T(8,128)(2,1)S(1)}, bf16[128,2176]{1,0:T(8,128)(2,1)S(1)}, u32[]{:S(2)}, u32[]{:S(2)}) collective-permute-start(bf16[128,2176]{1,0:T(8,128)(2,1)S(1)} %get-tuple-element.28.refs_0_), channel_id=1, source_target_pairs={{0,8},{1,3},{2,10},{3,5},{4,12},{5,7},{6,14},{7,1},{8,16},{9,11},{... | collective-permute-start | bytes 1671176 | tf_op jit(solution)/shard_map/ppermute | solution.py:374
  2.7 1.7 %collective-permute-start.1 = (bf16[128,2176]{1,0:T(8,128)(2,1)S(1)}, bf16[128,2176]{1,0:T(8,128)(2,1)S(1)}, u32[]{:S(2)}, u32[]{:S(2)}) collective-permute-start(bf16[128,2176]{1,0:T(8,128)(2,1)S(1)} %get-tuple-element.28.refs_0_), channel_id=1, source_target_pairs={{0,24},{1,7},{2,26},{3,1},{4,28},{5,3},{6,30},{7,5},{8,0},{9,15},{... | collective-permute-start | bytes 1671176 | tf_op jit(solution)/shard_map/ppermute | solution.py:374
  4.4 1.8 %collective-permute-start = (bf16[128,2176]{1,0:T(8,128)(2,1)S(1)}, bf16[128,2176]{1,0:T(8,128)(2,1)S(1)}, u32[]{:S(2)}, u32[]{:S(2)}) collective-permute-start(bf16[128,2176]{1,0:T(8,128)(2,1)S(1)} %get-tuple-element.28.refs_0_), channel_id=1, source_target_pairs={{0,16},{1,5},{2,18},{3,7},{4,20},{5,1},{6,22},{7,3},{8,24},{9,13},... | collective-permute-start | bytes 1671176 | tf_op jit(solution)/shard_map/ppermute | solution.py:374
  6.2 4.3 %hold.1 = (bf16[3072,1536]{1,0:T(8,128)(2,1)S(1)}, f32[8,128]{1,0:T(8,128)}) custom-call(bf16[1,2048,768]{2,1,0:T(8,128)(2,1)} %wg.1, bf16[1,2048,768]{2,1,0:T(8,128)(2,1)} %wu.1, bf16[1,768,2048]{2,1,0:T(8,128)(2,1)} %wd.1), custom_call_target="tpu_custom_call" | custom-call | bytes 18874368 | tf_op jit(solution)/shard_map/hold/pallas_call | solution.py:358
  10.6 1.4 %collective-permute-done.2.refs_2_.refs_0_ = bf16[128,2176]{1,0:T(8,128)(2,1)S(1)} collective-permute-done((bf16[128,2176]{1,0:T(8,128)(2,1)S(1)}, bf16[128,2176]{1,0:T(8,128)(2,1)S(1)}, u32[]{:S(2)}, u32[]{:S(2)}) %collective-permute-start.2) | collective-permute-done | bytes 557088 | tf_op jit(solution)/shard_map/ppermute | solution.py:374
  11.9 5.5 %collective-permute-done.1.refs_1_ = bf16[128,2176]{1,0:T(8,128)(2,1)S(1)} collective-permute-done((bf16[128,2176]{1,0:T(8,128)(2,1)S(1)}, bf16[128,2176]{1,0:T(8,128)(2,1)S(1)}, u32[]{:S(2)}, u32[]{:S(2)}) %collective-permute-start.1) | collective-permute-done | bytes 557088 | tf_op jit(solution)/shard_map/ppermute | solution.py:374
  17.5 1.4 %collective-permute-done.refs_3_.refs_1_ = bf16[128,2176]{1,0:T(8,128)(2,1)S(1)} collective-permute-done((bf16[128,2176]{1,0:T(8,128)(2,1)S(1)}, bf16[128,2176]{1,0:T(8,128)(2,1)S(1)}, u32[]{:S(2)}, u32[]{:S(2)}) %collective-permute-start) | collective-permute-done | bytes 557088 | tf_op jit(solution)/shard_map/ppermute | solution.py:374
  18.9 1.1 %pack.3 = (bf16[320,2048]{1,0:T(8,128)(2,1)S(1)}, bf16[320,2048]{1,0:T(8,128)(2,1)S(1)}) custom-call(bf16[2,16,128]{2,1,0:T(8,128)(2,1)S(1)} %get-tuple-element.27.q_ref, bf16[128,2176]{1,0:T(8,128)(2,1)S(1)} %get-tuple-element.28.refs_0_, bf16[128,2176]{1,0:T(8,128)(2,1)S(1)} %collective-permute-done.1.refs_1_, ...), custom_call_target="tpu_custom_call" | custom-call | flops 671088640 | bytes 4718592 | tf_op jit(solution)/shard_map/pack/pallas_call | solution.py:159
  20.0 0.1 collective-permute-start.5
  20.1 3.1 %collective-permute-start.3 = (bf16[320,2048]{1,0:T(8,128)(2,1)S(1)}, bf16[320,2048]{1,0:T(8,128)(2,1)S(1)}, u32[]{:S(2)}, u32[]{:S(2)}) collective-permute-start(bf16[320,2048]{1,0:T(8,128)(2,1)S(1)} %get-tuple-element.30), channel_id=1, source_target_pairs={{0,6},{1,25},{2,0},{3,27},{4,2},{5,29},{6,4},{7,31},{8,14},{9,1},{... | collective-permute-start | bytes 3932168 | tf_op jit(solution)/shard_map/ppermute | solution.py:374
  23.2 0.0 collective-permute-start.7
  23.2 1.1 %pack.2 = (bf16[320,2048]{1,0:T(8,128)(2,1)S(1)}, bf16[320,2048]{1,0:T(8,128)(2,1)S(1)}) custom-call(bf16[2,16,128]{2,1,0:T(8,128)(2,1)S(1)} %get-tuple-element.27.q_ref, bf16[128,2176]{1,0:T(8,128)(2,1)S(1)} %get-tuple-element.28.refs_0_, bf16[128,2176]{1,0:T(8,128)(2,1)S(1)} %collective-permute-done.1.refs_1_, ...), custom_call_target="tpu_custom_call" | custom-call | flops 671088640 | bytes 4718592 | tf_op jit(solution)/shard_map/pack/pallas_call | solution.py:159
  24.3 14.0 %collective-permute-done.3.refs_1_ = bf16[320,2048]{1,0:T(8,128)(2,1)S(1)} collective-permute-done((bf16[320,2048]{1,0:T(8,128)(2,1)S(1)}, bf16[320,2048]{1,0:T(8,128)(2,1)S(1)}, u32[]{:S(2)}, u32[]{:S(2)}) %collective-permute-start.3) | collective-permute-done | bytes 1310752 | tf_op jit(solution)/shard_map/ppermute | solution.py:374
  38.3 2.7 %collective-permute-start.4 = (bf16[320,2048]{1,0:T(8,128)(2,1)S(1)}, bf16[320,2048]{1,0:T(8,128)(2,1)S(1)}, u32[]{:S(2)}, u32[]{:S(2)}) collective-permute-start(bf16[320,2048]{1,0:T(8,128)(2,1)S(1)} %get-tuple-element.31), channel_id=1, source_target_pairs={{0,4},{1,17},{2,6},{3,19},{4,0},{5,21},{6,2},{7,23},{8,12},{9,25},... | collective-permute-start | bytes 3932168 | tf_op jit(solution)/shard_map/ppermute | solution.py:374
  41.0 1.0 %collective-permute-done.7.refs_0_ = bf16[320,2048]{1,0:T(8,128)(2,1)S(1)} collective-permute-done((bf16[320,2048]{1,0:T(8,128)(2,1)S(1)}, bf16[320,2048]{1,0:T(8,128)(2,1)S(1)}, u32[]{:S(2)}, u32[]{:S(2)}) %collective-permute-start.7) | collective-permute-done | bytes 1310752 | tf_op jit(solution)/shard_map/ppermute | solution.py:374
  42.0 0.0 collective-permute-done.5.refs_2_.refs_3_
  42.0 6.3 %expert.5 = (bf16[320,2048]{1,0:T(8,128)(2,1)S(1)}, bf16[320,2048]{1,0:T(8,128)(2,1)S(1)}) custom-call(bf16[320,2048]{1,0:T(8,128)(2,1)S(1)} %collective-permute-done.7.refs_0_, bf16[320,2048]{1,0:T(8,128)(2,1)S(1)} %collective-permute-done.3.refs_1_, bf16[3072,1536]{1,0:T(8,128)(2,1)S(1)} %get-tuple-element.34.refs_1_.refs_2_, ...), custom_call_target="tpu_custom_call" | custom-call | flops 6039797760 | bytes 5242880 | tf_op jit(solution)/shard_map/expert/pallas_call | solution.py:319
  48.3 0.1 collective-permute-start.8
  48.4 2.0 %collective-permute-start.9 = (bf16[320,2048]{1,0:T(8,128)(2,1)S(1)}, bf16[320,2048]{1,0:T(8,128)(2,1)S(1)}, u32[]{:S(2)}, u32[]{:S(2)}) collective-permute-start(bf16[320,2048]{1,0:T(8,128)(2,1)S(1)} %get-tuple-element.38), channel_id=1, source_target_pairs={{6,0},{25,1},{0,2},{27,3},{2,4},{29,5},{4,6},{31,7},{14,8},{1,9},{... | collective-permute-start | bytes 3932168 | tf_op jit(solution)/shard_map/ppermute | solution.py:374
  50.4 7.1 %collective-permute-done.4.refs_0_ = bf16[320,2048]{1,0:T(8,128)(2,1)S(1)} collective-permute-done((bf16[320,2048]{1,0:T(8,128)(2,1)S(1)}, bf16[320,2048]{1,0:T(8,128)(2,1)S(1)}, u32[]{:S(2)}, u32[]{:S(2)}) %collective-permute-start.4) | collective-permute-done | bytes 1310752 | tf_op jit(solution)/shard_map/ppermute | solution.py:374
  57.5 3.3 %expert.3 = (bf16[160,2048]{1,0:T(8,128)(2,1)S(1)}, bf16[160,2048]{1,0:T(8,128)(2,1)S(1)}) custom-call(bf16[320,2048]{1,0:T(8,128)(2,1)S(1)} %collective-permute-done.4.refs_0_, bf16[3072,1536]{1,0:T(8,128)(2,1)S(1)} %get-tuple-element.34.refs_1_.refs_2_, bf16[3072,1536]{1,0:T(8,128)(2,1)S(1)} %collective-permute-done.5.refs_2_.refs_3_), custom_call_target="tpu_custom_call" | custom-call | flops 3019898880 | bytes 2621440 | tf_op jit(solution)/shard_map/expert/pallas_call | solution.py:319
  60.8 2.7 %collective-permute-start.6 = (bf16[160,2048]{1,0:T(8,128)(2,1)S(1)}, bf16[160,2048]{1,0:T(8,128)(2,1)S(1)}, u32[]{:S(2)}, u32[]{:S(2)}) collective-permute-start(bf16[160,2048]{1,0:T(8,128)(2,1)S(1)} %get-tuple-element.35), channel_id=1, source_target_pairs={{4,0},{17,1},{6,2},{19,3},{0,4},{21,5},{2,6},{23,7},{12,8},{25,9},... | collective-permute-start | bytes 1966088 | tf_op jit(solution)/shard_map/ppermute | solution.py:374
  63.5 9.0 %collective-permute-done.8.refs_5_ = bf16[320,2048]{1,0:T(8,128)(2,1)S(1)} collective-permute-done((bf16[320,2048]{1,0:T(8,128)(2,1)S(1)}, bf16[320,2048]{1,0:T(8,128)(2,1)S(1)}, u32[]{:S(2)}, u32[]{:S(2)}) %collective-permute-start.8) | collective-permute-done | bytes 1310752 | tf_op jit(solution)/shard_map/ppermute | solution.py:374
  72.5 0.0 collective-permute-done.9.refs_6_
  72.5 1.6 %collective-permute-start.11 = (bf16[160,2048]{1,0:T(8,128)(2,1)S(1)}, bf16[160,2048]{1,0:T(8,128)(2,1)S(1)}, u32[]{:S(2)}, u32[]{:S(2)}) collective-permute-start(bf16[160,2048]{1,0:T(8,128)(2,1)S(1)} %get-tuple-element.44), channel_id=1, source_target_pairs={{4,0},{17,1},{6,2},{19,3},{0,4},{21,5},{2,6},{23,7},{12,8},{25,9},... | collective-permute-start | bytes 1966088 | tf_op jit(solution)/shard_map/ppermute | solution.py:374
  74.1 3.3 %expert.4.refs_4_ = bf16[320,2048]{1,0:T(8,128)(2,1)S(1)} custom-call(bf16[320,2048]{1,0:T(8,128)(2,1)S(1)} %get-tuple-element.36.refs_0_, bf16[3072,1536]{1,0:T(8,128)(2,1)S(1)} %get-tuple-element.34.refs_1_.refs_2_, bf16[3072,1536]{1,0:T(8,128)(2,1)S(1)} %collective-permute-done.5.refs_2_.refs_3_), custom_call_target="tpu_custom_call" | custom-call | flops 3019898880 | bytes 2621440 | tf_op jit(solution)/shard_map/expert/pallas_call | solution.py:319
  77.4 2.4 %combine.1 = (f32[128,2048]{1,0:T(8,128)S(1)}, f32[128,2048]{1,0:T(8,128)S(1)}, f32[128,2048]{1,0:T(8,128)S(1)}, f32[128,2048]{1,0:T(8,128)S(1)}) custom-call(bf16[2,16,128]{2,1,0:T(8,128)(2,1)S(1)} %get-tuple-element.27.q_ref, bf16[128,2176]{1,0:T(8,128)(2,1)S(1)} %get-tuple-element.28.refs_0_, bf16[128,2176]{1,0:T(8,128)(2,1)S(1)} %collective-permute-done.1.refs_1_, ...), custom_call_target="tpu_custom_call" | custom-call | flops 1006632960 | bytes 7077888 | tf_op jit(solution)/shard_map/combine/pallas_call | solution.py:221
  79.8 0.0 collective-permute-done.6.refs_2_
  79.8 1.0 finish.2
  80.8 0.9 collective-permute-start.10
  81.7 7.1 %collective-permute-done.11.refs_2_ = bf16[160,2048]{1,0:T(8,128)(2,1)S(1)} collective-permute-done((bf16[160,2048]{1,0:T(8,128)(2,1)S(1)}, bf16[160,2048]{1,0:T(8,128)(2,1)S(1)}, u32[]{:S(2)}, u32[]{:S(2)}) %collective-permute-start.11) | collective-permute-done | bytes 655392 | tf_op jit(solution)/shard_map/ppermute | solution.py:374
  88.8 1.0 finish.3
  89.7 1.5 %collective-permute-start.12 = (bf16[128,2048]{1,0:T(8,128)(2,1)S(1)}, bf16[128,2048]{1,0:T(8,128)(2,1)S(1)}, u32[]{:S(2)}, u32[]{:S(2)}) collective-permute-start(bf16[128,2048]{1,0:T(8,128)(2,1)S(1)} %get-tuple-element.47), channel_id=1, source_target_pairs={{8,0},{3,1},{10,2},{5,3},{12,4},{7,5},{14,6},{1,7},{16,8},{11,9},{... | collective-permute-start | bytes 1572872 | tf_op jit(solution)/shard_map/ppermute | solution.py:374
  91.3 0.6 collective-permute-start.13
  91.8 0.0 collective-permute-done.10
  91.8 0.1 convert_add_fusion
  92.0 7.0 %collective-permute-done.12 = bf16[128,2048]{1,0:T(8,128)(2,1)S(1)} collective-permute-done((bf16[128,2048]{1,0:T(8,128)(2,1)S(1)}, bf16[128,2048]{1,0:T(8,128)(2,1)S(1)}, u32[]{:S(2)}, u32[]{:S(2)}) %collective-permute-start.12) | collective-permute-done | bytes 524320 | tf_op jit(solution)/shard_map/ppermute | solution.py:374
  99.0 2.7 %collective-permute-done.13 = bf16[128,2048]{1,0:T(8,128)(2,1)S(1)} collective-permute-done((bf16[128,2048]{1,0:T(8,128)(2,1)S(1)}, bf16[128,2048]{1,0:T(8,128)(2,1)S(1)}, u32[]{:S(2)}, u32[]{:S(2)}) %collective-permute-start.13) | collective-permute-done | bytes 524320 | tf_op jit(solution)/shard_map/ppermute | solution.py:374
  101.6 1.0 add_convert_fusion
Async XLA Ops:
  1.1 10.8 %collective-permute-start.2 = (bf16[128,2176]{1,0:T(8,128)(2,1)S(1)}, bf16[128,2176]{1,0:T(8,128)(2,1)S(1)}, u32[]{:S(2)}, u32[]{:S(2)}) collective-permute-start(bf16[128,2176]{1,0:T(8,128)(2,1)S(1)} %get-tuple-element.28.refs_0_), channel_id=1, source_target_pairs={{0,8},{1,3},{2,10},{3,5},{4,12},{5,7},{6,14},{7,1},{8,16},{9,11},{... | collective-permute-start | bytes 1671176 | tf_op jit(solution)/shard_map/ppermute | solution.py:374
  2.7 14.8 %collective-permute-start.1 = (bf16[128,2176]{1,0:T(8,128)(2,1)S(1)}, bf16[128,2176]{1,0:T(8,128)(2,1)S(1)}, u32[]{:S(2)}, u32[]{:S(2)}) collective-permute-start(bf16[128,2176]{1,0:T(8,128)(2,1)S(1)} %get-tuple-element.28.refs_0_), channel_id=1, source_target_pairs={{0,24},{1,7},{2,26},{3,1},{4,28},{5,3},{6,30},{7,5},{8,0},{9,15},{... | collective-permute-start | bytes 1671176 | tf_op jit(solution)/shard_map/ppermute | solution.py:374
  4.4 14.5 %collective-permute-start = (bf16[128,2176]{1,0:T(8,128)(2,1)S(1)}, bf16[128,2176]{1,0:T(8,128)(2,1)S(1)}, u32[]{:S(2)}, u32[]{:S(2)}) collective-permute-start(bf16[128,2176]{1,0:T(8,128)(2,1)S(1)} %get-tuple-element.28.refs_0_), channel_id=1, source_target_pairs={{0,16},{1,5},{2,18},{3,7},{4,20},{5,1},{6,22},{7,3},{8,24},{9,13},... | collective-permute-start | bytes 1671176 | tf_op jit(solution)/shard_map/ppermute | solution.py:374
  20.0 22.0 %collective-permute-start.5 = (bf16[3072,1536]{1,0:T(8,128)(2,1)S(1)}, bf16[3072,1536]{1,0:T(8,128)(2,1)S(1)}, u32[]{:S(2)}, u32[]{:S(2)}) collective-permute-start(bf16[3072,1536]{1,0:T(8,128)(2,1)S(1)} %get-tuple-element.34.refs_1_.refs_2_), channel_id=1, source_target_pairs={{0,1},{1,0},{2,3},{3,2},{4,5},{5,4},{6,7},{7,6},{8,9},{9,8},{10,11... | collective-permute-start | bytes 28311560 | tf_op jit(solution)/shard_map/ppermute | solution.py:374
  20.1 18.2 %collective-permute-start.3 = (bf16[320,2048]{1,0:T(8,128)(2,1)S(1)}, bf16[320,2048]{1,0:T(8,128)(2,1)S(1)}, u32[]{:S(2)}, u32[]{:S(2)}) collective-permute-start(bf16[320,2048]{1,0:T(8,128)(2,1)S(1)} %get-tuple-element.30), channel_id=1, source_target_pairs={{0,6},{1,25},{2,0},{3,27},{4,2},{5,29},{6,4},{7,31},{8,14},{9,1},{... | collective-permute-start | bytes 3932168 | tf_op jit(solution)/shard_map/ppermute | solution.py:374
  23.2 18.8 %collective-permute-start.7 = (bf16[320,2048]{1,0:T(8,128)(2,1)S(1)}, bf16[320,2048]{1,0:T(8,128)(2,1)S(1)}, u32[]{:S(2)}, u32[]{:S(2)}) collective-permute-start(bf16[320,2048]{1,0:T(8,128)(2,1)S(1)} %get-tuple-element.33), channel_id=1, source_target_pairs={{0,2},{1,9},{2,4},{3,11},{4,6},{5,13},{6,0},{7,15},{8,10},{9,17},{... | collective-permute-start | bytes 3932168 | tf_op jit(solution)/shard_map/ppermute | solution.py:374
  38.3 19.2 %collective-permute-start.4 = (bf16[320,2048]{1,0:T(8,128)(2,1)S(1)}, bf16[320,2048]{1,0:T(8,128)(2,1)S(1)}, u32[]{:S(2)}, u32[]{:S(2)}) collective-permute-start(bf16[320,2048]{1,0:T(8,128)(2,1)S(1)} %get-tuple-element.31), channel_id=1, source_target_pairs={{0,4},{1,17},{2,6},{3,19},{4,0},{5,21},{6,2},{7,23},{8,12},{9,25},... | collective-permute-start | bytes 3932168 | tf_op jit(solution)/shard_map/ppermute | solution.py:374
  48.3 24.2 %collective-permute-start.8 = (bf16[320,2048]{1,0:T(8,128)(2,1)S(1)}, bf16[320,2048]{1,0:T(8,128)(2,1)S(1)}, u32[]{:S(2)}, u32[]{:S(2)}) collective-permute-start(bf16[320,2048]{1,0:T(8,128)(2,1)S(1)} %get-tuple-element.37), channel_id=1, source_target_pairs={{2,0},{9,1},{4,2},{11,3},{6,4},{13,5},{0,6},{15,7},{10,8},{17,9},{... | collective-permute-start | bytes 3932168 | tf_op jit(solution)/shard_map/ppermute | solution.py:374
  48.4 24.1 %collective-permute-start.9 = (bf16[320,2048]{1,0:T(8,128)(2,1)S(1)}, bf16[320,2048]{1,0:T(8,128)(2,1)S(1)}, u32[]{:S(2)}, u32[]{:S(2)}) collective-permute-start(bf16[320,2048]{1,0:T(8,128)(2,1)S(1)} %get-tuple-element.38), channel_id=1, source_target_pairs={{6,0},{25,1},{0,2},{27,3},{2,4},{29,5},{4,6},{31,7},{14,8},{1,9},{... | collective-permute-start | bytes 3932168 | tf_op jit(solution)/shard_map/ppermute | solution.py:374
  60.8 19.0 %collective-permute-start.6 = (bf16[160,2048]{1,0:T(8,128)(2,1)S(1)}, bf16[160,2048]{1,0:T(8,128)(2,1)S(1)}, u32[]{:S(2)}, u32[]{:S(2)}) collective-permute-start(bf16[160,2048]{1,0:T(8,128)(2,1)S(1)} %get-tuple-element.35), channel_id=1, source_target_pairs={{4,0},{17,1},{6,2},{19,3},{0,4},{21,5},{2,6},{23,7},{12,8},{25,9},... | collective-permute-start | bytes 1966088 | tf_op jit(solution)/shard_map/ppermute | solution.py:374
  72.5 16.2 %collective-permute-start.11 = (bf16[160,2048]{1,0:T(8,128)(2,1)S(1)}, bf16[160,2048]{1,0:T(8,128)(2,1)S(1)}, u32[]{:S(2)}, u32[]{:S(2)}) collective-permute-start(bf16[160,2048]{1,0:T(8,128)(2,1)S(1)} %get-tuple-element.44), channel_id=1, source_target_pairs={{4,0},{17,1},{6,2},{19,3},{0,4},{21,5},{2,6},{23,7},{12,8},{25,9},... | collective-permute-start | bytes 1966088 | tf_op jit(solution)/shard_map/ppermute | solution.py:374
  80.8 11.1 %collective-permute-start.10 = (bf16[128,2048]{1,0:T(8,128)(2,1)S(1)}, bf16[128,2048]{1,0:T(8,128)(2,1)S(1)}, u32[]{:S(2)}, u32[]{:S(2)}) collective-permute-start(bf16[128,2048]{1,0:T(8,128)(2,1)S(1)} %get-tuple-element.42), channel_id=1, source_target_pairs={{16,0},{5,1},{18,2},{7,3},{20,4},{1,5},{22,6},{3,7},{24,8},{13,9},... | collective-permute-start | bytes 1572872 | tf_op jit(solution)/shard_map/ppermute | solution.py:374
  89.7 9.3 %collective-permute-start.12 = (bf16[128,2048]{1,0:T(8,128)(2,1)S(1)}, bf16[128,2048]{1,0:T(8,128)(2,1)S(1)}, u32[]{:S(2)}, u32[]{:S(2)}) collective-permute-start(bf16[128,2048]{1,0:T(8,128)(2,1)S(1)} %get-tuple-element.47), channel_id=1, source_target_pairs={{8,0},{3,1},{10,2},{5,3},{12,4},{7,5},{14,6},{1,7},{16,8},{11,9},{... | collective-permute-start | bytes 1572872 | tf_op jit(solution)/shard_map/ppermute | solution.py:374
  91.3 10.4 %collective-permute-start.13 = (bf16[128,2048]{1,0:T(8,128)(2,1)S(1)}, bf16[128,2048]{1,0:T(8,128)(2,1)S(1)}, u32[]{:S(2)}, u32[]{:S(2)}) collective-permute-start(bf16[128,2048]{1,0:T(8,128)(2,1)S(1)} %get-tuple-element.48), channel_id=1, source_target_pairs={{24,0},{7,1},{26,2},{1,3},{28,4},{3,5},{30,6},{5,7},{0,8},{15,9},{... | collective-permute-start | bytes 1572872 | tf_op jit(solution)/shard_map/ppermute | solution.py:374

commit v10 on v9

--- a/solution.py
+++ b/solution.py
@@ -233,8 +233,8 @@
     )(q, *[blocks[n] for n in (0, 3, 2, 1)], *backs, *sums)
 
 
-def finish_kernel(q_ref, *refs):
-    pair, back_ref, sums, outs = refs[:2], refs[2], refs[3:5], refs[5:]
+def finish_kernel(back_ref, *refs):
+    sums, q_ref, pair, outs = refs[:2], refs[2], refs[3:5], refs[5:]
     tok, width = outs[0].shape
     half = 2 * CAP
     span = half * NC
@@ -279,7 +279,7 @@
             transcendentals=0,
         ),
         name="finish",
-    )(q, *pair, slab, *sums)
+    )(slab, *sums, q, *pair)
 
 
 def halves(refs):
@@ -399,7 +399,7 @@
         parts[p] = finish(q, pairs[p], slab, sums[2 * p : 2 * p + 2], kinds)
     part0, part2 = parts[0]
     part1, part3 = parts[1]
-    mixed = part0 + send(part2, back(spread_pairs(2))).astype(f32)
+    mixed = part0 + send(after(part2, late), back(spread_pairs(2))).astype(f32)
     mixed = lax.optimization_barrier(mixed)
     for j, part in ((1, part1), (3, part3)):
         mixed = mixed + send(part, back(spread_pairs(j))).astype(f32)

time: 104 us -> 103 us (level)
  waiting for transfers between devices: 56.2 us -> 53.5 us
  starting transfers between devices: 20.4 us -> 22.8 us
    ppermute x14, waiting for transfers between devices: 56.2 us -> 53.5 us  [per_device(): send = lambda v, pairs: lax.ppermute(v, 'expert', pairs)]
    ppermute x14, starting transfers between devices: 20.4 us -> 22.8 us  [per_device(): send = lambda v, pairs: lax.ppermute(v, 'expert', pairs)]
where the time goes in v10:
time: 103 us; the launch traced here: 102 us
  waiting for transfers between devices  53.5 us (52%)
  Pallas kernels  24.7 us (24%)
  starting transfers between devices  22.8 us (22%)
  other arithmetic  1.09 us (1%)
    ppermute x14, waiting for transfers between devices, per_device(): send = lambda v, pairs: lax.ppermute(v, 'expert', pairs)  53.5 us
    ppermute x14, starting transfers between devices, per_device(): send = lambda v, pairs: lax.ppermute(v, 'expert', pairs)  22.8 us
    pallas_call x3, Pallas kernels, expert(): pl.pallas_call(functools.partial(expert_kernel, count, ff), in_specs=[vme...  12.8 us
    pallas_call x1, Pallas kernels, hold(): pl.pallas_call(hold_kernel, in_specs=[pl.BlockSpec(memory_space=pl.ANY)]...  4.33 us
    pallas_call x1, Pallas kernels, combine(): pl.pallas_call(functools.partial(combine_kernel, which), in_specs=[vmem]...  2.4 us
    pallas_call x2, Pallas kernels, pack(): pl.pallas_call(functools.partial(pack_kernel, which), in_specs=[vmem] * (...  2.19 us
  transfers between devices with their start and end apart: 14, of which 10 were waited for; matrix products, arithmetic and copies ran while one was open for 0% of the time, Pallas kernels for 22%

profile of v10, /device:TPU:96, one launch (start us, length us, event | category | flops | bytes accessed | tf_op | source)
XLA Modules:
  0.0 102.3 jit_solution(7721135698832169684)
XLA Ops:
  0.0 1.1 %prep.1 = (bf16[128,2176]{1,0:T(8,128)(2,1)S(1)}, bf16[2,16,128]{2,1,0:T(8,128)(2,1)S(1)}) custom-call(s32[8,128]{1,0:T(8,128)} %bitcast.2, f32[8,128]{1,0:T(8,128)} %bitcast.3, bf16[128,2048]{1,0:T(8,128)(2,1)} %tok_hbm.1), custom_call_target="tpu_custom_call" | custom-call | flops 1048576 | bytes 1048576 | tf_op jit(solution)/shard_map/prep/pallas_call | solution.py:92
  1.1 3.1 %collective-permute-start.2 = (bf16[128,2176]{1,0:T(8,128)(2,1)S(1)}, bf16[128,2176]{1,0:T(8,128)(2,1)S(1)}, u32[]{:S(2)}, u32[]{:S(2)}) collective-permute-start(bf16[128,2176]{1,0:T(8,128)(2,1)S(1)} %get-tuple-element.29.refs_0_.refs_3_), channel_id=1, source_target_pairs={{0,16},{1,5},{2,18},{3,7},{4,20},{5,1},{6,22},{7,3},{8,24},{9,13},... | collective-permute-start | bytes 1671176 | tf_op jit(solution)/shard_map/ppermute | solution.py:374
  4.2 0.6 collective-permute-start.1
  4.8 2.6 %collective-permute-start = (bf16[128,2176]{1,0:T(8,128)(2,1)S(1)}, bf16[128,2176]{1,0:T(8,128)(2,1)S(1)}, u32[]{:S(2)}, u32[]{:S(2)}) collective-permute-start(bf16[128,2176]{1,0:T(8,128)(2,1)S(1)} %get-tuple-element.29.refs_0_.refs_3_), channel_id=1, source_target_pairs={{0,24},{1,7},{2,26},{3,1},{4,28},{5,3},{6,30},{7,5},{8,0},{9,15},{... | collective-permute-start | bytes 1671176 | tf_op jit(solution)/shard_map/ppermute | solution.py:374
  7.5 4.3 %hold.1 = (bf16[3072,1536]{1,0:T(8,128)(2,1)S(1)}, f32[8,128]{1,0:T(8,128)}) custom-call(bf16[1,2048,768]{2,1,0:T(8,128)(2,1)} %wg.1, bf16[1,2048,768]{2,1,0:T(8,128)(2,1)} %wu.1, bf16[1,768,2048]{2,1,0:T(8,128)(2,1)} %wd.1), custom_call_target="tpu_custom_call" | custom-call | bytes 18874368 | tf_op jit(solution)/shard_map/hold/pallas_call | solution.py:358
  11.8 0.5 collective-permute-done.2.refs_3_.refs_4_
  12.3 5.9 %collective-permute-done.1.refs_2_.refs_3_ = bf16[128,2176]{1,0:T(8,128)(2,1)S(1)} collective-permute-done((bf16[128,2176]{1,0:T(8,128)(2,1)S(1)}, bf16[128,2176]{1,0:T(8,128)(2,1)S(1)}, u32[]{:S(2)}, u32[]{:S(2)}) %collective-permute-start.1) | collective-permute-done | bytes 557088 | tf_op jit(solution)/shard_map/ppermute | solution.py:374
  18.2 0.1 collective-permute-done.refs_1_.refs_4_
  18.3 1.1 %pack.3 = (bf16[320,2048]{1,0:T(8,128)(2,1)S(1)}, bf16[320,2048]{1,0:T(8,128)(2,1)S(1)}) custom-call(bf16[2,16,128]{2,1,0:T(8,128)(2,1)S(1)} %get-tuple-element.28.q_ref.refs_2_, bf16[128,2176]{1,0:T(8,128)(2,1)S(1)} %get-tuple-element.29.refs_0_.refs_3_, bf16[128,2176]{1,0:T(8,128)(2,1)S(1)} %collective-permute-done.refs_1_.refs_4_, ...), custom_call_target="tpu_custom_call" | custom-call | flops 671088640 | bytes 4718592 | tf_op jit(solution)/shard_map/pack/pallas_call | solution.py:159
  19.4 0.1 collective-permute-start.5
  19.5 3.1 %collective-permute-start.3 = (bf16[320,2048]{1,0:T(8,128)(2,1)S(1)}, bf16[320,2048]{1,0:T(8,128)(2,1)S(1)}, u32[]{:S(2)}, u32[]{:S(2)}) collective-permute-start(bf16[320,2048]{1,0:T(8,128)(2,1)S(1)} %get-tuple-element.31), channel_id=1, source_target_pairs={{0,6},{1,25},{2,0},{3,27},{4,2},{5,29},{6,4},{7,31},{8,14},{9,1},{... | collective-permute-start | bytes 3932168 | tf_op jit(solution)/shard_map/ppermute | solution.py:374
  22.6 0.0 collective-permute-start.7
  22.6 1.1 %pack.2 = (bf16[320,2048]{1,0:T(8,128)(2,1)S(1)}, bf16[320,2048]{1,0:T(8,128)(2,1)S(1)}) custom-call(bf16[2,16,128]{2,1,0:T(8,128)(2,1)S(1)} %get-tuple-element.28.q_ref.refs_2_, bf16[128,2176]{1,0:T(8,128)(2,1)S(1)} %get-tuple-element.29.refs_0_.refs_3_, bf16[128,2176]{1,0:T(8,128)(2,1)S(1)} %collective-permute-done.refs_1_.refs_4_, ...), custom_call_target="tpu_custom_call" | custom-call | flops 671088640 | bytes 4718592 | tf_op jit(solution)/shard_map/pack/pallas_call | solution.py:159
  23.7 14.0 %collective-permute-done.3.refs_1_ = bf16[320,2048]{1,0:T(8,128)(2,1)S(1)} collective-permute-done((bf16[320,2048]{1,0:T(8,128)(2,1)S(1)}, bf16[320,2048]{1,0:T(8,128)(2,1)S(1)}, u32[]{:S(2)}, u32[]{:S(2)}) %collective-permute-start.3) | collective-permute-done | bytes 1310752 | tf_op jit(solution)/shard_map/ppermute | solution.py:374
  37.8 2.7 %collective-permute-start.4 = (bf16[320,2048]{1,0:T(8,128)(2,1)S(1)}, bf16[320,2048]{1,0:T(8,128)(2,1)S(1)}, u32[]{:S(2)}, u32[]{:S(2)}) collective-permute-start(bf16[320,2048]{1,0:T(8,128)(2,1)S(1)} %get-tuple-element.32), channel_id=1, source_target_pairs={{0,4},{1,17},{2,6},{3,19},{4,0},{5,21},{6,2},{7,23},{8,12},{9,25},... | collective-permute-start | bytes 3932168 | tf_op jit(solution)/shard_map/ppermute | solution.py:374
  40.4 1.0 %collective-permute-done.7.refs_0_ = bf16[320,2048]{1,0:T(8,128)(2,1)S(1)} collective-permute-done((bf16[320,2048]{1,0:T(8,128)(2,1)S(1)}, bf16[320,2048]{1,0:T(8,128)(2,1)S(1)}, u32[]{:S(2)}, u32[]{:S(2)}) %collective-permute-start.7) | collective-permute-done | bytes 1310752 | tf_op jit(solution)/shard_map/ppermute | solution.py:374
  41.4 0.0 collective-permute-done.5.refs_2_.refs_3_
  41.4 6.3 %expert.5 = (bf16[320,2048]{1,0:T(8,128)(2,1)S(1)}, bf16[320,2048]{1,0:T(8,128)(2,1)S(1)}) custom-call(bf16[320,2048]{1,0:T(8,128)(2,1)S(1)} %collective-permute-done.7.refs_0_, bf16[320,2048]{1,0:T(8,128)(2,1)S(1)} %collective-permute-done.3.refs_1_, bf16[3072,1536]{1,0:T(8,128)(2,1)S(1)} %get-tuple-element.35.refs_1_.refs_2_, ...), custom_call_target="tpu_custom_call" | custom-call | flops 6039797760 | bytes 5242880 | tf_op jit(solution)/shard_map/expert/pallas_call | solution.py:319
  47.7 0.1 collective-permute-start.8
  47.8 2.0 %collective-permute-start.9 = (bf16[320,2048]{1,0:T(8,128)(2,1)S(1)}, bf16[320,2048]{1,0:T(8,128)(2,1)S(1)}, u32[]{:S(2)}, u32[]{:S(2)}) collective-permute-start(bf16[320,2048]{1,0:T(8,128)(2,1)S(1)} %get-tuple-element.39), channel_id=1, source_target_pairs={{6,0},{25,1},{0,2},{27,3},{2,4},{29,5},{4,6},{31,7},{14,8},{1,9},{... | collective-permute-start | bytes 3932168 | tf_op jit(solution)/shard_map/ppermute | solution.py:374
  49.8 7.1 %collective-permute-done.4.refs_0_ = bf16[320,2048]{1,0:T(8,128)(2,1)S(1)} collective-permute-done((bf16[320,2048]{1,0:T(8,128)(2,1)S(1)}, bf16[320,2048]{1,0:T(8,128)(2,1)S(1)}, u32[]{:S(2)}, u32[]{:S(2)}) %collective-permute-start.4) | collective-permute-done | bytes 1310752 | tf_op jit(solution)/shard_map/ppermute | solution.py:374
  57.0 3.3 %expert.3 = (bf16[160,2048]{1,0:T(8,128)(2,1)S(1)}, bf16[160,2048]{1,0:T(8,128)(2,1)S(1)}) custom-call(bf16[320,2048]{1,0:T(8,128)(2,1)S(1)} %collective-permute-done.4.refs_0_, bf16[3072,1536]{1,0:T(8,128)(2,1)S(1)} %get-tuple-element.35.refs_1_.refs_2_, bf16[3072,1536]{1,0:T(8,128)(2,1)S(1)} %collective-permute-done.5.refs_2_.refs_3_), custom_call_target="tpu_custom_call" | custom-call | flops 3019898880 | bytes 2621440 | tf_op jit(solution)/shard_map/expert/pallas_call | solution.py:319
  60.2 2.7 %collective-permute-start.6 = (bf16[160,2048]{1,0:T(8,128)(2,1)S(1)}, bf16[160,2048]{1,0:T(8,128)(2,1)S(1)}, u32[]{:S(2)}, u32[]{:S(2)}) collective-permute-start(bf16[160,2048]{1,0:T(8,128)(2,1)S(1)} %get-tuple-element.36), channel_id=1, source_target_pairs={{4,0},{17,1},{6,2},{19,3},{0,4},{21,5},{2,6},{23,7},{12,8},{25,9},... | collective-permute-start | bytes 1966088 | tf_op jit(solution)/shard_map/ppermute | solution.py:374
  63.0 9.0 %collective-permute-done.8.refs_5_ = bf16[320,2048]{1,0:T(8,128)(2,1)S(1)} collective-permute-done((bf16[320,2048]{1,0:T(8,128)(2,1)S(1)}, bf16[320,2048]{1,0:T(8,128)(2,1)S(1)}, u32[]{:S(2)}, u32[]{:S(2)}) %collective-permute-start.8) | collective-permute-done | bytes 1310752 | tf_op jit(solution)/shard_map/ppermute | solution.py:374
  72.0 0.0 collective-permute-done.9.refs_6_
  72.0 1.6 %collective-permute-start.10 = (bf16[160,2048]{1,0:T(8,128)(2,1)S(1)}, bf16[160,2048]{1,0:T(8,128)(2,1)S(1)}, u32[]{:S(2)}, u32[]{:S(2)}) collective-permute-start(bf16[160,2048]{1,0:T(8,128)(2,1)S(1)} %get-tuple-element.45), channel_id=1, source_target_pairs={{4,0},{17,1},{6,2},{19,3},{0,4},{21,5},{2,6},{23,7},{12,8},{25,9},... | collective-permute-start | bytes 1966088 | tf_op jit(solution)/shard_map/ppermute | solution.py:374
  73.6 3.3 %expert.4.refs_4_ = bf16[320,2048]{1,0:T(8,128)(2,1)S(1)} custom-call(bf16[320,2048]{1,0:T(8,128)(2,1)S(1)} %get-tuple-element.37.refs_0_, bf16[3072,1536]{1,0:T(8,128)(2,1)S(1)} %get-tuple-element.35.refs_1_.refs_2_, bf16[3072,1536]{1,0:T(8,128)(2,1)S(1)} %collective-permute-done.5.refs_2_.refs_3_), custom_call_target="tpu_custom_call" | custom-call | flops 3019898880 | bytes 2621440 | tf_op jit(solution)/shard_map/expert/pallas_call | solution.py:319
  76.8 2.4 %combine.1 = (f32[128,2048]{1,0:T(8,128)S(1)}, f32[128,2048]{1,0:T(8,128)S(1)}, f32[128,2048]{1,0:T(8,128)S(1)}, f32[128,2048]{1,0:T(8,128)S(1)}) custom-call(bf16[2,16,128]{2,1,0:T(8,128)(2,1)S(1)} %get-tuple-element.28.q_ref.refs_2_, bf16[128,2176]{1,0:T(8,128)(2,1)S(1)} %get-tuple-element.29.refs_0_.refs_3_, ...), custom_call_target="tpu_custom_call" | custom-call | flops 1006632960 | bytes 7077888 | tf_op jit(solution)/shard_map/combine/pallas_call | solution.py:221
  79.2 0.0 collective-permute-done.6.back_ref
  79.2 1.0 finish.2
  80.2 4.8 %collective-permute-done.10.back_ref = bf16[160,2048]{1,0:T(8,128)(2,1)S(1)} collective-permute-done((bf16[160,2048]{1,0:T(8,128)(2,1)S(1)}, bf16[160,2048]{1,0:T(8,128)(2,1)S(1)}, u32[]{:S(2)}, u32[]{:S(2)}) %collective-permute-start.10) | collective-permute-done | bytes 655392 | tf_op jit(solution)/shard_map/ppermute | solution.py:374
  85.0 2.0 %collective-permute-start.11 = (bf16[128,2048]{1,0:T(8,128)(2,1)S(1)}, bf16[128,2048]{1,0:T(8,128)(2,1)S(1)}, u32[]{:S(2)}, u32[]{:S(2)}) collective-permute-start(bf16[128,2048]{1,0:T(8,128)(2,1)S(1)} %get-tuple-element.46), channel_id=1, source_target_pairs={{16,0},{5,1},{18,2},{7,3},{20,4},{1,5},{22,6},{3,7},{24,8},{13,9},... | collective-permute-start | bytes 1572872 | tf_op jit(solution)/shard_map/ppermute | solution.py:374
  87.0 1.0 finish.3
  88.0 2.2 %collective-permute-start.12 = (bf16[128,2048]{1,0:T(8,128)(2,1)S(1)}, bf16[128,2048]{1,0:T(8,128)(2,1)S(1)}, u32[]{:S(2)}, u32[]{:S(2)}) collective-permute-start(bf16[128,2048]{1,0:T(8,128)(2,1)S(1)} %get-tuple-element.49), channel_id=1, source_target_pairs={{8,0},{3,1},{10,2},{5,3},{12,4},{7,5},{14,6},{1,7},{16,8},{11,9},{... | collective-permute-start | bytes 1572872 | tf_op jit(solution)/shard_map/ppermute | solution.py:374
  90.2 0.0 collective-permute-start.13
  90.2 5.6 %collective-permute-done.11 = bf16[128,2048]{1,0:T(8,128)(2,1)S(1)} collective-permute-done((bf16[128,2048]{1,0:T(8,128)(2,1)S(1)}, bf16[128,2048]{1,0:T(8,128)(2,1)S(1)}, u32[]{:S(2)}, u32[]{:S(2)}) %collective-permute-start.11) | collective-permute-done | bytes 524320 | tf_op jit(solution)/shard_map/ppermute | solution.py:374
  95.8 0.1 convert_add_fusion
  95.9 5.4 %collective-permute-done.12 = bf16[128,2048]{1,0:T(8,128)(2,1)S(1)} collective-permute-done((bf16[128,2048]{1,0:T(8,128)(2,1)S(1)}, bf16[128,2048]{1,0:T(8,128)(2,1)S(1)}, u32[]{:S(2)}, u32[]{:S(2)}) %collective-permute-start.12) | collective-permute-done | bytes 524320 | tf_op jit(solution)/shard_map/ppermute | solution.py:374
  101.3 0.0 collective-permute-done.13
  101.3 1.0 add_convert_fusion
Async XLA Ops:
  1.1 11.2 %collective-permute-start.2 = (bf16[128,2176]{1,0:T(8,128)(2,1)S(1)}, bf16[128,2176]{1,0:T(8,128)(2,1)S(1)}, u32[]{:S(2)}, u32[]{:S(2)}) collective-permute-start(bf16[128,2176]{1,0:T(8,128)(2,1)S(1)} %get-tuple-element.29.refs_0_.refs_3_), channel_id=1, source_target_pairs={{0,16},{1,5},{2,18},{3,7},{4,20},{5,1},{6,22},{7,3},{8,24},{9,13},... | collective-permute-start | bytes 1671176 | tf_op jit(solution)/shard_map/ppermute | solution.py:374
  4.2 14.0 %collective-permute-start.1 = (bf16[128,2176]{1,0:T(8,128)(2,1)S(1)}, bf16[128,2176]{1,0:T(8,128)(2,1)S(1)}, u32[]{:S(2)}, u32[]{:S(2)}) collective-permute-start(bf16[128,2176]{1,0:T(8,128)(2,1)S(1)} %get-tuple-element.29.refs_0_.refs_3_), channel_id=1, source_target_pairs={{0,8},{1,3},{2,10},{3,5},{4,12},{5,7},{6,14},{7,1},{8,16},{9,11},{... | collective-permute-start | bytes 1671176 | tf_op jit(solution)/shard_map/ppermute | solution.py:374
  4.8 13.5 %collective-permute-start = (bf16[128,2176]{1,0:T(8,128)(2,1)S(1)}, bf16[128,2176]{1,0:T(8,128)(2,1)S(1)}, u32[]{:S(2)}, u32[]{:S(2)}) collective-permute-start(bf16[128,2176]{1,0:T(8,128)(2,1)S(1)} %get-tuple-element.29.refs_0_.refs_3_), channel_id=1, source_target_pairs={{0,24},{1,7},{2,26},{3,1},{4,28},{5,3},{6,30},{7,5},{8,0},{9,15},{... | collective-permute-start | bytes 1671176 | tf_op jit(solution)/shard_map/ppermute | solution.py:374
  19.4 22.0 %collective-permute-start.5 = (bf16[3072,1536]{1,0:T(8,128)(2,1)S(1)}, bf16[3072,1536]{1,0:T(8,128)(2,1)S(1)}, u32[]{:S(2)}, u32[]{:S(2)}) collective-permute-start(bf16[3072,1536]{1,0:T(8,128)(2,1)S(1)} %get-tuple-element.35.refs_1_.refs_2_), channel_id=1, source_target_pairs={{0,1},{1,0},{2,3},{3,2},{4,5},{5,4},{6,7},{7,6},{8,9},{9,8},{10,11... | collective-permute-start | bytes 28311560 | tf_op jit(solution)/shard_map/ppermute | solution.py:374
  19.5 18.2 %collective-permute-start.3 = (bf16[320,2048]{1,0:T(8,128)(2,1)S(1)}, bf16[320,2048]{1,0:T(8,128)(2,1)S(1)}, u32[]{:S(2)}, u32[]{:S(2)}) collective-permute-start(bf16[320,2048]{1,0:T(8,128)(2,1)S(1)} %get-tuple-element.31), channel_id=1, source_target_pairs={{0,6},{1,25},{2,0},{3,27},{4,2},{5,29},{6,4},{7,31},{8,14},{9,1},{... | collective-permute-start | bytes 3932168 | tf_op jit(solution)/shard_map/ppermute | solution.py:374
  22.6 18.8 %collective-permute-start.7 = (bf16[320,2048]{1,0:T(8,128)(2,1)S(1)}, bf16[320,2048]{1,0:T(8,128)(2,1)S(1)}, u32[]{:S(2)}, u32[]{:S(2)}) collective-permute-start(bf16[320,2048]{1,0:T(8,128)(2,1)S(1)} %get-tuple-element.34), channel_id=1, source_target_pairs={{0,2},{1,9},{2,4},{3,11},{4,6},{5,13},{6,0},{7,15},{8,10},{9,17},{... | collective-permute-start | bytes 3932168 | tf_op jit(solution)/shard_map/ppermute | solution.py:374
  37.8 19.2 %collective-permute-start.4 = (bf16[320,2048]{1,0:T(8,128)(2,1)S(1)}, bf16[320,2048]{1,0:T(8,128)(2,1)S(1)}, u32[]{:S(2)}, u32[]{:S(2)}) collective-permute-start(bf16[320,2048]{1,0:T(8,128)(2,1)S(1)} %get-tuple-element.32), channel_id=1, source_target_pairs={{0,4},{1,17},{2,6},{3,19},{4,0},{5,21},{6,2},{7,23},{8,12},{9,25},... | collective-permute-start | bytes 3932168 | tf_op jit(solution)/shard_map/ppermute | solution.py:374
  47.7 24.2 %collective-permute-start.8 = (bf16[320,2048]{1,0:T(8,128)(2,1)S(1)}, bf16[320,2048]{1,0:T(8,128)(2,1)S(1)}, u32[]{:S(2)}, u32[]{:S(2)}) collective-permute-start(bf16[320,2048]{1,0:T(8,128)(2,1)S(1)} %get-tuple-element.38), channel_id=1, source_target_pairs={{2,0},{9,1},{4,2},{11,3},{6,4},{13,5},{0,6},{15,7},{10,8},{17,9},{... | collective-permute-start | bytes 3932168 | tf_op jit(solution)/shard_map/ppermute | solution.py:374
  47.8 24.1 %collective-permute-start.9 = (bf16[320,2048]{1,0:T(8,128)(2,1)S(1)}, bf16[320,2048]{1,0:T(8,128)(2,1)S(1)}, u32[]{:S(2)}, u32[]{:S(2)}) collective-permute-start(bf16[320,2048]{1,0:T(8,128)(2,1)S(1)} %get-tuple-element.39), channel_id=1, source_target_pairs={{6,0},{25,1},{0,2},{27,3},{2,4},{29,5},{4,6},{31,7},{14,8},{1,9},{... | collective-permute-start | bytes 3932168 | tf_op jit(solution)/shard_map/ppermute | solution.py:374
  60.2 19.0 %collective-permute-start.6 = (bf16[160,2048]{1,0:T(8,128)(2,1)S(1)}, bf16[160,2048]{1,0:T(8,128)(2,1)S(1)}, u32[]{:S(2)}, u32[]{:S(2)}) collective-permute-start(bf16[160,2048]{1,0:T(8,128)(2,1)S(1)} %get-tuple-element.36), channel_id=1, source_target_pairs={{4,0},{17,1},{6,2},{19,3},{0,4},{21,5},{2,6},{23,7},{12,8},{25,9},... | collective-permute-start | bytes 1966088 | tf_op jit(solution)/shard_map/ppermute | solution.py:374
  72.0 13.0 %collective-permute-start.10 = (bf16[160,2048]{1,0:T(8,128)(2,1)S(1)}, bf16[160,2048]{1,0:T(8,128)(2,1)S(1)}, u32[]{:S(2)}, u32[]{:S(2)}) collective-permute-start(bf16[160,2048]{1,0:T(8,128)(2,1)S(1)} %get-tuple-element.45), channel_id=1, source_target_pairs={{4,0},{17,1},{6,2},{19,3},{0,4},{21,5},{2,6},{23,7},{12,8},{25,9},... | collective-permute-start | bytes 1966088 | tf_op jit(solution)/shard_map/ppermute | solution.py:374
  85.0 10.8 %collective-permute-start.11 = (bf16[128,2048]{1,0:T(8,128)(2,1)S(1)}, bf16[128,2048]{1,0:T(8,128)(2,1)S(1)}, u32[]{:S(2)}, u32[]{:S(2)}) collective-permute-start(bf16[128,2048]{1,0:T(8,128)(2,1)S(1)} %get-tuple-element.46), channel_id=1, source_target_pairs={{16,0},{5,1},{18,2},{7,3},{20,4},{1,5},{22,6},{3,7},{24,8},{13,9},... | collective-permute-start | bytes 1572872 | tf_op jit(solution)/shard_map/ppermute | solution.py:374
  88.0 13.3 %collective-permute-start.12 = (bf16[128,2048]{1,0:T(8,128)(2,1)S(1)}, bf16[128,2048]{1,0:T(8,128)(2,1)S(1)}, u32[]{:S(2)}, u32[]{:S(2)}) collective-permute-start(bf16[128,2048]{1,0:T(8,128)(2,1)S(1)} %get-tuple-element.49), channel_id=1, source_target_pairs={{8,0},{3,1},{10,2},{5,3},{12,4},{7,5},{14,6},{1,7},{16,8},{11,9},{... | collective-permute-start | bytes 1572872 | tf_op jit(solution)/shard_map/ppermute | solution.py:374
  90.2 11.1 %collective-permute-start.13 = (bf16[128,2048]{1,0:T(8,128)(2,1)S(1)}, bf16[128,2048]{1,0:T(8,128)(2,1)S(1)}, u32[]{:S(2)}, u32[]{:S(2)}) collective-permute-start(bf16[128,2048]{1,0:T(8,128)(2,1)S(1)} %get-tuple-element.50), channel_id=1, source_target_pairs={{24,0},{7,1},{26,2},{1,3},{28,4},{3,5},{30,6},{5,7},{0,8},{15,9},{... | collective-permute-start | bytes 1572872 | tf_op jit(solution)/shard_map/ppermute | solution.py:374

commit v11 on v10

--- a/solution.py
+++ b/solution.py
@@ -392,16 +392,16 @@
     late = send(after(halves2[1], (backs[1], backs[3])), back(deliver_pairs(2)))
 
     f32, bf16 = jnp.float32, jnp.bfloat16
-    sums = combine((0, 1, 3), q, pairs[0] + pairs[1], [backs[k] for k in (0, 1, 3)], [], [f32] * 4)
+    sums = combine((0, 1, 3), after(q, early), pairs[0] + pairs[1], [backs[k] for k in (0, 1, 3)], [], [f32] * 4)
     parts = {}
     for p, slab in ((0, early), (1, late)):
         kinds = (f32, bf16) if p == 0 else (bf16, bf16)
         parts[p] = finish(q, pairs[p], slab, sums[2 * p : 2 * p + 2], kinds)
     part0, part2 = parts[0]
     part1, part3 = parts[1]
-    mixed = part0 + send(after(part2, late), back(spread_pairs(2))).astype(f32)
+    mixed = part0 + send(part2, back(spread_pairs(2))).astype(f32)
     mixed = lax.optimization_barrier(mixed)
-    for j, part in ((1, part1), (3, part3)):
+    for j, part in ((3, part3), (1, part1)):
         mixed = mixed + send(part, back(spread_pairs(j))).astype(f32)
     return mixed.astype(bf16)
 

time: 103 us -> 100 us (0.971)
  waiting for transfers between devices: 53.5 us -> 48.8 us
  starting transfers between devices: 22.8 us -> 24.1 us
    ppermute x14, waiting for transfers between devices: 53.5 us -> 48.8 us  [per_device(): send = lambda v, pairs: lax.ppermute(v, 'expert', pairs)]
    ppermute x14, starting transfers between devices: 22.8 us -> 24.1 us  [per_device(): send = lambda v, pairs: lax.ppermute(v, 'expert', pairs)]
  transfers between devices with their start and end apart: 14 -> 14, of which waited for: 10 -> 12; matrix products, arithmetic and copies ran while one was open for 0% -> 0% of each run, Pallas kernels for 22% -> 23%
where the time goes in v11:
time: 100 us; the launch traced here: 98.8 us
  waiting for transfers between devices  48.8 us (49%)
  Pallas kernels  24.7 us (25%)
  starting transfers between devices  24.1 us (24%)
  other arithmetic  1.12 us (1%)
    ppermute x14, waiting for transfers between devices, per_device(): send = lambda v, pairs: lax.ppermute(v, 'expert', pairs)  48.8 us
    ppermute x14, starting transfers between devices, per_device(): send = lambda v, pairs: lax.ppermute(v, 'expert', pairs)  24.1 us
    pallas_call x3, Pallas kernels, expert(): pl.pallas_call(functools.partial(expert_kernel, count, ff), in_specs=[vme...  12.8 us
    pallas_call x1, Pallas kernels, hold(): pl.pallas_call(hold_kernel, in_specs=[pl.BlockSpec(memory_space=pl.ANY)]...  4.33 us
    pallas_call x1, Pallas kernels, combine(): pl.pallas_call(functools.partial(combine_kernel, which), in_specs=[vmem]...  2.4 us
    pallas_call x2, Pallas kernels, pack(): pl.pallas_call(functools.partial(pack_kernel, which), in_specs=[vmem] * (...  2.19 us
  transfers between devices with their start and end apart: 14, of which 12 were waited for; matrix products, arithmetic and copies ran while one was open for 0% of the time, Pallas kernels for 23%

profile of v11, /device:TPU:96, one launch (start us, length us, event | category | flops | bytes accessed | tf_op | source)
XLA Modules:
  0.0 98.8 jit_solution(15012421984080768269)
XLA Ops:
  0.0 1.1 %prep.1 = (bf16[128,2176]{1,0:T(8,128)(2,1)S(1)}, bf16[2,16,128]{2,1,0:T(8,128)(2,1)S(1)}) custom-call(s32[8,128]{1,0:T(8,128)} %bitcast.2, f32[8,128]{1,0:T(8,128)} %bitcast.3, bf16[128,2048]{1,0:T(8,128)(2,1)} %tok_hbm.1), custom_call_target="tpu_custom_call" | custom-call | flops 1048576 | bytes 1048576 | tf_op jit(solution)/shard_map/prep/pallas_call | solution.py:92
  1.1 3.1 %collective-permute-start.2 = (bf16[128,2176]{1,0:T(8,128)(2,1)S(1)}, bf16[128,2176]{1,0:T(8,128)(2,1)S(1)}, u32[]{:S(2)}, u32[]{:S(2)}) collective-permute-start(bf16[128,2176]{1,0:T(8,128)(2,1)S(1)} %get-tuple-element.29.refs_0_.refs_3_), channel_id=1, source_target_pairs={{0,16},{1,5},{2,18},{3,7},{4,20},{5,1},{6,22},{7,3},{8,24},{9,13},... | collective-permute-start | bytes 1671176 | tf_op jit(solution)/shard_map/ppermute | solution.py:374
  4.2 0.6 collective-permute-start.1
  4.8 2.6 %collective-permute-start = (bf16[128,2176]{1,0:T(8,128)(2,1)S(1)}, bf16[128,2176]{1,0:T(8,128)(2,1)S(1)}, u32[]{:S(2)}, u32[]{:S(2)}) collective-permute-start(bf16[128,2176]{1,0:T(8,128)(2,1)S(1)} %get-tuple-element.29.refs_0_.refs_3_), channel_id=1, source_target_pairs={{0,24},{1,7},{2,26},{3,1},{4,28},{5,3},{6,30},{7,5},{8,0},{9,15},{... | collective-permute-start | bytes 1671176 | tf_op jit(solution)/shard_map/ppermute | solution.py:374
  7.5 4.3 %hold.1 = (bf16[3072,1536]{1,0:T(8,128)(2,1)S(1)}, f32[8,128]{1,0:T(8,128)}) custom-call(bf16[1,2048,768]{2,1,0:T(8,128)(2,1)} %wg.1, bf16[1,2048,768]{2,1,0:T(8,128)(2,1)} %wu.1, bf16[1,768,2048]{2,1,0:T(8,128)(2,1)} %wd.1), custom_call_target="tpu_custom_call" | custom-call | bytes 18874368 | tf_op jit(solution)/shard_map/hold/pallas_call | solution.py:358
  11.8 0.5 collective-permute-done.2.refs_3_.refs_4_
  12.3 5.9 %collective-permute-done.1.refs_2_.refs_3_ = bf16[128,2176]{1,0:T(8,128)(2,1)S(1)} collective-permute-done((bf16[128,2176]{1,0:T(8,128)(2,1)S(1)}, bf16[128,2176]{1,0:T(8,128)(2,1)S(1)}, u32[]{:S(2)}, u32[]{:S(2)}) %collective-permute-start.1) | collective-permute-done | bytes 557088 | tf_op jit(solution)/shard_map/ppermute | solution.py:374
  18.2 0.1 collective-permute-done.refs_1_.refs_4_
  18.3 1.1 %pack.3 = (bf16[320,2048]{1,0:T(8,128)(2,1)S(1)}, bf16[320,2048]{1,0:T(8,128)(2,1)S(1)}) custom-call(bf16[2,16,128]{2,1,0:T(8,128)(2,1)S(1)} %get-tuple-element.37.q_ref.refs_2_, bf16[128,2176]{1,0:T(8,128)(2,1)S(1)} %get-tuple-element.29.refs_0_.refs_3_, bf16[128,2176]{1,0:T(8,128)(2,1)S(1)} %collective-permute-done.refs_1_.refs_4_, ...), custom_call_target="tpu_custom_call" | custom-call | flops 671088640 | bytes 4718592 | tf_op jit(solution)/shard_map/pack/pallas_call | solution.py:159
  19.4 0.1 collective-permute-start.5
  19.5 3.1 %collective-permute-start.3 = (bf16[320,2048]{1,0:T(8,128)(2,1)S(1)}, bf16[320,2048]{1,0:T(8,128)(2,1)S(1)}, u32[]{:S(2)}, u32[]{:S(2)}) collective-permute-start(bf16[320,2048]{1,0:T(8,128)(2,1)S(1)} %get-tuple-element.31), channel_id=1, source_target_pairs={{0,6},{1,25},{2,0},{3,27},{4,2},{5,29},{6,4},{7,31},{8,14},{9,1},{... | collective-permute-start | bytes 3932168 | tf_op jit(solution)/shard_map/ppermute | solution.py:374
  22.6 0.0 collective-permute-start.7
  22.6 1.1 %pack.2 = (bf16[320,2048]{1,0:T(8,128)(2,1)S(1)}, bf16[320,2048]{1,0:T(8,128)(2,1)S(1)}) custom-call(bf16[2,16,128]{2,1,0:T(8,128)(2,1)S(1)} %get-tuple-element.37.q_ref.refs_2_, bf16[128,2176]{1,0:T(8,128)(2,1)S(1)} %get-tuple-element.29.refs_0_.refs_3_, bf16[128,2176]{1,0:T(8,128)(2,1)S(1)} %collective-permute-done.refs_1_.refs_4_, ...), custom_call_target="tpu_custom_call" | custom-call | flops 671088640 | bytes 4718592 | tf_op jit(solution)/shard_map/pack/pallas_call | solution.py:159
  23.7 14.0 %collective-permute-done.3.refs_1_ = bf16[320,2048]{1,0:T(8,128)(2,1)S(1)} collective-permute-done((bf16[320,2048]{1,0:T(8,128)(2,1)S(1)}, bf16[320,2048]{1,0:T(8,128)(2,1)S(1)}, u32[]{:S(2)}, u32[]{:S(2)}) %collective-permute-start.3) | collective-permute-done | bytes 1310752 | tf_op jit(solution)/shard_map/ppermute | solution.py:374
  37.8 2.7 %collective-permute-start.4 = (bf16[320,2048]{1,0:T(8,128)(2,1)S(1)}, bf16[320,2048]{1,0:T(8,128)(2,1)S(1)}, u32[]{:S(2)}, u32[]{:S(2)}) collective-permute-start(bf16[320,2048]{1,0:T(8,128)(2,1)S(1)} %get-tuple-element.32), channel_id=1, source_target_pairs={{0,4},{1,17},{2,6},{3,19},{4,0},{5,21},{6,2},{7,23},{8,12},{9,25},... | collective-permute-start | bytes 3932168 | tf_op jit(solution)/shard_map/ppermute | solution.py:374
  40.4 1.0 %collective-permute-done.7.refs_0_ = bf16[320,2048]{1,0:T(8,128)(2,1)S(1)} collective-permute-done((bf16[320,2048]{1,0:T(8,128)(2,1)S(1)}, bf16[320,2048]{1,0:T(8,128)(2,1)S(1)}, u32[]{:S(2)}, u32[]{:S(2)}) %collective-permute-start.7) | collective-permute-done | bytes 1310752 | tf_op jit(solution)/shard_map/ppermute | solution.py:374
  41.4 0.0 collective-permute-done.5.refs_2_.refs_3_
  41.4 6.3 %expert.5 = (bf16[320,2048]{1,0:T(8,128)(2,1)S(1)}, bf16[320,2048]{1,0:T(8,128)(2,1)S(1)}) custom-call(bf16[320,2048]{1,0:T(8,128)(2,1)S(1)} %collective-permute-done.7.refs_0_, bf16[320,2048]{1,0:T(8,128)(2,1)S(1)} %collective-permute-done.3.refs_1_, bf16[3072,1536]{1,0:T(8,128)(2,1)S(1)} %get-tuple-element.35.refs_1_.refs_2_, ...), custom_call_target="tpu_custom_call" | custom-call | flops 6039797760 | bytes 5242880 | tf_op jit(solution)/shard_map/expert/pallas_call | solution.py:319
  47.7 0.1 collective-permute-start.8
  47.8 2.0 %collective-permute-start.9 = (bf16[320,2048]{1,0:T(8,128)(2,1)S(1)}, bf16[320,2048]{1,0:T(8,128)(2,1)S(1)}, u32[]{:S(2)}, u32[]{:S(2)}) collective-permute-start(bf16[320,2048]{1,0:T(8,128)(2,1)S(1)} %get-tuple-element.40), channel_id=1, source_target_pairs={{6,0},{25,1},{0,2},{27,3},{2,4},{29,5},{4,6},{31,7},{14,8},{1,9},{... | collective-permute-start | bytes 3932168 | tf_op jit(solution)/shard_map/ppermute | solution.py:374
  49.8 7.1 %collective-permute-done.4.refs_0_ = bf16[320,2048]{1,0:T(8,128)(2,1)S(1)} collective-permute-done((bf16[320,2048]{1,0:T(8,128)(2,1)S(1)}, bf16[320,2048]{1,0:T(8,128)(2,1)S(1)}, u32[]{:S(2)}, u32[]{:S(2)}) %collective-permute-start.4) | collective-permute-done | bytes 1310752 | tf_op jit(solution)/shard_map/ppermute | solution.py:374
  57.0 3.3 %expert.3 = (bf16[160,2048]{1,0:T(8,128)(2,1)S(1)}, bf16[160,2048]{1,0:T(8,128)(2,1)S(1)}) custom-call(bf16[320,2048]{1,0:T(8,128)(2,1)S(1)} %collective-permute-done.4.refs_0_, bf16[3072,1536]{1,0:T(8,128)(2,1)S(1)} %get-tuple-element.35.refs_1_.refs_2_, bf16[3072,1536]{1,0:T(8,128)(2,1)S(1)} %collective-permute-done.5.refs_2_.refs_3_), custom_call_target="tpu_custom_call" | custom-call | flops 3019898880 | bytes 2621440 | tf_op jit(solution)/shard_map/expert/pallas_call | solution.py:319
  60.2 2.7 %collective-permute-start.6 = (bf16[160,2048]{1,0:T(8,128)(2,1)S(1)}, bf16[160,2048]{1,0:T(8,128)(2,1)S(1)}, u32[]{:S(2)}, u32[]{:S(2)}) collective-permute-start(bf16[160,2048]{1,0:T(8,128)(2,1)S(1)} %get-tuple-element.36), channel_id=1, source_target_pairs={{4,0},{17,1},{6,2},{19,3},{0,4},{21,5},{2,6},{23,7},{12,8},{25,9},... | collective-permute-start | bytes 1966088 | tf_op jit(solution)/shard_map/ppermute | solution.py:374
  63.0 9.0 %collective-permute-done.8.refs_5_ = bf16[320,2048]{1,0:T(8,128)(2,1)S(1)} collective-permute-done((bf16[320,2048]{1,0:T(8,128)(2,1)S(1)}, bf16[320,2048]{1,0:T(8,128)(2,1)S(1)}, u32[]{:S(2)}, u32[]{:S(2)}) %collective-permute-start.8) | collective-permute-done | bytes 1310752 | tf_op jit(solution)/shard_map/ppermute | solution.py:374
  72.0 0.0 collective-permute-done.9.refs_6_
  72.0 1.6 %collective-permute-start.11 = (bf16[160,2048]{1,0:T(8,128)(2,1)S(1)}, bf16[160,2048]{1,0:T(8,128)(2,1)S(1)}, u32[]{:S(2)}, u32[]{:S(2)}) collective-permute-start(bf16[160,2048]{1,0:T(8,128)(2,1)S(1)} %get-tuple-element.46), channel_id=1, source_target_pairs={{4,0},{17,1},{6,2},{19,3},{0,4},{21,5},{2,6},{23,7},{12,8},{25,9},... | collective-permute-start | bytes 1966088 | tf_op jit(solution)/shard_map/ppermute | solution.py:374
  73.6 3.3 %expert.4.refs_4_ = bf16[320,2048]{1,0:T(8,128)(2,1)S(1)} custom-call(bf16[320,2048]{1,0:T(8,128)(2,1)S(1)} %get-tuple-element.38.refs_0_, bf16[3072,1536]{1,0:T(8,128)(2,1)S(1)} %get-tuple-element.35.refs_1_.refs_2_, bf16[3072,1536]{1,0:T(8,128)(2,1)S(1)} %collective-permute-done.5.refs_2_.refs_3_), custom_call_target="tpu_custom_call" | custom-call | flops 3019898880 | bytes 2621440 | tf_op jit(solution)/shard_map/expert/pallas_call | solution.py:319
  76.8 1.1 %collective-permute-done.6.back_ref = bf16[160,2048]{1,0:T(8,128)(2,1)S(1)} collective-permute-done((bf16[160,2048]{1,0:T(8,128)(2,1)S(1)}, bf16[160,2048]{1,0:T(8,128)(2,1)S(1)}, u32[]{:S(2)}, u32[]{:S(2)}) %collective-permute-start.6) | collective-permute-done | bytes 655392 | tf_op jit(solution)/shard_map/ppermute | solution.py:374
  78.0 2.4 %combine.1 = (f32[128,2048]{1,0:T(8,128)S(1)}, f32[128,2048]{1,0:T(8,128)S(1)}, f32[128,2048]{1,0:T(8,128)S(1)}, f32[128,2048]{1,0:T(8,128)S(1)}) custom-call(bf16[2,16,128]{2,1,0:T(8,128)(2,1)S(1)} %get-tuple-element.37.q_ref.refs_2_, bf16[128,2176]{1,0:T(8,128)(2,1)S(1)} %get-tuple-element.29.refs_0_.refs_3_, ...), custom_call_target="tpu_custom_call" | custom-call | flops 1006632960 | bytes 7077888 | tf_op jit(solution)/shard_map/combine/pallas_call | solution.py:221
  80.4 1.0 finish.2
  81.4 2.1 %collective-permute-start.10 = (bf16[128,2048]{1,0:T(8,128)(2,1)S(1)}, bf16[128,2048]{1,0:T(8,128)(2,1)S(1)}, u32[]{:S(2)}, u32[]{:S(2)}) collective-permute-start(bf16[128,2048]{1,0:T(8,128)(2,1)S(1)} %get-tuple-element.44), channel_id=1, source_target_pairs={{16,0},{5,1},{18,2},{7,3},{20,4},{1,5},{22,6},{3,7},{24,8},{13,9},... | collective-permute-start | bytes 1572872 | tf_op jit(solution)/shard_map/ppermute | solution.py:374
  83.5 2.6 %collective-permute-done.11.back_ref = bf16[160,2048]{1,0:T(8,128)(2,1)S(1)} collective-permute-done((bf16[160,2048]{1,0:T(8,128)(2,1)S(1)}, bf16[160,2048]{1,0:T(8,128)(2,1)S(1)}, u32[]{:S(2)}, u32[]{:S(2)}) %collective-permute-start.11) | collective-permute-done | bytes 655392 | tf_op jit(solution)/shard_map/ppermute | solution.py:374
  86.1 1.0 finish.3
  87.0 1.7 %collective-permute-start.12 = (bf16[128,2048]{1,0:T(8,128)(2,1)S(1)}, bf16[128,2048]{1,0:T(8,128)(2,1)S(1)}, u32[]{:S(2)}, u32[]{:S(2)}) collective-permute-start(bf16[128,2048]{1,0:T(8,128)(2,1)S(1)} %get-tuple-element.49), channel_id=1, source_target_pairs={{24,0},{7,1},{26,2},{1,3},{28,4},{3,5},{30,6},{5,7},{0,8},{15,9},{... | collective-permute-start | bytes 1572872 | tf_op jit(solution)/shard_map/ppermute | solution.py:374
  88.7 1.7 %collective-permute-start.13 = (bf16[128,2048]{1,0:T(8,128)(2,1)S(1)}, bf16[128,2048]{1,0:T(8,128)(2,1)S(1)}, u32[]{:S(2)}, u32[]{:S(2)}) collective-permute-start(bf16[128,2048]{1,0:T(8,128)(2,1)S(1)} %get-tuple-element.50), channel_id=1, source_target_pairs={{8,0},{3,1},{10,2},{5,3},{12,4},{7,5},{14,6},{1,7},{16,8},{11,9},{... | collective-permute-start | bytes 1572872 | tf_op jit(solution)/shard_map/ppermute | solution.py:374
  90.3 1.8 %collective-permute-done.10 = bf16[128,2048]{1,0:T(8,128)(2,1)S(1)} collective-permute-done((bf16[128,2048]{1,0:T(8,128)(2,1)S(1)}, bf16[128,2048]{1,0:T(8,128)(2,1)S(1)}, u32[]{:S(2)}, u32[]{:S(2)}) %collective-permute-start.10) | collective-permute-done | bytes 524320 | tf_op jit(solution)/shard_map/ppermute | solution.py:374
  92.2 0.1 convert_add_fusion
  92.3 5.5 %collective-permute-done.12 = bf16[128,2048]{1,0:T(8,128)(2,1)S(1)} collective-permute-done((bf16[128,2048]{1,0:T(8,128)(2,1)S(1)}, bf16[128,2048]{1,0:T(8,128)(2,1)S(1)}, u32[]{:S(2)}, u32[]{:S(2)}) %collective-permute-start.12) | collective-permute-done | bytes 524320 | tf_op jit(solution)/shard_map/ppermute | solution.py:374
  97.7 0.1 collective-permute-done.13
  97.9 1.0 add_convert_fusion
Async XLA Ops:
  1.1 11.2 %collective-permute-start.2 = (bf16[128,2176]{1,0:T(8,128)(2,1)S(1)}, bf16[128,2176]{1,0:T(8,128)(2,1)S(1)}, u32[]{:S(2)}, u32[]{:S(2)}) collective-permute-start(bf16[128,2176]{1,0:T(8,128)(2,1)S(1)} %get-tuple-element.29.refs_0_.refs_3_), channel_id=1, source_target_pairs={{0,16},{1,5},{2,18},{3,7},{4,20},{5,1},{6,22},{7,3},{8,24},{9,13},... | collective-permute-start | bytes 1671176 | tf_op jit(solution)/shard_map/ppermute | solution.py:374
  4.2 14.0 %collective-permute-start.1 = (bf16[128,2176]{1,0:T(8,128)(2,1)S(1)}, bf16[128,2176]{1,0:T(8,128)(2,1)S(1)}, u32[]{:S(2)}, u32[]{:S(2)}) collective-permute-start(bf16[128,2176]{1,0:T(8,128)(2,1)S(1)} %get-tuple-element.29.refs_0_.refs_3_), channel_id=1, source_target_pairs={{0,8},{1,3},{2,10},{3,5},{4,12},{5,7},{6,14},{7,1},{8,16},{9,11},{... | collective-permute-start | bytes 1671176 | tf_op jit(solution)/shard_map/ppermute | solution.py:374
  4.8 13.5 %collective-permute-start = (bf16[128,2176]{1,0:T(8,128)(2,1)S(1)}, bf16[128,2176]{1,0:T(8,128)(2,1)S(1)}, u32[]{:S(2)}, u32[]{:S(2)}) collective-permute-start(bf16[128,2176]{1,0:T(8,128)(2,1)S(1)} %get-tuple-element.29.refs_0_.refs_3_), channel_id=1, source_target_pairs={{0,24},{1,7},{2,26},{3,1},{4,28},{5,3},{6,30},{7,5},{8,0},{9,15},{... | collective-permute-start | bytes 1671176 | tf_op jit(solution)/shard_map/ppermute | solution.py:374
  19.4 22.0 %collective-permute-start.5 = (bf16[3072,1536]{1,0:T(8,128)(2,1)S(1)}, bf16[3072,1536]{1,0:T(8,128)(2,1)S(1)}, u32[]{:S(2)}, u32[]{:S(2)}) collective-permute-start(bf16[3072,1536]{1,0:T(8,128)(2,1)S(1)} %get-tuple-element.35.refs_1_.refs_2_), channel_id=1, source_target_pairs={{0,1},{1,0},{2,3},{3,2},{4,5},{5,4},{6,7},{7,6},{8,9},{9,8},{10,11... | collective-permute-start | bytes 28311560 | tf_op jit(solution)/shard_map/ppermute | solution.py:374
  19.5 18.2 %collective-permute-start.3 = (bf16[320,2048]{1,0:T(8,128)(2,1)S(1)}, bf16[320,2048]{1,0:T(8,128)(2,1)S(1)}, u32[]{:S(2)}, u32[]{:S(2)}) collective-permute-start(bf16[320,2048]{1,0:T(8,128)(2,1)S(1)} %get-tuple-element.31), channel_id=1, source_target_pairs={{0,6},{1,25},{2,0},{3,27},{4,2},{5,29},{6,4},{7,31},{8,14},{9,1},{... | collective-permute-start | bytes 3932168 | tf_op jit(solution)/shard_map/ppermute | solution.py:374
  22.6 18.8 %collective-permute-start.7 = (bf16[320,2048]{1,0:T(8,128)(2,1)S(1)}, bf16[320,2048]{1,0:T(8,128)(2,1)S(1)}, u32[]{:S(2)}, u32[]{:S(2)}) collective-permute-start(bf16[320,2048]{1,0:T(8,128)(2,1)S(1)} %get-tuple-element.34), channel_id=1, source_target_pairs={{0,2},{1,9},{2,4},{3,11},{4,6},{5,13},{6,0},{7,15},{8,10},{9,17},{... | collective-permute-start | bytes 3932168 | tf_op jit(solution)/shard_map/ppermute | solution.py:374
  37.8 19.2 %collective-permute-start.4 = (bf16[320,2048]{1,0:T(8,128)(2,1)S(1)}, bf16[320,2048]{1,0:T(8,128)(2,1)S(1)}, u32[]{:S(2)}, u32[]{:S(2)}) collective-permute-start(bf16[320,2048]{1,0:T(8,128)(2,1)S(1)} %get-tuple-element.32), channel_id=1, source_target_pairs={{0,4},{1,17},{2,6},{3,19},{4,0},{5,21},{6,2},{7,23},{8,12},{9,25},... | collective-permute-start | bytes 3932168 | tf_op jit(solution)/shard_map/ppermute | solution.py:374
  47.7 24.2 %collective-permute-start.8 = (bf16[320,2048]{1,0:T(8,128)(2,1)S(1)}, bf16[320,2048]{1,0:T(8,128)(2,1)S(1)}, u32[]{:S(2)}, u32[]{:S(2)}) collective-permute-start(bf16[320,2048]{1,0:T(8,128)(2,1)S(1)} %get-tuple-element.39), channel_id=1, source_target_pairs={{2,0},{9,1},{4,2},{11,3},{6,4},{13,5},{0,6},{15,7},{10,8},{17,9},{... | collective-permute-start | bytes 3932168 | tf_op jit(solution)/shard_map/ppermute | solution.py:374
  47.8 24.1 %collective-permute-start.9 = (bf16[320,2048]{1,0:T(8,128)(2,1)S(1)}, bf16[320,2048]{1,0:T(8,128)(2,1)S(1)}, u32[]{:S(2)}, u32[]{:S(2)}) collective-permute-start(bf16[320,2048]{1,0:T(8,128)(2,1)S(1)} %get-tuple-element.40), channel_id=1, source_target_pairs={{6,0},{25,1},{0,2},{27,3},{2,4},{29,5},{4,6},{31,7},{14,8},{1,9},{... | collective-permute-start | bytes 3932168 | tf_op jit(solution)/shard_map/ppermute | solution.py:374
  60.2 17.7 %collective-permute-start.6 = (bf16[160,2048]{1,0:T(8,128)(2,1)S(1)}, bf16[160,2048]{1,0:T(8,128)(2,1)S(1)}, u32[]{:S(2)}, u32[]{:S(2)}) collective-permute-start(bf16[160,2048]{1,0:T(8,128)(2,1)S(1)} %get-tuple-element.36), channel_id=1, source_target_pairs={{4,0},{17,1},{6,2},{19,3},{0,4},{21,5},{2,6},{23,7},{12,8},{25,9},... | collective-permute-start | bytes 1966088 | tf_op jit(solution)/shard_map/ppermute | solution.py:374
  72.0 14.1 %collective-permute-start.11 = (bf16[160,2048]{1,0:T(8,128)(2,1)S(1)}, bf16[160,2048]{1,0:T(8,128)(2,1)S(1)}, u32[]{:S(2)}, u32[]{:S(2)}) collective-permute-start(bf16[160,2048]{1,0:T(8,128)(2,1)S(1)} %get-tuple-element.46), channel_id=1, source_target_pairs={{4,0},{17,1},{6,2},{19,3},{0,4},{21,5},{2,6},{23,7},{12,8},{25,9},... | collective-permute-start | bytes 1966088 | tf_op jit(solution)/shard_map/ppermute | solution.py:374
  81.4 10.8 %collective-permute-start.10 = (bf16[128,2048]{1,0:T(8,128)(2,1)S(1)}, bf16[128,2048]{1,0:T(8,128)(2,1)S(1)}, u32[]{:S(2)}, u32[]{:S(2)}) collective-permute-start(bf16[128,2048]{1,0:T(8,128)(2,1)S(1)} %get-tuple-element.44), channel_id=1, source_target_pairs={{16,0},{5,1},{18,2},{7,3},{20,4},{1,5},{22,6},{3,7},{24,8},{13,9},... | collective-permute-start | bytes 1572872 | tf_op jit(solution)/shard_map/ppermute | solution.py:374
  87.0 10.7 %collective-permute-start.12 = (bf16[128,2048]{1,0:T(8,128)(2,1)S(1)}, bf16[128,2048]{1,0:T(8,128)(2,1)S(1)}, u32[]{:S(2)}, u32[]{:S(2)}) collective-permute-start(bf16[128,2048]{1,0:T(8,128)(2,1)S(1)} %get-tuple-element.49), channel_id=1, source_target_pairs={{24,0},{7,1},{26,2},{1,3},{28,4},{3,5},{30,6},{5,7},{0,8},{15,9},{... | collective-permute-start | bytes 1572872 | tf_op jit(solution)/shard_map/ppermute | solution.py:374
  88.7 9.2 %collective-permute-start.13 = (bf16[128,2048]{1,0:T(8,128)(2,1)S(1)}, bf16[128,2048]{1,0:T(8,128)(2,1)S(1)}, u32[]{:S(2)}, u32[]{:S(2)}) collective-permute-start(bf16[128,2048]{1,0:T(8,128)(2,1)S(1)} %get-tuple-element.50), channel_id=1, source_target_pairs={{8,0},{3,1},{10,2},{5,3},{12,4},{7,5},{14,6},{1,7},{16,8},{11,9},{... | collective-permute-start | bytes 1572872 | tf_op jit(solution)/shard_map/ppermute | solution.py:374

commit v12 on v11

--- a/solution.py
+++ b/solution.py
@@ -389,7 +389,7 @@
         backs[k] = send(slab, back(deliver_pairs(k)))
     halves2 = expert([arrived[2]], weights, 2)
     early = send(halves2[0], back(deliver_pairs(2)))
-    late = send(after(halves2[1], (backs[1], backs[3])), back(deliver_pairs(2)))
+    late = send(after(halves2[1], backs[0]), back(deliver_pairs(2)))
 
     f32, bf16 = jnp.float32, jnp.bfloat16
     sums = combine((0, 1, 3), after(q, early), pairs[0] + pairs[1], [backs[k] for k in (0, 1, 3)], [], [f32] * 4)

time: 100 us -> 100 us (level)
  transfers between devices with their start and end apart: 14 -> 14, of which waited for: 12 -> 11; matrix products, arithmetic and copies ran while one was open for 0% -> 0% of each run, Pallas kernels for 23% -> 23%
where the time goes in v12:
time: 100 us; the launch traced here: 98.8 us
  waiting for transfers between devices  49.5 us (50%)
  Pallas kernels  24.8 us (25%)
  starting transfers between devices  23.4 us (23%)
  other arithmetic  1.12 us (1%)
    ppermute x14, waiting for transfers between devices, per_device(): send = lambda v, pairs: lax.ppermute(v, 'expert', pairs)  49.5 us
    ppermute x14, starting transfers between devices, per_device(): send = lambda v, pairs: lax.ppermute(v, 'expert', pairs)  23.4 us
    pallas_call x3, Pallas kernels, expert(): pl.pallas_call(functools.partial(expert_kernel, count, ff), in_specs=[vme...  12.8 us
    pallas_call x1, Pallas kernels, hold(): pl.pallas_call(hold_kernel, in_specs=[pl.BlockSpec(memory_space=pl.ANY)]...  4.33 us
    pallas_call x1, Pallas kernels, combine(): pl.pallas_call(functools.partial(combine_kernel, which), in_specs=[vmem]...  2.41 us
    pallas_call x2, Pallas kernels, pack(): pl.pallas_call(functools.partial(pack_kernel, which), in_specs=[vmem] * (...  2.19 us
  transfers between devices with their start and end apart: 14, of which 11 were waited for; matrix products, arithmetic and copies ran while one was open for 0% of the time, Pallas kernels for 23%

profile of v12, /device:TPU:96, one launch (start us, length us, event | category | flops | bytes accessed | tf_op | source)
XLA Modules:
  0.0 98.8 jit_solution(13852748519309670762)
XLA Ops:
  0.0 1.1 %prep.1 = (bf16[128,2176]{1,0:T(8,128)(2,1)S(1)}, bf16[2,16,128]{2,1,0:T(8,128)(2,1)S(1)}) custom-call(s32[8,128]{1,0:T(8,128)} %bitcast.2, f32[8,128]{1,0:T(8,128)} %bitcast.3, bf16[128,2048]{1,0:T(8,128)(2,1)} %tok_hbm.1), custom_call_target="tpu_custom_call" | custom-call | flops 1048576 | bytes 1048576 | tf_op jit(solution)/shard_map/prep/pallas_call | solution.py:92
  1.1 3.1 %collective-permute-start.2 = (bf16[128,2176]{1,0:T(8,128)(2,1)S(1)}, bf16[128,2176]{1,0:T(8,128)(2,1)S(1)}, u32[]{:S(2)}, u32[]{:S(2)}) collective-permute-start(bf16[128,2176]{1,0:T(8,128)(2,1)S(1)} %get-tuple-element.29.refs_0_.refs_3_), channel_id=1, source_target_pairs={{0,16},{1,5},{2,18},{3,7},{4,20},{5,1},{6,22},{7,3},{8,24},{9,13},... | collective-permute-start | bytes 1671176 | tf_op jit(solution)/shard_map/ppermute | solution.py:374
  4.2 0.6 collective-permute-start.1
  4.8 2.6 %collective-permute-start = (bf16[128,2176]{1,0:T(8,128)(2,1)S(1)}, bf16[128,2176]{1,0:T(8,128)(2,1)S(1)}, u32[]{:S(2)}, u32[]{:S(2)}) collective-permute-start(bf16[128,2176]{1,0:T(8,128)(2,1)S(1)} %get-tuple-element.29.refs_0_.refs_3_), channel_id=1, source_target_pairs={{0,24},{1,7},{2,26},{3,1},{4,28},{5,3},{6,30},{7,5},{8,0},{9,15},{... | collective-permute-start | bytes 1671176 | tf_op jit(solution)/shard_map/ppermute | solution.py:374
  7.5 4.3 %hold.1 = (bf16[3072,1536]{1,0:T(8,128)(2,1)S(1)}, f32[8,128]{1,0:T(8,128)}) custom-call(bf16[1,2048,768]{2,1,0:T(8,128)(2,1)} %wg.1, bf16[1,2048,768]{2,1,0:T(8,128)(2,1)} %wu.1, bf16[1,768,2048]{2,1,0:T(8,128)(2,1)} %wd.1), custom_call_target="tpu_custom_call" | custom-call | bytes 18874368 | tf_op jit(solution)/shard_map/hold/pallas_call | solution.py:358
  11.8 0.5 collective-permute-done.2.refs_3_.refs_4_
  12.3 5.9 %collective-permute-done.1.refs_2_.refs_3_ = bf16[128,2176]{1,0:T(8,128)(2,1)S(1)} collective-permute-done((bf16[128,2176]{1,0:T(8,128)(2,1)S(1)}, bf16[128,2176]{1,0:T(8,128)(2,1)S(1)}, u32[]{:S(2)}, u32[]{:S(2)}) %collective-permute-start.1) | collective-permute-done | bytes 557088 | tf_op jit(solution)/shard_map/ppermute | solution.py:374
  18.2 0.1 collective-permute-done.refs_1_.refs_4_
  18.3 1.1 %pack.3 = (bf16[320,2048]{1,0:T(8,128)(2,1)S(1)}, bf16[320,2048]{1,0:T(8,128)(2,1)S(1)}) custom-call(bf16[2,16,128]{2,1,0:T(8,128)(2,1)S(1)} %get-tuple-element.37.q_ref.refs_2_, bf16[128,2176]{1,0:T(8,128)(2,1)S(1)} %get-tuple-element.29.refs_0_.refs_3_, bf16[128,2176]{1,0:T(8,128)(2,1)S(1)} %collective-permute-done.refs_1_.refs_4_, ...), custom_call_target="tpu_custom_call" | custom-call | flops 671088640 | bytes 4718592 | tf_op jit(solution)/shard_map/pack/pallas_call | solution.py:159
  19.4 0.1 collective-permute-start.5
  19.5 3.1 %collective-permute-start.3 = (bf16[320,2048]{1,0:T(8,128)(2,1)S(1)}, bf16[320,2048]{1,0:T(8,128)(2,1)S(1)}, u32[]{:S(2)}, u32[]{:S(2)}) collective-permute-start(bf16[320,2048]{1,0:T(8,128)(2,1)S(1)} %get-tuple-element.31), channel_id=1, source_target_pairs={{0,6},{1,25},{2,0},{3,27},{4,2},{5,29},{6,4},{7,31},{8,14},{9,1},{... | collective-permute-start | bytes 3932168 | tf_op jit(solution)/shard_map/ppermute | solution.py:374
  22.6 0.0 collective-permute-start.7
  22.6 1.1 %pack.2 = (bf16[320,2048]{1,0:T(8,128)(2,1)S(1)}, bf16[320,2048]{1,0:T(8,128)(2,1)S(1)}) custom-call(bf16[2,16,128]{2,1,0:T(8,128)(2,1)S(1)} %get-tuple-element.37.q_ref.refs_2_, bf16[128,2176]{1,0:T(8,128)(2,1)S(1)} %get-tuple-element.29.refs_0_.refs_3_, bf16[128,2176]{1,0:T(8,128)(2,1)S(1)} %collective-permute-done.refs_1_.refs_4_, ...), custom_call_target="tpu_custom_call" | custom-call | flops 671088640 | bytes 4718592 | tf_op jit(solution)/shard_map/pack/pallas_call | solution.py:159
  23.7 14.0 %collective-permute-done.3.refs_1_ = bf16[320,2048]{1,0:T(8,128)(2,1)S(1)} collective-permute-done((bf16[320,2048]{1,0:T(8,128)(2,1)S(1)}, bf16[320,2048]{1,0:T(8,128)(2,1)S(1)}, u32[]{:S(2)}, u32[]{:S(2)}) %collective-permute-start.3) | collective-permute-done | bytes 1310752 | tf_op jit(solution)/shard_map/ppermute | solution.py:374
  37.8 2.7 %collective-permute-start.4 = (bf16[320,2048]{1,0:T(8,128)(2,1)S(1)}, bf16[320,2048]{1,0:T(8,128)(2,1)S(1)}, u32[]{:S(2)}, u32[]{:S(2)}) collective-permute-start(bf16[320,2048]{1,0:T(8,128)(2,1)S(1)} %get-tuple-element.32), channel_id=1, source_target_pairs={{0,4},{1,17},{2,6},{3,19},{4,0},{5,21},{6,2},{7,23},{8,12},{9,25},... | collective-permute-start | bytes 3932168 | tf_op jit(solution)/shard_map/ppermute | solution.py:374
  40.4 1.0 %collective-permute-done.7.refs_0_ = bf16[320,2048]{1,0:T(8,128)(2,1)S(1)} collective-permute-done((bf16[320,2048]{1,0:T(8,128)(2,1)S(1)}, bf16[320,2048]{1,0:T(8,128)(2,1)S(1)}, u32[]{:S(2)}, u32[]{:S(2)}) %collective-permute-start.7) | collective-permute-done | bytes 1310752 | tf_op jit(solution)/shard_map/ppermute | solution.py:374
  41.4 0.0 collective-permute-done.5.refs_2_.refs_3_
  41.4 6.3 %expert.5 = (bf16[320,2048]{1,0:T(8,128)(2,1)S(1)}, bf16[320,2048]{1,0:T(8,128)(2,1)S(1)}) custom-call(bf16[320,2048]{1,0:T(8,128)(2,1)S(1)} %collective-permute-done.7.refs_0_, bf16[320,2048]{1,0:T(8,128)(2,1)S(1)} %collective-permute-done.3.refs_1_, bf16[3072,1536]{1,0:T(8,128)(2,1)S(1)} %get-tuple-element.35.refs_1_.refs_2_, ...), custom_call_target="tpu_custom_call" | custom-call | flops 6039797760 | bytes 5242880 | tf_op jit(solution)/shard_map/expert/pallas_call | solution.py:319
  47.7 0.1 collective-permute-start.8
  47.8 2.0 %collective-permute-start.9 = (bf16[320,2048]{1,0:T(8,128)(2,1)S(1)}, bf16[320,2048]{1,0:T(8,128)(2,1)S(1)}, u32[]{:S(2)}, u32[]{:S(2)}) collective-permute-start(bf16[320,2048]{1,0:T(8,128)(2,1)S(1)} %get-tuple-element.40), channel_id=1, source_target_pairs={{6,0},{25,1},{0,2},{27,3},{2,4},{29,5},{4,6},{31,7},{14,8},{1,9},{... | collective-permute-start | bytes 3932168 | tf_op jit(solution)/shard_map/ppermute | solution.py:374
  49.8 7.1 %collective-permute-done.4.refs_0_ = bf16[320,2048]{1,0:T(8,128)(2,1)S(1)} collective-permute-done((bf16[320,2048]{1,0:T(8,128)(2,1)S(1)}, bf16[320,2048]{1,0:T(8,128)(2,1)S(1)}, u32[]{:S(2)}, u32[]{:S(2)}) %collective-permute-start.4) | collective-permute-done | bytes 1310752 | tf_op jit(solution)/shard_map/ppermute | solution.py:374
  57.0 3.3 %expert.3 = (bf16[160,2048]{1,0:T(8,128)(2,1)S(1)}, bf16[160,2048]{1,0:T(8,128)(2,1)S(1)}) custom-call(bf16[320,2048]{1,0:T(8,128)(2,1)S(1)} %collective-permute-done.4.refs_0_, bf16[3072,1536]{1,0:T(8,128)(2,1)S(1)} %get-tuple-element.35.refs_1_.refs_2_, bf16[3072,1536]{1,0:T(8,128)(2,1)S(1)} %collective-permute-done.5.refs_2_.refs_3_), custom_call_target="tpu_custom_call" | custom-call | flops 3019898880 | bytes 2621440 | tf_op jit(solution)/shard_map/expert/pallas_call | solution.py:319
  60.2 2.7 %collective-permute-start.6 = (bf16[160,2048]{1,0:T(8,128)(2,1)S(1)}, bf16[160,2048]{1,0:T(8,128)(2,1)S(1)}, u32[]{:S(2)}, u32[]{:S(2)}) collective-permute-start(bf16[160,2048]{1,0:T(8,128)(2,1)S(1)} %get-tuple-element.36), channel_id=1, source_target_pairs={{4,0},{17,1},{6,2},{19,3},{0,4},{21,5},{2,6},{23,7},{12,8},{25,9},... | collective-permute-start | bytes 1966088 | tf_op jit(solution)/shard_map/ppermute | solution.py:374
  63.0 3.3 %expert.4.refs_4_ = bf16[320,2048]{1,0:T(8,128)(2,1)S(1)} custom-call(bf16[320,2048]{1,0:T(8,128)(2,1)S(1)} %get-tuple-element.38.refs_0_, bf16[3072,1536]{1,0:T(8,128)(2,1)S(1)} %get-tuple-element.35.refs_1_.refs_2_, bf16[3072,1536]{1,0:T(8,128)(2,1)S(1)} %collective-permute-done.5.refs_2_.refs_3_), custom_call_target="tpu_custom_call" | custom-call | flops 3019898880 | bytes 2621440 | tf_op jit(solution)/shard_map/expert/pallas_call | solution.py:319
  66.2 1.0 collective-permute-start.11
  67.2 10.8 %collective-permute-done.6.back_ref = bf16[160,2048]{1,0:T(8,128)(2,1)S(1)} collective-permute-done((bf16[160,2048]{1,0:T(8,128)(2,1)S(1)}, bf16[160,2048]{1,0:T(8,128)(2,1)S(1)}, u32[]{:S(2)}, u32[]{:S(2)}) %collective-permute-start.6) | collective-permute-done | bytes 655392 | tf_op jit(solution)/shard_map/ppermute | solution.py:374
  78.0 0.0 collective-permute-done.8.refs_5_
  78.0 0.0 collective-permute-done.9.refs_6_
  78.0 2.4 %combine.1 = (f32[128,2048]{1,0:T(8,128)S(1)}, f32[128,2048]{1,0:T(8,128)S(1)}, f32[128,2048]{1,0:T(8,128)S(1)}, f32[128,2048]{1,0:T(8,128)S(1)}) custom-call(bf16[2,16,128]{2,1,0:T(8,128)(2,1)S(1)} %get-tuple-element.37.q_ref.refs_2_, bf16[128,2176]{1,0:T(8,128)(2,1)S(1)} %get-tuple-element.29.refs_0_.refs_3_, ...), custom_call_target="tpu_custom_call" | custom-call | flops 1006632960 | bytes 7077888 | tf_op jit(solution)/shard_map/combine/pallas_call | solution.py:221
  80.4 1.0 finish.2
  81.4 2.1 %collective-permute-start.10 = (bf16[128,2048]{1,0:T(8,128)(2,1)S(1)}, bf16[128,2048]{1,0:T(8,128)(2,1)S(1)}, u32[]{:S(2)}, u32[]{:S(2)}) collective-permute-start(bf16[128,2048]{1,0:T(8,128)(2,1)S(1)} %get-tuple-element.44), channel_id=1, source_target_pairs={{16,0},{5,1},{18,2},{7,3},{20,4},{1,5},{22,6},{3,7},{24,8},{13,9},... | collective-permute-start | bytes 1572872 | tf_op jit(solution)/shard_map/ppermute | solution.py:374
  83.5 2.6 %collective-permute-done.11.back_ref = bf16[160,2048]{1,0:T(8,128)(2,1)S(1)} collective-permute-done((bf16[160,2048]{1,0:T(8,128)(2,1)S(1)}, bf16[160,2048]{1,0:T(8,128)(2,1)S(1)}, u32[]{:S(2)}, u32[]{:S(2)}) %collective-permute-start.11) | collective-permute-done | bytes 655392 | tf_op jit(solution)/shard_map/ppermute | solution.py:374
  86.0 1.0 finish.3
  87.0 1.7 %collective-permute-start.12 = (bf16[128,2048]{1,0:T(8,128)(2,1)S(1)}, bf16[128,2048]{1,0:T(8,128)(2,1)S(1)}, u32[]{:S(2)}, u32[]{:S(2)}) collective-permute-start(bf16[128,2048]{1,0:T(8,128)(2,1)S(1)} %get-tuple-element.49), channel_id=1, source_target_pairs={{24,0},{7,1},{26,2},{1,3},{28,4},{3,5},{30,6},{5,7},{0,8},{15,9},{... | collective-permute-start | bytes 1572872 | tf_op jit(solution)/shard_map/ppermute | solution.py:374
  88.7 1.6 %collective-permute-start.13 = (bf16[128,2048]{1,0:T(8,128)(2,1)S(1)}, bf16[128,2048]{1,0:T(8,128)(2,1)S(1)}, u32[]{:S(2)}, u32[]{:S(2)}) collective-permute-start(bf16[128,2048]{1,0:T(8,128)(2,1)S(1)} %get-tuple-element.50), channel_id=1, source_target_pairs={{8,0},{3,1},{10,2},{5,3},{12,4},{7,5},{14,6},{1,7},{16,8},{11,9},{... | collective-permute-start | bytes 1572872 | tf_op jit(solution)/shard_map/ppermute | solution.py:374
  90.3 1.8 %collective-permute-done.10 = bf16[128,2048]{1,0:T(8,128)(2,1)S(1)} collective-permute-done((bf16[128,2048]{1,0:T(8,128)(2,1)S(1)}, bf16[128,2048]{1,0:T(8,128)(2,1)S(1)}, u32[]{:S(2)}, u32[]{:S(2)}) %collective-permute-start.10) | collective-permute-done | bytes 524320 | tf_op jit(solution)/shard_map/ppermute | solution.py:374
  92.2 0.1 convert_add_fusion
  92.3 5.4 %collective-permute-done.12 = bf16[128,2048]{1,0:T(8,128)(2,1)S(1)} collective-permute-done((bf16[128,2048]{1,0:T(8,128)(2,1)S(1)}, bf16[128,2048]{1,0:T(8,128)(2,1)S(1)}, u32[]{:S(2)}, u32[]{:S(2)}) %collective-permute-start.12) | collective-permute-done | bytes 524320 | tf_op jit(solution)/shard_map/ppermute | solution.py:374
  97.8 0.1 collective-permute-done.13
  97.9 1.0 add_convert_fusion
Async XLA Ops:
  1.1 11.2 %collective-permute-start.2 = (bf16[128,2176]{1,0:T(8,128)(2,1)S(1)}, bf16[128,2176]{1,0:T(8,128)(2,1)S(1)}, u32[]{:S(2)}, u32[]{:S(2)}) collective-permute-start(bf16[128,2176]{1,0:T(8,128)(2,1)S(1)} %get-tuple-element.29.refs_0_.refs_3_), channel_id=1, source_target_pairs={{0,16},{1,5},{2,18},{3,7},{4,20},{5,1},{6,22},{7,3},{8,24},{9,13},... | collective-permute-start | bytes 1671176 | tf_op jit(solution)/shard_map/ppermute | solution.py:374
  4.2 14.0 %collective-permute-start.1 = (bf16[128,2176]{1,0:T(8,128)(2,1)S(1)}, bf16[128,2176]{1,0:T(8,128)(2,1)S(1)}, u32[]{:S(2)}, u32[]{:S(2)}) collective-permute-start(bf16[128,2176]{1,0:T(8,128)(2,1)S(1)} %get-tuple-element.29.refs_0_.refs_3_), channel_id=1, source_target_pairs={{0,8},{1,3},{2,10},{3,5},{4,12},{5,7},{6,14},{7,1},{8,16},{9,11},{... | collective-permute-start | bytes 1671176 | tf_op jit(solution)/shard_map/ppermute | solution.py:374
  4.8 13.5 %collective-permute-start = (bf16[128,2176]{1,0:T(8,128)(2,1)S(1)}, bf16[128,2176]{1,0:T(8,128)(2,1)S(1)}, u32[]{:S(2)}, u32[]{:S(2)}) collective-permute-start(bf16[128,2176]{1,0:T(8,128)(2,1)S(1)} %get-tuple-element.29.refs_0_.refs_3_), channel_id=1, source_target_pairs={{0,24},{1,7},{2,26},{3,1},{4,28},{5,3},{6,30},{7,5},{8,0},{9,15},{... | collective-permute-start | bytes 1671176 | tf_op jit(solution)/shard_map/ppermute | solution.py:374
  19.4 22.0 %collective-permute-start.5 = (bf16[3072,1536]{1,0:T(8,128)(2,1)S(1)}, bf16[3072,1536]{1,0:T(8,128)(2,1)S(1)}, u32[]{:S(2)}, u32[]{:S(2)}) collective-permute-start(bf16[3072,1536]{1,0:T(8,128)(2,1)S(1)} %get-tuple-element.35.refs_1_.refs_2_), channel_id=1, source_target_pairs={{0,1},{1,0},{2,3},{3,2},{4,5},{5,4},{6,7},{7,6},{8,9},{9,8},{10,11... | collective-permute-start | bytes 28311560 | tf_op jit(solution)/shard_map/ppermute | solution.py:374
  19.5 18.2 %collective-permute-start.3 = (bf16[320,2048]{1,0:T(8,128)(2,1)S(1)}, bf16[320,2048]{1,0:T(8,128)(2,1)S(1)}, u32[]{:S(2)}, u32[]{:S(2)}) collective-permute-start(bf16[320,2048]{1,0:T(8,128)(2,1)S(1)} %get-tuple-element.31), channel_id=1, source_target_pairs={{0,6},{1,25},{2,0},{3,27},{4,2},{5,29},{6,4},{7,31},{8,14},{9,1},{... | collective-permute-start | bytes 3932168 | tf_op jit(solution)/shard_map/ppermute | solution.py:374
  22.6 18.8 %collective-permute-start.7 = (bf16[320,2048]{1,0:T(8,128)(2,1)S(1)}, bf16[320,2048]{1,0:T(8,128)(2,1)S(1)}, u32[]{:S(2)}, u32[]{:S(2)}) collective-permute-start(bf16[320,2048]{1,0:T(8,128)(2,1)S(1)} %get-tuple-element.34), channel_id=1, source_target_pairs={{0,2},{1,9},{2,4},{3,11},{4,6},{5,13},{6,0},{7,15},{8,10},{9,17},{... | collective-permute-start | bytes 3932168 | tf_op jit(solution)/shard_map/ppermute | solution.py:374
  37.8 19.2 %collective-permute-start.4 = (bf16[320,2048]{1,0:T(8,128)(2,1)S(1)}, bf16[320,2048]{1,0:T(8,128)(2,1)S(1)}, u32[]{:S(2)}, u32[]{:S(2)}) collective-permute-start(bf16[320,2048]{1,0:T(8,128)(2,1)S(1)} %get-tuple-element.32), channel_id=1, source_target_pairs={{0,4},{1,17},{2,6},{3,19},{4,0},{5,21},{6,2},{7,23},{8,12},{9,25},... | collective-permute-start | bytes 3932168 | tf_op jit(solution)/shard_map/ppermute | solution.py:374
  47.7 30.2 %collective-permute-start.8 = (bf16[320,2048]{1,0:T(8,128)(2,1)S(1)}, bf16[320,2048]{1,0:T(8,128)(2,1)S(1)}, u32[]{:S(2)}, u32[]{:S(2)}) collective-permute-start(bf16[320,2048]{1,0:T(8,128)(2,1)S(1)} %get-tuple-element.39), channel_id=1, source_target_pairs={{2,0},{9,1},{4,2},{11,3},{6,4},{13,5},{0,6},{15,7},{10,8},{17,9},{... | collective-permute-start | bytes 3932168 | tf_op jit(solution)/shard_map/ppermute | solution.py:374
  47.8 30.1 %collective-permute-start.9 = (bf16[320,2048]{1,0:T(8,128)(2,1)S(1)}, bf16[320,2048]{1,0:T(8,128)(2,1)S(1)}, u32[]{:S(2)}, u32[]{:S(2)}) collective-permute-start(bf16[320,2048]{1,0:T(8,128)(2,1)S(1)} %get-tuple-element.40), channel_id=1, source_target_pairs={{6,0},{25,1},{0,2},{27,3},{2,4},{29,5},{4,6},{31,7},{14,8},{1,9},{... | collective-permute-start | bytes 3932168 | tf_op jit(solution)/shard_map/ppermute | solution.py:374
  60.2 17.7 %collective-permute-start.6 = (bf16[160,2048]{1,0:T(8,128)(2,1)S(1)}, bf16[160,2048]{1,0:T(8,128)(2,1)S(1)}, u32[]{:S(2)}, u32[]{:S(2)}) collective-permute-start(bf16[160,2048]{1,0:T(8,128)(2,1)S(1)} %get-tuple-element.36), channel_id=1, source_target_pairs={{4,0},{17,1},{6,2},{19,3},{0,4},{21,5},{2,6},{23,7},{12,8},{25,9},... | collective-permute-start | bytes 1966088 | tf_op jit(solution)/shard_map/ppermute | solution.py:374
  66.2 19.8 %collective-permute-start.11 = (bf16[160,2048]{1,0:T(8,128)(2,1)S(1)}, bf16[160,2048]{1,0:T(8,128)(2,1)S(1)}, u32[]{:S(2)}, u32[]{:S(2)}) collective-permute-start(bf16[160,2048]{1,0:T(8,128)(2,1)S(1)} %get-tuple-element.46), channel_id=1, source_target_pairs={{4,0},{17,1},{6,2},{19,3},{0,4},{21,5},{2,6},{23,7},{12,8},{25,9},... | collective-permute-start | bytes 1966088 | tf_op jit(solution)/shard_map/ppermute | solution.py:374
  81.4 10.8 %collective-permute-start.10 = (bf16[128,2048]{1,0:T(8,128)(2,1)S(1)}, bf16[128,2048]{1,0:T(8,128)(2,1)S(1)}, u32[]{:S(2)}, u32[]{:S(2)}) collective-permute-start(bf16[128,2048]{1,0:T(8,128)(2,1)S(1)} %get-tuple-element.44), channel_id=1, source_target_pairs={{16,0},{5,1},{18,2},{7,3},{20,4},{1,5},{22,6},{3,7},{24,8},{13,9},... | collective-permute-start | bytes 1572872 | tf_op jit(solution)/shard_map/ppermute | solution.py:374
  87.0 10.7 %collective-permute-start.12 = (bf16[128,2048]{1,0:T(8,128)(2,1)S(1)}, bf16[128,2048]{1,0:T(8,128)(2,1)S(1)}, u32[]{:S(2)}, u32[]{:S(2)}) collective-permute-start(bf16[128,2048]{1,0:T(8,128)(2,1)S(1)} %get-tuple-element.49), channel_id=1, source_target_pairs={{24,0},{7,1},{26,2},{1,3},{28,4},{3,5},{30,6},{5,7},{0,8},{15,9},{... | collective-permute-start | bytes 1572872 | tf_op jit(solution)/shard_map/ppermute | solution.py:374
  88.7 9.2 %collective-permute-start.13 = (bf16[128,2048]{1,0:T(8,128)(2,1)S(1)}, bf16[128,2048]{1,0:T(8,128)(2,1)S(1)}, u32[]{:S(2)}, u32[]{:S(2)}) collective-permute-start(bf16[128,2048]{1,0:T(8,128)(2,1)S(1)} %get-tuple-element.50), channel_id=1, source_target_pairs={{8,0},{3,1},{10,2},{5,3},{12,4},{7,5},{14,6},{1,7},{16,8},{11,9},{... | collective-permute-start | bytes 1572872 | tf_op jit(solution)/shard_map/ppermute | solution.py:374
